TPU v7x, 32 devices: a whole 2x2x4 slice. The times are simulated.
32 devices in a mesh: group: 4 (over y, x), member: 8 (over z, core).
Axes of the slice: x: 2, y: 2, z: 4, core: 2. Of those that a mesh axis runs over, the one named last changes fastest.
Arguments:
- clips: bfloat16 [32, 14, 64, 640], P(('group', 'member')), may hold values from -4 to 4
- targets: bfloat16 [32, 14, 64, 640], P(('group', 'member')), may hold values from -6 to 6
- timestep: int32 [32], P(('group', 'member')), may hold values from 0 to 999
- identity: int32 [32], P(('group', 'member')), may hold values from 0 to 63
- conv1_weight: bfloat16 [1920, 640], P('member', 'group'), may hold values from -6 to 6
- conv2_weight: bfloat16 [1920, 640], P('member', 'group'), may hold values from -6 to 6
- rate1: bfloat16 [1920, 640], P('member', 'group'), may hold values from 0.029907227 to 0.29882812
- rate2: bfloat16 [1920, 640], P('member', 'group'), may hold values from 0.029907227 to 0.29882812
- time_proj: bfloat16 [1280, 640], replicated, may hold values from -0.15625 to 0.15625
- subject_table: float32 [64, 1280], replicated, may hold values from -6 to 6
Outputs:
- adapted_first: float32 [4, 1920, 640], P('group', 'member')
- adapted_second: float32 [4, 1920, 640], P('group', 'member')
All inputs are finite; a program needn't handle non-finite values.
Results may differ from a plain program's by a relative error of at most 0.0016.
Values may be sent and summed in bfloat16 or wider, within the bound.
No kernel may reach another device: no remote copies, remote signals or barrier semaphores. Data moves between devices by JAX's collectives and lax.ppermute only.
A program may use at most 128 MiB of HBM per device.

v0:
```python
import math

import jax
import jax.numpy as jnp
from jax import lax
from jax.sharding import PartitionSpec as P

GN_GROUPS = 32


def time_bias(step_index, ident, subject_table, time_proj):
    half_width = subject_table.shape[1] // 2
    freqs = jnp.exp(-math.log(10000.0) * jnp.arange(half_width, dtype=jnp.float32) / half_width)
    angles = step_index.astype(jnp.float32) * freqs
    embedding = jnp.concatenate([jnp.cos(angles), jnp.sin(angles)])
    onehot = (jnp.arange(subject_table.shape[0], dtype=jnp.int32) == ident).astype(jnp.float32)
    embedding = embedding + jnp.dot(onehot, subject_table, precision=lax.Precision.HIGHEST)
    activated = jax.nn.silu(embedding).astype(jnp.bfloat16)
    return jnp.dot(activated[None, :], time_proj, preferred_element_type=jnp.float32)[0]


def group_norm(values):
    channels = values.shape[2]
    per_group = channels // GN_GROUPS
    counted = values.shape[0] * values.shape[1] * per_group

    def spread(sums):
        return jnp.repeat(sums.reshape(GN_GROUPS, per_group).sum(axis=1) / counted, per_group)

    centre = spread(values.sum(axis=(0, 1)))
    centred = values - centre
    variance = spread((centred * centred).sum(axis=(0, 1)))
    return centred * lax.rsqrt(variance + 1e-05)


def activate(values):
    return jax.nn.silu(group_norm(values))


def stack_taps(act_values):
    frames, points, channels = act_values.shape
    blank = jnp.zeros((1, points, channels), act_values.dtype)
    before = jnp.concatenate([blank, act_values[:-1]], axis=0)
    after = jnp.concatenate([act_values[1:], blank], axis=0)
    return jnp.concatenate([before, act_values, after], axis=2).reshape(
        frames * points, 3 * channels
    )


def fold_taps(grad_rows, frames, points, channels):
    shaped = grad_rows.reshape(frames, points, 3 * channels)
    blank = jnp.zeros((1, points, channels), jnp.float32)
    from_before = jnp.concatenate([shaped[1:, :, :channels], blank], axis=0)
    from_after = jnp.concatenate([blank, shaped[:-1, :, 2 * channels :]], axis=0)
    return shaped[:, :, channels : 2 * channels] + from_before + from_after


def fold_rows(stacked, portion):
    return jnp.dot(stacked, portion, preferred_element_type=jnp.float32)


def grad_terms(stacked, cotangent, weight_scale):
    product = lax.dot_general(
        stacked, cotangent, (((0,), (0,)), ((), ())), preferred_element_type=jnp.float32
    )
    return weight_scale * product


def shards(
    clips,
    targets,
    timestep,
    identity,
    conv1_weight,
    conv2_weight,
    rate1,
    rate2,
    time_proj,
    subject_table,
):
    frames, points, channels = (clips.shape[1], clips.shape[2], clips.shape[3])
    weight_scale = 1.0 / math.sqrt(3 * channels)
    latent = clips[0].astype(jnp.float32)
    bias_row = time_bias(timestep[0], identity[0], subject_table, time_proj)
    stacked_one = stack_taps(activate(latent).astype(jnp.bfloat16))
    contract_last = (((1,), (1,)), ((), ()))
    own_one, own_two, rate_one, rate_two = (
        lax.all_gather(conv1_weight, "group", axis=1, tiled=True),
        lax.all_gather(conv2_weight, "group", axis=1, tiled=True),
        lax.all_gather(rate1, "group", axis=1, tiled=True),
        lax.all_gather(rate2, "group", axis=1, tiled=True),
    )
    mixed_one = fold_rows(stacked_one, lax.all_gather(own_one, "member", axis=0, tiled=True))
    hidden = (weight_scale * mixed_one + bias_row).reshape(frames, points, channels)
    act_two, backward = jax.vjp(activate, hidden)
    stacked_two = stack_taps(act_two.astype(jnp.bfloat16))
    mixed_two = fold_rows(stacked_two, lax.all_gather(own_two, "member", axis=0, tiled=True))
    output = latent + (weight_scale * mixed_two).reshape(frames, points, channels)
    error = (
        (output - targets[0].astype(jnp.float32))
        .reshape(frames * points, channels)
        .astype(jnp.bfloat16)
    )
    grad_two = lax.psum_scatter(
        grad_terms(stacked_two, error, weight_scale), "member", scatter_dimension=0, tiled=True
    )
    back_rows = lax.dot_general(
        error,
        lax.all_gather(own_two, "member", axis=0, tiled=True),
        contract_last,
        preferred_element_type=jnp.float32,
    )
    grad_act = fold_taps(weight_scale * back_rows, frames, points, channels)
    grad_hidden = backward(grad_act)[0].reshape(frames * points, channels).astype(jnp.bfloat16)
    grad_one = lax.psum_scatter(
        grad_terms(stacked_one, grad_hidden, weight_scale),
        "member",
        scatter_dimension=0,
        tiled=True,
    )
    adapted_one = own_one.astype(jnp.float32) - rate_one.astype(jnp.float32) * grad_one
    adapted_two = own_two.astype(jnp.float32) - rate_two.astype(jnp.float32) * grad_two
    return (adapted_one[None], adapted_two[None])


def solution(mesh):
    return jax.shard_map(
        shards,
        mesh=mesh,
        in_specs=(
            P(("group", "member"), None, None, None),
            P(("group", "member"), None, None, None),
            P(("group", "member")),
            P(("group", "member")),
            P("member", "group"),
            P("member", "group"),
            P("member", "group"),
            P("member", "group"),
            P(),
            P(),
        ),
        out_specs=(P("group", "member", None), P("group", "member", None)),
        check_vma=False,
    )
```

profile of v0, /device:TPU:0, one launch (start us, length us, event | category | flops | bytes accessed | tf_op | source)
XLA Modules:
  0.0 220.9 jit_solution(18239354853555878876)
XLA Ops:
  7.2 11.2 %all_gather.19 = bf16[240,640]{0,1:T(8,128)(2,1)S(1)} all-gather(bf16[240,160]{0,1:T(8,128)(2,1)} %param.14), channel_id=1, replica_groups=mesh['group'=4,'member'=8] {'group'}, dimensions={1}, use_global_device_ids=true | all-gather | bytes 384000 | tf_op jit(solution)/shard_map/all_gather | solution.py:88
  18.4 0.9 copy.24
  19.4 8.9 %all_gather.22 = bf16[240,640]{0,1:T(8,128)(2,1)S(1)} all-gather(bf16[240,160]{0,1:T(8,128)(2,1)} %param.15), channel_id=1, replica_groups=mesh['group'=4,'member'=8] {'group'}, dimensions={1}, use_global_device_ids=true | all-gather | bytes 384000 | tf_op jit(solution)/shard_map/all_gather | solution.py:89
  28.3 0.9 copy.27
  29.9 0.4 multiply_reduce_fusion.2
  32.3 0.3 convolution_reduce_fusion.1
  32.7 0.9 copy-done.3
  33.5 0.7 multiply_convert_fusion.1
  34.5 1.0 copy-done.4
  35.8 1.9 fusion.5
  37.7 14.5 %all-gather.3.cloned.1.call-done = bf16[1920,640]{1,0:T(8,128)(2,1)} async-done(((bf16[240,640]{1,0:T(8,128)(2,1)}), bf16[1920,640]{1,0:T(8,128)(2,1)}) %all-gather.3.cloned.1.call-update) | async-done | bytes 2457616 | tf_op jit(solution)/shard_map/all_gather | solution.py:93
  52.2 7.1 %fusion.26 = (f32[640]{0:T(1024)S(1)}, f32[896,640]{1,0:T(8,128)}) fusion(f32[640]{0:T(1024)S(1)} %convolution_reduce_fusion.1, bf16[896,1920]{1,0:T(8,128)(2,1)} %bitcast.45, bf16[1920,640]{1,0:T(8,128)(2,1)} %all-gather.3.cloned.1.call-done), kind=kOutput, calls=%fused_computation.59 | convolution fusion | flops 2203729408 | bytes 8197120 | tf_op jit(solution)/shard_map/dot_general | solution.py:59
  59.7 2.0 multiply_reduce_fusion.1
  62.1 2.3 %multiply_convert_fusion = bf16[14,64,640]{2,1,0:T(8,128)(2,1)S(1)} fusion(f32[14,64,640]{2,1,0:T(8,128)} %bitcast.39, f32[640]{0:T(1024)S(1)} %rsqrt.28, f32[640]{0:T(1024)S(1)} %sub.42), kind=kLoop, calls=%fused_computation.25 | loop fusion | flops 4014080 | bytes 3445760 | tf_op jit(solution)/shard_map/convert_element_type | solution.py:96
  64.8 1.9 fusion.7
  66.7 19.3 %all-gather.5.cloned.1.call-done = bf16[1920,640]{1,0:T(8,128)(2,1)} async-done(((bf16[240,640]{1,0:T(8,128)(2,1)}), bf16[1920,640]{1,0:T(8,128)(2,1)}) %all-gather.5.cloned.1.call-update) | async-done | bytes 2457616 | tf_op jit(solution)/shard_map/all_gather | solution.py:97
  86.0 6.4 %fusion.11 = bf16[896,640]{1,0:T(8,128)(2,1)S(1)} fusion(bf16[896,640]{1,0:T(8,128)(2,1)} %bitcast.48, bf16[1,14,64,640]{3,2,1,0:T(8,128)(2,1)} %param.10, bf16[896,1920]{1,0:T(8,128)(2,1)} %bitcast.46, bf16[1920,640]{1,0:T(8,128)(2,1)} %all-gather.5.cloned.1.call-done), kind=kOutput, calls=%fused_computation.20 | convolution fusion | flops 2205450240 | bytes 9338880 | tf_op jit(solution)/shard_map/dot_general | solution.py:59
  92.5 1.0 copy-done.12
  93.5 5.4 %convolution_multiply_fusion.1 = f32[1920,640]{1,0:T(8,128)} fusion(bf16[896,1920]{1,0:T(8,128)(2,1)S(1)} %bitcast.47, bf16[896,640]{1,0:T(8,128)(2,1)S(1)} %fusion.11), kind=kOutput, calls=%fused_computation.8 | convolution fusion | flops 2203238400 | bytes 9502720 | tf_op jit(solution)/shard_map/dot_general | solution.py:63
  99.1 5.0 %convolution_multiply_fusion = f32[896,1920]{1,0:T(8,128)S(1)} fusion(bf16[896,640]{1,0:T(8,128)(2,1)} %copy-done.12, bf16[1920,640]{1,0:T(8,128)(2,1)} %all-gather.5.cloned.1.call-done), kind=kOutput, calls=%fused_computation.7 | convolution fusion | flops 2203729920 | bytes 10485760 | tf_op jit(solution)/shard_map/dot_general | solution.py:107
  104.2 0.5 fusion.23
  104.7 1.1 copy-done.1
  105.9 2.6 %multiply_reduce_fusion = (f32[640]{0:T(1024)S(1)}, f32[14,64,640]{2,1,0:T(8,128)}) fusion(f32[14,64,640]{2,1,0:T(8,128)S(1)} %bitcast.42, f32[640]{0:T(1024)S(1)} %sub.42, f32[640]{0:T(1024)S(1)} %rsqrt.28, f32[13,64,640]{2,1,0:T(8,128)S(1)} %get-tuple-element.5, f32[13,64,640]{2,1,0:T(8,128)S(1)} %get-tuple-element.4, f32[14,64,1920]{2,1,0:T(8,128)S(1)} %bitcast.44), kind=kLoop, calls=%fused_computation.24 | loop fusion | flops 8600960 | bytes 11148800 | tf_op jit(solution)/shard_map/transpose(jvp())/reduce_sum | solution.py:33
  109.0 2.9 %fusion.13 = f32[640]{0:T(1024)S(1)} fusion(f32[640]{0:T(1024)S(1)} %reshape.93, f32[14,64,640]{2,1,0:T(8,128)} %bitcast.40, f32[640]{0:T(1024)S(1)} %sub.42, f32[14,64,640]{2,1,0:T(8,128)} %get-tuple-element.3, f32[640]{0:T(1024)S(1)} %rsqrt.28), kind=kLoop, calls=%fused_computation.37 | loop fusion | flops 3440000 | bytes 4597760 | tf_op jit(solution)/shard_map/transpose(jvp())/reduce_sum | solution.py:31
  112.2 8.5 %bitcast_multiply_fusion = f32[1920,640]{1,0:T(8,128)} fusion(f32[640]{0:T(1024)S(1)} %reshape.94, f32[14,64,640]{2,1,0:T(8,128)} %get-tuple-element.3, f32[14,64,640]{2,1,0:T(8,128)} %bitcast.41, f32[640]{0:T(1024)S(1)} %reshape.93, f32[640]{0:T(1024)S(1)} %rsqrt.28, f32[640]{0:T(1024)S(1)} %sub.42, bf16[13,64,640]{2,1,0:T(8,128)(2,1)} %copy-done.5, ...), kind=kOutput, calls=%fused_computation.6 | convolution fusion | flops 2224455680 | bytes 12789760 | tf_op jit(solution)/shard_map/dot_general | solution.py:63
  120.8 0.9 copy-done.10
  121.6 9.4 %all_gather.24 = bf16[240,640]{0,1:T(8,128)(2,1)S(1)} all-gather(bf16[240,160]{0,1:T(8,128)(2,1)S(1)} %copy-done.10), channel_id=1, replica_groups=mesh['group'=4,'member'=8] {'group'}, dimensions={1}, use_global_device_ids=true | all-gather | bytes 384000 | tf_op jit(solution)/shard_map/all_gather | solution.py:91
  131.3 9.5 %all_gather.20 = bf16[240,640]{0,1:T(8,128)(2,1)S(1)} all-gather(bf16[240,160]{0,1:T(8,128)(2,1)S(1)} %copy-done.11), channel_id=1, replica_groups=mesh['group'=4,'member'=8] {'group'}, dimensions={1}, use_global_device_ids=true | all-gather | bytes 384000 | tf_op jit(solution)/shard_map/all_gather | solution.py:90
  141.0 14.0 %reduce-scatter.5.cloned.1.call-done = f32[240,640]{1,0:T(8,128)} async-done(((f32[1920,640]{1,0:T(8,128)}), f32[240,640]{1,0:T(8,128)}) %reduce-scatter.5.cloned.1.call-update) | async-done | bytes 614416 | tf_op jit(solution)/shard_map/reduce_scatter | solution.py:104
  155.0 2.0 subtract_bitcast_fusion
  157.0 55.4 %reduce-scatter.3.cloned.1.call-done = f32[240,640]{1,0:T(8,128)} async-done(((f32[1920,640]{1,0:T(8,128)}), f32[240,640]{1,0:T(8,128)}) %reduce-scatter.3.cloned.1.call-update) | async-done | bytes 614416 | tf_op jit(solution)/shard_map/reduce_scatter | solution.py:115
  212.3 2.0 subtract_bitcast_fusion.1
  (68 shorter events, 4.7 us)
Async XLA Ops:
  7.2 25.2 %copy-start = (bf16[1280,640]{1,0:T(8,128)(2,1)S(1)}, bf16[1280,640]{1,0:T(8,128)(2,1)}, u32[]{:S(2)}) copy-start(bf16[1280,640]{1,0:T(8,128)(2,1)} %param.18) | copy-start | bytes 4915204
  7.2 22.1 %copy-start.2 = (bf16[1,14,64,640]{3,2,1,0:T(8,128)(2,1)S(1)}, bf16[1,14,64,640]{3,2,1,0:T(8,128)(2,1)}, u32[]{:S(2)}) copy-start(bf16[1,14,64,640]{3,2,1,0:T(8,128)(2,1)} %param.10) | copy-start | bytes 3440644
  7.2 45.0 %all-gather.3.cloned.1.call-start = ((), (), s32[]{:S(2)}) async-start(), calls=%async_computation.2 | async-start | bytes 2764800 | tf_op jit(solution)/shard_map/all_gather | solution.py:93
  18.4 13.4 %copy-start.9 = (f32[64,1280]{1,0:T(8,128)S(1)}, f32[64,1280]{1,0:T(8,128)}, u32[]{:S(2)}) copy-start(f32[64,1280]{1,0:T(8,128)} %param.19) | copy-start | bytes 983044
  19.3 66.7 %all-gather.5.cloned.1.call-start = ((), (), s32[]{:S(2)}) async-start(), calls=%async_computation.3 | async-start | bytes 2764800 | tf_op jit(solution)/shard_map/all_gather | solution.py:97
  29.2 125.8 %reduce-scatter.5.cloned.1.call-start = ((), (), s32[]{:S(2)}) async-start(), calls=%async_computation.5 | async-start | bytes 5529600 | tf_op jit(solution)/shard_map/reduce_scatter | solution.py:104
  32.3 1.3 copy-start.3
  34.5 1.0 copy-start.4
  34.5 1.3 copy-start.5
  86.0 7.5 %copy-start.6 = (bf16[14,64,1920]{2,1,0:T(8,128)(2,1)S(1)}, bf16[14,64,1920]{2,1,0:T(8,128)(2,1)}, u32[]{:S(2)}) copy-start(bf16[14,64,1920]{2,1,0:T(8,128)(2,1)} %fusion.7) | copy-start | bytes 10321924
  92.5 1.0 copy-start.12
  98.9 113.4 %reduce-scatter.3.cloned.1.call-start = ((), (), s32[]{:S(2)}) async-start(), calls=%async_computation.4 | async-start | bytes 5529600 | tf_op jit(solution)/shard_map/reduce_scatter | solution.py:115
  104.2 1.7 copy-start.1
  120.7 0.9 copy-start.10
  120.7 10.5 %copy-start.11 = (bf16[240,160]{0,1:T(8,128)(2,1)S(1)}, bf16[240,160]{0,1:T(8,128)(2,1)}, u32[]{:S(2)}) copy-start(bf16[240,160]{0,1:T(8,128)(2,1)} %param.16) | copy-start | bytes 230404
  120.7 34.2 %copy-start.8 = (bf16[240,640]{1,0:T(8,128)(2,1)S(1)}, bf16[240,640]{1,0:T(8,128)(2,1)}, u32[]{:S(2)}) copy-start(bf16[240,640]{1,0:T(8,128)(2,1)} %copy.27) | copy-start | bytes 921604
  121.6 90.7 %copy-start.7 = (bf16[240,640]{1,0:T(8,128)(2,1)S(1)}, bf16[240,640]{1,0:T(8,128)(2,1)}, u32[]{:S(2)}) copy-start(bf16[240,640]{1,0:T(8,128)(2,1)} %copy.24) | copy-start | bytes 921604
Sparse Core Ops, SparseCore 0:
  19.4 32.7 all-gather.2
  54.4 31.5 all-gather.4
  99.0 55.8 reduce-scatter.4
  157.1 55.1 reduce-scatter.2
where the time goes:
time: 221 us
  waiting for transfers between devices  103 us (47%)
  blocking collectives  39 us (18%)
  matrix products  33 us (15%)
  other arithmetic  19.8 us (9%)
  between operations  15.4 us (7%)
  local copies, waits for them, and re-layouts  10.2 us (5%)
    reduce_scatter x1, waiting for transfers between devices, shards(): lax.psum_scatter(grad_terms(stacked_one, grad_hidden, weight_scale), 'mem...  55.4 us
    all_gather x1, waiting for transfers between devices, shards(): lax.all_gather(own_two, 'member', axis=0, tiled=True)  19.3 us
    all_gather x1, waiting for transfers between devices, shards(): lax.all_gather(own_one, 'member', axis=0, tiled=True)  14.5 us
    reduce_scatter x1, waiting for transfers between devices, shards(): lax.psum_scatter(grad_terms(stacked_two, error, weight_scale), 'member',...  14 us
    dot_general x2, matrix products, grad_terms(): lax.dot_general(stacked, cotangent, (((0,), (0,)), ((), ())), preferred_e...  13.9 us
    dot_general x2, matrix products, fold_rows(): return jnp.dot(stacked, portion, preferred_element_type=jnp.float32)  13.5 us
    all_gather x1, blocking collectives, shards(): lax.all_gather(conv1_weight, 'group', axis=1, tiled=True)  11.2 us
    all_gather x1, blocking collectives, shards(): lax.all_gather(rate1, 'group', axis=1, tiled=True)  9.52 us
  transfers between devices with their start and end apart: 4, of which 4 were waited for; matrix products, arithmetic and copies ran while one was open for 19% of the time, Pallas kernels for 0%

commit v1 on v0

--- a/solution.py
+++ b/solution.py
@@ -55,10 +55,6 @@
     return shaped[:, :, channels : 2 * channels] + from_before + from_after
 
 
-def fold_rows(stacked, portion):
-    return jnp.dot(stacked, portion, preferred_element_type=jnp.float32)
-
-
 def grad_terms(stacked, cotangent, weight_scale):
     product = lax.dot_general(
         stacked, cotangent, (((0,), (0,)), ((), ())), preferred_element_type=jnp.float32
@@ -66,7 +62,42 @@
     return weight_scale * product
 
 
+def swap(value, axis, size, offset):
+    return lax.ppermute(value, axis, [(i, i ^ offset) for i in range(size)])
+
+
+def gather_xor(value, axis, size, stride):
+    count = size // stride
+    place = lax.axis_index(axis) // stride
+    blocks = [value] + [swap(value, axis, size, k * stride) for k in range(1, count)]
+    bit = 1
+    while bit < count:
+        odd = (place & bit) != 0
+        blocks = [
+            jnp.where(odd, blocks[i ^ bit], blocks[i]) for i in range(count)
+        ]
+        bit *= 2
+    return blocks
+
+
+def sum_to_owner(grad, axis, size):
+    rows, cols = grad.shape[0] // size, grad.shape[1]
+    me = lax.axis_index(axis)
+    core, place = me % 2, me // 2
+    shaped = grad.reshape(size // 2, 2, rows, cols)
+    away = lax.dynamic_index_in_dim(shaped, 1 - core, 1, keepdims=False).astype(jnp.bfloat16)
+    home = lax.dynamic_index_in_dim(shaped, core, 1, keepdims=False)
+    pair = home + swap(away, axis, size, 1).astype(jnp.float32)
+    total = lax.dynamic_index_in_dim(pair, place, 0, keepdims=False)
+    for k in reversed(range(1, size // 2)):
+        piece = lax.dynamic_index_in_dim(pair, place ^ k, 0, keepdims=False)
+        total = total + swap(piece.astype(jnp.bfloat16), axis, size, 2 * k).astype(jnp.float32)
+    return total
+
+
 def shards(
+    n_group,
+    n_member,
     clips,
     targets,
     timestep,
@@ -80,52 +111,60 @@
 ):
     frames, points, channels = (clips.shape[1], clips.shape[2], clips.shape[3])
     weight_scale = 1.0 / math.sqrt(3 * channels)
+    me = lax.axis_index("member")
+    rows = conv1_weight.shape[0]
+    contract_last = (((1,), (1,)), ((), ()))
+    gathered = lax.all_gather(conv1_weight, ("member", "group"), axis=0, tiled=False)
+    full_one = (
+        gathered.reshape(n_member, n_group, rows, conv1_weight.shape[1])
+        .transpose(0, 2, 1, 3)
+        .reshape(3 * channels, channels)
+    )
+    own_two = jnp.concatenate(gather_xor(conv2_weight, "group", n_group, 1), axis=1)
+    same_core = jnp.stack(gather_xor(own_two, "member", n_member, 2))
+    other_core = swap(same_core, "member", n_member, 1)
+    odd = (me % 2) != 0
+    full_two = jnp.stack(
+        [jnp.where(odd, other_core, same_core), jnp.where(odd, same_core, other_core)], axis=1
+    ).reshape(3 * channels, channels)
+
     latent = clips[0].astype(jnp.float32)
     bias_row = time_bias(timestep[0], identity[0], subject_table, time_proj)
     stacked_one = stack_taps(activate(latent).astype(jnp.bfloat16))
-    contract_last = (((1,), (1,)), ((), ()))
-    own_one, own_two, rate_one, rate_two = (
-        lax.all_gather(conv1_weight, "group", axis=1, tiled=True),
-        lax.all_gather(conv2_weight, "group", axis=1, tiled=True),
-        lax.all_gather(rate1, "group", axis=1, tiled=True),
-        lax.all_gather(rate2, "group", axis=1, tiled=True),
-    )
-    mixed_one = fold_rows(stacked_one, lax.all_gather(own_one, "member", axis=0, tiled=True))
+    mixed_one = jnp.dot(stacked_one, full_one, preferred_element_type=jnp.float32)
     hidden = (weight_scale * mixed_one + bias_row).reshape(frames, points, channels)
     act_two, backward = jax.vjp(activate, hidden)
     stacked_two = stack_taps(act_two.astype(jnp.bfloat16))
-    mixed_two = fold_rows(stacked_two, lax.all_gather(own_two, "member", axis=0, tiled=True))
+    mixed_two = jnp.dot(stacked_two, full_two, preferred_element_type=jnp.float32)
     output = latent + (weight_scale * mixed_two).reshape(frames, points, channels)
     error = (
         (output - targets[0].astype(jnp.float32))
         .reshape(frames * points, channels)
         .astype(jnp.bfloat16)
     )
-    grad_two = lax.psum_scatter(
-        grad_terms(stacked_two, error, weight_scale), "member", scatter_dimension=0, tiled=True
-    )
+    local_two = grad_terms(stacked_two, error, weight_scale)
+    grad_two = sum_to_owner(local_two, "member", n_member)
+    rates, error = lax.optimization_barrier((jnp.concatenate([rate1, rate2]), error))
+    rates = jnp.concatenate(gather_xor(rates, "group", n_group, 1), axis=1)
+    rate_one, rate_two = rates[:rows], rates[rows:]
     back_rows = lax.dot_general(
-        error,
-        lax.all_gather(own_two, "member", axis=0, tiled=True),
-        contract_last,
-        preferred_element_type=jnp.float32,
+        error, full_two, contract_last, preferred_element_type=jnp.float32
     )
     grad_act = fold_taps(weight_scale * back_rows, frames, points, channels)
     grad_hidden = backward(grad_act)[0].reshape(frames * points, channels).astype(jnp.bfloat16)
-    grad_one = lax.psum_scatter(
-        grad_terms(stacked_one, grad_hidden, weight_scale),
-        "member",
-        scatter_dimension=0,
-        tiled=True,
+    grad_one = sum_to_owner(
+        grad_terms(stacked_one, grad_hidden, weight_scale), "member", n_member
     )
+    own_one = lax.dynamic_slice_in_dim(full_one, me * rows, rows, 0)
     adapted_one = own_one.astype(jnp.float32) - rate_one.astype(jnp.float32) * grad_one
     adapted_two = own_two.astype(jnp.float32) - rate_two.astype(jnp.float32) * grad_two
     return (adapted_one[None], adapted_two[None])
 
 
 def solution(mesh):
+    n_group, n_member = mesh.shape["group"], mesh.shape["member"]
     return jax.shard_map(
-        shards,
+        lambda *arrays: shards(n_group, n_member, *arrays),
         mesh=mesh,
         in_specs=(
             P(("group", "member"), None, None, None),

time: 221 us -> 222 us (level)
  blocking collectives: 39 us -> 0 us
  local copies, waits for them, and re-layouts: 10.2 us -> 48.6 us
  starting transfers between devices: 0.34 us -> 26.4 us
  waiting for transfers between devices: 103 us -> 83.9 us
  matrix products: 33 us -> 21.3 us
  other arithmetic: 19.8 us -> 25.5 us
    reduce_scatter x2 -> x0, waiting for transfers between devices: 69.3 us -> none  [the longest x1 55.4 us: shards(): lax.psum_scatter(grad_terms(stacked_one, grad_hidden, weight_scale), 'mem...]
    ppermute x0 -> x18, waiting for transfers between devices: none -> 63.4 us  [swap(): return lax.ppermute(value, axis, [(i, i ^ offset) for i in range(size)])]
    all_gather x4 -> x0, blocking collectives: 39 us -> none  [the longest x1 11.2 us: shards(): lax.all_gather(conv1_weight, 'group', axis=1, tiled=True)]
    ppermute x0 -> x18, starting transfers between devices: none -> 26.4 us  [swap(): return lax.ppermute(value, axis, [(i, i ^ offset) for i in range(size)])]
    all_gather x2 -> x1, waiting for transfers between devices: 33.8 us -> 19.7 us  [shards(): lax.all_gather(conv1_weight, ('member', 'group'), axis=0, tiled=False)]
    reshape x0 -> x2, local copies, waits for them, and re-layouts: none -> 10.6 us  [the longest x1 5.82 us: shards(): full_one = gathered.reshape(n_member, n_group, rows, conv1_weight.shape[1...]
    dynamic_slice x0 -> x4, local copies, waits for them, and re-layouts: none -> 9.34 us  [sum_to_owner(): home = lax.dynamic_index_in_dim(shaped, core, 1, keepdims=False)]
    dot_general x3, matrix products: 18.5 us -> 11.7 us  [the longest x1 5.72 us: shards(): jnp.dot(stacked_one, full_one, preferred_element_type=jnp.float32)]
  transfers between devices with their start and end apart: 4 -> 19, of which waited for: 4 -> 7; matrix products, arithmetic and copies ran while one was open for 19% -> 26% of each run, Pallas kernels for 0% -> 0%
where the time goes in v1:
time: 222 us
  waiting for transfers between devices  83.9 us (38%)
  local copies, waits for them, and re-layouts  48.6 us (22%)
  starting transfers between devices  26.4 us (12%)
  other arithmetic  25.5 us (11%)
  matrix products  21.3 us (10%)
  between operations  16 us (7%)
    ppermute x18, waiting for transfers between devices, swap(): return lax.ppermute(value, axis, [(i, i ^ offset) for i in range(size)])  63.4 us
    ppermute x18, starting transfers between devices, swap(): return lax.ppermute(value, axis, [(i, i ^ offset) for i in range(size)])  26.4 us
    all_gather x1, waiting for transfers between devices, shards(): lax.all_gather(conv1_weight, ('member', 'group'), axis=0, tiled=False)  19.7 us
    unnamed x64, local copies, waits for them, and re-layouts  10.1 us
    dynamic_slice x4, local copies, waits for them, and re-layouts, sum_to_owner(): home = lax.dynamic_index_in_dim(shaped, core, 1, keepdims=False)  9.34 us
    dot_general x2, matrix products, grad_terms(): lax.dot_general(stacked, cotangent, (((0,), (0,)), ((), ())), preferred_e...  9.07 us
    ppermute x3, local copies, waits for them, and re-layouts, swap(): return lax.ppermute(value, axis, [(i, i ^ offset) for i in range(size)])  6.46 us
    reshape x1, local copies, waits for them, and re-layouts, shards(): full_one = gathered.reshape(n_member, n_group, rows, conv1_weight.shape[1...  5.82 us
  transfers between devices with their start and end apart: 19, of which 7 were waited for; matrix products, arithmetic and copies ran while one was open for 26% of the time, Pallas kernels for 0%

profile of v1, /device:TPU:0, one launch (start us, length us, event | category | flops | bytes accessed | tf_op | source)
XLA Modules:
  0.0 221.7 jit_solution(3963739433380443269)
XLA Ops:
  8.0 3.0 %collective-permute-start.1 = (bf16[240,160]{0,1:T(8,128)(2,1)}, bf16[240,160]{0,1:T(8,128)(2,1)S(1)}, u32[]{:S(2)}, u32[]{:S(2)}) collective-permute-start(bf16[240,160]{0,1:T(8,128)(2,1)} %param.15), channel_id=1, source_target_pairs={{0,16},{8,24},{16,0},{24,8},{1,17},{9,25},{17,1},{25,9},{2,18},{10... | collective-permute-start | bytes 230408 | tf_op jit(solution)/shard_map/ppermute | solution.py:66
  18.3 2.1 collective-permute-start.5
  20.4 2.6 %collective-permute-start.4 = (bf16[240,640]{0,1:T(8,128)(2,1)S(1)}, bf16[240,640]{0,1:T(8,128)(2,1)S(1)}, u32[]{:S(2)}, u32[]{:S(2)}) collective-permute-start(bf16[240,640]{0,1:T(8,128)(2,1)S(1)} %pad_maximum_fusion.3), channel_id=1, source_target_pairs={{0,4},{1,5},{2,6},{3,7},{4,0},{5,1},{6,2},{7,3},{8,12},{9,13},{10,... | collective-permute-start | bytes 921608 | tf_op jit(solution)/shard_map/ppermute | solution.py:66
  24.1 10.5 %collective-permute-done.5 = bf16[240,640]{0,1:T(8,128)(2,1)S(1)} collective-permute-done((bf16[240,640]{0,1:T(8,128)(2,1)S(1)}, bf16[240,640]{0,1:T(8,128)(2,1)S(1)}, u32[]{:S(2)}, u32[]{:S(2)}) %collective-permute-start.5) | collective-permute-done | bytes 307232 | tf_op jit(solution)/shard_map/ppermute | solution.py:66
  34.6 13.1 %collective-permute-done.4 = bf16[240,640]{0,1:T(8,128)(2,1)S(1)} collective-permute-done((bf16[240,640]{0,1:T(8,128)(2,1)S(1)}, bf16[240,640]{0,1:T(8,128)(2,1)S(1)}, u32[]{:S(2)}, u32[]{:S(2)}) %collective-permute-start.4) | collective-permute-done | bytes 307232 | tf_op jit(solution)/shard_map/ppermute | solution.py:66
  51.9 2.1 fusion.5
  57.4 2.1 pad_maximum_fusion
  59.4 4.4 %copy.34 = bf16[4,2,240,640]{3,2,1,0:T(8,128)(2,1)} copy(bf16[4,2,240,640]{2,3,0,1:T(8,128)(2,1)} %pad_maximum_fusion) | data formatting | bytes 4915200 | tf_op jit(solution)/shard_map/stack | solution.py:127
  63.8 19.7 %all-gather.4.cloned.1.call-done = bf16[32,240,160]{1,2,0:T(8,128)(2,1)} async-done(((bf16[1,240,160]{1,2,0:T(8,128)(2,1)}), bf16[32,240,160]{1,2,0:T(8,128)(2,1)}) %all-gather.4.cloned.1.call-update) | async-done | bytes 2457616 | tf_op jit(solution)/shard_map/all_gather | solution.py:117
  83.6 4.8 %copy.46 = bf16[8,4,240,160]{2,0,3,1:T(8,128)(2,1)} copy(bf16[8,4,240,160]{2,3,1,0:T(8,128)(2,1)} %bitcast.129) | data formatting | bytes 4915200 | tf_op jit(solution)/shard_map/reshape | solution.py:119
  88.4 5.8 %reshape.109 = bf16[1920,640]{0,1:T(8,128)(2,1)} reshape(bf16[8,240,4,160]{1,0,3,2:T(8,128)(2,1)} %bitcast.119) | data formatting | bytes 4915200 | tf_op jit(solution)/shard_map/reshape | solution.py:121
  94.2 5.7 %fusion.44 = (f32[640]{0:T(1024)S(1)}, f32[896,640]{1,0:T(8,128)S(1)}) fusion(f32[640]{0:T(1024)S(1)} %convolution_reduce_fusion.1, bf16[896,1920]{1,0:T(8,128)(2,1)} %bitcast.122, bf16[1920,640]{0,1:T(8,128)(2,1)} %reshape.109), kind=kOutput, calls=%fused_computation.121 | convolution fusion | flops 2203729408 | bytes 8197120 | tf_op jit(solution)/shard_map/dot_general | solution.py:134
  104.4 3.0 %fusion.11 = bf16[896,640]{1,0:T(8,128)(2,1)S(1)} fusion(bf16[896,640]{1,0:T(8,128)(2,1)S(1)} %bitcast.133, bf16[1,14,64,640]{3,2,1,0:T(8,128)(2,1)S(1)} %copy-done.3, bf16[896,1920]{1,0:T(8,128)(2,1)S(1)} %bitcast.123, bf16[1920,640]{1,0:T(8,128)(2,1)S(1)} %bitcast.130), kind=kOutput, calls=%fused_computation.26 | convolution fusion | flops 2205450240 | bytes 9338880 | tf_op jit(solution)/shard_map/dot_general | solution.py:138
  107.4 3.2 %convolution_multiply_fusion.1 = f32[1920,640]{1,0:T(8,128)S(1)} fusion(bf16[896,1920]{1,0:T(8,128)(2,1)S(1)} %bitcast.124, bf16[896,640]{1,0:T(8,128)(2,1)S(1)} %fusion.11), kind=kOutput, calls=%fused_computation.8 | convolution fusion | flops 2203238400 | bytes 9502720 | tf_op jit(solution)/shard_map/dot_general | solution.py:59
  113.4 3.0 %convolution_multiply_fusion = f32[896,1920]{1,0:T(8,128)S(1)} fusion(bf16[896,640]{1,0:T(8,128)(2,1)S(1)} %fusion.11, bf16[1920,640]{1,0:T(8,128)(2,1)S(1)} %bitcast.131), kind=kOutput, calls=%fused_computation.7 | convolution fusion | flops 2203729920 | bytes 10485760 | tf_op jit(solution)/shard_map/dot_general | solution.py:150
  116.9 2.6 %multiply_reduce_fusion = (f32[640]{0:T(1024)S(1)}, f32[14,64,640]{2,1,0:T(8,128)}) fusion(f32[14,64,640]{2,1,0:T(8,128)S(1)} %bitcast.116, f32[640]{0:T(1024)S(1)} %sub.54, f32[640]{0:T(1024)S(1)} %rsqrt.28, f32[13,64,640]{2,1,0:T(8,128)S(1)} %get-tuple-element.13, f32[13,64,640]{2,1,0:T(8,128)S(1)} %get-tuple-element.12, f32[14,64,1920]{2,1,0:T(8,128)S(1)} %bitcast.121), kind=kLoop, calls=%fused_computation.30 | loop fusion | flops 8600960 | bytes 11148800 | tf_op jit(solution)/shard_map/transpose(jvp())/reduce_sum | solution.py:33
  120.1 2.1 fusion.25
  122.6 5.9 %bitcast_multiply_fusion = f32[1920,640]{1,0:T(8,128)S(1)} fusion(f32[640]{0:T(1024)S(1)} %reshape.120, f32[14,64,640]{2,1,0:T(8,128)} %get-tuple-element.11, f32[14,64,640]{2,1,0:T(8,128)S(1)} %bitcast.118, f32[640]{0:T(1024)S(1)} %reshape.119, f32[640]{0:T(1024)S(1)} %rsqrt.28, f32[640]{0:T(1024)S(1)} %sub.54, bf16[13,64,640]{2,1,0:T(8,128)(2,1)} %copy-done.6, ...), kind=kOutput, calls=%fused_computation.6 | convolution fusion | flops 2224455680 | bytes 12789760 | tf_op jit(solution)/shard_map/dot_general | solution.py:59
  128.5 2.2 copy-done.15
  137.5 2.1 copy.38
  139.6 3.3 %constant_dynamic-slice_fusion.1 = f32[4,1,240,640]{3,2,1,0:T(8,128)} fusion(f32[4,2,240,640]{3,2,1,0:T(8,128)} %bitcast.128, s32[]{:T(128)S(6)} %select_n.210), kind=kLoop, calls=%fused_computation.105 | loop fusion | bytes 4915204 | tf_op jit(solution)/shard_map/jit(dynamic_index_in_dim)/dynamic_slice | solution.py:89
  142.9 2.1 copy.35
  145.0 2.4 %copy.40 = bf16[4,240,640]{1,2,0:T(8,128)(2,1)} copy(bf16[4,240,640]{2,1,0:T(8,128)(2,1)} %collective-permute-done.14) | data formatting | bytes 2457600 | tf_op jit(solution)/shard_map/ppermute | solution.py:66
  147.4 2.4 %bitcast_add_fusion = f32[4,240,640]{1,2,0:T(8,128)S(1)} fusion(f32[4,1,240,640]{2,3,0,1:T(8,128)} %copy.38, bf16[4,240,640]{1,2,0:T(8,128)(2,1)} %copy.40), kind=kLoop, calls=%fused_computation.16 | loop fusion | flops 1228800 | bytes 6144000 | tf_op jit(solution)/shard_map/add | solution.py:90
  152.2 2.2 %collective-permute-start.15 = (bf16[240,640]{0,1:T(8,128)(2,1)}, bf16[240,640]{0,1:T(8,128)(2,1)}, u32[]{:S(2)}, u32[]{:S(2)}) collective-permute-start(bf16[240,640]{0,1:T(8,128)(2,1)} %get-tuple-element.14), channel_id=1, source_target_pairs={{0,6},{1,7},{2,4},{3,5},{4,2},{5,3},{6,0},{7,1},{8,14},{9,15},{10,... | collective-permute-start | bytes 921608 | tf_op jit(solution)/shard_map/ppermute | solution.py:66
  154.5 2.4 %copy.37 = bf16[4,240,640]{1,2,0:T(8,128)(2,1)} copy(bf16[4,240,640]{2,1,0:T(8,128)(2,1)} %collective-permute-done.10) | data formatting | bytes 2457600 | tf_op jit(solution)/shard_map/ppermute | solution.py:66
  158.7 2.2 collective-permute-start.16
  160.9 2.2 %collective-permute-start.11 = (bf16[240,640]{0,1:T(8,128)(2,1)S(1)}, bf16[240,640]{0,1:T(8,128)(2,1)S(1)}, u32[]{:S(2)}, u32[]{:S(2)}) collective-permute-start(bf16[240,640]{0,1:T(8,128)(2,1)S(1)} %get-tuple-element.17), channel_id=1, source_target_pairs={{0,6},{1,7},{2,4},{3,5},{4,2},{5,3},{6,0},{7,1},{8,14},{9,15},{10,... | collective-permute-start | bytes 921608 | tf_op jit(solution)/shard_map/ppermute | solution.py:66
  165.1 6.4 %collective-permute-start.12 = (bf16[240,640]{0,1:T(8,128)(2,1)S(1)}, bf16[240,640]{0,1:T(8,128)(2,1)S(1)}, u32[]{:S(2)}, u32[]{:S(2)}) collective-permute-start(bf16[240,640]{0,1:T(8,128)(2,1)S(1)} %get-tuple-element.19), channel_id=1, source_target_pairs={{0,4},{1,5},{2,6},{3,7},{4,0},{5,1},{6,2},{7,3},{8,12},{9,13},{10,... | collective-permute-start | bytes 921608 | tf_op jit(solution)/shard_map/ppermute | solution.py:66
  172.8 19.4 %collective-permute-done.16 = bf16[240,640]{0,1:T(8,128)(2,1)S(1)} collective-permute-done((bf16[240,640]{0,1:T(8,128)(2,1)S(1)}, bf16[240,640]{0,1:T(8,128)(2,1)S(1)}, u32[]{:S(2)}, u32[]{:S(2)}) %collective-permute-start.16) | collective-permute-done | bytes 307232 | tf_op jit(solution)/shard_map/ppermute | solution.py:66
  192.2 18.4 %collective-permute-done.12 = bf16[240,640]{0,1:T(8,128)(2,1)S(1)} collective-permute-done((bf16[240,640]{0,1:T(8,128)(2,1)S(1)}, bf16[240,640]{0,1:T(8,128)(2,1)S(1)}, u32[]{:S(2)}, u32[]{:S(2)}) %collective-permute-start.12) | collective-permute-done | bytes 307232 | tf_op jit(solution)/shard_map/ppermute | solution.py:66
  210.5 2.2 fusion.19
  (151 shorter events, 40.1 us)
Async XLA Ops:
  7.2 16.6 %copy-start = (bf16[1280,640]{1,0:T(8,128)(2,1)S(1)}, bf16[1280,640]{1,0:T(8,128)(2,1)}, u32[]{:S(2)}) copy-start(bf16[1280,640]{1,0:T(8,128)(2,1)} %param.18) | copy-start | bytes 4915204
  7.2 11.0 %copy-start.27 = (bf16[240,160]{0,1:T(8,128)(2,1)S(1)}, bf16[240,160]{0,1:T(8,128)(2,1)}, u32[]{:S(2)}) copy-start(bf16[240,160]{0,1:T(8,128)(2,1)} %param.15) | copy-start | bytes 230404
  7.2 10.4 %copy-start.24 = (f32[64,1280]{1,0:T(8,128)S(1)}, f32[64,1280]{1,0:T(8,128)}, u32[]{:S(2)}) copy-start(f32[64,1280]{1,0:T(8,128)} %param.19) | copy-start | bytes 983044
  7.2 15.8 %copy-start.28 = (bf16[240,160]{0,1:T(8,128)(2,1)S(1)}, bf16[240,160]{0,1:T(8,128)(2,1)}, u32[]{:S(2)}) copy-start(bf16[240,160]{0,1:T(8,128)(2,1)} %param.17) | copy-start | bytes 230404
  7.2 15.8 %copy-start.29 = (bf16[240,160]{0,1:T(8,128)(2,1)S(1)}, bf16[240,160]{0,1:T(8,128)(2,1)}, u32[]{:S(2)}) copy-start(bf16[240,160]{0,1:T(8,128)(2,1)} %param.16) | copy-start | bytes 230404
  7.2 76.4 %all-gather.4.cloned.1.call-start = ((), (), s32[]{:S(2)}) async-start(), calls=%async_computation | async-start | bytes 2703360 | tf_op jit(solution)/shard_map/all_gather | solution.py:117
  8.0 10.2 %collective-permute-start.1 = (bf16[240,160]{0,1:T(8,128)(2,1)}, bf16[240,160]{0,1:T(8,128)(2,1)S(1)}, u32[]{:S(2)}, u32[]{:S(2)}) collective-permute-start(bf16[240,160]{0,1:T(8,128)(2,1)} %param.15), channel_id=1, source_target_pairs={{0,16},{8,24},{16,0},{24,8},{1,17},{9,25},{17,1},{25,9},{2,18},{10... | collective-permute-start | bytes 230408 | tf_op jit(solution)/shard_map/ppermute | solution.py:66
  11.0 7.2 %collective-permute-start = (bf16[240,160]{0,1:T(8,128)(2,1)}, bf16[240,160]{0,1:T(8,128)(2,1)S(1)}, u32[]{:S(2)}, u32[]{:S(2)}) collective-permute-start(bf16[240,160]{0,1:T(8,128)(2,1)} %param.15), channel_id=1, source_target_pairs={{0,24},{8,16},{16,8},{24,0},{1,25},{9,17},{17,9},{25,1},{2,26},{10... | collective-permute-start | bytes 230408 | tf_op jit(solution)/shard_map/ppermute | solution.py:66
  12.4 5.7 %collective-permute-start.2 = (bf16[240,160]{0,1:T(8,128)(2,1)}, bf16[240,160]{0,1:T(8,128)(2,1)S(1)}, u32[]{:S(2)}, u32[]{:S(2)}) collective-permute-start(bf16[240,160]{0,1:T(8,128)(2,1)} %param.15), channel_id=1, source_target_pairs={{0,8},{8,0},{16,24},{24,16},{1,9},{9,1},{17,25},{25,17},{2,10},{10... | collective-permute-start | bytes 230408 | tf_op jit(solution)/shard_map/ppermute | solution.py:66
  18.2 30.0 %copy-start.17 = (bf16[240,160]{0,1:T(8,128)(2,1)}, bf16[240,160]{0,1:T(8,128)(2,1)S(1)}, u32[]{:S(2)}) copy-start(bf16[240,160]{0,1:T(8,128)(2,1)S(1)} %get-tuple-element.36) | copy-start | bytes 230404
  18.2 30.0 %copy-start.19 = (bf16[240,160]{0,1:T(8,128)(2,1)}, bf16[240,160]{0,1:T(8,128)(2,1)S(1)}, u32[]{:S(2)}) copy-start(bf16[240,160]{0,1:T(8,128)(2,1)S(1)} %get-tuple-element.37) | copy-start | bytes 230404
  18.2 30.0 %copy-start.21 = (bf16[240,160]{0,1:T(8,128)(2,1)}, bf16[240,160]{0,1:T(8,128)(2,1)S(1)}, u32[]{:S(2)}) copy-start(bf16[240,160]{0,1:T(8,128)(2,1)S(1)} %get-tuple-element.38) | copy-start | bytes 230404
  18.3 16.3 %collective-permute-start.5 = (bf16[240,640]{0,1:T(8,128)(2,1)S(1)}, bf16[240,640]{0,1:T(8,128)(2,1)S(1)}, u32[]{:S(2)}, u32[]{:S(2)}) collective-permute-start(bf16[240,640]{0,1:T(8,128)(2,1)S(1)} %pad_maximum_fusion.3), channel_id=1, source_target_pairs={{0,2},{1,3},{2,0},{3,1},{4,6},{5,7},{6,4},{7,5},{8,10},{9,11},{10,... | collective-permute-start | bytes 921608 | tf_op jit(solution)/shard_map/ppermute | solution.py:66
  20.4 27.3 %collective-permute-start.4 = (bf16[240,640]{0,1:T(8,128)(2,1)S(1)}, bf16[240,640]{0,1:T(8,128)(2,1)S(1)}, u32[]{:S(2)}, u32[]{:S(2)}) collective-permute-start(bf16[240,640]{0,1:T(8,128)(2,1)S(1)} %pad_maximum_fusion.3), channel_id=1, source_target_pairs={{0,4},{1,5},{2,6},{3,7},{4,0},{5,1},{6,2},{7,3},{8,12},{9,13},{10,... | collective-permute-start | bytes 921608 | tf_op jit(solution)/shard_map/ppermute | solution.py:66
  23.0 24.7 %collective-permute-start.3 = (bf16[240,640]{0,1:T(8,128)(2,1)S(1)}, bf16[240,640]{0,1:T(8,128)(2,1)S(1)}, u32[]{:S(2)}, u32[]{:S(2)}) collective-permute-start(bf16[240,640]{0,1:T(8,128)(2,1)S(1)} %pad_maximum_fusion.3), channel_id=1, source_target_pairs={{0,6},{1,7},{2,4},{3,5},{4,2},{5,3},{6,0},{7,1},{8,14},{9,15},{10,... | collective-permute-start | bytes 921608 | tf_op jit(solution)/shard_map/ppermute | solution.py:66
  50.9 3.4 %collective-permute-start.6 = (bf16[4,240,640]{2,1,0:T(8,128)(2,1)}, bf16[4,240,640]{2,1,0:T(8,128)(2,1)}, u32[]{:S(2)}, u32[]{:S(2)}) collective-permute-start(bf16[4,240,640]{2,1,0:T(8,128)(2,1)} %copy.31), channel_id=1, source_target_pairs={{0,1},{1,0},{2,3},{3,2},{4,5},{5,4},{6,7},{7,6},{8,9},{9,8},{10,11... | collective-permute-start | bytes 3686408 | tf_op jit(solution)/shard_map/ppermute | solution.py:66
  113.2 31.8 %collective-permute-start.14 = (bf16[4,240,640]{2,1,0:T(8,128)(2,1)}, bf16[4,240,640]{2,1,0:T(8,128)(2,1)}, u32[]{:S(2)}, u32[]{:S(2)}) collective-permute-start(bf16[4,240,640]{2,1,0:T(8,128)(2,1)} %fusion.13), channel_id=1, source_target_pairs={{0,1},{1,0},{2,3},{3,2},{4,5},{5,4},{6,7},{7,6},{8,9},{9,8},{10,11... | collective-permute-start | bytes 3686408 | tf_op jit(solution)/shard_map/ppermute | solution.py:66
  131.9 22.6 %collective-permute-start.10 = (bf16[4,240,640]{2,1,0:T(8,128)(2,1)}, bf16[4,240,640]{2,1,0:T(8,128)(2,1)}, u32[]{:S(2)}, u32[]{:S(2)}) collective-permute-start(bf16[4,240,640]{2,1,0:T(8,128)(2,1)} %fusion.12), channel_id=1, source_target_pairs={{0,1},{1,0},{2,3},{3,2},{4,5},{5,4},{6,7},{7,6},{8,9},{9,8},{10,11... | collective-permute-start | bytes 3686408 | tf_op jit(solution)/shard_map/ppermute | solution.py:66
  132.2 26.5 %collective-permute-start.9 = (bf16[480,160]{0,1:T(8,128)(2,1)S(1)}, bf16[480,160]{0,1:T(8,128)(2,1)S(1)}, u32[]{:S(2)}, u32[]{:S(2)}) collective-permute-start(bf16[480,160]{0,1:T(8,128)(2,1)S(1)} %copy-done.23), channel_id=1, source_target_pairs={{0,8},{8,0},{16,24},{24,16},{1,9},{9,1},{17,25},{25,17},{2,10},{10... | collective-permute-start | bytes 460808 | tf_op jit(solution)/shard_map/ppermute | solution.py:66
  133.4 27.5 %collective-permute-start.8 = (bf16[480,160]{0,1:T(8,128)(2,1)S(1)}, bf16[480,160]{0,1:T(8,128)(2,1)S(1)}, u32[]{:S(2)}, u32[]{:S(2)}) collective-permute-start(bf16[480,160]{0,1:T(8,128)(2,1)S(1)} %copy-done.23), channel_id=1, source_target_pairs={{0,16},{8,24},{16,0},{24,8},{1,17},{9,25},{17,1},{25,9},{2,18},{10... | collective-permute-start | bytes 460808 | tf_op jit(solution)/shard_map/ppermute | solution.py:66
  134.2 28.9 %collective-permute-start.7 = (bf16[480,160]{0,1:T(8,128)(2,1)S(1)}, bf16[480,160]{0,1:T(8,128)(2,1)}, u32[]{:S(2)}, u32[]{:S(2)}) collective-permute-start(bf16[480,160]{0,1:T(8,128)(2,1)S(1)} %copy-done.23), channel_id=1, source_target_pairs={{0,24},{8,16},{16,8},{24,0},{1,25},{9,17},{17,9},{25,1},{2,26},{10... | collective-permute-start | bytes 460808 | tf_op jit(solution)/shard_map/ppermute | solution.py:66
  152.2 12.8 %collective-permute-start.15 = (bf16[240,640]{0,1:T(8,128)(2,1)}, bf16[240,640]{0,1:T(8,128)(2,1)}, u32[]{:S(2)}, u32[]{:S(2)}) collective-permute-start(bf16[240,640]{0,1:T(8,128)(2,1)} %get-tuple-element.14), channel_id=1, source_target_pairs={{0,6},{1,7},{2,4},{3,5},{4,2},{5,3},{6,0},{7,1},{8,14},{9,15},{10,... | collective-permute-start | bytes 921608 | tf_op jit(solution)/shard_map/ppermute | solution.py:66
  154.5 18.3 %collective-permute-start.17 = (bf16[240,640]{0,1:T(8,128)(2,1)}, bf16[240,640]{0,1:T(8,128)(2,1)}, u32[]{:S(2)}, u32[]{:S(2)}) collective-permute-start(bf16[240,640]{0,1:T(8,128)(2,1)} %get-tuple-element.15), channel_id=1, source_target_pairs={{0,2},{1,3},{2,0},{3,1},{4,6},{5,7},{6,4},{7,5},{8,10},{9,11},{10,... | collective-permute-start | bytes 921608 | tf_op jit(solution)/shard_map/ppermute | solution.py:66
  158.5 52.0 %copy-start.18 = (bf16[240,160]{0,1:T(8,128)(2,1)S(1)}, bf16[240,160]{0,1:T(8,128)(2,1)}, u32[]{:S(2)}) copy-start(bf16[240,160]{0,1:T(8,128)(2,1)} %copy-done.17) | copy-start | bytes 230404
  158.5 52.0 %copy-start.20 = (bf16[240,160]{0,1:T(8,128)(2,1)S(1)}, bf16[240,160]{0,1:T(8,128)(2,1)}, u32[]{:S(2)}) copy-start(bf16[240,160]{0,1:T(8,128)(2,1)} %copy-done.19) | copy-start | bytes 230404
  158.5 52.0 %copy-start.22 = (bf16[240,160]{0,1:T(8,128)(2,1)S(1)}, bf16[240,160]{0,1:T(8,128)(2,1)}, u32[]{:S(2)}) copy-start(bf16[240,160]{0,1:T(8,128)(2,1)} %copy-done.21) | copy-start | bytes 230404
  158.7 33.5 %collective-permute-start.16 = (bf16[240,640]{0,1:T(8,128)(2,1)S(1)}, bf16[240,640]{0,1:T(8,128)(2,1)S(1)}, u32[]{:S(2)}, u32[]{:S(2)}) collective-permute-start(bf16[240,640]{0,1:T(8,128)(2,1)S(1)} %copy-done.25), channel_id=1, source_target_pairs={{0,4},{1,5},{2,6},{3,7},{4,0},{5,1},{6,2},{7,3},{8,12},{9,13},{10,... | collective-permute-start | bytes 921608 | tf_op jit(solution)/shard_map/ppermute | solution.py:66
  160.9 4.2 %copy-start.26 = (bf16[480,160]{0,1:T(8,128)(2,1)}, bf16[480,160]{0,1:T(8,128)(2,1)S(1)}, u32[]{:S(2)}) copy-start(bf16[480,160]{0,1:T(8,128)(2,1)S(1)} %collective-permute-done.8) | copy-start | bytes 460804
  160.9 31.3 %collective-permute-start.11 = (bf16[240,640]{0,1:T(8,128)(2,1)S(1)}, bf16[240,640]{0,1:T(8,128)(2,1)S(1)}, u32[]{:S(2)}, u32[]{:S(2)}) collective-permute-start(bf16[240,640]{0,1:T(8,128)(2,1)S(1)} %get-tuple-element.17), channel_id=1, source_target_pairs={{0,6},{1,7},{2,4},{3,5},{4,2},{5,3},{6,0},{7,1},{8,14},{9,15},{10,... | collective-permute-start | bytes 921608 | tf_op jit(solution)/shard_map/ppermute | solution.py:66
  163.1 29.0 %collective-permute-start.13 = (bf16[240,640]{0,1:T(8,128)(2,1)S(1)}, bf16[240,640]{0,1:T(8,128)(2,1)S(1)}, u32[]{:S(2)}, u32[]{:S(2)}) collective-permute-start(bf16[240,640]{0,1:T(8,128)(2,1)S(1)} %get-tuple-element.18), channel_id=1, source_target_pairs={{0,2},{1,3},{2,0},{3,1},{4,6},{5,7},{6,4},{7,5},{8,10},{9,11},{10,... | collective-permute-start | bytes 921608 | tf_op jit(solution)/shard_map/ppermute | solution.py:66
  165.1 45.5 %collective-permute-start.12 = (bf16[240,640]{0,1:T(8,128)(2,1)S(1)}, bf16[240,640]{0,1:T(8,128)(2,1)S(1)}, u32[]{:S(2)}, u32[]{:S(2)}) collective-permute-start(bf16[240,640]{0,1:T(8,128)(2,1)S(1)} %get-tuple-element.19), channel_id=1, source_target_pairs={{0,4},{1,5},{2,6},{3,7},{4,0},{5,1},{6,2},{7,3},{8,12},{9,13},{10,... | collective-permute-start | bytes 921608 | tf_op jit(solution)/shard_map/ppermute | solution.py:66
  210.5 4.3 %copy-start.1 = (bf16[1280,640]{1,0:T(8,128)(2,1)S(1)}, bf16[1280,640]{1,0:T(8,128)(2,1)}, u32[]{:S(2)}) copy-start(bf16[1280,640]{1,0:T(8,128)(2,1)} %param.18) | copy-start | bytes 4915204
  (18 other events, 31.9 us)
Sparse Core Ops, SparseCore 0:
  10.9 72.5 all-gather.3

commit v2 on v0

v2 whole, which is shorter than its diff:
```python
import functools
import math

import jax
import jax.numpy as jnp
import numpy as np
from jax import lax
from jax.experimental import pallas as pl
from jax.experimental.pallas import tpu as pltpu
from jax.sharding import PartitionSpec as P

GN_GROUPS = 32
CHUNK = 128
MEGA = 1024 * 1024
BF16 = jnp.bfloat16
F32 = jnp.float32


def time_bias(step_index, ident, subject_table, time_proj):
    half_width = subject_table.shape[1] // 2
    freqs = jnp.exp(-math.log(10000.0) * jnp.arange(half_width, dtype=F32) / half_width)
    angles = step_index.astype(F32) * freqs
    embedding = jnp.concatenate([jnp.cos(angles), jnp.sin(angles)])
    onehot = (jnp.arange(subject_table.shape[0], dtype=jnp.int32) == ident).astype(F32)
    embedding = embedding + jnp.dot(onehot, subject_table, precision=lax.Precision.HIGHEST)
    activated = jax.nn.silu(embedding).astype(BF16)
    return jnp.dot(activated[None, :], time_proj, preferred_element_type=F32)


def vmem(count):
    return [pl.BlockSpec(memory_space=pltpu.VMEM)] * count


def smem(count):
    return [pl.BlockSpec(memory_space=pltpu.SMEM)] * count


def call(body, out_shape, scratch, flops, moved, name, in_specs):
    outs = len(out_shape)
    return pl.pallas_call(
        body,
        out_shape=tuple(jax.ShapeDtypeStruct(s, d) for s, d in out_shape),
        in_specs=in_specs,
        out_specs=tuple(vmem(outs)),
        scratch_shapes=scratch,
        compiler_params=pltpu.CompilerParams(vmem_limit_bytes=40 * MEGA),
        cost_estimate=pl.CostEstimate(flops=flops, bytes_accessed=moved, transcendentals=0),
        name=name,
    )


def spread(row, same_group):
    high = row.astype(BF16)
    rest = row - high.astype(F32)
    middle = rest.astype(BF16)
    low = (rest - middle.astype(F32)).astype(BF16)
    stacked = jnp.concatenate(
        [jnp.broadcast_to(part, (16, row.shape[1])) for part in (high, middle, low)], axis=0
    )
    sums = jnp.dot(stacked, same_group, preferred_element_type=F32)
    return sums[0:1] + sums[16:17] + sums[32:33]


def norm_stats(read, rows, channels, same_group):
    counted = rows * (channels // GN_GROUPS)
    steps = rows // CHUNK
    total = lax.fori_loop(
        0,
        steps,
        lambda i, acc: acc + read(i).reshape(CHUNK // 8, 8, channels).sum(axis=0),
        jnp.zeros((8, channels), F32),
    ).sum(axis=0, keepdims=True)
    centre = spread(total, same_group) * (1.0 / counted)

    def squares(i, acc):
        centred = read(i) - centre
        return acc + (centred * centred).reshape(CHUNK // 8, 8, channels).sum(axis=0)

    square = lax.fori_loop(0, steps, squares, jnp.zeros((8, channels), F32)).sum(
        axis=0, keepdims=True
    )
    variance = spread(square, same_group) * (1.0 / counted)
    return centre, lax.rsqrt(variance + 1e-05)


def at(i, shift=0):
    return pl.ds(pl.multiple_of(i * CHUNK + shift, 64), CHUNK)


def clear_edges(padded_ref, points):
    edge = jnp.zeros((points, padded_ref.shape[1]), padded_ref.dtype)
    padded_ref[0:points] = edge
    padded_ref[padded_ref.shape[0] - points :] = edge


def enter_kernel(points, clip_ref, same_ref, padded_ref, turned_ref):
    rows, channels = clip_ref.shape
    same_group = same_ref[...]
    centre, inverse = norm_stats(
        lambda i: clip_ref[at(i)].astype(F32), rows, channels, same_group
    )
    clear_edges(padded_ref, points)

    @pl.loop(0, rows // CHUNK)
    def _(i):
        normal = (clip_ref[at(i)].astype(F32) - centre) * inverse
        act = (normal / (1.0 + jnp.exp(-normal))).astype(BF16)
        padded_ref[at(i, points)] = act
        turned_ref[:, at(i)] = act.T


def taps_of(padded_ref, start, size, points):
    return jnp.concatenate(
        [padded_ref[pl.ds(start + t * points, size)] for t in range(3)], axis=1
    )


def first_kernel(
    points, scale, in_ref, weight_ref, bias_ref, same_ref,
    normal_ref, inverse_ref, padded_ref, turned_ref, hidden_ref,
):
    rows, channels = normal_ref.shape
    half = rows // 2
    bias = bias_ref[...]

    @pl.loop(0, 2)
    def _(i):
        start = pl.multiple_of(i * half, 64)
        mixed = jnp.dot(
            taps_of(in_ref, start, half, points), weight_ref[...], preferred_element_type=F32
        )
        hidden_ref[pl.ds(start, half)] = scale * mixed + bias

    centre, inverse = norm_stats(lambda i: hidden_ref[at(i)], rows, channels, same_ref[...])
    inverse_ref[...] = inverse
    clear_edges(padded_ref, points)

    @pl.loop(0, rows // CHUNK)
    def _(i):
        normal = (hidden_ref[at(i)] - centre) * inverse
        normal_ref[at(i)] = normal
        act = (normal / (1.0 + jnp.exp(-normal))).astype(BF16)
        padded_ref[at(i, points)] = act
        turned_ref[:, at(i)] = act.T


def second_kernel(points, scale, in_ref, weight_ref, clip_ref, target_ref, error_ref):
    rows = clip_ref.shape[0]
    half = rows // 2
    clear_edges(error_ref, points)

    @pl.loop(0, 2)
    def _(i):
        start = pl.multiple_of(i * half, 64)
        mixed = jnp.dot(
            taps_of(in_ref, start, half, points), weight_ref[...], preferred_element_type=F32
        )
        here = pl.ds(start, half)
        output = clip_ref[here].astype(F32) + scale * mixed
        error_ref[pl.ds(pl.multiple_of(start + points, 64), half)] = (
            output - target_ref[here].astype(F32)
        ).astype(BF16)


def back_kernel(
    points, scale, error_ref, weight_ref, normal_ref, inverse_ref, same_ref, out_ref, grad_ref
):
    rows, channels = normal_ref.shape
    half = rows // 2
    counted = rows * (channels // GN_GROUPS)
    last = (((1,), (1,)), ((), ()))

    @pl.loop(0, 2)
    def _(i):
        start = pl.multiple_of(i * half, 64)
        total = None
        for t in range(3):
            part = lax.dot_general(
                error_ref[pl.ds(pl.multiple_of(start + (2 - t) * points, 64), half)],
                weight_ref[t * channels : (t + 1) * channels],
                last,
                preferred_element_type=F32,
            )
            total = part if total is None else total + part
        grad_ref[pl.ds(start, half)] = total

    def through(i, sums):
        normal = normal_ref[at(i)]
        gate = 1.0 / (1.0 + jnp.exp(-normal))
        grad = scale * grad_ref[at(i)] * (gate * (1.0 + normal * (1.0 - gate)))
        grad_ref[at(i)] = grad

        def fold(value):
            return value.reshape(CHUNK // 8, 8, channels).sum(axis=0)

        return sums[0] + fold(grad), sums[1] + fold(grad * normal)

    zero = jnp.zeros((8, channels), F32)
    plain, crossed = lax.fori_loop(0, rows // CHUNK, through, (zero, zero))
    same_group = same_ref[...]
    mean = spread(plain.sum(axis=0, keepdims=True), same_group) * (1.0 / counted)
    slope = spread(crossed.sum(axis=0, keepdims=True), same_group) * (1.0 / counted)
    inverse = inverse_ref[...]
    clear_edges(out_ref, points)

    @pl.loop(0, rows // CHUNK)
    def _(i):
        value = (grad_ref[at(i)] - mean - normal_ref[at(i)] * slope) * inverse
        out_ref[at(i, points)] = value.astype(BF16)


def grad_kernel(points, scale, block, me_ref, turned_ref, cotangent_ref, *refs):
    channels, rows = turned_ref.shape
    total_ref = refs[-1]

    @pl.loop(0, 3)
    def _(t):
        shifted = cotangent_ref[pl.ds(pl.multiple_of((2 - t) * points, 64), rows)]
        total_ref[pl.ds(pl.multiple_of(t * channels, 128), channels)] = scale * jnp.dot(
            turned_ref[...], shifted, preferred_element_type=F32
        )

    if block is not None:
        away_ref, home_ref = refs[0], refs[1]
        me = me_ref[0]

        @pl.loop(0, away_ref.shape[0])
        def _(j):
            away = pl.multiple_of((me ^ (2 * j + 1)) * block, 16)
            home = pl.multiple_of((me ^ (2 * j)) * block, 16)
            away_ref[j] = total_ref[pl.ds(away, block)].astype(BF16)
            home_ref[j] = total_ref[pl.ds(home, block)]


def gradient(turned, cotangent, me, n_member, points, scale):
    channels, rows = turned.shape
    block = 3 * channels // n_member
    flops, moved = 6 * rows * channels * channels, 8 * rows * channels
    specs = smem(1) + vmem(2)
    if block % 16 == 0:
        shape = (n_member // 2, block, channels)
        return call(
            functools.partial(grad_kernel, points, scale, block),
            [(shape, BF16), (shape, F32)],
            [pltpu.VMEM((3 * channels, channels), F32)],
            flops, moved, "gradient", specs,
        )(me[None], turned, cotangent)
    (total,) = call(
        functools.partial(grad_kernel, points, scale, None),
        [((3 * channels, channels), F32)],
        [], flops, moved, "gradient", specs,
    )(me[None], turned, cotangent)
    total = total.reshape(n_member, block, channels)
    order = [lax.dynamic_index_in_dim(total, me ^ j, 0, keepdims=False) for j in range(n_member)]
    return jnp.stack(order[1::2]).astype(BF16), jnp.stack(order[0::2])


def swap(value, axis, size, offset):
    return lax.ppermute(value, axis, [(i, i ^ offset) for i in range(size)])


def order_after(value, *others):
    return lax.optimization_barrier((value,) + others)[0]


TAIL = 64


def pack_kernel(*refs):
    count = len(refs) // 2
    for source, packed in zip(refs[:count], refs[count:]):
        rows, cols = source.shape
        packed[0:rows] = source[:, 0:128]
        rest = source[:, 128:cols]
        short = 4 * TAIL - rows
        rest = jnp.concatenate([rest, jnp.zeros((short, cols - 128), rest.dtype)], axis=0)
        packed[rows:] = jnp.concatenate(
            [rest[q * TAIL : (q + 1) * TAIL] for q in range(4)], axis=1
        )


def unpacked(block_of, rows, n_group):
    parts = []
    for g in range(n_group):
        block = block_of(g)
        rest = block[rows:]
        pieces = [rest[:, 32 * q : 32 * q + 32] for q in range(4)]
        parts += [block[0:rows], jnp.concatenate(pieces, axis=0)[0:rows]]
    return jnp.concatenate(parts, axis=1)


def weight_kernel(rows, n_group, place_ref, mine_ref, other_ref, full_ref):
    group, member = place_ref[0], place_ref[1]

    @pl.loop(0, mine_ref.shape[0])
    def _(k):
        for half, source in ((0, mine_ref), (1, other_ref)):
            start = pl.multiple_of((member ^ (2 * k + half)) * rows, 16)
            full_ref[pl.ds(start, rows)] = unpacked(
                lambda g: source[k, g ^ group], rows, n_group
            )


def rate_kernel(rows, n_group, place_ref, packed_ref, one_ref, two_ref):
    group = place_ref[0]
    for which, out in enumerate((one_ref, two_ref)):
        out[...] = unpacked(lambda g: packed_ref[g ^ group, which], rows, n_group)


def gather_weight(packed, n_group, n_member):
    chips = n_member // 2
    along = [packed] + [swap(packed, "member", n_member, 2 * k) for k in range(1, chips)]
    first, second = jnp.stack(along[: chips // 2]), jnp.stack(along[chips // 2 :])
    first_x = swap(first, "group", n_group, 1)
    second_y = swap(second, "group", n_group, 2)
    first = jnp.stack([first, first_x], axis=1)
    second = jnp.stack([second, second_y], axis=1)
    first_y = swap(first, "group", n_group, 2)
    second_x = swap(second, "group", n_group, 1)
    first = jnp.concatenate([first, first_y], axis=1)
    second = jnp.stack(
        [second[:, 0], second_x[:, 0], second[:, 1], second_x[:, 1]], axis=1
    )
    mine = jnp.concatenate([first, second])
    return mine, swap(mine, "member", n_member, 1)


def weights_and_rates(n_group, n_member, conv1, conv2, rate1, rate2, place):
    rows, cols = conv1.shape
    whole = (n_member * rows, n_group * cols)
    if (cols, n_group, rows % 16) != (160, 4, 0) or rows > 4 * TAIL:

        def full(weight):
            return lax.all_gather(
                lax.all_gather(weight, "group", axis=1, tiled=True), "member", axis=0, tiled=True
            )

        def rates(after):
            return (
                lax.all_gather(rate1, "group", axis=1, tiled=True),
                lax.all_gather(rate2, "group", axis=1, tiled=True),
            )

        return full(conv1), full(conv2), rates
    packed_shape = (rows + TAIL, 128)
    one, two, slow, fast = call(
        pack_kernel, [(packed_shape, BF16)] * 4, [], 0, 8 * rows * cols, "pack", vmem(4)
    )(conv1, conv2, rate1, rate2)

    def unpack(halves):
        return call(
            functools.partial(weight_kernel, rows, n_group),
            [(whole, BF16)], [], 0, 4 * whole[0] * whole[1], "unpack", smem(1) + vmem(2),
        )(place, *halves)[0]

    halves_one = gather_weight(one, n_group, n_member)
    halves_two = gather_weight(two, n_group, n_member)

    def rates(after):
        both = order_after(jnp.stack([slow, fast]), after)
        shape = (rows, whole[1])
        blocks = jnp.stack([both] + [swap(both, "group", n_group, k) for k in range(1, n_group)])
        return call(
            functools.partial(rate_kernel, rows, n_group),
            [(shape, BF16)] * 2, [], 0, 8 * rows * whole[1], "rates", smem(1) + vmem(1),
        )(place, blocks)

    return unpack(halves_one), unpack(halves_two), rates


def pair_sum(home, received):
    return [home[j] + received[j].astype(F32) for j in range(home.shape[0])]


def halve_to_owner(pairs, n_member):
    pairs = list(pairs)
    bit = 1
    while bit < len(pairs):
        away = [k for k in range(len(pairs)) if k & bit and not k & (bit - 1)]
        for k in reversed(away):
            received = swap(pairs[k].astype(BF16), "member", n_member, 2 * bit)
            pairs[k ^ bit] = pairs[k ^ bit] + received.astype(F32)
        bit *= 2
    return pairs[0]


def direct_to_owner(pairs, n_member):
    total = pairs[0]
    for k in reversed(range(1, len(pairs))):
        total = total + swap(pairs[k].astype(BF16), "member", n_member, 2 * k).astype(F32)
    return total


def shards(
    n_group,
    n_member,
    clips,
    targets,
    timestep,
    identity,
    conv1_weight,
    conv2_weight,
    rate1,
    rate2,
    time_proj,
    subject_table,
):
    frames, points, channels = (clips.shape[1], clips.shape[2], clips.shape[3])
    rows, padded = frames * points, (frames + 2) * points
    scale = 1.0 / math.sqrt(3 * channels)
    group, me = lax.axis_index("group"), lax.axis_index("member")
    place = jnp.stack([group, me]).astype(jnp.int32)
    own_rows = conv1_weight.shape[0]
    clip, target = clips.reshape(rows, channels), targets.reshape(rows, channels)
    blocks = np.arange(channels) // (channels // GN_GROUPS)
    same_group = jnp.asarray((blocks[:, None] == blocks[None, :]), BF16)
    product = 6 * rows * channels * channels
    passed = 8 * rows * channels

    full_one, full_two, rates = weights_and_rates(
        n_group, n_member, conv1_weight, conv2_weight, rate1, rate2, place
    )
    bias_row = time_bias(timestep[0], identity[0], subject_table, time_proj)
    act_one, turned_one = call(
        functools.partial(enter_kernel, points),
        [((padded, channels), BF16), ((channels, rows), BF16)],
        [], passed, passed, "enter", vmem(2),
    )(clip, same_group)
    normal, inverse, act_two, turned_two = call(
        functools.partial(first_kernel, points, scale),
        [
            ((rows, channels), F32),
            ((1, channels), F32),
            ((padded, channels), BF16),
            ((channels, rows), BF16),
        ],
        [pltpu.VMEM((rows, channels), F32)],
        product, passed, "conv_norm", vmem(4),
    )(act_one, full_one, bias_row, same_group)
    (error,) = call(
        functools.partial(second_kernel, points, scale),
        [((padded, channels), BF16)],
        [], product, passed, "conv_error", vmem(4),
    )(act_two, full_two, clip, target)
    away_two, home_two = gradient(turned_two, error, me, n_member, points, scale)
    received_two = swap(away_two, "member", n_member, 1)
    (grad_hidden,) = call(
        functools.partial(back_kernel, points, scale),
        [((padded, channels), BF16)],
        [pltpu.VMEM((rows, channels), F32)],
        product, passed, "back_norm", vmem(5),
    )(order_after(error, away_two), full_two, normal, inverse, same_group)
    received_two = order_after(received_two, grad_hidden)
    pairs_two = pair_sum(home_two, received_two)
    grad_hidden = order_after(grad_hidden, *pairs_two)
    grad_two = direct_to_owner(pairs_two, n_member)
    away_one, home_one = gradient(turned_one, grad_hidden, me, n_member, points, scale)
    received_one = swap(away_one, "member", n_member, 1)
    rate_one, rate_two = rates(away_one)
    grad_one = halve_to_owner(pair_sum(home_one, received_one), n_member)
    own_one = lax.dynamic_slice_in_dim(full_one, me * own_rows, own_rows, 0)
    own_two = lax.dynamic_slice_in_dim(full_two, me * own_rows, own_rows, 0)
    adapted_one = own_one.astype(F32) - rate_one.astype(F32) * grad_one
    adapted_two = own_two.astype(F32) - rate_two.astype(F32) * grad_two
    return (adapted_one[None], adapted_two[None])


def solution(mesh):
    n_group, n_member = mesh.shape["group"], mesh.shape["member"]
    return jax.shard_map(
        lambda *arrays: shards(n_group, n_member, *arrays),
        mesh=mesh,
        in_specs=(
            P(("group", "member"), None, None, None),
            P(("group", "member"), None, None, None),
            P(("group", "member")),
            P(("group", "member")),
            P("member", "group"),
            P("member", "group"),
            P("member", "group"),
            P("member", "group"),
            P(),
            P(),
        ),
        out_specs=(P("group", "member", None), P("group", "member", None)),
        check_vma=False,
    )
```

time: 221 us -> 138 us (0.62)
  waiting for transfers between devices: 103 us -> 47.7 us
  starting transfers between devices: 0.34 us -> 39.8 us
  blocking collectives: 39 us -> 0 us
  matrix products: 33 us -> 0.56 us
  Pallas kernels: 0 us -> 31.2 us
  between operations: 15.4 us -> 2.33 us
  other arithmetic: 19.8 us -> 8.84 us
  local copies, waits for them, and re-layouts: 10.2 us -> 6.7 us
    reduce_scatter x2 -> x0, waiting for transfers between devices: 69.3 us -> none  [the longest x1 55.4 us: shards(): lax.psum_scatter(grad_terms(stacked_one, grad_hidden, weight_scale), 'mem...]
    ppermute x0 -> x27, waiting for transfers between devices: none -> 47.7 us  [swap(): return lax.ppermute(value, axis, [(i, i ^ offset) for i in range(size)])]
    ppermute x0 -> x27, starting transfers between devices: none -> 39.8 us  [swap(): return lax.ppermute(value, axis, [(i, i ^ offset) for i in range(size)])]
    all_gather x4 -> x0, blocking collectives: 39 us -> none  [the longest x1 11.2 us: shards(): lax.all_gather(conv1_weight, 'group', axis=1, tiled=True)]
    all_gather x2 -> x0, waiting for transfers between devices: 33.8 us -> none  [the longest x1 19.3 us: shards(): lax.all_gather(own_two, 'member', axis=0, tiled=True)]
    dot_general x6 -> x1, matrix products: 32.7 us -> 0.32 us  [time_bias(): return jnp.dot(activated[None, :], time_proj, preferred_element_type=F32)]
    pallas_call x0 -> x10, Pallas kernels: none -> 31.2 us  [the longest x2 7.56 us: gradient(): call(functools.partial(grad_kernel, points, scale, block), [(shape, BF16)...]
    reduce_sum x11 -> x0, other arithmetic: 8.86 us -> none  [the longest x1 2.86 us: group_norm(): centred = values - centre]
  transfers between devices with their start and end apart: 4 -> 27, of which waited for: 4 -> 13; matrix products, arithmetic and copies ran while one was open for 19% -> 4% of each run, Pallas kernels for 0% -> 12%
where the time goes in v2:
time: 138 us; the launch traced here: 137 us
  waiting for transfers between devices  47.7 us (35%)
  starting transfers between devices  39.8 us (29%)
  Pallas kernels  31.2 us (23%)
  other arithmetic  8.84 us (6%)
  local copies, waits for them, and re-layouts  6.7 us (5%)
  between operations  2.33 us (2%)
    ppermute x27, waiting for transfers between devices, swap(): return lax.ppermute(value, axis, [(i, i ^ offset) for i in range(size)])  47.7 us
    ppermute x27, starting transfers between devices, swap(): return lax.ppermute(value, axis, [(i, i ^ offset) for i in range(size)])  39.8 us
    pallas_call x2, Pallas kernels, gradient(): call(functools.partial(grad_kernel, points, scale, block), [(shape, BF16)...  7.56 us
    unnamed x28, local copies, waits for them, and re-layouts  6.65 us
    pallas_call x2, Pallas kernels, unpack(): call(functools.partial(weight_kernel, rows, n_group), [(whole, BF16)], []...  6.11 us
    pallas_call x1, Pallas kernels, shards(): call(functools.partial(back_kernel, points, scale), [((padded, channels),...  5.35 us
    pallas_call x1, Pallas kernels, shards(): call(functools.partial(first_kernel, points, scale), [((rows, channels),...  5.35 us
    broadcast_in_dim x2, other arithmetic, shards(): return (adapted_one[None], adapted_two[None])  4.32 us
  transfers between devices with their start and end apart: 27, of which 13 were waited for; matrix products, arithmetic and copies ran while one was open for 4% of the time, Pallas kernels for 12%

profile of v2, /device:TPU:0, one launch (start us, length us, event | category | flops | bytes accessed | tf_op | source)
XLA Modules:
  0.0 137.2 jit_solution(7376685440404447408)
XLA Ops:
  4.9 5.1 %collective-permute-start.4 = (bf16[304,128]{1,0:T(8,128)(2,1)S(1)}, bf16[304,128]{1,0:T(8,128)(2,1)S(1)}, u32[]{:S(2)}, u32[]{:S(2)}) collective-permute-start(bf16[304,128]{1,0:T(8,128)(2,1)S(1)} %get-tuple-element.22), channel_id=1, source_target_pairs={{0,6},{1,7},{2,4},{3,5},{4,2},{5,3},{6,0},{7,1},{8,14},{9,15},{10,... | collective-permute-start | bytes 233480 | tf_op jit(solution)/shard_map/ppermute | solution.py:259
  10.6 3.7 %collective-permute-start.12 = (bf16[304,128]{1,0:T(8,128)(2,1)S(1)}, bf16[304,128]{1,0:T(8,128)(2,1)S(1)}, u32[]{:S(2)}, u32[]{:S(2)}) collective-permute-start(bf16[304,128]{1,0:T(8,128)(2,1)S(1)} %get-tuple-element.28), channel_id=1, source_target_pairs={{0,6},{1,7},{2,4},{3,5},{4,2},{5,3},{6,0},{7,1},{8,14},{9,15},{10,... | collective-permute-start | bytes 233480 | tf_op jit(solution)/shard_map/ppermute | solution.py:259
  14.4 3.1 %collective-permute-start.8 = (bf16[304,128]{1,0:T(8,128)(2,1)S(1)}, bf16[304,128]{1,0:T(8,128)(2,1)S(1)}, u32[]{:S(2)}, u32[]{:S(2)}) collective-permute-start(bf16[304,128]{1,0:T(8,128)(2,1)S(1)} %get-tuple-element.28), channel_id=1, source_target_pairs={{0,2},{1,3},{2,0},{3,1},{4,6},{5,7},{6,4},{7,5},{8,10},{9,11},{10,... | collective-permute-start | bytes 233480 | tf_op jit(solution)/shard_map/ppermute | solution.py:259
  17.5 3.1 %collective-permute-done.3 = bf16[304,128]{1,0:T(8,128)(2,1)S(1)} collective-permute-done((bf16[304,128]{1,0:T(8,128)(2,1)S(1)}, bf16[304,128]{1,0:T(8,128)(2,1)S(1)}, u32[]{:S(2)}, u32[]{:S(2)}) %collective-permute-start.3) | collective-permute-done | bytes 77856 | tf_op jit(solution)/shard_map/ppermute | solution.py:259
  20.6 1.4 %collective-permute-start.5 = (bf16[2,304,128]{2,1,0:T(8,128)(2,1)S(1)}, bf16[2,304,128]{2,1,0:T(8,128)(2,1)S(1)}, u32[]{:S(2)}, u32[]{:S(2)}) collective-permute-start(bf16[2,304,128]{2,1,0:T(8,128)(2,1)S(1)} %get-tuple-element.58), channel_id=1, source_target_pairs={{0,16},{8,24},{16,0},{24,8},{1,17},{9,25},{17,1},{25,9},{2,18},{10... | collective-permute-start | bytes 466952 | tf_op jit(solution)/shard_map/ppermute | solution.py:259
  22.0 1.6 %collective-permute-start.1 = (bf16[2,304,128]{2,1,0:T(8,128)(2,1)S(1)}, bf16[2,304,128]{2,1,0:T(8,128)(2,1)S(1)}, u32[]{:S(2)}, u32[]{:S(2)}) collective-permute-start(bf16[2,304,128]{2,1,0:T(8,128)(2,1)S(1)} %get-tuple-element.56), channel_id=1, source_target_pairs={{0,8},{8,0},{16,24},{24,16},{1,9},{9,1},{17,25},{25,17},{2,10},{10... | collective-permute-start | bytes 466952 | tf_op jit(solution)/shard_map/ppermute | solution.py:259
  24.8 1.6 %collective-permute-start.9 = (bf16[2,304,128]{2,1,0:T(8,128)(2,1)S(1)}, bf16[2,304,128]{2,1,0:T(8,128)(2,1)S(1)}, u32[]{:S(2)}, u32[]{:S(2)}) collective-permute-start(bf16[2,304,128]{2,1,0:T(8,128)(2,1)S(1)} %get-tuple-element.52), channel_id=1, source_target_pairs={{0,8},{8,0},{16,24},{24,16},{1,9},{9,1},{17,25},{25,17},{2,10},{10... | collective-permute-start | bytes 466952 | tf_op jit(solution)/shard_map/ppermute | solution.py:259
  31.9 1.6 %collective-permute-start.10 = (bf16[2,2,304,128]{3,2,1,0:T(8,128)(2,1)S(1)}, bf16[2,2,304,128]{3,2,1,0:T(8,128)(2,1)S(1)}, u32[]{:S(2)}, u32[]{:S(2)}) collective-permute-start(bf16[2,2,304,128]{3,2,1,0:T(8,128)(2,1)S(1)} %pad_maximum_fusion.3), channel_id=1, source_target_pairs={{0,16},{8,24},{16,0},{24,8},{1,17},{9,25},{17,1},{25,9},{2,18},{10... | collective-permute-start | bytes 933896 | tf_op jit(solution)/shard_map/ppermute | solution.py:259
  33.4 5.1 %collective-permute-done.6 = bf16[2,2,304,128]{3,2,1,0:T(8,128)(2,1)S(1)} collective-permute-done((bf16[2,2,304,128]{3,2,1,0:T(8,128)(2,1)S(1)}, bf16[2,2,304,128]{3,2,1,0:T(8,128)(2,1)S(1)}, u32[]{:S(2)}, u32[]{:S(2)}) %collective-permute-start.6) | collective-permute-done | bytes 311328 | tf_op jit(solution)/shard_map/ppermute | solution.py:259
  38.8 5.2 %collective-permute-done.14 = bf16[2,2,304,128]{3,2,1,0:T(8,128)(2,1)S(1)} collective-permute-done((bf16[2,2,304,128]{3,2,1,0:T(8,128)(2,1)S(1)}, bf16[2,2,304,128]{3,2,1,0:T(8,128)(2,1)S(1)}, u32[]{:S(2)}, u32[]{:S(2)}) %collective-permute-start.14) | collective-permute-done | bytes 311328 | tf_op jit(solution)/shard_map/ppermute | solution.py:259
  49.3 2.6 %enter.1 = (bf16[1024,640]{1,0:T(8,128)(2,1)S(1)}, bf16[640,896]{1,0:T(8,128)(2,1)S(1)}) custom-call(bf16[896,640]{1,0:T(8,128)(2,1)S(1)} %bitcast.81, bf16[640,640]{1,0:T(8,128)(2,1)S(1)} %copy-done.2), custom_call_target="tpu_custom_call" | custom-call | flops 4587520 | bytes 4587520 | tf_op jit(solution)/shard_map/enter/pallas_call | solution.py:424
  52.3 2.8 %unpack.2.weight_ref = bf16[1920,640]{1,0:T(8,128)(2,1)S(1)} custom-call(s32[2]{0:T(128)S(1)} %pad_add_fusion.place_ref, bf16[4,4,304,128]{3,2,1,0:T(8,128)(2,1)S(1)} %maximum_maximum_fusion.mine_ref, bf16[4,4,304,128]{3,2,1,0:T(8,128)(2,1)} %collective-permute-done.7.other_ref), custom_call_target="tpu_custom_call" | custom-call | bytes 4915200 | tf_op jit(solution)/shard_map/unpack/pallas_call | solution.py:351
  55.2 5.3 %conv_norm.1 = (f32[896,640]{1,0:T(8,128)S(1)}, f32[1,640]{1,0:T(1,128)S(1)}, bf16[1024,640]{1,0:T(8,128)(2,1)S(1)}, bf16[640,896]{1,0:T(8,128)(2,1)S(1)}) custom-call(bf16[1024,640]{1,0:T(8,128)(2,1)S(1)} %get-tuple-element.26.in_ref, bf16[1920,640]{1,0:T(8,128)(2,1)S(1)} %unpack.2.weight_ref, f32[1,640]{1,0:T(1,128)S(1)} %fusion.19.bias_ref, ...), custom_call_target="tpu_custom_call" | custom-call | flops 2202009600 | bytes 4587520 | tf_op jit(solution)/shard_map/conv_norm/pallas_call | solution.py:429
  60.6 3.3 %unpack.3.weight_ref = bf16[1920,640]{1,0:T(8,128)(2,1)S(1)} custom-call(s32[2]{0:T(128)S(1)} %pad_add_fusion.place_ref, bf16[4,4,304,128]{3,2,1,0:T(8,128)(2,1)} %maximum_maximum_fusion.1.mine_ref, bf16[4,4,304,128]{3,2,1,0:T(8,128)(2,1)} %collective-permute-done.15.other_ref), custom_call_target="tpu_custom_call" | custom-call | bytes 4915200 | tf_op jit(solution)/shard_map/unpack/pallas_call | solution.py:351
  63.9 3.2 %conv_error.1.cotangent_ref.error_ref = bf16[1024,640]{1,0:T(8,128)(2,1)S(1)} custom-call(bf16[1024,640]{1,0:T(8,128)(2,1)S(1)} %get-tuple-element.27.in_ref, bf16[1920,640]{1,0:T(8,128)(2,1)S(1)} %unpack.3.weight_ref, bf16[896,640]{1,0:T(8,128)(2,1)S(1)} %bitcast.82, bf16[896,640]{1,0:T(8,128)(2,1)S(1)} %bitcast.87), custom_call_target="tpu_custom_call" | custom-call | flops 2202009600 | bytes 4587520 | tf_op jit(solution)/shard_map/conv_error/pallas_call | solution.py:440
  67.1 3.8 %gradient.2 = (bf16[4,240,640]{2,1,0:T(8,128)(2,1)S(1)}, f32[4,240,640]{2,1,0:T(8,128)S(1)}) custom-call(s32[1]{0:T(128)} %bitcast.1.me_ref, bf16[640,896]{1,0:T(8,128)(2,1)S(1)} %get-tuple-element.29.turned_ref, bf16[1024,640]{1,0:T(8,128)(2,1)S(1)} %conv_error.1.cotangent_ref.error_ref), custom_call_target="tpu_custom_call" | custom-call | flops 2202009600 | bytes 4587520 | tf_op jit(solution)/shard_map/gradient/pallas_call | solution.py:242
  71.4 5.3 %back_norm.1.cotangent_ref = bf16[1024,640]{1,0:T(8,128)(2,1)S(1)} custom-call(bf16[1024,640]{1,0:T(8,128)(2,1)S(1)} %conv_error.1.cotangent_ref.error_ref, bf16[1920,640]{1,0:T(8,128)(2,1)S(1)} %unpack.3.weight_ref, f32[896,640]{1,0:T(8,128)S(1)} %get-tuple-element.32.normal_ref, f32[1,640]{1,0:T(1,128)S(1)} %get-tuple-element.33.inverse_ref, ...), custom_call_target="tpu_custom_call" | custom-call | flops 2202009600 | bytes 4587520 | tf_op jit(solution)/shard_map/back_norm/pallas_call | solution.py:447
  77.1 3.8 %gradient.3 = (bf16[4,240,640]{2,1,0:T(8,128)(2,1)S(1)}, f32[4,240,640]{2,1,0:T(8,128)S(1)}) custom-call(s32[1]{0:T(128)} %bitcast.1.me_ref, bf16[640,896]{1,0:T(8,128)(2,1)S(1)} %get-tuple-element.25.turned_ref, bf16[1024,640]{1,0:T(8,128)(2,1)S(1)} %back_norm.1.cotangent_ref), custom_call_target="tpu_custom_call" | custom-call | flops 2202009600 | bytes 4587520 | tf_op jit(solution)/shard_map/gradient/pallas_call | solution.py:242
  81.0 2.9 %collective-permute-done.20 = bf16[4,240,640]{2,1,0:T(8,128)(2,1)S(1)} collective-permute-done((bf16[4,240,640]{2,1,0:T(8,128)(2,1)S(1)}, bf16[4,240,640]{2,1,0:T(8,128)(2,1)S(1)}, u32[]{:S(2)}, u32[]{:S(2)}) %collective-permute-start.20) | collective-permute-done | bytes 1228832 | tf_op jit(solution)/shard_map/ppermute | solution.py:259
  85.2 1.5 %collective-permute-start.19 = (bf16[2,304,128]{2,1,0:T(8,128)(2,1)S(1)}, bf16[2,304,128]{2,1,0:T(8,128)(2,1)S(1)}, u32[]{:S(2)}, u32[]{:S(2)}) collective-permute-start(bf16[2,304,128]{2,1,0:T(8,128)(2,1)S(1)} %pad_maximum_fusion.7), channel_id=1, source_target_pairs={{0,24},{8,16},{16,8},{24,0},{1,25},{9,17},{17,9},{25,1},{2,26},{10... | collective-permute-start | bytes 466952 | tf_op jit(solution)/shard_map/ppermute | solution.py:259
  86.6 1.5 %collective-permute-start.18 = (bf16[2,304,128]{2,1,0:T(8,128)(2,1)S(1)}, bf16[2,304,128]{2,1,0:T(8,128)(2,1)S(1)}, u32[]{:S(2)}, u32[]{:S(2)}) collective-permute-start(bf16[2,304,128]{2,1,0:T(8,128)(2,1)S(1)} %pad_maximum_fusion.7), channel_id=1, source_target_pairs={{0,16},{8,24},{16,0},{24,8},{1,17},{9,25},{17,1},{25,9},{2,18},{10... | collective-permute-start | bytes 466952 | tf_op jit(solution)/shard_map/ppermute | solution.py:259
  88.7 2.0 %collective-permute-start.26 = (bf16[240,640]{1,0:T(8,128)(2,1)S(1)}, bf16[240,640]{1,0:T(8,128)(2,1)S(1)}, u32[]{:S(2)}, u32[]{:S(2)}) collective-permute-start(bf16[240,640]{1,0:T(8,128)(2,1)S(1)} %get-tuple-element.46), channel_id=1, source_target_pairs={{0,2},{1,3},{2,0},{3,1},{4,6},{5,7},{6,4},{7,5},{8,10},{9,11},{10,... | collective-permute-start | bytes 921608 | tf_op jit(solution)/shard_map/ppermute | solution.py:259
  90.6 2.4 %collective-permute-done.19 = bf16[2,304,128]{2,1,0:T(8,128)(2,1)S(1)} collective-permute-done((bf16[2,304,128]{2,1,0:T(8,128)(2,1)S(1)}, bf16[2,304,128]{2,1,0:T(8,128)(2,1)S(1)}, u32[]{:S(2)}, u32[]{:S(2)}) %collective-permute-start.19) | collective-permute-done | bytes 155680 | tf_op jit(solution)/shard_map/ppermute | solution.py:259
  93.0 3.6 %collective-permute-start.25 = (bf16[240,640]{1,0:T(8,128)(2,1)S(1)}, bf16[240,640]{1,0:T(8,128)(2,1)S(1)}, u32[]{:S(2)}, u32[]{:S(2)}) collective-permute-start(bf16[240,640]{1,0:T(8,128)(2,1)S(1)} %get-tuple-element.45), channel_id=1, source_target_pairs={{0,4},{1,5},{2,6},{3,7},{4,0},{5,1},{6,2},{7,3},{8,12},{9,13},{10,... | collective-permute-start | bytes 921608 | tf_op jit(solution)/shard_map/ppermute | solution.py:259
  96.6 6.3 %collective-permute-start.24 = (bf16[240,640]{1,0:T(8,128)(2,1)S(1)}, bf16[240,640]{1,0:T(8,128)(2,1)S(1)}, u32[]{:S(2)}, u32[]{:S(2)}) collective-permute-start(bf16[240,640]{1,0:T(8,128)(2,1)S(1)} %get-tuple-element.44), channel_id=1, source_target_pairs={{0,6},{1,7},{2,4},{3,5},{4,2},{5,3},{6,0},{7,1},{8,14},{9,15},{10,... | collective-permute-start | bytes 921608 | tf_op jit(solution)/shard_map/ppermute | solution.py:259
  102.9 1.3 fusion
  105.8 1.5 %collective-permute-done.26 = bf16[240,640]{1,0:T(8,128)(2,1)S(1)} collective-permute-done((bf16[240,640]{1,0:T(8,128)(2,1)S(1)}, bf16[240,640]{1,0:T(8,128)(2,1)S(1)}, u32[]{:S(2)}, u32[]{:S(2)}) %collective-permute-start.26) | collective-permute-done | bytes 307232 | tf_op jit(solution)/shard_map/ppermute | solution.py:259
  107.4 10.6 %collective-permute-done.25 = bf16[240,640]{1,0:T(8,128)(2,1)S(1)} collective-permute-done((bf16[240,640]{1,0:T(8,128)(2,1)S(1)}, bf16[240,640]{1,0:T(8,128)(2,1)S(1)}, u32[]{:S(2)}, u32[]{:S(2)}) %collective-permute-start.25) | collective-permute-done | bytes 307232 | tf_op jit(solution)/shard_map/ppermute | solution.py:259
  118.0 2.0 %subtract_bitcast_fusion = f32[1,240,640]{2,1,0:T(8,128)} fusion(bf16[240,640]{1,0:T(8,128)(2,1)S(1)} %collective-permute-done.26, bf16[240,640]{1,0:T(8,128)(2,1)S(1)} %collective-permute-done.25, f32[240,640]{1,0:T(8,128)S(1)} %add_bitcast_fusion.3, bf16[240,640]{1,0:T(8,128)(2,1)S(1)} %collective-permute-done.24, ...), kind=kLoop, calls=%fused_computation.11 | loop fusion | flops 1536000 | bytes 2764804 | tf_op jit(solution)/shard_map/broadcast_in_dim | solution.py:465
  120.0 2.5 %collective-permute-done.21 = bf16[240,640]{1,0:T(8,128)(2,1)S(1)} collective-permute-done((bf16[240,640]{1,0:T(8,128)(2,1)S(1)}, bf16[240,640]{1,0:T(8,128)(2,1)S(1)}, u32[]{:S(2)}, u32[]{:S(2)}) %collective-permute-start.21) | collective-permute-done | bytes 307232 | tf_op jit(solution)/shard_map/ppermute | solution.py:259
  122.5 12.4 %collective-permute-done.23 = bf16[240,640]{1,0:T(8,128)(2,1)S(1)} collective-permute-done((bf16[240,640]{1,0:T(8,128)(2,1)S(1)}, bf16[240,640]{1,0:T(8,128)(2,1)S(1)}, u32[]{:S(2)}, u32[]{:S(2)}) %collective-permute-start.23) | collective-permute-done | bytes 307232 | tf_op jit(solution)/shard_map/ppermute | solution.py:259
  134.9 2.3 %fusion.4 = f32[1,240,640]{2,1,0:T(8,128)} fusion(bf16[240,640]{1,0:T(8,128)(2,1)S(1)} %collective-permute-done.23, bf16[240,640]{1,0:T(8,128)(2,1)S(1)} %collective-permute-done.21, f32[4,240,640]{2,1,0:T(8,128)} %copy-done.5, bf16[240,640]{1,0:T(8,128)(2,1)S(1)} %get-tuple-element.39, bf16[4,240,640]{2,1,0:T(8,128)(2,1)} %copy-done.9, ...), kind=kLoop, calls=%fused_computation.10 | loop fusion | flops 1536000 | bytes 2764804 | tf_op jit(solution)/shard_map/broadcast_in_dim | solution.py:465
  (86 shorter events, 20.5 us)
Async XLA Ops:
  0.6 51.4 %copy-start = (bf16[1280,640]{1,0:T(8,128)(2,1)S(1)}, bf16[1280,640]{1,0:T(8,128)(2,1)}, u32[]{:S(2)}) copy-start(bf16[1280,640]{1,0:T(8,128)(2,1)} %param.19) | copy-start | bytes 4915204
  4.9 9.5 %collective-permute-start.4 = (bf16[304,128]{1,0:T(8,128)(2,1)S(1)}, bf16[304,128]{1,0:T(8,128)(2,1)S(1)}, u32[]{:S(2)}, u32[]{:S(2)}) collective-permute-start(bf16[304,128]{1,0:T(8,128)(2,1)S(1)} %get-tuple-element.22), channel_id=1, source_target_pairs={{0,6},{1,7},{2,4},{3,5},{4,2},{5,3},{6,0},{7,1},{8,14},{9,15},{10,... | collective-permute-start | bytes 233480 | tf_op jit(solution)/shard_map/ppermute | solution.py:259
  10.0 10.6 %collective-permute-start.3 = (bf16[304,128]{1,0:T(8,128)(2,1)S(1)}, bf16[304,128]{1,0:T(8,128)(2,1)S(1)}, u32[]{:S(2)}, u32[]{:S(2)}) collective-permute-start(bf16[304,128]{1,0:T(8,128)(2,1)S(1)} %get-tuple-element.22), channel_id=1, source_target_pairs={{0,4},{1,5},{2,6},{3,7},{4,0},{5,1},{6,2},{7,3},{8,12},{9,13},{10,... | collective-permute-start | bytes 233480 | tf_op jit(solution)/shard_map/ppermute | solution.py:259
  10.0 12.0 %collective-permute-start = (bf16[304,128]{1,0:T(8,128)(2,1)S(1)}, bf16[304,128]{1,0:T(8,128)(2,1)S(1)}, u32[]{:S(2)}, u32[]{:S(2)}) collective-permute-start(bf16[304,128]{1,0:T(8,128)(2,1)S(1)} %get-tuple-element.22), channel_id=1, source_target_pairs={{0,2},{1,3},{2,0},{3,1},{4,6},{5,7},{6,4},{7,5},{8,10},{9,11},{10,... | collective-permute-start | bytes 233480 | tf_op jit(solution)/shard_map/ppermute | solution.py:259
  10.6 13.0 %collective-permute-start.12 = (bf16[304,128]{1,0:T(8,128)(2,1)S(1)}, bf16[304,128]{1,0:T(8,128)(2,1)S(1)}, u32[]{:S(2)}, u32[]{:S(2)}) collective-permute-start(bf16[304,128]{1,0:T(8,128)(2,1)S(1)} %get-tuple-element.28), channel_id=1, source_target_pairs={{0,6},{1,7},{2,4},{3,5},{4,2},{5,3},{6,0},{7,1},{8,14},{9,15},{10,... | collective-permute-start | bytes 233480 | tf_op jit(solution)/shard_map/ppermute | solution.py:259
  14.4 9.2 %collective-permute-start.11 = (bf16[304,128]{1,0:T(8,128)(2,1)S(1)}, bf16[304,128]{1,0:T(8,128)(2,1)S(1)}, u32[]{:S(2)}, u32[]{:S(2)}) collective-permute-start(bf16[304,128]{1,0:T(8,128)(2,1)S(1)} %get-tuple-element.28), channel_id=1, source_target_pairs={{0,4},{1,5},{2,6},{3,7},{4,0},{5,1},{6,2},{7,3},{8,12},{9,13},{10,... | collective-permute-start | bytes 233480 | tf_op jit(solution)/shard_map/ppermute | solution.py:259
  14.4 10.4 %collective-permute-start.8 = (bf16[304,128]{1,0:T(8,128)(2,1)S(1)}, bf16[304,128]{1,0:T(8,128)(2,1)S(1)}, u32[]{:S(2)}, u32[]{:S(2)}) collective-permute-start(bf16[304,128]{1,0:T(8,128)(2,1)S(1)} %get-tuple-element.28), channel_id=1, source_target_pairs={{0,2},{1,3},{2,0},{3,1},{4,6},{5,7},{6,4},{7,5},{8,10},{9,11},{10,... | collective-permute-start | bytes 233480 | tf_op jit(solution)/shard_map/ppermute | solution.py:259
  20.6 6.0 %collective-permute-start.5 = (bf16[2,304,128]{2,1,0:T(8,128)(2,1)S(1)}, bf16[2,304,128]{2,1,0:T(8,128)(2,1)S(1)}, u32[]{:S(2)}, u32[]{:S(2)}) collective-permute-start(bf16[2,304,128]{2,1,0:T(8,128)(2,1)S(1)} %get-tuple-element.58), channel_id=1, source_target_pairs={{0,16},{8,24},{16,0},{24,8},{1,17},{9,25},{17,1},{25,9},{2,18},{10... | collective-permute-start | bytes 466952 | tf_op jit(solution)/shard_map/ppermute | solution.py:259
  22.0 5.8 %collective-permute-start.1 = (bf16[2,304,128]{2,1,0:T(8,128)(2,1)S(1)}, bf16[2,304,128]{2,1,0:T(8,128)(2,1)S(1)}, u32[]{:S(2)}, u32[]{:S(2)}) collective-permute-start(bf16[2,304,128]{2,1,0:T(8,128)(2,1)S(1)} %get-tuple-element.56), channel_id=1, source_target_pairs={{0,8},{8,0},{16,24},{24,16},{1,9},{9,1},{17,25},{25,17},{2,10},{10... | collective-permute-start | bytes 466952 | tf_op jit(solution)/shard_map/ppermute | solution.py:259
  23.6 6.4 %collective-permute-start.13 = (bf16[2,304,128]{2,1,0:T(8,128)(2,1)S(1)}, bf16[2,304,128]{2,1,0:T(8,128)(2,1)S(1)}, u32[]{:S(2)}, u32[]{:S(2)}) collective-permute-start(bf16[2,304,128]{2,1,0:T(8,128)(2,1)S(1)} %get-tuple-element.54), channel_id=1, source_target_pairs={{0,16},{8,24},{16,0},{24,8},{1,17},{9,25},{17,1},{25,9},{2,18},{10... | collective-permute-start | bytes 466952 | tf_op jit(solution)/shard_map/ppermute | solution.py:259
  24.8 7.0 %collective-permute-start.9 = (bf16[2,304,128]{2,1,0:T(8,128)(2,1)S(1)}, bf16[2,304,128]{2,1,0:T(8,128)(2,1)S(1)}, u32[]{:S(2)}, u32[]{:S(2)}) collective-permute-start(bf16[2,304,128]{2,1,0:T(8,128)(2,1)S(1)} %get-tuple-element.52), channel_id=1, source_target_pairs={{0,8},{8,0},{16,24},{24,16},{1,9},{9,1},{17,25},{25,17},{2,10},{10... | collective-permute-start | bytes 466952 | tf_op jit(solution)/shard_map/ppermute | solution.py:259
  26.6 11.9 %collective-permute-start.6 = (bf16[2,2,304,128]{3,2,1,0:T(8,128)(2,1)S(1)}, bf16[2,2,304,128]{3,2,1,0:T(8,128)(2,1)S(1)}, u32[]{:S(2)}, u32[]{:S(2)}) collective-permute-start(bf16[2,2,304,128]{3,2,1,0:T(8,128)(2,1)S(1)} %pad_maximum_fusion.2), channel_id=1, source_target_pairs={{0,8},{8,0},{16,24},{24,16},{1,9},{9,1},{17,25},{25,17},{2,10},{10... | collective-permute-start | bytes 933896 | tf_op jit(solution)/shard_map/ppermute | solution.py:259
  27.9 10.6 %collective-permute-start.2 = (bf16[2,2,304,128]{3,2,1,0:T(8,128)(2,1)S(1)}, bf16[2,2,304,128]{3,2,1,0:T(8,128)(2,1)S(1)}, u32[]{:S(2)}, u32[]{:S(2)}) collective-permute-start(bf16[2,2,304,128]{3,2,1,0:T(8,128)(2,1)S(1)} %pad_maximum_fusion.1), channel_id=1, source_target_pairs={{0,16},{8,24},{16,0},{24,8},{1,17},{9,25},{17,1},{25,9},{2,18},{10... | collective-permute-start | bytes 933896 | tf_op jit(solution)/shard_map/ppermute | solution.py:259
  30.0 14.0 %collective-permute-start.14 = (bf16[2,2,304,128]{3,2,1,0:T(8,128)(2,1)S(1)}, bf16[2,2,304,128]{3,2,1,0:T(8,128)(2,1)S(1)}, u32[]{:S(2)}, u32[]{:S(2)}) collective-permute-start(bf16[2,2,304,128]{3,2,1,0:T(8,128)(2,1)S(1)} %pad_maximum_fusion.4), channel_id=1, source_target_pairs={{0,8},{8,0},{16,24},{24,16},{1,9},{9,1},{17,25},{25,17},{2,10},{10... | collective-permute-start | bytes 933896 | tf_op jit(solution)/shard_map/ppermute | solution.py:259
  31.9 12.2 %collective-permute-start.10 = (bf16[2,2,304,128]{3,2,1,0:T(8,128)(2,1)S(1)}, bf16[2,2,304,128]{3,2,1,0:T(8,128)(2,1)S(1)}, u32[]{:S(2)}, u32[]{:S(2)}) collective-permute-start(bf16[2,2,304,128]{3,2,1,0:T(8,128)(2,1)S(1)} %pad_maximum_fusion.3), channel_id=1, source_target_pairs={{0,16},{8,24},{16,0},{24,8},{1,17},{9,25},{17,1},{25,9},{2,18},{10... | collective-permute-start | bytes 933896 | tf_op jit(solution)/shard_map/ppermute | solution.py:259
  38.7 13.6 %collective-permute-start.7 = (bf16[4,4,304,128]{3,2,1,0:T(8,128)(2,1)S(1)}, bf16[4,4,304,128]{3,2,1,0:T(8,128)(2,1)}, u32[]{:S(2)}, u32[]{:S(2)}) collective-permute-start(bf16[4,4,304,128]{3,2,1,0:T(8,128)(2,1)S(1)} %maximum_maximum_fusion.mine_ref), channel_id=1, source_target_pairs={{0,1},{1,0},{2,3},{3,2},{4,5},{5,4},{6,7},{7,6},{8,9},{9,8},{10,11... | collective-permute-start | bytes 3735560 | tf_op jit(solution)/shard_map/ppermute | solution.py:259
  45.2 15.3 %collective-permute-start.15 = (bf16[4,4,304,128]{3,2,1,0:T(8,128)(2,1)}, bf16[4,4,304,128]{3,2,1,0:T(8,128)(2,1)}, u32[]{:S(2)}, u32[]{:S(2)}) collective-permute-start(bf16[4,4,304,128]{3,2,1,0:T(8,128)(2,1)} %maximum_maximum_fusion.1.mine_ref), channel_id=1, source_target_pairs={{0,1},{1,0},{2,3},{3,2},{4,5},{5,4},{6,7},{7,6},{8,9},{9,8},{10,11... | collective-permute-start | bytes 3735560 | tf_op jit(solution)/shard_map/ppermute | solution.py:259
  55.2 5.4 %copy-start.4 = (bf16[1920,640]{1,0:T(8,128)(2,1)}, bf16[1920,640]{1,0:T(8,128)(2,1)S(1)}, u32[]{:S(2)}) copy-start(bf16[1920,640]{1,0:T(8,128)(2,1)S(1)} %unpack.2.weight_ref) | copy-start | bytes 7372804
  63.9 7.6 %copy-start.1 = (bf16[1920,640]{1,0:T(8,128)(2,1)}, bf16[1920,640]{1,0:T(8,128)(2,1)S(1)}, u32[]{:S(2)}) copy-start(bf16[1920,640]{1,0:T(8,128)(2,1)S(1)} %unpack.3.weight_ref) | copy-start | bytes 7372804
  70.9 5.9 %collective-permute-start.16 = (bf16[4,240,640]{2,1,0:T(8,128)(2,1)S(1)}, bf16[4,240,640]{2,1,0:T(8,128)(2,1)S(1)}, u32[]{:S(2)}, u32[]{:S(2)}) collective-permute-start(bf16[4,240,640]{2,1,0:T(8,128)(2,1)S(1)} %get-tuple-element.30), channel_id=1, source_target_pairs={{0,1},{1,0},{2,3},{3,2},{4,5},{5,4},{6,7},{7,6},{8,9},{9,8},{10,11... | collective-permute-start | bytes 3686408 | tf_op jit(solution)/shard_map/ppermute | solution.py:259
  80.9 4.2 %copy-start.5 = (f32[4,240,640]{2,1,0:T(8,128)}, f32[4,240,640]{2,1,0:T(8,128)S(1)}, u32[]{:S(2)}) copy-start(f32[4,240,640]{2,1,0:T(8,128)S(1)} %get-tuple-element.40) | copy-start | bytes 7372804
  80.9 3.0 %collective-permute-start.20 = (bf16[4,240,640]{2,1,0:T(8,128)(2,1)S(1)}, bf16[4,240,640]{2,1,0:T(8,128)(2,1)S(1)}, u32[]{:S(2)}, u32[]{:S(2)}) collective-permute-start(bf16[4,240,640]{2,1,0:T(8,128)(2,1)S(1)} %get-tuple-element.37), channel_id=1, source_target_pairs={{0,1},{1,0},{2,3},{3,2},{4,5},{5,4},{6,7},{7,6},{8,9},{9,8},{10,11... | collective-permute-start | bytes 3686408 | tf_op jit(solution)/shard_map/ppermute | solution.py:259
  85.0 11.6 %collective-permute-start.22 = (bf16[240,640]{1,0:T(8,128)(2,1)}, bf16[240,640]{1,0:T(8,128)(2,1)}, u32[]{:S(2)}, u32[]{:S(2)}) collective-permute-start(bf16[240,640]{1,0:T(8,128)(2,1)} %get-tuple-element.43), channel_id=1, source_target_pairs={{0,2},{1,3},{2,0},{3,1},{4,6},{5,7},{6,4},{7,5},{8,10},{9,11},{10,... | collective-permute-start | bytes 921608 | tf_op jit(solution)/shard_map/ppermute | solution.py:259
  85.2 7.8 %collective-permute-start.19 = (bf16[2,304,128]{2,1,0:T(8,128)(2,1)S(1)}, bf16[2,304,128]{2,1,0:T(8,128)(2,1)S(1)}, u32[]{:S(2)}, u32[]{:S(2)}) collective-permute-start(bf16[2,304,128]{2,1,0:T(8,128)(2,1)S(1)} %pad_maximum_fusion.7), channel_id=1, source_target_pairs={{0,24},{8,16},{16,8},{24,0},{1,25},{9,17},{17,9},{25,1},{2,26},{10... | collective-permute-start | bytes 466952 | tf_op jit(solution)/shard_map/ppermute | solution.py:259
  86.6 17.6 %copy-start.11 = (bf16[240,640]{1,0:T(8,128)(2,1)S(1)}, bf16[240,640]{1,0:T(8,128)(2,1)}, u32[]{:S(2)}) copy-start(bf16[240,640]{1,0:T(8,128)(2,1)} %get-tuple-element.42) | copy-start | bytes 921604
  86.6 17.6 %collective-permute-start.18 = (bf16[2,304,128]{2,1,0:T(8,128)(2,1)S(1)}, bf16[2,304,128]{2,1,0:T(8,128)(2,1)S(1)}, u32[]{:S(2)}, u32[]{:S(2)}) collective-permute-start(bf16[2,304,128]{2,1,0:T(8,128)(2,1)S(1)} %pad_maximum_fusion.7), channel_id=1, source_target_pairs={{0,16},{8,24},{16,0},{24,8},{1,17},{9,25},{17,1},{25,9},{2,18},{10... | collective-permute-start | bytes 466952 | tf_op jit(solution)/shard_map/ppermute | solution.py:259
  88.2 16.1 %collective-permute-start.17 = (bf16[2,304,128]{2,1,0:T(8,128)(2,1)S(1)}, bf16[2,304,128]{2,1,0:T(8,128)(2,1)S(1)}, u32[]{:S(2)}, u32[]{:S(2)}) collective-permute-start(bf16[2,304,128]{2,1,0:T(8,128)(2,1)S(1)} %pad_maximum_fusion.7), channel_id=1, source_target_pairs={{0,8},{8,0},{16,24},{24,16},{1,9},{9,1},{17,25},{25,17},{2,10},{10... | collective-permute-start | bytes 466952 | tf_op jit(solution)/shard_map/ppermute | solution.py:259
  88.7 18.7 %collective-permute-start.26 = (bf16[240,640]{1,0:T(8,128)(2,1)S(1)}, bf16[240,640]{1,0:T(8,128)(2,1)S(1)}, u32[]{:S(2)}, u32[]{:S(2)}) collective-permute-start(bf16[240,640]{1,0:T(8,128)(2,1)S(1)} %get-tuple-element.46), channel_id=1, source_target_pairs={{0,2},{1,3},{2,0},{3,1},{4,6},{5,7},{6,4},{7,5},{8,10},{9,11},{10,... | collective-permute-start | bytes 921608 | tf_op jit(solution)/shard_map/ppermute | solution.py:259
  93.0 25.0 %collective-permute-start.25 = (bf16[240,640]{1,0:T(8,128)(2,1)S(1)}, bf16[240,640]{1,0:T(8,128)(2,1)S(1)}, u32[]{:S(2)}, u32[]{:S(2)}) collective-permute-start(bf16[240,640]{1,0:T(8,128)(2,1)S(1)} %get-tuple-element.45), channel_id=1, source_target_pairs={{0,4},{1,5},{2,6},{3,7},{4,0},{5,1},{6,2},{7,3},{8,12},{9,13},{10,... | collective-permute-start | bytes 921608 | tf_op jit(solution)/shard_map/ppermute | solution.py:259
  96.6 21.4 %collective-permute-start.24 = (bf16[240,640]{1,0:T(8,128)(2,1)S(1)}, bf16[240,640]{1,0:T(8,128)(2,1)S(1)}, u32[]{:S(2)}, u32[]{:S(2)}) collective-permute-start(bf16[240,640]{1,0:T(8,128)(2,1)S(1)} %get-tuple-element.44), channel_id=1, source_target_pairs={{0,6},{1,7},{2,4},{3,5},{4,2},{5,3},{6,0},{7,1},{8,14},{9,15},{10,... | collective-permute-start | bytes 921608 | tf_op jit(solution)/shard_map/ppermute | solution.py:259
  104.2 18.3 %collective-permute-start.21 = (bf16[240,640]{1,0:T(8,128)(2,1)S(1)}, bf16[240,640]{1,0:T(8,128)(2,1)S(1)}, u32[]{:S(2)}, u32[]{:S(2)}) collective-permute-start(bf16[240,640]{1,0:T(8,128)(2,1)S(1)} %copy-done.11), channel_id=1, source_target_pairs={{0,2},{1,3},{2,0},{3,1},{4,6},{5,7},{6,4},{7,5},{8,10},{9,11},{10,... | collective-permute-start | bytes 921608 | tf_op jit(solution)/shard_map/ppermute | solution.py:259
  104.3 30.6 %collective-permute-start.23 = (bf16[240,640]{1,0:T(8,128)(2,1)S(1)}, bf16[240,640]{1,0:T(8,128)(2,1)S(1)}, u32[]{:S(2)}, u32[]{:S(2)}) collective-permute-start(bf16[240,640]{1,0:T(8,128)(2,1)S(1)} %fusion), channel_id=1, source_target_pairs={{0,4},{1,5},{2,6},{3,7},{4,0},{5,1},{6,2},{7,3},{8,12},{9,13},{10,... | collective-permute-start | bytes 921608 | tf_op jit(solution)/shard_map/ppermute | solution.py:259
  (7 other events, 15.8 us)

commit v3 on v2

v3 whole, which is shorter than its diff:
```python
import functools
import math

import jax
import jax.numpy as jnp
import numpy as np
from jax import lax
from jax.experimental import pallas as pl
from jax.experimental.pallas import tpu as pltpu
from jax.sharding import PartitionSpec as P

GN_GROUPS = 32
CHUNK = 128
MEGA = 1024 * 1024
BF16 = jnp.bfloat16
F32 = jnp.float32


def time_bias(step_index, ident, subject_table, time_proj):
    half_width = subject_table.shape[1] // 2
    freqs = jnp.exp(-math.log(10000.0) * jnp.arange(half_width, dtype=F32) / half_width)
    angles = step_index.astype(F32) * freqs
    embedding = jnp.concatenate([jnp.cos(angles), jnp.sin(angles)])
    onehot = (jnp.arange(subject_table.shape[0], dtype=jnp.int32) == ident).astype(F32)
    embedding = embedding + jnp.dot(onehot, subject_table, precision=lax.Precision.HIGHEST)
    activated = jax.nn.silu(embedding).astype(BF16)
    return jnp.dot(activated[None, :], time_proj, preferred_element_type=F32)


def vmem(count):
    return [pl.BlockSpec(memory_space=pltpu.VMEM)] * count


def smem(count):
    return [pl.BlockSpec(memory_space=pltpu.SMEM)] * count


def call(body, out_shape, scratch, name, in_specs):
    outs = len(out_shape)
    return pl.pallas_call(
        body,
        out_shape=tuple(jax.ShapeDtypeStruct(s, d) for s, d in out_shape),
        in_specs=in_specs,
        out_specs=tuple(vmem(outs)),
        scratch_shapes=scratch,
        compiler_params=pltpu.CompilerParams(vmem_limit_bytes=40 * MEGA),
        cost_estimate=pl.CostEstimate(flops=0, bytes_accessed=1024, transcendentals=0),
        name=name,
    )


def spread(row, same_group):
    high = row.astype(BF16)
    rest = row - high.astype(F32)
    middle = rest.astype(BF16)
    low = (rest - middle.astype(F32)).astype(BF16)
    stacked = jnp.concatenate(
        [jnp.broadcast_to(part, (16, row.shape[1])) for part in (high, middle, low)], axis=0
    )
    sums = jnp.dot(stacked, same_group, preferred_element_type=F32)
    return sums[0:1] + sums[16:17] + sums[32:33]


def norm_stats(read, rows, channels, same_group):
    counted = rows * (channels // GN_GROUPS)
    steps = rows // CHUNK
    total = lax.fori_loop(
        0,
        steps,
        lambda i, acc: acc + read(i).reshape(CHUNK // 8, 8, channels).sum(axis=0),
        jnp.zeros((8, channels), F32),
    ).sum(axis=0, keepdims=True)
    centre = spread(total, same_group) * (1.0 / counted)

    def squares(i, acc):
        centred = read(i) - centre
        return acc + (centred * centred).reshape(CHUNK // 8, 8, channels).sum(axis=0)

    square = lax.fori_loop(0, steps, squares, jnp.zeros((8, channels), F32)).sum(
        axis=0, keepdims=True
    )
    variance = spread(square, same_group) * (1.0 / counted)
    return centre, lax.rsqrt(variance + 1e-05)


def at(i, shift=0):
    return pl.ds(pl.multiple_of(i * CHUNK + shift, 64), CHUNK)


def clear_edges(padded_ref, points):
    edge = jnp.zeros((points, padded_ref.shape[1]), padded_ref.dtype)
    padded_ref[0:points] = edge
    padded_ref[padded_ref.shape[0] - points :] = edge


def enter_kernel(points, clip_ref, same_ref, padded_ref, turned_ref):
    rows, channels = clip_ref.shape
    same_group = same_ref[...]
    centre, inverse = norm_stats(
        lambda i: clip_ref[at(i)].astype(F32), rows, channels, same_group
    )
    clear_edges(padded_ref, points)

    @pl.loop(0, rows // CHUNK)
    def _(i):
        normal = (clip_ref[at(i)].astype(F32) - centre) * inverse
        act = (normal / (1.0 + jnp.exp(-normal))).astype(BF16)
        padded_ref[at(i, points)] = act
        turned_ref[:, at(i)] = act.T


def taps_of(padded_ref, start, size, points):
    return jnp.concatenate(
        [padded_ref[pl.ds(start + t * points, size)] for t in range(3)], axis=1
    )


def full_weight(weight_refs, full_ref):
    if len(weight_refs) == 1:
        return weight_refs[0]
    place_ref, mine_ref, other_ref = weight_refs
    member, rows = place_ref[1], mine_ref.shape[1]

    @pl.loop(0, mine_ref.shape[0])
    def _(k):
        for half, source in ((0, mine_ref), (1, other_ref)):
            start = pl.multiple_of((member ^ (2 * k + half)) * rows, 16)
            full_ref[pl.ds(start, rows)] = source[k]

    return full_ref


def first_kernel(points, scale, in_ref, bias_ref, *refs):
    weight_refs = refs[:-2]
    hidden_ref, full_ref = refs[-2:]
    half = hidden_ref.shape[0] // 2
    bias = bias_ref[...]
    weight_ref = full_weight(weight_refs, full_ref)

    @pl.loop(0, 2)
    def _(i):
        start = pl.multiple_of(i * half, 64)
        mixed = jnp.dot(
            taps_of(in_ref, start, half, points), weight_ref[...], preferred_element_type=F32
        )
        hidden_ref[pl.ds(start, half)] = scale * mixed + bias


def norm_kernel(
    points, hidden_ref, same_ref, normal_ref, inverse_ref, padded_ref, turned_ref
):
    rows, channels = normal_ref.shape
    centre, inverse = norm_stats(lambda i: hidden_ref[at(i)], rows, channels, same_ref[...])
    inverse_ref[...] = inverse
    clear_edges(padded_ref, points)

    @pl.loop(0, rows // CHUNK)
    def _(i):
        normal = (hidden_ref[at(i)] - centre) * inverse
        normal_ref[at(i)] = normal
        act = (normal / (1.0 + jnp.exp(-normal))).astype(BF16)
        padded_ref[at(i, points)] = act
        turned_ref[:, at(i)] = act.T


def second_kernel(points, scale, in_ref, clip_ref, target_ref, *refs):
    weight_refs = refs[:-2]
    error_ref, full_ref = refs[-2:]
    rows = clip_ref.shape[0]
    half = rows // 2
    clear_edges(error_ref, points)
    weight_ref = full_weight(weight_refs, full_ref)
    if len(weight_refs) == 1:
        full_ref[...] = weight_ref[...]

    @pl.loop(0, 2)
    def _(i):
        start = pl.multiple_of(i * half, 64)
        mixed = jnp.dot(
            taps_of(in_ref, start, half, points), weight_ref[...], preferred_element_type=F32
        )
        here = pl.ds(start, half)
        output = clip_ref[here].astype(F32) + scale * mixed
        error_ref[pl.ds(pl.multiple_of(start + points, 64), half)] = (
            output - target_ref[here].astype(F32)
        ).astype(BF16)


def back_kernel(points, scale, error_ref, weight_ref, grad_ref):
    rows, channels = grad_ref.shape
    half = rows // 2
    last = (((1,), (1,)), ((), ()))

    @pl.loop(0, 2)
    def _(i):
        start = pl.multiple_of(i * half, 64)
        total = None
        for t in range(3):
            part = lax.dot_general(
                error_ref[pl.ds(pl.multiple_of(start + (2 - t) * points, 64), half)],
                weight_ref[t * channels : (t + 1) * channels],
                last,
                preferred_element_type=F32,
            )
            total = part if total is None else total + part
        grad_ref[pl.ds(start, half)] = scale * total


def norm_back_kernel(
    points, act_grad_ref, normal_ref, inverse_ref, same_ref, out_ref, grad_ref
):
    rows, channels = normal_ref.shape
    counted = rows * (channels // GN_GROUPS)

    def through(i, sums):
        normal = normal_ref[at(i)]
        gate = 1.0 / (1.0 + jnp.exp(-normal))
        grad = act_grad_ref[at(i)] * (gate * (1.0 + normal * (1.0 - gate)))
        grad_ref[at(i)] = grad

        def fold(value):
            return value.reshape(CHUNK // 8, 8, channels).sum(axis=0)

        return sums[0] + fold(grad), sums[1] + fold(grad * normal)

    zero = jnp.zeros((8, channels), F32)
    plain, crossed = lax.fori_loop(0, rows // CHUNK, through, (zero, zero))
    same_group = same_ref[...]
    mean = spread(plain.sum(axis=0, keepdims=True), same_group) * (1.0 / counted)
    slope = spread(crossed.sum(axis=0, keepdims=True), same_group) * (1.0 / counted)
    inverse = inverse_ref[...]
    clear_edges(out_ref, points)

    @pl.loop(0, rows // CHUNK)
    def _(i):
        value = (grad_ref[at(i)] - mean - normal_ref[at(i)] * slope) * inverse
        out_ref[at(i, points)] = value.astype(BF16)


def grad_kernel(points, scale, block, centred, me_ref, turned_ref, cotangent_ref, *refs):
    channels, rows = turned_ref.shape
    refs = list(refs)
    total_ref = refs.pop()
    if centred:
        factor_ref = refs.pop()
        ones = jnp.ones((rows, 128), BF16)
        mean = jnp.dot(turned_ref[...], ones, preferred_element_type=F32) * (1.0 / rows)
        sums = scale * jnp.dot(
            jnp.ones((16, rows), BF16),
            cotangent_ref[pl.ds(points, rows)],
            preferred_element_type=F32,
        )
        factor_ref[0:1] = mean.T[0:1]
        factor_ref[1:2] = sums[0:1]
        factor_ref[2:8] = jnp.zeros((6, channels), F32)
        common = jnp.concatenate([mean] * (channels // 128), axis=1) * sums[0:1]

    @pl.loop(0, 3)
    def _(t):
        shifted = cotangent_ref[pl.ds(pl.multiple_of((2 - t) * points, 64), rows)]
        product = scale * jnp.dot(turned_ref[...], shifted, preferred_element_type=F32)
        if centred:
            product = product - common
        total_ref[pl.ds(pl.multiple_of(t * channels, 128), channels)] = product

    if block is not None:
        away_ref, home_ref = refs
        me = me_ref[0]

        @pl.loop(0, away_ref.shape[0])
        def _(j):
            away = pl.multiple_of((me ^ (2 * j + 1)) * block, 16)
            home = pl.multiple_of((me ^ (2 * j)) * block, 16)
            away_ref[j] = total_ref[pl.ds(away, block)].astype(BF16)
            home_ref[j] = total_ref[pl.ds(home, block)]


def gradient(turned, cotangent, me, n_member, points, scale, centred):
    channels, rows = turned.shape
    block = 3 * channels // n_member
    specs = smem(1) + vmem(2)
    factors = [((8, channels), F32)] if centred else []
    if block % 16 == 0:
        shape = (n_member // 2, block, channels)
        return call(
            functools.partial(grad_kernel, points, scale, block, centred),
            [(shape, BF16), (shape, F32)] + factors,
            [pltpu.VMEM((3 * channels, channels), F32)],
            "gradient", specs,
        )(me[None], turned, cotangent)
    found = call(
        functools.partial(grad_kernel, points, scale, None, centred),
        factors + [((3 * channels, channels), F32)],
        [], "gradient", specs,
    )(me[None], turned, cotangent)
    total = found[-1].reshape(n_member, block, channels)
    order = [lax.dynamic_index_in_dim(total, me ^ j, 0, keepdims=False) for j in range(n_member)]
    return (jnp.stack(order[1::2]).astype(BF16), jnp.stack(order[0::2])) + tuple(found[:-1])


def swap(value, axis, size, offset):
    return lax.ppermute(value, axis, [(i, i ^ offset) for i in range(size)])


def order_after(value, *others):
    return lax.optimization_barrier((value, others))[0]


TAIL = 64


def cut_of(rows):
    return -(-(rows + TAIL) // 32) * 16


def pack_kernel(*refs):
    sources, (early_ref, late_ref, rates_ref) = refs[:4], refs[4:7]
    held, sems = refs[7:11], refs[11]
    copies = [
        pltpu.make_async_copy(source, held[i], sems.at[i]) for i, source in enumerate(sources)
    ]
    for copy in copies:
        copy.start()
    cols, rows = held[0].shape
    size, cut = rows + TAIL, cut_of(rows)

    def packed(i):
        copies[i].wait()
        whole = held[i][...].T
        rest = jnp.concatenate(
            [whole[:, 128:cols], jnp.zeros((4 * TAIL - rows, cols - 128), BF16)], axis=0
        )
        rest = [rest[q * TAIL : (q + 1) * TAIL] for q in range(4)]
        return jnp.concatenate([whole[:, 0:128], jnp.concatenate(rest, axis=1)], axis=0)

    early_ref[0:size] = packed(0)
    second = packed(1)
    early_ref[size:] = second[0:cut]
    late_ref[...] = second[cut:]
    rates_ref[0] = packed(2)
    rates_ref[1] = packed(3)


def unpacked(block_of, rows, n_group):
    parts = []
    for g in range(n_group):
        block = block_of(g)
        rest = block[rows:]
        pieces = [rest[:, 32 * q : 32 * q + 32] for q in range(4)]
        parts += [block[0:rows], jnp.concatenate(pieces, axis=0)[0:rows]]
    return jnp.concatenate(parts, axis=1)


def split_kernel(*refs):
    count = len(refs) - 2
    one_ref, two_ref = refs[count:]
    size = one_ref.shape[1]
    for k, source in enumerate(refs[:count]):
        one_ref[k] = source[0:size]
        two_ref[k] = source[size:]


def weight_kernel(rows, n_group, place_ref, *refs):
    early_refs, late_refs, half_ref = refs[:n_group], refs[n_group:-1], refs[-1]
    for group in range(n_group):

        @pl.when(place_ref[0] == group)
        def _():
            @pl.loop(0, half_ref.shape[0])
            def _(k):
                def block_of(g):
                    parts = [early_refs[g ^ group][k]] + [ref[k, g ^ group] for ref in late_refs]
                    return jnp.concatenate(parts, axis=0)

                half_ref[k] = unpacked(block_of, rows, n_group)


def rate_kernel(rows, n_group, place_ref, packed_ref, one_ref, two_ref):
    group = place_ref[0]
    for which, out in enumerate((one_ref, two_ref)):
        out[...] = unpacked(lambda g: packed_ref[g ^ group, which], rows, n_group)


def along_z(value, n_member):
    chips = n_member // 2
    return [value] + [swap(value, "member", n_member, 2 * k) for k in range(1, chips)]


def across_groups(value, n_group):
    return [value] + [swap(value, "group", n_group, k) for k in range(1, n_group)]


def weights_and_rates(n_group, n_member, conv1, conv2, rate1, rate2, place, early):
    rows, cols = conv1.shape
    width = n_group * cols
    if (cols, n_group, rows % 16) != (160, 4, 0) or rows > 4 * TAIL:
        own = [lax.all_gather(w, "group", axis=1, tiled=True) for w in (conv1, conv2)]
        full = [lax.all_gather(w, "member", axis=0, tiled=True) for w in own]

        def rates(after):
            return [lax.all_gather(w, "group", axis=1, tiled=True) for w in (rate1, rate2)]

        return (full[0],), (full[1],), own[0], own[1], rates
    size, cut = rows + TAIL, cut_of(rows)
    early_rows, late_rows, both_rates = pl.pallas_call(
        pack_kernel,
        out_shape=(
            jax.ShapeDtypeStruct((size + cut, 128), BF16),
            jax.ShapeDtypeStruct((size - cut, 128), BF16),
            jax.ShapeDtypeStruct((2, size, 128), BF16),
        ),
        in_specs=[pl.BlockSpec(memory_space=pltpu.HBM)] * 4,
        out_specs=tuple(vmem(3)),
        scratch_shapes=[pltpu.VMEM((cols, rows), BF16)] * 4 + [pltpu.SemaphoreType.DMA((4,))],
        cost_estimate=pl.CostEstimate(flops=0, bytes_accessed=1024, transcendentals=0),
        name="pack",
    )(conv1.T, conv2.T, rate1.T, rate2.T)

    def unpack(*packed):
        shape = (n_member // 2, rows, width)
        (mine,) = call(
            functools.partial(weight_kernel, rows, n_group),
            [(shape, BF16)], [], "unpack", smem(1) + vmem(len(packed)),
        )(place, *packed)
        return place, mine, swap(mine, "member", n_member, 1)

    along = along_z(early_rows, n_member)
    late = jnp.stack(across_groups(order_after(late_rows, along[1]), n_group))
    along, late = order_after((along, late), early)
    chips = n_member // 2
    along_one, along_two = call(
        split_kernel,
        [((chips, size, 128), BF16), ((chips, cut, 128), BF16)], [], "split", vmem(chips),
    )(*along)
    crossed_one = across_groups(along_one, n_group)
    late = jnp.stack(along_z(order_after(late, crossed_one[1]), n_member))
    halves_one = unpack(*crossed_one)
    along_two = order_after(along_two, crossed_one)
    halves_two = unpack(*across_groups(along_two, n_group), late)

    def rates(after):
        blocks = jnp.stack(across_groups(order_after(both_rates, after), n_group))
        return call(
            functools.partial(rate_kernel, rows, n_group),
            [((rows, width), BF16)] * 2, [], "rates", smem(1) + vmem(1),
        )(place, blocks)

    return halves_one, halves_two, halves_one[1][0], halves_two[1][0], rates


def add_kernel(kept_ref, received_ref, *out_refs):
    away_ref, kept_out = out_refs[0], out_refs[1]

    for k in range(away_ref.shape[0]):
        away_ref[k] = (kept_ref[2 * k + 1] + received_ref[2 * k + 1].astype(F32)).astype(BF16)
        kept_out[k] = kept_ref[2 * k] + received_ref[2 * k].astype(F32)


def add_received(kept, received):
    half = (kept.shape[0] // 2,) + kept.shape[1:]
    return call(add_kernel, [(half, BF16), (half, F32)], [], "add", vmem(2))(kept, received)


def halve_to_owner(away, kept, received, n_member, bit=1):
    while True:
        if received is None:
            received = swap(away, "member", n_member, 2 * bit)
        if kept.shape[0] == 1:
            return kept[0], received[0]
        away, kept = add_received(kept, received)
        received = None
        bit *= 2


def update_kernel(own_ref, rate_ref, kept_ref, received_ref, *refs):
    total = kept_ref[...] + received_ref[...].astype(F32)
    if len(refs) > 1:
        total = total + refs[0][...]
    refs[-1][...] = own_ref[...].astype(F32) - rate_ref[...].astype(F32) * total


def update(*terms):
    shape = terms[0].shape
    return call(update_kernel, [(shape, F32)], [], "update", vmem(len(terms)))(*terms)[0]


def every_member(value, n_member):
    value = value[None]
    bit = 1
    while bit < n_member:
        value = jnp.concatenate([value, swap(value, "member", n_member, bit)])
        bit *= 2
    return value


def common_term(every, me, own_rows):
    mean = jnp.concatenate([every[:, 0]] * 3, axis=1)
    mean = lax.dynamic_slice_in_dim(mean, me * own_rows, own_rows, 1)
    return lax.dot_general(
        mean, every[:, 1], (((0,), (0,)), ((), ())), precision=lax.Precision.HIGHEST
    )


def shards(
    n_group,
    n_member,
    clips,
    targets,
    timestep,
    identity,
    conv1_weight,
    conv2_weight,
    rate1,
    rate2,
    time_proj,
    subject_table,
):
    frames, points, channels = (clips.shape[1], clips.shape[2], clips.shape[3])
    rows, padded = frames * points, (frames + 2) * points
    scale = 1.0 / math.sqrt(3 * channels)
    group, me = lax.axis_index("group"), lax.axis_index("member")
    place = jnp.stack([group, me]).astype(jnp.int32)
    own_rows = conv1_weight.shape[0]
    clip, target = clips.reshape(rows, channels), targets.reshape(rows, channels)
    blocks = np.arange(channels) // (channels // GN_GROUPS)
    same_group = jnp.asarray((blocks[:, None] == blocks[None, :]), BF16)

    bias_row = time_bias(timestep[0], identity[0], subject_table, time_proj)
    act_one, turned_one = call(
        functools.partial(enter_kernel, points),
        [((padded, channels), BF16), ((channels, rows), BF16)],
        [], "enter", vmem(2),
    )(clip, same_group)
    weight_one, weight_two, own_one, own_two, rates = weights_and_rates(
        n_group, n_member, conv1_weight, conv2_weight, rate1, rate2, place, (act_one, bias_row)
    )

    def weight_specs(weight):
        return vmem(1) if len(weight) == 1 else smem(1) + vmem(2)

    (hidden,) = call(
        functools.partial(first_kernel, points, scale),
        [((rows, channels), F32)],
        [pltpu.VMEM((3 * channels, channels), BF16)],
        "conv", vmem(2) + weight_specs(weight_one),
    )(act_one, bias_row, *weight_one)
    normal, inverse, act_two, turned_two = call(
        functools.partial(norm_kernel, points),
        [
            ((rows, channels), F32),
            ((1, channels), F32),
            ((padded, channels), BF16),
            ((channels, rows), BF16),
        ],
        [], "norm", vmem(2),
    )(order_after(hidden, weight_two[:2]), same_group)
    error, full_two = call(
        functools.partial(second_kernel, points, scale),
        [((padded, channels), BF16), ((3 * channels, channels), BF16)],
        [], "conv_error", vmem(3) + weight_specs(weight_two),
    )(act_two, clip, target, *weight_two)
    away_two, home_two, factors = gradient(
        turned_two, error, me, n_member, points, scale, True
    )
    received_two = swap(away_two, "member", n_member, 1)
    (grad_act,) = call(
        functools.partial(back_kernel, points, scale),
        [((rows, channels), F32)], [], "back", vmem(2),
    )(order_after(error, away_two), full_two)
    received_two, grad_act = lax.optimization_barrier((received_two, grad_act))
    away_two, kept_two = add_received(home_two, received_two)
    received_two = swap(away_two, "member", n_member, 2)
    rate_one, rate_two = rates(away_two)
    every = every_member(factors, n_member)
    (grad_hidden,) = call(
        functools.partial(norm_back_kernel, points),
        [((padded, channels), BF16)],
        [pltpu.VMEM((rows, channels), F32)],
        "norm_back", vmem(4),
    )(order_after(grad_act, away_two), normal, inverse, same_group)
    second = 1
    if kept_two.shape[0] > 1:
        second = 2
        away_two, kept_two = add_received(kept_two, received_two)
        received_two = None
    away_two, grad_hidden, every, rate_one, rate_two = lax.optimization_barrier(
        (away_two, grad_hidden, every, rate_one, rate_two)
    )
    away_one, home_one = gradient(
        turned_one, grad_hidden, me, n_member, points, scale, False
    )
    received_one = swap(away_one, "member", n_member, 1)
    common = common_term(every, me, own_rows)
    terms_two = halve_to_owner(away_two, kept_two, received_two, n_member, second)
    adapted_two = update(own_two, rate_two, *terms_two, common)
    away_one, kept_one = add_received(*order_after((home_one, received_one), terms_two[1]))
    adapted_one = update(
        own_one, rate_one, *halve_to_owner(away_one, kept_one, None, n_member)
    )
    return (adapted_one[None], adapted_two[None])


def solution(mesh):
    n_group, n_member = mesh.shape["group"], mesh.shape["member"]
    return jax.shard_map(
        lambda *arrays: shards(n_group, n_member, *arrays),
        mesh=mesh,
        in_specs=(
            P(("group", "member"), None, None, None),
            P(("group", "member"), None, None, None),
            P(("group", "member")),
            P(("group", "member")),
            P("member", "group"),
            P("member", "group"),
            P("member", "group"),
            P("member", "group"),
            P(),
            P(),
        ),
        out_specs=(P("group", "member", None), P("group", "member", None)),
        check_vma=False,
    )
```

time: 138 us -> 160 us (1.16)
  waiting for transfers between devices: 47.7 us -> 74.7 us
  starting transfers between devices: 39.8 us -> 34 us
  other arithmetic: 8.84 us -> 3.13 us
  Pallas kernels: 31.2 us -> 36.4 us
  matrix products: 0.56 us -> 2.92 us
    ppermute x27 -> x29, waiting for transfers between devices: 47.7 us -> 74.7 us  [swap(): return lax.ppermute(value, axis, [(i, i ^ offset) for i in range(size)])]
    pallas_call x7 -> x16, Pallas kernels: 20 us -> 26.1 us  [the longest x2 8.32 us: gradient(): call(functools.partial(grad_kernel, points, scale, block, centred), [(sha...]
    ppermute x27 -> x29, starting transfers between devices: 39.8 us -> 34 us  [swap(): return lax.ppermute(value, axis, [(i, i ^ offset) for i in range(size)])]
    broadcast_in_dim x2 -> x0, other arithmetic: 4.32 us -> none  [shards(): return (adapted_one[None], adapted_two[None])]
    unnamed x28 -> x47, local copies, waits for them, and re-layouts: 6.65 us -> 2.95 us
    convert_element_type x2 -> x0, other arithmetic: 2.48 us -> none  [halve_to_owner(): received = swap(pairs[k].astype(BF16), 'member', n_member, 2 * bit)]
    another operation x10 -> x3, other arithmetic: 0.3 us -> 2.31 us  [the longest x1 1.54 us: weights_and_rates(): late = jnp.stack(along_z(order_after(late, crossed_one[1]), n_member))]
    squeeze x0 -> x2, local copies, waits for them, and re-layouts: none -> 1.99 us  [weights_and_rates(): return (halves_one, halves_two, halves_one[1][0], halves_two[1][0], rates)]
  transfers between devices with their start and end apart: 27 -> 29, of which waited for: 13 -> 12; matrix products, arithmetic and copies ran while one was open for 4% -> 6% of each run, Pallas kernels for 12% -> 12%
where the time goes in v3:
time: 160 us
  waiting for transfers between devices  74.7 us (47%)
  Pallas kernels  36.4 us (23%)
  starting transfers between devices  34 us (21%)
  local copies, waits for them, and re-layouts  5.96 us (4%)
  other arithmetic  3.13 us (2%)
  matrix products  2.92 us (2%)
  between operations  2.44 us (2%)
    ppermute x29, waiting for transfers between devices, swap(): return lax.ppermute(value, axis, [(i, i ^ offset) for i in range(size)])  74.7 us
    ppermute x29, starting transfers between devices, swap(): return lax.ppermute(value, axis, [(i, i ^ offset) for i in range(size)])  34 us
    pallas_call x2, Pallas kernels, gradient(): call(functools.partial(grad_kernel, points, scale, block, centred), [(sha...  8.32 us
    pallas_call x1, Pallas kernels, shards(): call(functools.partial(second_kernel, points, scale), [((padded, channels...  3.93 us
    pallas_call x1, Pallas kernels, shards(): call(functools.partial(first_kernel, points, scale), [((rows, channels),...  3.92 us
    pallas_call x2, Pallas kernels, unpack(): call(functools.partial(weight_kernel, rows, n_group), [(shape, BF16)], []...  3.46 us
    pallas_call x1, Pallas kernels, shards(): call(functools.partial(back_kernel, points, scale), [((rows, channels), F...  3.43 us
  transfers between devices with their start and end apart: 29, of which 12 were waited for; matrix products, arithmetic and copies ran while one was open for 6% of the time, Pallas kernels for 12%

profile of v3, /device:TPU:0, one launch (start us, length us, event | category | flops | bytes accessed | tf_op | source)
XLA Modules:
  0.0 159.6 jit_solution(4066019554809681915)
XLA Ops:
  0.7 2.4 %pack.1 = (bf16[464,128]{1,0:T(8,128)(2,1)}, bf16[144,128]{1,0:T(8,128)(2,1)}, bf16[2,304,128]{2,1,0:T(8,128)(2,1)}) custom-call(bf16[160,240]{1,0:T(8,128)(2,1)} %bitcast.64, bf16[160,240]{1,0:T(8,128)(2,1)} %bitcast.65, bf16[160,240]{1,0:T(8,128)(2,1)} %bitcast.66, bf16[160,240]{1,0:T(8,128)(2,1)} %bitcast.67), custom_call_target="tpu_custom_call" | custom-call | bytes 1024 | tf_op jit(solution)/shard_map/pack/pallas_call | solution.py:405
  3.1 5.1 %collective-permute-start.2 = (bf16[464,128]{1,0:T(8,128)(2,1)}, bf16[464,128]{1,0:T(8,128)(2,1)S(1)}, u32[]{:S(2)}, u32[]{:S(2)}) collective-permute-start(bf16[464,128]{1,0:T(8,128)(2,1)} %get-tuple-element.55.refs_0_), channel_id=1, source_target_pairs={{0,6},{1,7},{2,4},{3,5},{4,2},{5,3},{6,0},{7,1},{8,14},{9,15},{10,... | collective-permute-start | bytes 356360 | tf_op jit(solution)/shard_map/ppermute | solution.py:302
  11.4 4.7 %collective-permute-done.refs_1_ = bf16[464,128]{1,0:T(8,128)(2,1)S(1)} collective-permute-done((bf16[464,128]{1,0:T(8,128)(2,1)}, bf16[464,128]{1,0:T(8,128)(2,1)S(1)}, u32[]{:S(2)}, u32[]{:S(2)}) %collective-permute-start) | collective-permute-done | bytes 118816 | tf_op jit(solution)/shard_map/ppermute | solution.py:302
  16.1 2.4 %collective-permute-start.5 = (bf16[144,128]{1,0:T(8,128)(2,1)}, bf16[144,128]{1,0:T(8,128)(2,1)S(1)}, u32[]{:S(2)}, u32[]{:S(2)}) collective-permute-start(bf16[144,128]{1,0:T(8,128)(2,1)} %get-tuple-element.53), channel_id=1, source_target_pairs={{0,24},{8,16},{16,8},{24,0},{1,25},{9,17},{17,9},{25,1},{2,26},{10... | collective-permute-start | bytes 110600 | tf_op jit(solution)/shard_map/ppermute | solution.py:302
  20.6 2.4 %enter.1 = (bf16[1024,640]{1,0:T(8,128)(2,1)S(1)}, bf16[640,896]{1,0:T(8,128)(2,1)S(1)}) custom-call(bf16[896,640]{1,0:T(8,128)(2,1)S(1)} %bitcast.46, bf16[640,640]{1,0:T(8,128)(2,1)S(1)} %copy-done.1), custom_call_target="tpu_custom_call" | custom-call | bytes 1024 | tf_op jit(solution)/shard_map/enter/pallas_call | solution.py:529
  25.9 1.6 collective-permute-start.6
  27.5 1.5 collective-permute-start.8
  29.5 6.8 %collective-permute-done.6.refs_1_ = bf16[4,304,128]{2,1,0:T(8,128)(2,1)S(1)} collective-permute-done((bf16[4,304,128]{2,1,0:T(8,128)(2,1)S(1)}, bf16[4,304,128]{2,1,0:T(8,128)(2,1)S(1)}, u32[]{:S(2)}, u32[]{:S(2)}) %collective-permute-start.6) | collective-permute-done | bytes 311328 | tf_op jit(solution)/shard_map/ppermute | solution.py:302
  36.3 2.0 %collective-permute-start.15 = (bf16[4,144,128]{2,1,0:T(8,128)(2,1)}, bf16[4,144,128]{2,1,0:T(8,128)(2,1)}, u32[]{:S(2)}, u32[]{:S(2)}) collective-permute-start(bf16[4,144,128]{2,1,0:T(8,128)(2,1)} %pad_maximum_fusion.3), channel_id=1, source_target_pairs={{0,6},{1,7},{2,4},{3,5},{4,2},{5,3},{6,0},{7,1},{8,14},{9,15},{10,... | collective-permute-start | bytes 442376 | tf_op jit(solution)/shard_map/ppermute | solution.py:302
  38.3 1.8 %collective-permute-start.14 = (bf16[4,144,128]{2,1,0:T(8,128)(2,1)}, bf16[4,144,128]{2,1,0:T(8,128)(2,1)}, u32[]{:S(2)}, u32[]{:S(2)}) collective-permute-start(bf16[4,144,128]{2,1,0:T(8,128)(2,1)} %pad_maximum_fusion.3), channel_id=1, source_target_pairs={{0,4},{1,5},{2,6},{3,7},{4,0},{5,1},{6,2},{7,3},{8,12},{9,13},{10,... | collective-permute-start | bytes 442376 | tf_op jit(solution)/shard_map/ppermute | solution.py:302
  41.1 3.8 %collective-permute-done.7.refs_2_ = bf16[4,304,128]{2,1,0:T(8,128)(2,1)} collective-permute-done((bf16[4,304,128]{2,1,0:T(8,128)(2,1)S(1)}, bf16[4,304,128]{2,1,0:T(8,128)(2,1)}, u32[]{:S(2)}, u32[]{:S(2)}) %collective-permute-start.7) | collective-permute-done | bytes 311328 | tf_op jit(solution)/shard_map/ppermute | solution.py:302
  44.9 1.4 collective-permute-start.12
  46.3 2.3 %collective-permute-start.11 = (bf16[4,160,128]{2,1,0:T(8,128)(2,1)S(1)}, bf16[4,160,128]{2,1,0:T(8,128)(2,1)S(1)}, u32[]{:S(2)}, u32[]{:S(2)}) collective-permute-start(bf16[4,160,128]{2,1,0:T(8,128)(2,1)S(1)} %get-tuple-element.61.refs_0_), channel_id=1, source_target_pairs={{0,16},{8,24},{16,0},{24,8},{1,17},{9,25},{17,1},{25,9},{2,18},{10... | collective-permute-start | bytes 491528 | tf_op jit(solution)/shard_map/ppermute | solution.py:302
  48.7 1.9 %unpack.2.refs_1_ = bf16[4,240,640]{2,1,0:T(8,128)(2,1)S(1)} custom-call(s32[2]{0:T(128)S(1)} %pad_add_fusion.place_ref.refs_0_, bf16[4,304,128]{2,1,0:T(8,128)(2,1)S(1)} %get-tuple-element.59.refs_0_, bf16[4,304,128]{2,1,0:T(8,128)(2,1)S(1)} %collective-permute-done.6.refs_1_, bf16[4,304,128]{2,1,0:T(8,128)(2,1)} %collective-permute-done.7.refs_2_, ...), custom_call_target="tpu_custom_call" | custom-call | bytes 1024 | tf_op jit(solution)/shard_map/unpack/pallas_call | solution.py:421
  50.7 1.5 pad_maximum_fusion.1.refs_4_
  53.9 1.6 %unpack.3.refs_1_ = bf16[4,240,640]{2,1,0:T(8,128)(2,1)S(1)} custom-call(s32[2]{0:T(128)S(1)} %pad_add_fusion.place_ref.refs_0_, bf16[4,160,128]{2,1,0:T(8,128)(2,1)S(1)} %get-tuple-element.61.refs_0_, bf16[4,160,128]{2,1,0:T(8,128)(2,1)S(1)} %collective-permute-done.10.refs_1_, bf16[4,160,128]{2,1,0:T(8,128)(2,1)S(1)} %collective-permute-done.11.refs_2_, ...), custom_call_target="tpu_custom_call" | custom-call | bytes 1024 | tf_op jit(solution)/shard_map/unpack/pallas_call | solution.py:421
  55.7 3.9 %conv.1.hidden_ref = f32[896,640]{1,0:T(8,128)S(1)} custom-call(bf16[1024,640]{1,0:T(8,128)(2,1)S(1)} %copy-done.7, f32[1,640]{1,0:T(1,128)S(1)} %copy-done.20, s32[2]{0:T(128)S(1)} %pad_add_fusion.place_ref.refs_0_, bf16[4,240,640]{2,1,0:T(8,128)(2,1)S(1)} %unpack.2.refs_1_, bf16[4,240,640]{2,1,0:T(8,128)(2,1)S(1)} %collective-permute-done.9.refs_2_), custom_call_target="tpu_custom_call" | custom-call | bytes 1024 | tf_op jit(solution)/shard_map/conv/pallas_call | solution.py:541
  59.6 2.2 %norm.1 = (f32[896,640]{1,0:T(8,128)S(1)}, f32[1,640]{1,0:T(1,128)S(1)}, bf16[1024,640]{1,0:T(8,128)(2,1)S(1)}, bf16[640,896]{1,0:T(8,128)(2,1)S(1)}) custom-call(f32[896,640]{1,0:T(8,128)S(1)} %conv.1.hidden_ref, bf16[640,640]{1,0:T(8,128)(2,1)S(1)} %copy-done.1), custom_call_target="tpu_custom_call" | custom-call | bytes 1024 | tf_op jit(solution)/shard_map/norm/pallas_call | solution.py:547
  61.9 3.9 %conv_error.1 = (bf16[1024,640]{1,0:T(8,128)(2,1)S(1)}, bf16[1920,640]{1,0:T(8,128)(2,1)S(1)}) custom-call(bf16[1024,640]{1,0:T(8,128)(2,1)S(1)} %get-tuple-element.66.in_ref, bf16[896,640]{1,0:T(8,128)(2,1)S(1)} %bitcast.47, bf16[896,640]{1,0:T(8,128)(2,1)S(1)} %bitcast.48, s32[2]{0:T(128)S(1)} %pad_add_fusion.place_ref.refs_0_, ...), custom_call_target="tpu_custom_call" | custom-call | bytes 1024 | tf_op jit(solution)/shard_map/conv_error/pallas_call | solution.py:557
  65.8 4.5 %gradient.2 = (bf16[4,240,640]{2,1,0:T(8,128)(2,1)S(1)}, f32[4,240,640]{2,1,0:T(8,128)S(1)}, f32[8,640]{1,0:T(8,128)S(1)}) custom-call(s32[1]{0:T(128)} %bitcast.1.me_ref, bf16[640,896]{1,0:T(8,128)(2,1)S(1)} %get-tuple-element.65.turned_ref, bf16[1024,640]{1,0:T(8,128)(2,1)S(1)} %get-tuple-element.70.cotangent_ref.error_ref), custom_call_target="tpu_custom_call" | custom-call | bytes 1024 | tf_op jit(solution)/shard_map/gradient/pallas_call | solution.py:285
  71.0 3.4 %back.1.act_grad_ref = f32[896,640]{1,0:T(8,128)S(1)} custom-call(bf16[1024,640]{1,0:T(8,128)(2,1)S(1)} %get-tuple-element.70.cotangent_ref.error_ref, bf16[1920,640]{1,0:T(8,128)(2,1)S(1)} %get-tuple-element.71.weight_ref), custom_call_target="tpu_custom_call" | custom-call | bytes 1024 | tf_op jit(solution)/shard_map/back/pallas_call | solution.py:566
  74.6 2.5 %collective-permute-start.18 = (bf16[2,240,640]{2,1,0:T(8,128)(2,1)S(1)}, bf16[2,240,640]{2,1,0:T(8,128)(2,1)S(1)}, u32[]{:S(2)}, u32[]{:S(2)}) collective-permute-start(bf16[2,240,640]{2,1,0:T(8,128)(2,1)S(1)} %get-tuple-element.74), channel_id=1, source_target_pairs={{0,2},{1,3},{2,0},{3,1},{4,6},{5,7},{6,4},{7,5},{8,10},{9,11},{10,... | collective-permute-start | bytes 1843208 | tf_op jit(solution)/shard_map/ppermute | solution.py:302
  77.2 15.2 %collective-permute-done.20 = f32[2,8,640]{2,1,0:T(8,128)S(1)} collective-permute-done((f32[2,8,640]{2,1,0:T(8,128)S(1)}, f32[2,8,640]{2,1,0:T(8,128)S(1)}, u32[]{:S(2)}, u32[]{:S(2)}) %collective-permute-start.20) | collective-permute-done | bytes 40992 | tf_op jit(solution)/shard_map/ppermute | solution.py:302
  94.5 1.6 %collective-permute-start.22 = (bf16[2,304,128]{2,1,0:T(8,128)(2,1)S(1)}, bf16[2,304,128]{2,1,0:T(8,128)(2,1)S(1)}, u32[]{:S(2)}, u32[]{:S(2)}) collective-permute-start(bf16[2,304,128]{2,1,0:T(8,128)(2,1)S(1)} %copy-done.21), channel_id=1, source_target_pairs={{0,8},{8,0},{16,24},{24,16},{1,9},{9,1},{17,25},{25,17},{2,10},{10... | collective-permute-start | bytes 466952 | tf_op jit(solution)/shard_map/ppermute | solution.py:302
  96.1 3.3 %collective-permute-done.21 = f32[4,8,640]{2,1,0:T(8,128)S(1)} collective-permute-done((f32[4,8,640]{2,1,0:T(8,128)S(1)}, f32[4,8,640]{2,1,0:T(8,128)S(1)}, u32[]{:S(2)}, u32[]{:S(2)}) %collective-permute-start.21) | collective-permute-done | bytes 81952 | tf_op jit(solution)/shard_map/ppermute | solution.py:302
  100.1 1.9 %norm_back.1.cotangent_ref = bf16[1024,640]{1,0:T(8,128)(2,1)S(1)} custom-call(f32[896,640]{1,0:T(8,128)S(1)} %back.1.act_grad_ref, f32[896,640]{1,0:T(8,128)S(1)} %get-tuple-element.78.normal_ref, f32[1,640]{1,0:T(1,128)S(1)} %get-tuple-element.79.inverse_ref, bf16[640,640]{1,0:T(8,128)(2,1)S(1)} %copy-done.1), custom_call_target="tpu_custom_call" | custom-call | bytes 1024 | tf_op jit(solution)/shard_map/norm_back/pallas_call | solution.py:575
  104.4 3.8 %gradient.3 = (bf16[4,240,640]{2,1,0:T(8,128)(2,1)S(1)}, f32[4,240,640]{2,1,0:T(8,128)S(1)}) custom-call(s32[1]{0:T(128)} %bitcast.1.me_ref, bf16[640,896]{1,0:T(8,128)(2,1)S(1)} %copy-done.9, bf16[1024,640]{1,0:T(8,128)(2,1)S(1)} %norm_back.1.cotangent_ref), custom_call_target="tpu_custom_call" | custom-call | bytes 1024 | tf_op jit(solution)/shard_map/gradient/pallas_call | solution.py:285
  108.3 2.6 %collective-permute-start.26 = (bf16[1,240,640]{2,1,0:T(8,128)(2,1)S(1)}, bf16[1,240,640]{2,1,0:T(8,128)(2,1)S(1)}, u32[]{:S(2)}, u32[]{:S(2)}) collective-permute-start(bf16[1,240,640]{2,1,0:T(8,128)(2,1)S(1)} %get-tuple-element.90), channel_id=1, source_target_pairs={{0,4},{1,5},{2,6},{3,7},{4,0},{5,1},{6,2},{7,3},{8,12},{9,13},{10,... | collective-permute-start | bytes 921608 | tf_op jit(solution)/shard_map/ppermute | solution.py:302
  110.9 14.5 %collective-permute-done.26 = bf16[1,240,640]{2,1,0:T(8,128)(2,1)S(1)} collective-permute-done((bf16[1,240,640]{2,1,0:T(8,128)(2,1)S(1)}, bf16[1,240,640]{2,1,0:T(8,128)(2,1)S(1)}, u32[]{:S(2)}, u32[]{:S(2)}) %collective-permute-start.26) | collective-permute-done | bytes 307232 | tf_op jit(solution)/shard_map/ppermute | solution.py:302
  129.2 13.0 %collective-permute-done.27.received_ref = bf16[2,240,640]{2,1,0:T(8,128)(2,1)S(1)} collective-permute-done((bf16[2,240,640]{2,1,0:T(8,128)(2,1)}, bf16[2,240,640]{2,1,0:T(8,128)(2,1)S(1)}, u32[]{:S(2)}, u32[]{:S(2)}) %collective-permute-start.27) | collective-permute-done | bytes 614432 | tf_op jit(solution)/shard_map/ppermute | solution.py:302
  142.3 2.8 %collective-permute-start.28 = (bf16[1,240,640]{2,1,0:T(8,128)(2,1)S(1)}, bf16[1,240,640]{2,1,0:T(8,128)(2,1)S(1)}, u32[]{:S(2)}, u32[]{:S(2)}) collective-permute-start(bf16[1,240,640]{2,1,0:T(8,128)(2,1)S(1)} %get-tuple-element.96), channel_id=1, source_target_pairs={{0,4},{1,5},{2,6},{3,7},{4,0},{5,1},{6,2},{7,3},{8,12},{9,13},{10,... | collective-permute-start | bytes 921608 | tf_op jit(solution)/shard_map/ppermute | solution.py:302
  147.9 10.7 %collective-permute-done.28 = bf16[1,240,640]{2,1,0:T(8,128)(2,1)S(1)} collective-permute-done((bf16[1,240,640]{2,1,0:T(8,128)(2,1)S(1)}, bf16[1,240,640]{2,1,0:T(8,128)(2,1)S(1)}, u32[]{:S(2)}, u32[]{:S(2)}) %collective-permute-start.28) | collective-permute-done | bytes 307232 | tf_op jit(solution)/shard_map/ppermute | solution.py:302
  (108 shorter events, 23.9 us)
Async XLA Ops:
  0.6 19.0 %copy-start = (bf16[1280,640]{1,0:T(8,128)(2,1)S(1)}, bf16[1280,640]{1,0:T(8,128)(2,1)}, u32[]{:S(2)}) copy-start(bf16[1280,640]{1,0:T(8,128)(2,1)} %param.19) | copy-start | bytes 4915204
  0.6 19.9 %copy-start.1 = (bf16[640,640]{1,0:T(8,128)(2,1)S(1)}, bf16[640,640]{1,0:T(8,128)(2,1)}, u32[]{:S(2)}) copy-start(bf16[640,640]{1,0:T(8,128)(2,1)} %constant.24.clone.same_ref) | copy-start | bytes 2457604
  3.1 22.8 %collective-permute-start.2 = (bf16[464,128]{1,0:T(8,128)(2,1)}, bf16[464,128]{1,0:T(8,128)(2,1)S(1)}, u32[]{:S(2)}, u32[]{:S(2)}) collective-permute-start(bf16[464,128]{1,0:T(8,128)(2,1)} %get-tuple-element.55.refs_0_), channel_id=1, source_target_pairs={{0,6},{1,7},{2,4},{3,5},{4,2},{5,3},{6,0},{7,1},{8,14},{9,15},{10,... | collective-permute-start | bytes 356360 | tf_op jit(solution)/shard_map/ppermute | solution.py:302
  8.2 17.7 %collective-permute-start.1 = (bf16[464,128]{1,0:T(8,128)(2,1)}, bf16[464,128]{1,0:T(8,128)(2,1)S(1)}, u32[]{:S(2)}, u32[]{:S(2)}) collective-permute-start(bf16[464,128]{1,0:T(8,128)(2,1)} %get-tuple-element.55.refs_0_), channel_id=1, source_target_pairs={{0,4},{1,5},{2,6},{3,7},{4,0},{5,1},{6,2},{7,3},{8,12},{9,13},{10,... | collective-permute-start | bytes 356360 | tf_op jit(solution)/shard_map/ppermute | solution.py:302
  8.2 7.9 %collective-permute-start = (bf16[464,128]{1,0:T(8,128)(2,1)}, bf16[464,128]{1,0:T(8,128)(2,1)S(1)}, u32[]{:S(2)}, u32[]{:S(2)}) collective-permute-start(bf16[464,128]{1,0:T(8,128)(2,1)} %get-tuple-element.55.refs_0_), channel_id=1, source_target_pairs={{0,2},{1,3},{2,0},{3,1},{4,6},{5,7},{6,4},{7,5},{8,10},{9,11},{10,... | collective-permute-start | bytes 356360 | tf_op jit(solution)/shard_map/ppermute | solution.py:302
  16.1 9.0 %collective-permute-start.5 = (bf16[144,128]{1,0:T(8,128)(2,1)}, bf16[144,128]{1,0:T(8,128)(2,1)S(1)}, u32[]{:S(2)}, u32[]{:S(2)}) collective-permute-start(bf16[144,128]{1,0:T(8,128)(2,1)} %get-tuple-element.53), channel_id=1, source_target_pairs={{0,24},{8,16},{16,8},{24,0},{1,25},{9,17},{17,9},{25,1},{2,26},{10... | collective-permute-start | bytes 110600 | tf_op jit(solution)/shard_map/ppermute | solution.py:302
  18.6 6.6 %collective-permute-start.4 = (bf16[144,128]{1,0:T(8,128)(2,1)}, bf16[144,128]{1,0:T(8,128)(2,1)S(1)}, u32[]{:S(2)}, u32[]{:S(2)}) collective-permute-start(bf16[144,128]{1,0:T(8,128)(2,1)} %get-tuple-element.53), channel_id=1, source_target_pairs={{0,16},{8,24},{16,0},{24,8},{1,17},{9,25},{17,1},{25,9},{2,18},{10... | collective-permute-start | bytes 110600 | tf_op jit(solution)/shard_map/ppermute | solution.py:302
  19.1 6.1 %collective-permute-start.3 = (bf16[144,128]{1,0:T(8,128)(2,1)}, bf16[144,128]{1,0:T(8,128)(2,1)S(1)}, u32[]{:S(2)}, u32[]{:S(2)}) collective-permute-start(bf16[144,128]{1,0:T(8,128)(2,1)} %get-tuple-element.53), channel_id=1, source_target_pairs={{0,8},{8,0},{16,24},{24,16},{1,9},{9,1},{17,25},{25,17},{2,10},{10... | collective-permute-start | bytes 110600 | tf_op jit(solution)/shard_map/ppermute | solution.py:302
  25.9 10.4 %collective-permute-start.6 = (bf16[4,304,128]{2,1,0:T(8,128)(2,1)S(1)}, bf16[4,304,128]{2,1,0:T(8,128)(2,1)S(1)}, u32[]{:S(2)}, u32[]{:S(2)}) collective-permute-start(bf16[4,304,128]{2,1,0:T(8,128)(2,1)S(1)} %get-tuple-element.59.refs_0_), channel_id=1, source_target_pairs={{0,8},{8,0},{16,24},{24,16},{1,9},{9,1},{17,25},{25,17},{2,10},{10... | collective-permute-start | bytes 933896 | tf_op jit(solution)/shard_map/ppermute | solution.py:302
  27.5 13.7 %collective-permute-start.8 = (bf16[4,304,128]{2,1,0:T(8,128)(2,1)S(1)}, bf16[4,304,128]{2,1,0:T(8,128)(2,1)S(1)}, u32[]{:S(2)}, u32[]{:S(2)}) collective-permute-start(bf16[4,304,128]{2,1,0:T(8,128)(2,1)S(1)} %get-tuple-element.59.refs_0_), channel_id=1, source_target_pairs={{0,24},{8,16},{16,8},{24,0},{1,25},{9,17},{17,9},{25,1},{2,26},{10... | collective-permute-start | bytes 933896 | tf_op jit(solution)/shard_map/ppermute | solution.py:302
  28.9 16.0 %collective-permute-start.7 = (bf16[4,304,128]{2,1,0:T(8,128)(2,1)S(1)}, bf16[4,304,128]{2,1,0:T(8,128)(2,1)}, u32[]{:S(2)}, u32[]{:S(2)}) collective-permute-start(bf16[4,304,128]{2,1,0:T(8,128)(2,1)S(1)} %get-tuple-element.59.refs_0_), channel_id=1, source_target_pairs={{0,16},{8,24},{16,0},{24,8},{1,17},{9,25},{17,1},{25,9},{2,18},{10... | collective-permute-start | bytes 933896 | tf_op jit(solution)/shard_map/ppermute | solution.py:302
  36.3 12.3 %collective-permute-start.15 = (bf16[4,144,128]{2,1,0:T(8,128)(2,1)}, bf16[4,144,128]{2,1,0:T(8,128)(2,1)}, u32[]{:S(2)}, u32[]{:S(2)}) collective-permute-start(bf16[4,144,128]{2,1,0:T(8,128)(2,1)} %pad_maximum_fusion.3), channel_id=1, source_target_pairs={{0,6},{1,7},{2,4},{3,5},{4,2},{5,3},{6,0},{7,1},{8,14},{9,15},{10,... | collective-permute-start | bytes 442376 | tf_op jit(solution)/shard_map/ppermute | solution.py:302
  38.3 12.3 %collective-permute-start.14 = (bf16[4,144,128]{2,1,0:T(8,128)(2,1)}, bf16[4,144,128]{2,1,0:T(8,128)(2,1)}, u32[]{:S(2)}, u32[]{:S(2)}) collective-permute-start(bf16[4,144,128]{2,1,0:T(8,128)(2,1)} %pad_maximum_fusion.3), channel_id=1, source_target_pairs={{0,4},{1,5},{2,6},{3,7},{4,0},{5,1},{6,2},{7,3},{8,12},{9,13},{10,... | collective-permute-start | bytes 442376 | tf_op jit(solution)/shard_map/ppermute | solution.py:302
  40.1 10.5 %collective-permute-start.13 = (bf16[4,144,128]{2,1,0:T(8,128)(2,1)}, bf16[4,144,128]{2,1,0:T(8,128)(2,1)}, u32[]{:S(2)}, u32[]{:S(2)}) collective-permute-start(bf16[4,144,128]{2,1,0:T(8,128)(2,1)} %pad_maximum_fusion.3), channel_id=1, source_target_pairs={{0,2},{1,3},{2,0},{3,1},{4,6},{5,7},{6,4},{7,5},{8,10},{9,11},{10,... | collective-permute-start | bytes 442376 | tf_op jit(solution)/shard_map/ppermute | solution.py:302
  44.9 7.3 %collective-permute-start.12 = (bf16[4,160,128]{2,1,0:T(8,128)(2,1)S(1)}, bf16[4,160,128]{2,1,0:T(8,128)(2,1)S(1)}, u32[]{:S(2)}, u32[]{:S(2)}) collective-permute-start(bf16[4,160,128]{2,1,0:T(8,128)(2,1)S(1)} %get-tuple-element.61.refs_0_), channel_id=1, source_target_pairs={{0,24},{8,16},{16,8},{24,0},{1,25},{9,17},{17,9},{25,1},{2,26},{10... | collective-permute-start | bytes 491528 | tf_op jit(solution)/shard_map/ppermute | solution.py:302
  46.3 6.5 %collective-permute-start.11 = (bf16[4,160,128]{2,1,0:T(8,128)(2,1)S(1)}, bf16[4,160,128]{2,1,0:T(8,128)(2,1)S(1)}, u32[]{:S(2)}, u32[]{:S(2)}) collective-permute-start(bf16[4,160,128]{2,1,0:T(8,128)(2,1)S(1)} %get-tuple-element.61.refs_0_), channel_id=1, source_target_pairs={{0,16},{8,24},{16,0},{24,8},{1,17},{9,25},{17,1},{25,9},{2,18},{10... | collective-permute-start | bytes 491528 | tf_op jit(solution)/shard_map/ppermute | solution.py:302
  48.6 5.3 %collective-permute-start.10 = (bf16[4,160,128]{2,1,0:T(8,128)(2,1)S(1)}, bf16[4,160,128]{2,1,0:T(8,128)(2,1)S(1)}, u32[]{:S(2)}, u32[]{:S(2)}) collective-permute-start(bf16[4,160,128]{2,1,0:T(8,128)(2,1)S(1)} %get-tuple-element.61.refs_0_), channel_id=1, source_target_pairs={{0,8},{8,0},{16,24},{24,16},{1,9},{9,1},{17,25},{25,17},{2,10},{10... | collective-permute-start | bytes 491528 | tf_op jit(solution)/shard_map/ppermute | solution.py:302
  50.6 5.1 %collective-permute-start.9 = (bf16[4,240,640]{2,1,0:T(8,128)(2,1)S(1)}, bf16[4,240,640]{2,1,0:T(8,128)(2,1)S(1)}, u32[]{:S(2)}, u32[]{:S(2)}) collective-permute-start(bf16[4,240,640]{2,1,0:T(8,128)(2,1)S(1)} %unpack.2.refs_1_), channel_id=1, source_target_pairs={{0,1},{1,0},{2,3},{3,2},{4,5},{5,4},{6,7},{7,6},{8,9},{9,8},{10,11... | collective-permute-start | bytes 3686408 | tf_op jit(solution)/shard_map/ppermute | solution.py:302
  55.5 6.3 %collective-permute-start.16 = (bf16[4,240,640]{2,1,0:T(8,128)(2,1)S(1)}, bf16[4,240,640]{2,1,0:T(8,128)(2,1)S(1)}, u32[]{:S(2)}, u32[]{:S(2)}) collective-permute-start(bf16[4,240,640]{2,1,0:T(8,128)(2,1)S(1)} %unpack.3.refs_1_), channel_id=1, source_target_pairs={{0,1},{1,0},{2,3},{3,2},{4,5},{5,4},{6,7},{7,6},{8,9},{9,8},{10,11... | collective-permute-start | bytes 3686408 | tf_op jit(solution)/shard_map/ppermute | solution.py:302
  70.3 4.1 %collective-permute-start.17 = (bf16[4,240,640]{2,1,0:T(8,128)(2,1)S(1)}, bf16[4,240,640]{2,1,0:T(8,128)(2,1)S(1)}, u32[]{:S(2)}, u32[]{:S(2)}) collective-permute-start(bf16[4,240,640]{2,1,0:T(8,128)(2,1)S(1)} %get-tuple-element.69), channel_id=1, source_target_pairs={{0,1},{1,0},{2,3},{3,2},{4,5},{5,4},{6,7},{7,6},{8,9},{9,8},{10,11... | collective-permute-start | bytes 3686408 | tf_op jit(solution)/shard_map/ppermute | solution.py:302
  70.9 6.2 %collective-permute-start.19 = (f32[1,8,640]{2,1,0:T(8,128)S(1)}, f32[1,8,640]{2,1,0:T(8,128)S(1)}, u32[]{:S(2)}, u32[]{:S(2)}) collective-permute-start(f32[1,8,640]{2,1,0:T(8,128)S(1)} %bitcast.53), channel_id=1, source_target_pairs={{0,1},{1,0},{2,3},{3,2},{4,5},{5,4},{6,7},{7,6},{8,9},{9,8},{10,11... | collective-permute-start | bytes 61448 | tf_op jit(solution)/shard_map/ppermute | solution.py:302
  74.4 18.2 %copy-start.21 = (bf16[2,304,128]{2,1,0:T(8,128)(2,1)S(1)}, bf16[2,304,128]{2,1,0:T(8,128)(2,1)}, u32[]{:S(2)}) copy-start(bf16[2,304,128]{2,1,0:T(8,128)(2,1)} %get-tuple-element.82) | copy-start | bytes 466948
  74.6 29.6 %collective-permute-start.18 = (bf16[2,240,640]{2,1,0:T(8,128)(2,1)S(1)}, bf16[2,240,640]{2,1,0:T(8,128)(2,1)S(1)}, u32[]{:S(2)}, u32[]{:S(2)}) collective-permute-start(bf16[2,240,640]{2,1,0:T(8,128)(2,1)S(1)} %get-tuple-element.74), channel_id=1, source_target_pairs={{0,2},{1,3},{2,0},{3,1},{4,6},{5,7},{6,4},{7,5},{8,10},{9,11},{10,... | collective-permute-start | bytes 1843208 | tf_op jit(solution)/shard_map/ppermute | solution.py:302
  77.1 15.3 %collective-permute-start.20 = (f32[2,8,640]{2,1,0:T(8,128)S(1)}, f32[2,8,640]{2,1,0:T(8,128)S(1)}, u32[]{:S(2)}, u32[]{:S(2)}) collective-permute-start(f32[2,8,640]{2,1,0:T(8,128)S(1)} %pad_maximum_fusion.5), channel_id=1, source_target_pairs={{0,2},{1,3},{2,0},{3,1},{4,6},{5,7},{6,4},{7,5},{8,10},{9,11},{10,... | collective-permute-start | bytes 122888 | tf_op jit(solution)/shard_map/ppermute | solution.py:302
  92.4 7.0 %collective-permute-start.21 = (f32[4,8,640]{2,1,0:T(8,128)S(1)}, f32[4,8,640]{2,1,0:T(8,128)S(1)}, u32[]{:S(2)}, u32[]{:S(2)}) collective-permute-start(f32[4,8,640]{2,1,0:T(8,128)S(1)} %pad_maximum_fusion.4), channel_id=1, source_target_pairs={{0,4},{1,5},{2,6},{3,7},{4,0},{5,1},{6,2},{7,3},{8,12},{9,13},{10,... | collective-permute-start | bytes 245768 | tf_op jit(solution)/shard_map/ppermute | solution.py:302
  92.6 9.4 %collective-permute-start.24 = (bf16[2,304,128]{2,1,0:T(8,128)(2,1)S(1)}, bf16[2,304,128]{2,1,0:T(8,128)(2,1)S(1)}, u32[]{:S(2)}, u32[]{:S(2)}) collective-permute-start(bf16[2,304,128]{2,1,0:T(8,128)(2,1)S(1)} %copy-done.21), channel_id=1, source_target_pairs={{0,24},{8,16},{16,8},{24,0},{1,25},{9,17},{17,9},{25,1},{2,26},{10... | collective-permute-start | bytes 466952 | tf_op jit(solution)/shard_map/ppermute | solution.py:302
  93.8 8.7 %collective-permute-start.23 = (bf16[2,304,128]{2,1,0:T(8,128)(2,1)S(1)}, bf16[2,304,128]{2,1,0:T(8,128)(2,1)S(1)}, u32[]{:S(2)}, u32[]{:S(2)}) collective-permute-start(bf16[2,304,128]{2,1,0:T(8,128)(2,1)S(1)} %copy-done.21), channel_id=1, source_target_pairs={{0,16},{8,24},{16,0},{24,8},{1,17},{9,25},{17,1},{25,9},{2,18},{10... | collective-permute-start | bytes 466952 | tf_op jit(solution)/shard_map/ppermute | solution.py:302
  94.5 8.1 %collective-permute-start.22 = (bf16[2,304,128]{2,1,0:T(8,128)(2,1)S(1)}, bf16[2,304,128]{2,1,0:T(8,128)(2,1)S(1)}, u32[]{:S(2)}, u32[]{:S(2)}) collective-permute-start(bf16[2,304,128]{2,1,0:T(8,128)(2,1)S(1)} %copy-done.21), channel_id=1, source_target_pairs={{0,8},{8,0},{16,24},{24,16},{1,9},{9,1},{17,25},{25,17},{2,10},{10... | collective-permute-start | bytes 466952 | tf_op jit(solution)/shard_map/ppermute | solution.py:302
  108.2 17.3 %collective-permute-start.25 = (bf16[4,240,640]{2,1,0:T(8,128)(2,1)S(1)}, bf16[4,240,640]{2,1,0:T(8,128)(2,1)S(1)}, u32[]{:S(2)}, u32[]{:S(2)}) collective-permute-start(bf16[4,240,640]{2,1,0:T(8,128)(2,1)S(1)} %get-tuple-element.89), channel_id=1, source_target_pairs={{0,1},{1,0},{2,3},{3,2},{4,5},{5,4},{6,7},{7,6},{8,9},{9,8},{10,11... | collective-permute-start | bytes 3686408 | tf_op jit(solution)/shard_map/ppermute | solution.py:302
  108.3 17.2 %collective-permute-start.26 = (bf16[1,240,640]{2,1,0:T(8,128)(2,1)S(1)}, bf16[1,240,640]{2,1,0:T(8,128)(2,1)S(1)}, u32[]{:S(2)}, u32[]{:S(2)}) collective-permute-start(bf16[1,240,640]{2,1,0:T(8,128)(2,1)S(1)} %get-tuple-element.90), channel_id=1, source_target_pairs={{0,4},{1,5},{2,6},{3,7},{4,0},{5,1},{6,2},{7,3},{8,12},{9,13},{10,... | collective-permute-start | bytes 921608 | tf_op jit(solution)/shard_map/ppermute | solution.py:302
  126.5 15.6 %collective-permute-start.27 = (bf16[2,240,640]{2,1,0:T(8,128)(2,1)}, bf16[2,240,640]{2,1,0:T(8,128)(2,1)S(1)}, u32[]{:S(2)}, u32[]{:S(2)}) collective-permute-start(bf16[2,240,640]{2,1,0:T(8,128)(2,1)} %get-tuple-element.94), channel_id=1, source_target_pairs={{0,2},{1,3},{2,0},{3,1},{4,6},{5,7},{6,4},{7,5},{8,10},{9,11},{10,... | collective-permute-start | bytes 1843208 | tf_op jit(solution)/shard_map/ppermute | solution.py:302
  142.3 16.3 %collective-permute-start.28 = (bf16[1,240,640]{2,1,0:T(8,128)(2,1)S(1)}, bf16[1,240,640]{2,1,0:T(8,128)(2,1)S(1)}, u32[]{:S(2)}, u32[]{:S(2)}) collective-permute-start(bf16[1,240,640]{2,1,0:T(8,128)(2,1)S(1)} %get-tuple-element.96), channel_id=1, source_target_pairs={{0,4},{1,5},{2,6},{3,7},{4,0},{5,1},{6,2},{7,3},{8,12},{9,13},{10,... | collective-permute-start | bytes 921608 | tf_op jit(solution)/shard_map/ppermute | solution.py:302
  (20 other events, 89.5 us)

commit v4 on v3

--- a/solution.py
+++ b/solution.py
@@ -31,6 +31,10 @@
     return [pl.BlockSpec(memory_space=pltpu.VMEM)] * count
 
 
+def hbm(count):
+    return [pl.BlockSpec(memory_space=pltpu.HBM)] * count
+
+
 def smem(count):
     return [pl.BlockSpec(memory_space=pltpu.SMEM)] * count
 
@@ -43,7 +47,7 @@
         in_specs=in_specs,
         out_specs=tuple(vmem(outs)),
         scratch_shapes=scratch,
-        compiler_params=pltpu.CompilerParams(vmem_limit_bytes=40 * MEGA),
+        compiler_params=pltpu.CompilerParams(vmem_limit_bytes=24 * MEGA),
         cost_estimate=pl.CostEstimate(flops=0, bytes_accessed=1024, transcendentals=0),
         name=name,
     )
@@ -93,11 +97,22 @@
     padded_ref[padded_ref.shape[0] - points :] = edge
 
 
-def enter_kernel(points, clip_ref, same_ref, padded_ref, turned_ref):
+def fetch(sources, held, sems):
+    copies = [
+        pltpu.make_async_copy(source, place, sems.at[i])
+        for i, (source, place) in enumerate(zip(sources, held))
+    ]
+    for copy in copies:
+        copy.start()
+    return copies
+
+
+def enter_kernel(points, clip_hbm, same_hbm, padded_ref, turned_ref, same_ref, clip_ref, sems):
     rows, channels = clip_ref.shape
-    same_group = same_ref[...]
+    for copy in fetch((clip_hbm, same_hbm), (clip_ref, same_ref), sems):
+        copy.wait()
     centre, inverse = norm_stats(
-        lambda i: clip_ref[at(i)].astype(F32), rows, channels, same_group
+        lambda i: clip_ref[at(i)].astype(F32), rows, channels, same_ref[...]
     )
     clear_edges(padded_ref, points)
 
@@ -163,15 +178,18 @@
         turned_ref[:, at(i)] = act.T
 
 
-def second_kernel(points, scale, in_ref, clip_ref, target_ref, *refs):
-    weight_refs = refs[:-2]
-    error_ref, full_ref = refs[-2:]
+def second_kernel(points, scale, in_ref, clip_hbm, target_hbm, *refs):
+    weight_refs = refs[:-5]
+    error_ref, full_ref, clip_ref, target_ref, sems = refs[-5:]
+    copies = fetch((clip_hbm, target_hbm), (clip_ref, target_ref), sems)
     rows = clip_ref.shape[0]
     half = rows // 2
     clear_edges(error_ref, points)
     weight_ref = full_weight(weight_refs, full_ref)
     if len(weight_refs) == 1:
         full_ref[...] = weight_ref[...]
+    for copy in copies:
+        copy.wait()
 
     @pl.loop(0, 2)
     def _(i):
@@ -237,12 +255,20 @@
         out_ref[at(i, points)] = value.astype(BF16)
 
 
+FACTOR_ROWS = 16
+
+
+def split_rows(row):
+    high = row.astype(BF16).astype(F32)
+    middle = (row - high).astype(BF16).astype(F32)
+    return [high, middle, row - high - middle]
+
+
 def grad_kernel(points, scale, block, centred, me_ref, turned_ref, cotangent_ref, *refs):
     channels, rows = turned_ref.shape
     refs = list(refs)
     total_ref = refs.pop()
     if centred:
-        factor_ref = refs.pop()
         ones = jnp.ones((rows, 128), BF16)
         mean = jnp.dot(turned_ref[...], ones, preferred_element_type=F32) * (1.0 / rows)
         sums = scale * jnp.dot(
@@ -250,9 +276,9 @@
             cotangent_ref[pl.ds(points, rows)],
             preferred_element_type=F32,
         )
-        factor_ref[0:1] = mean.T[0:1]
-        factor_ref[1:2] = sums[0:1]
-        factor_ref[2:8] = jnp.zeros((6, channels), F32)
+        factors = split_rows(mean.T[0:1]) + split_rows(sums[0:1])
+        factors += [jnp.zeros((FACTOR_ROWS - len(factors), channels), F32)]
+        factors = jnp.concatenate(factors, axis=0)
         common = jnp.concatenate([mean] * (channels // 128), axis=1) * sums[0:1]
 
     @pl.loop(0, 3)
@@ -264,30 +290,38 @@
         total_ref[pl.ds(pl.multiple_of(t * channels, 128), channels)] = product
 
     if block is not None:
-        away_ref, home_ref = refs
+        away_ref, home_ref = refs[:2]
         me = me_ref[0]
-
-        @pl.loop(0, away_ref.shape[0])
+        count = home_ref.shape[0]
+
+        @pl.loop(0, count)
         def _(j):
             away = pl.multiple_of((me ^ (2 * j + 1)) * block, 16)
             home = pl.multiple_of((me ^ (2 * j)) * block, 16)
-            away_ref[j] = total_ref[pl.ds(away, block)].astype(BF16)
+            place = pl.ds(pl.multiple_of(j * block, 16), block)
+            away_ref[place] = total_ref[pl.ds(away, block)].astype(BF16)
             home_ref[j] = total_ref[pl.ds(home, block)]
+
+        if centred:
+            away_ref[count * block :] = factors.astype(BF16)
+    elif centred:
+        refs[0][...] = factors
 
 
 def gradient(turned, cotangent, me, n_member, points, scale, centred):
     channels, rows = turned.shape
     block = 3 * channels // n_member
     specs = smem(1) + vmem(2)
-    factors = [((8, channels), F32)] if centred else []
     if block % 16 == 0:
-        shape = (n_member // 2, block, channels)
+        chips = n_member // 2
+        extra = FACTOR_ROWS if centred else 0
         return call(
             functools.partial(grad_kernel, points, scale, block, centred),
-            [(shape, BF16), (shape, F32)] + factors,
+            [((chips * block + extra, channels), BF16), ((chips, block, channels), F32)],
             [pltpu.VMEM((3 * channels, channels), F32)],
             "gradient", specs,
         )(me[None], turned, cotangent)
+    factors = [((FACTOR_ROWS, channels), F32)] if centred else []
     found = call(
         functools.partial(grad_kernel, points, scale, None, centred),
         factors + [((3 * channels, channels), F32)],
@@ -295,7 +329,8 @@
     )(me[None], turned, cotangent)
     total = found[-1].reshape(n_member, block, channels)
     order = [lax.dynamic_index_in_dim(total, me ^ j, 0, keepdims=False) for j in range(n_member)]
-    return (jnp.stack(order[1::2]).astype(BF16), jnp.stack(order[0::2])) + tuple(found[:-1])
+    away, home = jnp.stack(order[1::2]).astype(BF16), jnp.stack(order[0::2])
+    return (away, home) + tuple(found[:-1])
 
 
 def swap(value, axis, size, offset):
@@ -310,17 +345,13 @@
 
 
 def cut_of(rows):
-    return -(-(rows + TAIL) // 32) * 16
+    return (rows + TAIL) * 3 // 128 * 16
 
 
 def pack_kernel(*refs):
     sources, (early_ref, late_ref, rates_ref) = refs[:4], refs[4:7]
     held, sems = refs[7:11], refs[11]
-    copies = [
-        pltpu.make_async_copy(source, held[i], sems.at[i]) for i, source in enumerate(sources)
-    ]
-    for copy in copies:
-        copy.start()
+    copies = fetch(sources, held, sems)
     cols, rows = held[0].shape
     size, cut = rows + TAIL, cut_of(rows)
 
@@ -352,27 +383,51 @@
 
 
 def split_kernel(*refs):
-    count = len(refs) - 2
-    one_ref, two_ref = refs[count:]
-    size = one_ref.shape[1]
-    for k, source in enumerate(refs[:count]):
-        one_ref[k] = source[0:size]
+    first_ref, second_ref, two_ref = refs[-3:]
+    half, size = first_ref.shape[0], first_ref.shape[1]
+    for k, source in enumerate(refs[:-3]):
+        (first_ref if k < half else second_ref)[k % half] = source[0:size]
         two_ref[k] = source[size:]
 
 
-def weight_kernel(rows, n_group, place_ref, *refs):
-    early_refs, late_refs, half_ref = refs[:n_group], refs[n_group:-1], refs[-1]
+def for_group(place_ref, n_group, half_ref, rows, block_of):
     for group in range(n_group):
 
         @pl.when(place_ref[0] == group)
         def _():
-            @pl.loop(0, half_ref.shape[0])
-            def _(k):
-                def block_of(g):
-                    parts = [early_refs[g ^ group][k]] + [ref[k, g ^ group] for ref in late_refs]
-                    return jnp.concatenate(parts, axis=0)
-
-                half_ref[k] = unpacked(block_of, rows, n_group)
+            block_of(
+                lambda k, pick: half_ref.__setitem__(
+                    k, unpacked(lambda g: pick(g ^ group), rows, n_group)
+                )
+            )
+
+
+def two_step_kernel(rows, place_ref, *refs):
+    first, first_x, first_y, second, second_y, second_x, half_ref = refs
+    half = half_ref.shape[0] // 2
+
+    def fill(store):
+        @pl.loop(0, half)
+        def _(k):
+            pick = (first, first_x, first_y.at[0], first_y.at[1])
+            store(k, lambda d: pick[d][k])
+            late = (second, second_x.at[0], second_y, second_x.at[1])
+            store(half + k, lambda d: late[d][k])
+
+    for_group(place_ref, 4, half_ref, rows, fill)
+
+
+def direct_kernel(rows, n_group, place_ref, *refs):
+    early_refs, late_refs, half_ref = refs[:n_group], refs[n_group:-1], refs[-1]
+
+    def fill(store):
+        @pl.loop(0, half_ref.shape[0] // 2)
+        def _(i):
+            for odd, late_ref in enumerate(late_refs):
+                k = 2 * i + odd
+                store(k, lambda d: jnp.concatenate([early_refs[d][k], late_ref[i, d]], axis=0))
+
+    for_group(place_ref, n_group, half_ref, rows, fill)
 
 
 def rate_kernel(rows, n_group, place_ref, packed_ref, one_ref, two_ref):
@@ -390,53 +445,70 @@
     return [value] + [swap(value, "group", n_group, k) for k in range(1, n_group)]
 
 
-def weights_and_rates(n_group, n_member, conv1, conv2, rate1, rate2, place, early):
+def weights_and_rates(n_group, n_member, conv1, conv2, rate1, rate2, place, clip, enter, bias_row):
     rows, cols = conv1.shape
     width = n_group * cols
-    if (cols, n_group, rows % 16) != (160, 4, 0) or rows > 4 * TAIL:
+    if (cols, n_group, n_member, rows % 16) != (160, 4, 8, 0) or rows > 4 * TAIL:
         own = [lax.all_gather(w, "group", axis=1, tiled=True) for w in (conv1, conv2)]
         full = [lax.all_gather(w, "member", axis=0, tiled=True) for w in own]
 
         def rates(after):
             return [lax.all_gather(w, "group", axis=1, tiled=True) for w in (rate1, rate2)]
 
-        return (full[0],), (full[1],), own[0], own[1], rates
-    size, cut = rows + TAIL, cut_of(rows)
-    early_rows, late_rows, both_rates = pl.pallas_call(
+        second = lambda after: (full[1], own[1][None])
+        return (full[0],), second, own[0][None], rates, enter(clip), bias_row
+    size, cut, chips = rows + TAIL, cut_of(rows), n_member // 2
+    early_rows, late, both_rates = pl.pallas_call(
         pack_kernel,
         out_shape=(
             jax.ShapeDtypeStruct((size + cut, 128), BF16),
             jax.ShapeDtypeStruct((size - cut, 128), BF16),
             jax.ShapeDtypeStruct((2, size, 128), BF16),
         ),
-        in_specs=[pl.BlockSpec(memory_space=pltpu.HBM)] * 4,
+        in_specs=hbm(4),
         out_specs=tuple(vmem(3)),
         scratch_shapes=[pltpu.VMEM((cols, rows), BF16)] * 4 + [pltpu.SemaphoreType.DMA((4,))],
+        compiler_params=pltpu.CompilerParams(vmem_limit_bytes=40 * MEGA),
         cost_estimate=pl.CostEstimate(flops=0, bytes_accessed=1024, transcendentals=0),
         name="pack",
     )(conv1.T, conv2.T, rate1.T, rate2.T)
 
-    def unpack(*packed):
-        shape = (n_member // 2, rows, width)
+    def unpack(kernel, *packed):
         (mine,) = call(
-            functools.partial(weight_kernel, rows, n_group),
-            [(shape, BF16)], [], "unpack", smem(1) + vmem(len(packed)),
+            kernel, [((chips, rows, width), BF16)], [], "unpack", smem(1) + vmem(len(packed))
         )(place, *packed)
         return place, mine, swap(mine, "member", n_member, 1)
 
     along = along_z(early_rows, n_member)
-    late = jnp.stack(across_groups(order_after(late_rows, along[1]), n_group))
-    along, late = order_after((along, late), early)
-    chips = n_member // 2
-    along_one, along_two = call(
+    late_x = swap(late, "group", n_group, 1)
+    late_x, bias_row = order_after((late_x, bias_row), ())
+    late = jnp.stack([late, late_x])
+    late_y = swap(late, "group", n_group, 2)
+    act = enter(order_after(clip, (late, bias_row)))
+    along, late_y, act = order_after((along, late_y, act), ())
+    first, second, along_two = call(
         split_kernel,
-        [((chips, size, 128), BF16), ((chips, cut, 128), BF16)], [], "split", vmem(chips),
+        [((chips // 2, size, 128), BF16)] * 2 + [((chips, cut, 128), BF16)], [],
+        "split", vmem(chips),
     )(*along)
-    crossed_one = across_groups(along_one, n_group)
-    late = jnp.stack(along_z(order_after(late, crossed_one[1]), n_member))
-    halves_one = unpack(*crossed_one)
-    along_two = order_after(along_two, crossed_one)
-    halves_two = unpack(*across_groups(along_two, n_group), late)
+    first_x = swap(first, "group", n_group, 1)
+    second_y = swap(second, "group", n_group, 2)
+    late = order_after(jnp.concatenate([late, late_y]), first)
+    late = [late]
+    late_z = swap(late[0], "member", n_member, 2 * (chips // 2))
+    first_y = swap(jnp.stack([first, first_x]), "group", n_group, 2)
+    second_x = swap(jnp.stack([second, second_y]), "group", n_group, 1)
+    late = jnp.stack(late + [late_z])
+    late_z = swap(late, "member", n_member, 2)
+    halves_one = unpack(
+        functools.partial(two_step_kernel, rows),
+        order_after(first, late), first_x, first_y, second, second_y, second_x,
+    )
+    along_two = across_groups(order_after(along_two, halves_one[1]), n_group)
+
+    def halves_two(after):
+        kernel = functools.partial(direct_kernel, rows, n_group)
+        return unpack(kernel, *along_two, *order_after((late, late_z), after))
 
     def rates(after):
         blocks = jnp.stack(across_groups(order_after(both_rates, after), n_group))
@@ -445,7 +517,7 @@
             [((rows, width), BF16)] * 2, [], "rates", smem(1) + vmem(1),
         )(place, blocks)
 
-    return halves_one, halves_two, halves_one[1][0], halves_two[1][0], rates
+    return halves_one, halves_two, halves_one[1], rates, act, bias_row
 
 
 def add_kernel(kept_ref, received_ref, *out_refs):
@@ -472,32 +544,66 @@
         bit *= 2
 
 
-def update_kernel(own_ref, rate_ref, kept_ref, received_ref, *refs):
-    total = kept_ref[...] + received_ref[...].astype(F32)
-    if len(refs) > 1:
-        total = total + refs[0][...]
-    refs[-1][...] = own_ref[...].astype(F32) - rate_ref[...].astype(F32) * total
-
-
-def update(*terms):
-    shape = terms[0].shape
-    return call(update_kernel, [(shape, F32)], [], "update", vmem(len(terms)))(*terms)[0]
-
-
-def every_member(value, n_member):
-    value = value[None]
-    bit = 1
-    while bit < n_member:
-        value = jnp.concatenate([value, swap(value, "member", n_member, bit)])
-        bit *= 2
-    return value
+def pair_kernel(own_ref, home_ref, received_ref, far_ref, near_ref, middle_ref, kept_ref):
+    rows = home_ref.shape[1]
+    for k, out in ((3, far_ref), (1, near_ref), (2, middle_ref), (0, kept_ref)):
+        total = home_ref[k] + received_ref[k * rows : (k + 1) * rows].astype(F32)
+        out[0:rows] = total.astype(out.dtype)
+    last = home_ref.shape[0] * rows
+    if far_ref.shape[0] > rows:
+        far_ref[rows : rows + FACTOR_ROWS] = own_ref[last:]
+        far_ref[rows + FACTOR_ROWS :] = received_ref[last:]
+
+
+def pair_sums(own, home, received):
+    chips, rows, channels = home.shape
+    shape = (rows, channels)
+    extra = 2 * (own.shape[0] - chips * rows)
+    return call(
+        pair_kernel,
+        [((rows + extra, channels), BF16), (shape, BF16), (shape, F32), (shape, F32)], [],
+        "pair", vmem(3),
+    )(own, home, received)
+
+
+def merge_kernel(middle_ref, sent_ref, received_ref, out_ref):
+    rows = middle_ref.shape[0]
+    known = sent_ref.shape[0] - rows
+    out_ref[0:rows] = (middle_ref[...] + received_ref[0:rows].astype(F32)).astype(BF16)
+    if known:
+        out_ref[rows : rows + known] = sent_ref[rows:]
+        out_ref[rows + known :] = received_ref[rows:]
+
+
+def merge(middle, sent, received):
+    rows, channels = middle.shape
+    shape = (2 * sent.shape[0] - rows, channels)
+    return call(merge_kernel, [(shape, BF16)], [], "merge", vmem(3))(middle, sent, received)[0]
+
+
+def update_kernel(own_ref, rate_ref, *refs):
+    rows = rate_ref.shape[0]
+    total = refs[0][...]
+    for ref in refs[1:-1]:
+        total = total + ref[0:rows].astype(F32)
+    refs[-1][...] = own_ref[0].astype(F32) - rate_ref[...].astype(F32) * total
+
+
+def update(own, rate, *terms):
+    shape = rate.shape
+    return call(
+        update_kernel, [(shape, F32)], [], "update", vmem(2 + len(terms)),
+    )(own, rate, *terms)[0]
 
 
 def common_term(every, me, own_rows):
-    mean = jnp.concatenate([every[:, 0]] * 3, axis=1)
+    every = every.astype(F32)
+    mean = every[:, 0] + every[:, 1] + every[:, 2]
+    sums = every[:, 3] + every[:, 4] + every[:, 5]
+    mean = jnp.concatenate([mean] * 3, axis=1)
     mean = lax.dynamic_slice_in_dim(mean, me * own_rows, own_rows, 1)
     return lax.dot_general(
-        mean, every[:, 1], (((0,), (0,)), ((), ())), precision=lax.Precision.HIGHEST
+        mean, sums, (((0,), (0,)), ((), ())), precision=lax.Precision.HIGHEST
     )
 
 
@@ -526,14 +632,19 @@
     same_group = jnp.asarray((blocks[:, None] == blocks[None, :]), BF16)
 
     bias_row = time_bias(timestep[0], identity[0], subject_table, time_proj)
-    act_one, turned_one = call(
-        functools.partial(enter_kernel, points),
-        [((padded, channels), BF16), ((channels, rows), BF16)],
-        [], "enter", vmem(2),
-    )(clip, same_group)
-    weight_one, weight_two, own_one, own_two, rates = weights_and_rates(
-        n_group, n_member, conv1_weight, conv2_weight, rate1, rate2, place, (act_one, bias_row)
-    )
+
+    def enter(clip):
+        return call(
+            functools.partial(enter_kernel, points),
+            [((padded, channels), BF16), ((channels, rows), BF16), (same_group.shape, BF16)],
+            [pltpu.VMEM((rows, channels), BF16), pltpu.SemaphoreType.DMA((2,))],
+            "enter", hbm(2),
+        )(clip, same_group)
+
+    weight_one, weight_two, own_one, rates, acts, bias_row = weights_and_rates(
+        n_group, n_member, conv1_weight, conv2_weight, rate1, rate2, place, clip, enter, bias_row
+    )
+    act_one, turned_one, same_group = acts
 
     def weight_specs(weight):
         return vmem(1) if len(weight) == 1 else smem(1) + vmem(2)
@@ -544,6 +655,10 @@
         [pltpu.VMEM((3 * channels, channels), BF16)],
         "conv", vmem(2) + weight_specs(weight_one),
     )(act_one, bias_row, *weight_one)
+    weight_two = weight_two(hidden)
+    own_two = weight_two[1]
+    if len(weight_two) == 2:
+        weight_two = weight_two[:1]
     normal, inverse, act_two, turned_two = call(
         functools.partial(norm_kernel, points),
         [
@@ -557,9 +672,10 @@
     error, full_two = call(
         functools.partial(second_kernel, points, scale),
         [((padded, channels), BF16), ((3 * channels, channels), BF16)],
-        [], "conv_error", vmem(3) + weight_specs(weight_two),
+        [pltpu.VMEM((rows, channels), BF16)] * 2 + [pltpu.SemaphoreType.DMA((2,))],
+        "conv_error", vmem(1) + hbm(2) + weight_specs(weight_two),
     )(act_two, clip, target, *weight_two)
-    away_two, home_two, factors = gradient(
+    away_two, home_two, *factors = gradient(
         turned_two, error, me, n_member, points, scale, True
     )
     received_two = swap(away_two, "member", n_member, 1)
@@ -567,36 +683,49 @@
         functools.partial(back_kernel, points, scale),
         [((rows, channels), F32)], [], "back", vmem(2),
     )(order_after(error, away_two), full_two)
+    staged = n_member == 8 and not factors
     received_two, grad_act = lax.optimization_barrier((received_two, grad_act))
-    away_two, kept_two = add_received(home_two, received_two)
-    received_two = swap(away_two, "member", n_member, 2)
-    rate_one, rate_two = rates(away_two)
-    every = every_member(factors, n_member)
+    if staged:
+        far_two, near_two, middle_two, kept_two = pair_sums(away_two, home_two, received_two)
+        from_two = swap(far_two, "member", n_member, 2)
+        grad_act = order_after(grad_act, far_two)
     (grad_hidden,) = call(
         functools.partial(norm_back_kernel, points),
         [((padded, channels), BF16)],
         [pltpu.VMEM((rows, channels), F32)],
         "norm_back", vmem(4),
-    )(order_after(grad_act, away_two), normal, inverse, same_group)
-    second = 1
-    if kept_two.shape[0] > 1:
-        second = 2
-        away_two, kept_two = add_received(kept_two, received_two)
-        received_two = None
-    away_two, grad_hidden, every, rate_one, rate_two = lax.optimization_barrier(
-        (away_two, grad_hidden, every, rate_one, rate_two)
-    )
+    )(grad_act, normal, inverse, same_group)
     away_one, home_one = gradient(
         turned_one, grad_hidden, me, n_member, points, scale, False
     )
-    received_one = swap(away_one, "member", n_member, 1)
-    common = common_term(every, me, own_rows)
-    terms_two = halve_to_owner(away_two, kept_two, received_two, n_member, second)
-    adapted_two = update(own_two, rate_two, *terms_two, common)
-    away_one, kept_one = add_received(*order_after((home_one, received_one), terms_two[1]))
-    adapted_one = update(
-        own_one, rate_one, *halve_to_owner(away_one, kept_one, None, n_member)
-    )
+    if staged:
+        away_one, from_two = order_after((away_one, from_two), ())
+        received_one = swap(away_one, "member", n_member, 1)
+        merged_two = merge(middle_two, far_two, from_two)
+        across_two = swap(merged_two, "member", n_member, 4)
+        beside_two = swap(order_after(near_two, from_two), "member", n_member, 2)
+        far_one, near_one, middle_one, kept_one = pair_sums(away_one, home_one, received_one)
+        from_one = swap(far_one, "member", n_member, 2)
+        rate_one, rate_two = rates(far_one)
+        middle_one = order_after(middle_one, (rate_one, rate_two))
+        merged_one = merge(middle_one, far_one, from_one)
+        terms_one = [
+            kept_one,
+            swap(merged_one, "member", n_member, 4),
+            swap(order_after(near_one, from_one), "member", n_member, 2),
+        ]
+        across_two, beside_two = order_after((across_two, beside_two), merged_one)
+        terms_two = [kept_two, across_two, beside_two]
+        every = jnp.concatenate([merged_two[own_rows:], across_two[own_rows:]])
+        every = every.reshape(n_member, FACTOR_ROWS, channels)
+    else:
+        received_one = swap(away_one, "member", n_member, 1)
+        rate_one, rate_two = rates(away_one)
+        every = lax.all_gather(factors[0], "member")
+        terms_two = halve_to_owner(*add_received(home_two, received_two), None, n_member)
+        terms_one = halve_to_owner(*add_received(home_one, received_one), None, n_member)
+    adapted_two = update(own_two, rate_two, *terms_two, common_term(every, me, own_rows))
+    adapted_one = update(own_one, rate_one, *terms_one)
     return (adapted_one[None], adapted_two[None])
 
 

time: 160 us -> 131 us (0.82)
  waiting for transfers between devices: 74.7 us -> 39.8 us
  local copies, waits for them, and re-layouts: 5.96 us -> 12 us
  Pallas kernels: 36.4 us -> 39.4 us
  starting transfers between devices: 34 us -> 31.1 us
    ppermute x29 -> x27, waiting for transfers between devices: 74.7 us -> 39.8 us  [swap(): return lax.ppermute(value, axis, [(i, i ^ offset) for i in range(size)])]
    unnamed x47 -> x59, local copies, waits for them, and re-layouts: 2.95 us -> 10.2 us
    pallas_call x12, Pallas kernels: 17.7 us -> 20.8 us  [the longest x2 8.32 us: gradient(): call(functools.partial(grad_kernel, points, scale, block, centred), [((ch...]
    ppermute x29 -> x27, starting transfers between devices: 34 us -> 31.1 us  [swap(): return lax.ppermute(value, axis, [(i, i ^ offset) for i in range(size)])]
    squeeze x2 -> x0, local copies, waits for them, and re-layouts: 1.99 us -> none  [weights_and_rates(): return (halves_one, halves_two, halves_one[1][0], halves_two[1][0], rates)]
  transfers between devices with their start and end apart: 29 -> 27, of which waited for: 12 -> 12; matrix products, arithmetic and copies ran while one was open for 6% -> 6% of each run, Pallas kernels for 12% -> 18%
where the time goes in v4:
time: 131 us; the launch traced here: 130 us
  waiting for transfers between devices  39.8 us (30%)
  Pallas kernels  39.4 us (30%)
  starting transfers between devices  31.1 us (24%)
  local copies, waits for them, and re-layouts  12 us (9%)
  other arithmetic  3.3 us (3%)
  between operations  2.38 us (2%)
  matrix products  2.3 us (2%)
    ppermute x27, waiting for transfers between devices, swap(): return lax.ppermute(value, axis, [(i, i ^ offset) for i in range(size)])  39.8 us
    ppermute x27, starting transfers between devices, swap(): return lax.ppermute(value, axis, [(i, i ^ offset) for i in range(size)])  31.1 us
    unnamed x59, local copies, waits for them, and re-layouts  10.2 us
    pallas_call x2, Pallas kernels, gradient(): call(functools.partial(grad_kernel, points, scale, block, centred), [((ch...  8.32 us
    pallas_call x1, Pallas kernels, shards(): call(functools.partial(second_kernel, points, scale), [((padded, channels...  4.4 us
    pallas_call x1, Pallas kernels, shards(): call(functools.partial(first_kernel, points, scale), [((rows, channels),...  3.94 us
    pallas_call x1, Pallas kernels, shards(): call(functools.partial(back_kernel, points, scale), [((rows, channels), F...  3.44 us
    pallas_call x2, Pallas kernels, update(): call(update_kernel, [(shape, F32)], [], 'update', vmem(2 + len(terms)))  3.15 us
  transfers between devices with their start and end apart: 27, of which 12 were waited for; matrix products, arithmetic and copies ran while one was open for 6% of the time, Pallas kernels for 18%

profile of v4, /device:TPU:0, one launch (start us, length us, event | category | flops | bytes accessed | tf_op | source)
XLA Modules:
  0.0 130.4 jit_solution(2663611349896375842)
XLA Ops:
  4.4 1.7 %pack.1 = (bf16[416,128]{1,0:T(8,128)(2,1)S(1)}, bf16[192,128]{1,0:T(8,128)(2,1)S(1)}, bf16[2,304,128]{2,1,0:T(8,128)(2,1)}) custom-call(bf16[160,240]{1,0:T(8,128)(2,1)S(1)} %bitcast.48, bf16[160,240]{1,0:T(8,128)(2,1)S(1)} %bitcast.49, bf16[160,240]{1,0:T(8,128)(2,1)S(1)} %bitcast.50, bf16[160,240]{1,0:T(8,128)(2,1)S(1)} %bitcast.51), custom_call_target="tpu_custom_call" | custom-call | bytes 1024 | tf_op jit(solution)/shard_map/pack/pallas_call | solution.py:461
  6.2 3.1 %collective-permute-start = (bf16[416,128]{1,0:T(8,128)(2,1)S(1)}, bf16[416,128]{1,0:T(8,128)(2,1)S(1)}, u32[]{:S(2)}, u32[]{:S(2)}) collective-permute-start(bf16[416,128]{1,0:T(8,128)(2,1)S(1)} %get-tuple-element.68.refs_0_), channel_id=1, source_target_pairs={{0,2},{1,3},{2,0},{3,1},{4,6},{5,7},{6,4},{7,5},{8,10},{9,11},{10,... | collective-permute-start | bytes 319496 | tf_op jit(solution)/shard_map/ppermute | solution.py:337
  9.3 2.6 %collective-permute-start.1 = (bf16[416,128]{1,0:T(8,128)(2,1)S(1)}, bf16[416,128]{1,0:T(8,128)(2,1)S(1)}, u32[]{:S(2)}, u32[]{:S(2)}) collective-permute-start(bf16[416,128]{1,0:T(8,128)(2,1)S(1)} %get-tuple-element.68.refs_0_), channel_id=1, source_target_pairs={{0,4},{1,5},{2,6},{3,7},{4,0},{5,1},{6,2},{7,3},{8,12},{9,13},{10,... | collective-permute-start | bytes 319496 | tf_op jit(solution)/shard_map/ppermute | solution.py:337
  11.9 1.7 %collective-permute-start.3 = (bf16[192,128]{1,0:T(8,128)(2,1)S(1)}, bf16[192,128]{1,0:T(8,128)(2,1)S(1)}, u32[]{:S(2)}, u32[]{:S(2)}) collective-permute-start(bf16[192,128]{1,0:T(8,128)(2,1)S(1)} %get-tuple-element.61), channel_id=1, source_target_pairs={{0,8},{8,0},{16,24},{24,16},{1,9},{9,1},{17,25},{25,17},{2,10},{10... | collective-permute-start | bytes 147464 | tf_op jit(solution)/shard_map/ppermute | solution.py:337
  16.5 1.6 %collective-permute-start.4 = (bf16[2,192,128]{2,1,0:T(8,128)(2,1)S(1)}, bf16[2,192,128]{2,1,0:T(8,128)(2,1)S(1)}, u32[]{:S(2)}, u32[]{:S(2)}) collective-permute-start(bf16[2,192,128]{2,1,0:T(8,128)(2,1)S(1)} %pad_maximum_fusion.6), channel_id=1, source_target_pairs={{0,16},{8,24},{16,0},{24,8},{1,17},{9,25},{17,1},{25,9},{2,18},{10... | collective-permute-start | bytes 294920 | tf_op jit(solution)/shard_map/ppermute | solution.py:337
  18.1 2.7 %enter.1 = (bf16[1024,640]{1,0:T(8,128)(2,1)S(1)}, bf16[640,896]{1,0:T(8,128)(2,1)S(1)}, bf16[640,640]{1,0:T(8,128)(2,1)S(1)}) custom-call(bf16[896,640]{1,0:T(8,128)(2,1)S(1)} %bitcast.39, bf16[640,640]{1,0:T(8,128)(2,1)S(1)} %copy-done.12), custom_call_target="tpu_custom_call" | custom-call | bytes 1024 | tf_op jit(solution)/shard_map/enter/pallas_call | solution.py:637
  25.7 1.8 %collective-permute-start.5 = (bf16[4,192,128]{2,1,0:T(8,128)(2,1)S(1)}, bf16[4,192,128]{2,1,0:T(8,128)(2,1)}, u32[]{:S(2)}, u32[]{:S(2)}) collective-permute-start(bf16[4,192,128]{2,1,0:T(8,128)(2,1)S(1)} %pad_maximum_fusion.4), channel_id=1, source_target_pairs={{0,4},{1,5},{2,6},{3,7},{4,0},{5,1},{6,2},{7,3},{8,12},{9,13},{10,... | collective-permute-start | bytes 589832 | tf_op jit(solution)/shard_map/ppermute | solution.py:337
  27.4 1.8 %collective-permute-done.8.refs_4_ = bf16[2,304,128]{2,1,0:T(8,128)(2,1)S(1)} collective-permute-done((bf16[2,304,128]{2,1,0:T(8,128)(2,1)S(1)}, bf16[2,304,128]{2,1,0:T(8,128)(2,1)S(1)}, u32[]{:S(2)}, u32[]{:S(2)}) %collective-permute-start.8) | collective-permute-done | bytes 155680 | tf_op jit(solution)/shard_map/ppermute | solution.py:337
  31.2 2.3 %collective-permute-start.7 = (bf16[2,2,304,128]{3,2,1,0:T(8,128)(2,1)}, bf16[2,2,304,128]{3,2,1,0:T(8,128)(2,1)S(1)}, u32[]{:S(2)}, u32[]{:S(2)}) collective-permute-start(bf16[2,2,304,128]{3,2,1,0:T(8,128)(2,1)} %pad_maximum_fusion.2), channel_id=1, source_target_pairs={{0,16},{8,24},{16,0},{24,8},{1,17},{9,25},{17,1},{25,9},{2,18},{10... | collective-permute-start | bytes 933896 | tf_op jit(solution)/shard_map/ppermute | solution.py:337
  33.6 1.5 %collective-permute-done.5 = bf16[4,192,128]{2,1,0:T(8,128)(2,1)} collective-permute-done((bf16[4,192,128]{2,1,0:T(8,128)(2,1)S(1)}, bf16[4,192,128]{2,1,0:T(8,128)(2,1)}, u32[]{:S(2)}, u32[]{:S(2)}) %collective-permute-start.5) | collective-permute-done | bytes 196640 | tf_op jit(solution)/shard_map/ppermute | solution.py:337
  37.1 1.4 %collective-permute-done.7.refs_2_ = bf16[2,2,304,128]{3,2,1,0:T(8,128)(2,1)S(1)} collective-permute-done((bf16[2,2,304,128]{3,2,1,0:T(8,128)(2,1)}, bf16[2,2,304,128]{3,2,1,0:T(8,128)(2,1)S(1)}, u32[]{:S(2)}, u32[]{:S(2)}) %collective-permute-start.7) | collective-permute-done | bytes 311328 | tf_op jit(solution)/shard_map/ppermute | solution.py:337
  44.0 2.0 %collective-permute-start.12 = (bf16[4,112,128]{2,1,0:T(8,128)(2,1)S(1)}, bf16[4,112,128]{2,1,0:T(8,128)(2,1)S(1)}, u32[]{:S(2)}, u32[]{:S(2)}) collective-permute-start(bf16[4,112,128]{2,1,0:T(8,128)(2,1)S(1)} %copy-done.22), channel_id=1, source_target_pairs={{0,16},{8,24},{16,0},{24,8},{1,17},{9,25},{17,1},{25,9},{2,18},{10... | collective-permute-start | bytes 344072 | tf_op jit(solution)/shard_map/ppermute | solution.py:337
  46.6 3.9 %conv.1.hidden_ref = f32[896,640]{1,0:T(8,128)S(1)} custom-call(bf16[1024,640]{1,0:T(8,128)(2,1)S(1)} %copy-done.8, f32[1,640]{1,0:T(1,128)S(1)} %fusion.14.bias_ref, s32[2]{0:T(128)S(1)} %pad_add_fusion.place_ref.refs_0_, bf16[4,240,640]{2,1,0:T(8,128)(2,1)S(1)} %unpack.2.refs_1_.own_ref, bf16[4,240,640]{2,1,0:T(8,128)(2,1)S(1)} %collective-permute-done.10.refs_2_), custom_call_target="tpu_custom_call" | custom-call | bytes 1024 | tf_op jit(solution)/shard_map/conv/pallas_call | solution.py:652
  50.6 3.6 %collective-permute-done.14.refs_5_ = bf16[2,4,192,128]{3,2,1,0:T(8,128)(2,1)S(1)} collective-permute-done((bf16[2,4,192,128]{3,2,1,0:T(8,128)(2,1)S(1)}, bf16[2,4,192,128]{3,2,1,0:T(8,128)(2,1)S(1)}, u32[]{:S(2)}, u32[]{:S(2)}) %collective-permute-start.14) | collective-permute-done | bytes 393248 | tf_op jit(solution)/shard_map/ppermute | solution.py:337
  54.2 1.5 %unpack.3.refs_1_.own_ref = bf16[4,240,640]{2,1,0:T(8,128)(2,1)S(1)} custom-call(s32[2]{0:T(128)S(1)} %pad_add_fusion.place_ref.refs_0_, bf16[4,112,128]{2,1,0:T(8,128)(2,1)S(1)} %copy-done.22, bf16[4,112,128]{2,1,0:T(8,128)(2,1)S(1)} %collective-permute-done.11.refs_1_, bf16[4,112,128]{2,1,0:T(8,128)(2,1)S(1)} %collective-permute-done.12.refs_2_, ...), custom_call_target="tpu_custom_call" | custom-call | bytes 1024 | tf_op jit(solution)/shard_map/unpack/pallas_call | solution.py:477
  55.8 2.2 %norm.1 = (f32[896,640]{1,0:T(8,128)S(1)}, f32[1,640]{1,0:T(1,128)S(1)}, bf16[1024,640]{1,0:T(8,128)(2,1)S(1)}, bf16[640,896]{1,0:T(8,128)(2,1)S(1)}) custom-call(f32[896,640]{1,0:T(8,128)S(1)} %conv.1.hidden_ref, bf16[640,640]{1,0:T(8,128)(2,1)S(1)} %copy-done.6), custom_call_target="tpu_custom_call" | custom-call | bytes 1024 | tf_op jit(solution)/shard_map/norm/pallas_call | solution.py:662
  58.7 4.4 %conv_error.1 = (bf16[1024,640]{1,0:T(8,128)(2,1)S(1)}, bf16[1920,640]{1,0:T(8,128)(2,1)S(1)}) custom-call(bf16[1024,640]{1,0:T(8,128)(2,1)S(1)} %get-tuple-element.87.in_ref, bf16[896,640]{1,0:T(8,128)(2,1)S(1)} %bitcast.40, bf16[896,640]{1,0:T(8,128)(2,1)S(1)} %bitcast.41, s32[2]{0:T(128)S(1)} %pad_add_fusion.place_ref.refs_0_, ...), custom_call_target="tpu_custom_call" | custom-call | bytes 1024 | tf_op jit(solution)/shard_map/conv_error/pallas_call | solution.py:672
  63.1 4.6 %gradient.2 = (bf16[976,640]{1,0:T(8,128)(2,1)S(1)}, f32[4,240,640]{2,1,0:T(8,128)S(1)}) custom-call(s32[1]{0:T(128)} %bitcast.1.me_ref, bf16[640,896]{1,0:T(8,128)(2,1)S(1)} %get-tuple-element.86.turned_ref, bf16[1024,640]{1,0:T(8,128)(2,1)S(1)} %get-tuple-element.90.cotangent_ref.error_ref), custom_call_target="tpu_custom_call" | custom-call | bytes 1024 | tf_op jit(solution)/shard_map/gradient/pallas_call | solution.py:318
  67.8 3.4 %back.1.act_grad_ref = f32[896,640]{1,0:T(8,128)S(1)} custom-call(bf16[1024,640]{1,0:T(8,128)(2,1)S(1)} %get-tuple-element.90.cotangent_ref.error_ref, bf16[1920,640]{1,0:T(8,128)(2,1)S(1)} %get-tuple-element.91.weight_ref), custom_call_target="tpu_custom_call" | custom-call | bytes 1024 | tf_op jit(solution)/shard_map/back/pallas_call | solution.py:682
  72.6 1.9 %norm_back.1.cotangent_ref = bf16[1024,640]{1,0:T(8,128)(2,1)S(1)} custom-call(f32[896,640]{1,0:T(8,128)S(1)} %back.1.act_grad_ref, f32[896,640]{1,0:T(8,128)S(1)} %get-tuple-element.97.normal_ref, f32[1,640]{1,0:T(1,128)S(1)} %get-tuple-element.98.inverse_ref, bf16[640,640]{1,0:T(8,128)(2,1)S(1)} %copy-done.6), custom_call_target="tpu_custom_call" | custom-call | bytes 1024 | tf_op jit(solution)/shard_map/norm_back/pallas_call | solution.py:692
  74.6 3.8 %gradient.3 = (bf16[960,640]{1,0:T(8,128)(2,1)S(1)}, f32[4,240,640]{2,1,0:T(8,128)S(1)}) custom-call(s32[1]{0:T(128)} %bitcast.1.me_ref, bf16[640,896]{1,0:T(8,128)(2,1)S(1)} %copy-done.10, bf16[1024,640]{1,0:T(8,128)(2,1)S(1)} %norm_back.1.cotangent_ref), custom_call_target="tpu_custom_call" | custom-call | bytes 1024 | tf_op jit(solution)/shard_map/gradient/pallas_call | solution.py:318
  78.4 4.2 %collective-permute-done.17.received_ref = bf16[272,640]{1,0:T(8,128)(2,1)S(1)} collective-permute-done((bf16[272,640]{1,0:T(8,128)(2,1)S(1)}, bf16[272,640]{1,0:T(8,128)(2,1)S(1)}, u32[]{:S(2)}, u32[]{:S(2)}) %collective-permute-start.17) | collective-permute-done | bytes 348192 | tf_op jit(solution)/shard_map/ppermute | solution.py:337
  82.6 2.9 %collective-permute-done.18.received_ref = bf16[960,640]{1,0:T(8,128)(2,1)S(1)} collective-permute-done((bf16[960,640]{1,0:T(8,128)(2,1)S(1)}, bf16[960,640]{1,0:T(8,128)(2,1)S(1)}, u32[]{:S(2)}, u32[]{:S(2)}) %collective-permute-start.18) | collective-permute-done | bytes 1228832 | tf_op jit(solution)/shard_map/ppermute | solution.py:337
  88.6 2.5 %collective-permute-start.25 = (bf16[304,640]{1,0:T(8,128)(2,1)}, bf16[304,640]{1,0:T(8,128)(2,1)}, u32[]{:S(2)}, u32[]{:S(2)}) collective-permute-start(bf16[304,640]{1,0:T(8,128)(2,1)} %merge.3), channel_id=1, source_target_pairs={{0,4},{1,5},{2,6},{3,7},{4,0},{5,1},{6,2},{7,3},{8,12},{9,13},{10,... | collective-permute-start | bytes 1167368 | tf_op jit(solution)/shard_map/ppermute | solution.py:337
  91.1 1.7 %collective-permute-start.22 = (bf16[240,640]{1,0:T(8,128)(2,1)}, bf16[240,640]{1,0:T(8,128)(2,1)}, u32[]{:S(2)}, u32[]{:S(2)}) collective-permute-start(bf16[240,640]{1,0:T(8,128)(2,1)} %get-tuple-element.102.sent_ref), channel_id=1, source_target_pairs={{0,2},{1,3},{2,0},{3,1},{4,6},{5,7},{6,4},{7,5},{8,10},{9,11},{10,... | collective-permute-start | bytes 921608 | tf_op jit(solution)/shard_map/ppermute | solution.py:337
  93.1 1.9 %collective-permute-start.20 = (bf16[2,304,128]{2,1,0:T(8,128)(2,1)}, bf16[2,304,128]{2,1,0:T(8,128)(2,1)}, u32[]{:S(2)}, u32[]{:S(2)}) collective-permute-start(bf16[2,304,128]{2,1,0:T(8,128)(2,1)} %get-tuple-element.103), channel_id=1, source_target_pairs={{0,16},{8,24},{16,0},{24,8},{1,17},{9,25},{17,1},{25,9},{2,18},{10... | collective-permute-start | bytes 466952 | tf_op jit(solution)/shard_map/ppermute | solution.py:337
  96.5 5.5 %collective-permute-done.20 = bf16[2,304,128]{2,1,0:T(8,128)(2,1)} collective-permute-done((bf16[2,304,128]{2,1,0:T(8,128)(2,1)}, bf16[2,304,128]{2,1,0:T(8,128)(2,1)}, u32[]{:S(2)}, u32[]{:S(2)}) %collective-permute-start.20) | collective-permute-done | bytes 155680 | tf_op jit(solution)/shard_map/ppermute | solution.py:337
  104.1 3.3 %collective-permute-done.22.received_ref = bf16[240,640]{1,0:T(8,128)(2,1)} collective-permute-done((bf16[240,640]{1,0:T(8,128)(2,1)}, bf16[240,640]{1,0:T(8,128)(2,1)}, u32[]{:S(2)}, u32[]{:S(2)}) %collective-permute-start.22) | collective-permute-done | bytes 307232 | tf_op jit(solution)/shard_map/ppermute | solution.py:337
  108.6 2.2 %collective-permute-start.23 = (bf16[240,640]{1,0:T(8,128)(2,1)S(1)}, bf16[240,640]{1,0:T(8,128)(2,1)S(1)}, u32[]{:S(2)}, u32[]{:S(2)}) collective-permute-start(bf16[240,640]{1,0:T(8,128)(2,1)S(1)} %merge.2), channel_id=1, source_target_pairs={{0,4},{1,5},{2,6},{3,7},{4,0},{5,1},{6,2},{7,3},{8,12},{9,13},{10,... | collective-permute-start | bytes 921608 | tf_op jit(solution)/shard_map/ppermute | solution.py:337
  110.8 7.7 %collective-permute-done.26.refs_2_ = bf16[240,640]{1,0:T(8,128)(2,1)} collective-permute-done((bf16[240,640]{1,0:T(8,128)(2,1)}, bf16[240,640]{1,0:T(8,128)(2,1)}, u32[]{:S(2)}, u32[]{:S(2)}) %collective-permute-start.26) | collective-permute-done | bytes 307232 | tf_op jit(solution)/shard_map/ppermute | solution.py:337
  120.4 2.1 %update.3 = f32[240,640]{1,0:T(8,128)} custom-call(bf16[4,240,640]{2,1,0:T(8,128)(2,1)S(1)} %copy-done.2, bf16[240,640]{1,0:T(8,128)(2,1)S(1)} %get-tuple-element.107.rate_ref, f32[240,640]{1,0:T(8,128)S(1)} %copy-done.14, bf16[304,640]{1,0:T(8,128)(2,1)} %collective-permute-done.25.refs_1_, bf16[240,640]{1,0:T(8,128)(2,1)} %collective-permute-done.26.refs_2_, ...), custom_call_target="tpu_custom_call" | custom-call | bytes 1024 | tf_op jit(solution)/shard_map/update/pallas_call | solution.py:594
  122.6 6.8 %collective-permute-done.24.refs_2_ = bf16[240,640]{1,0:T(8,128)(2,1)S(1)} collective-permute-done((bf16[240,640]{1,0:T(8,128)(2,1)S(1)}, bf16[240,640]{1,0:T(8,128)(2,1)S(1)}, u32[]{:S(2)}, u32[]{:S(2)}) %collective-permute-start.24) | collective-permute-done | bytes 307232 | tf_op jit(solution)/shard_map/ppermute | solution.py:337
  (118 shorter events, 33.4 us)
Async XLA Ops:
  0.6 15.6 %copy-start = (bf16[1280,640]{1,0:T(8,128)(2,1)S(1)}, bf16[1280,640]{1,0:T(8,128)(2,1)}, u32[]{:S(2)}) copy-start(bf16[1280,640]{1,0:T(8,128)(2,1)} %param.19) | copy-start | bytes 4915204
  0.6 17.5 %copy-start.12 = (bf16[640,640]{1,0:T(8,128)(2,1)S(1)}, bf16[640,640]{1,0:T(8,128)(2,1)}, u32[]{:S(2)}) copy-start(bf16[640,640]{1,0:T(8,128)(2,1)} %constant.24.clone.same_hbm) | copy-start | bytes 2457604
  0.7 17.5 %copy-start.3 = (bf16[1,14,64,640]{3,2,1,0:T(8,128)(2,1)S(1)}, bf16[1,14,64,640]{3,2,1,0:T(8,128)(2,1)}, u32[]{:S(2)}) copy-start(bf16[1,14,64,640]{3,2,1,0:T(8,128)(2,1)} %param.11) | copy-start | bytes 3440644
  6.2 17.7 %collective-permute-start = (bf16[416,128]{1,0:T(8,128)(2,1)S(1)}, bf16[416,128]{1,0:T(8,128)(2,1)S(1)}, u32[]{:S(2)}, u32[]{:S(2)}) collective-permute-start(bf16[416,128]{1,0:T(8,128)(2,1)S(1)} %get-tuple-element.68.refs_0_), channel_id=1, source_target_pairs={{0,2},{1,3},{2,0},{3,1},{4,6},{5,7},{6,4},{7,5},{8,10},{9,11},{10,... | collective-permute-start | bytes 319496 | tf_op jit(solution)/shard_map/ppermute | solution.py:337
  9.3 14.6 %collective-permute-start.1 = (bf16[416,128]{1,0:T(8,128)(2,1)S(1)}, bf16[416,128]{1,0:T(8,128)(2,1)S(1)}, u32[]{:S(2)}, u32[]{:S(2)}) collective-permute-start(bf16[416,128]{1,0:T(8,128)(2,1)S(1)} %get-tuple-element.68.refs_0_), channel_id=1, source_target_pairs={{0,4},{1,5},{2,6},{3,7},{4,0},{5,1},{6,2},{7,3},{8,12},{9,13},{10,... | collective-permute-start | bytes 319496 | tf_op jit(solution)/shard_map/ppermute | solution.py:337
  11.9 12.0 %collective-permute-start.2 = (bf16[416,128]{1,0:T(8,128)(2,1)S(1)}, bf16[416,128]{1,0:T(8,128)(2,1)S(1)}, u32[]{:S(2)}, u32[]{:S(2)}) collective-permute-start(bf16[416,128]{1,0:T(8,128)(2,1)S(1)} %get-tuple-element.68.refs_0_), channel_id=1, source_target_pairs={{0,6},{1,7},{2,4},{3,5},{4,2},{5,3},{6,0},{7,1},{8,14},{9,15},{10,... | collective-permute-start | bytes 319496 | tf_op jit(solution)/shard_map/ppermute | solution.py:337
  11.9 4.7 %collective-permute-start.3 = (bf16[192,128]{1,0:T(8,128)(2,1)S(1)}, bf16[192,128]{1,0:T(8,128)(2,1)S(1)}, u32[]{:S(2)}, u32[]{:S(2)}) collective-permute-start(bf16[192,128]{1,0:T(8,128)(2,1)S(1)} %get-tuple-element.61), channel_id=1, source_target_pairs={{0,8},{8,0},{16,24},{24,16},{1,9},{9,1},{17,25},{25,17},{2,10},{10... | collective-permute-start | bytes 147464 | tf_op jit(solution)/shard_map/ppermute | solution.py:337
  16.5 7.3 %collective-permute-start.4 = (bf16[2,192,128]{2,1,0:T(8,128)(2,1)S(1)}, bf16[2,192,128]{2,1,0:T(8,128)(2,1)S(1)}, u32[]{:S(2)}, u32[]{:S(2)}) collective-permute-start(bf16[2,192,128]{2,1,0:T(8,128)(2,1)S(1)} %pad_maximum_fusion.6), channel_id=1, source_target_pairs={{0,16},{8,24},{16,0},{24,8},{1,17},{9,25},{17,1},{25,9},{2,18},{10... | collective-permute-start | bytes 294920 | tf_op jit(solution)/shard_map/ppermute | solution.py:337
  23.9 5.3 %collective-permute-start.8 = (bf16[2,304,128]{2,1,0:T(8,128)(2,1)S(1)}, bf16[2,304,128]{2,1,0:T(8,128)(2,1)S(1)}, u32[]{:S(2)}, u32[]{:S(2)}) collective-permute-start(bf16[2,304,128]{2,1,0:T(8,128)(2,1)S(1)} %get-tuple-element.76.refs_3_), channel_id=1, source_target_pairs={{0,16},{8,24},{16,0},{24,8},{1,17},{9,25},{17,1},{25,9},{2,18},{10... | collective-permute-start | bytes 466952 | tf_op jit(solution)/shard_map/ppermute | solution.py:337
  24.5 5.9 %collective-permute-start.6 = (bf16[2,304,128]{2,1,0:T(8,128)(2,1)S(1)}, bf16[2,304,128]{2,1,0:T(8,128)(2,1)S(1)}, u32[]{:S(2)}, u32[]{:S(2)}) collective-permute-start(bf16[2,304,128]{2,1,0:T(8,128)(2,1)S(1)} %get-tuple-element.75.refs_0_), channel_id=1, source_target_pairs={{0,8},{8,0},{16,24},{24,16},{1,9},{9,1},{17,25},{25,17},{2,10},{10... | collective-permute-start | bytes 466952 | tf_op jit(solution)/shard_map/ppermute | solution.py:337
  25.7 9.5 %collective-permute-start.5 = (bf16[4,192,128]{2,1,0:T(8,128)(2,1)S(1)}, bf16[4,192,128]{2,1,0:T(8,128)(2,1)}, u32[]{:S(2)}, u32[]{:S(2)}) collective-permute-start(bf16[4,192,128]{2,1,0:T(8,128)(2,1)S(1)} %pad_maximum_fusion.4), channel_id=1, source_target_pairs={{0,4},{1,5},{2,6},{3,7},{4,0},{5,1},{6,2},{7,3},{8,12},{9,13},{10,... | collective-permute-start | bytes 589832 | tf_op jit(solution)/shard_map/ppermute | solution.py:337
  29.3 7.1 %collective-permute-start.9 = (bf16[2,2,304,128]{3,2,1,0:T(8,128)(2,1)S(1)}, bf16[2,2,304,128]{3,2,1,0:T(8,128)(2,1)S(1)}, u32[]{:S(2)}, u32[]{:S(2)}) collective-permute-start(bf16[2,2,304,128]{3,2,1,0:T(8,128)(2,1)S(1)} %pad_maximum_fusion.3), channel_id=1, source_target_pairs={{0,8},{8,0},{16,24},{24,16},{1,9},{9,1},{17,25},{25,17},{2,10},{10... | collective-permute-start | bytes 933896 | tf_op jit(solution)/shard_map/ppermute | solution.py:337
  31.2 7.4 %collective-permute-start.7 = (bf16[2,2,304,128]{3,2,1,0:T(8,128)(2,1)}, bf16[2,2,304,128]{3,2,1,0:T(8,128)(2,1)S(1)}, u32[]{:S(2)}, u32[]{:S(2)}) collective-permute-start(bf16[2,2,304,128]{3,2,1,0:T(8,128)(2,1)} %pad_maximum_fusion.2), channel_id=1, source_target_pairs={{0,16},{8,24},{16,0},{24,8},{1,17},{9,25},{17,1},{25,9},{2,18},{10... | collective-permute-start | bytes 933896 | tf_op jit(solution)/shard_map/ppermute | solution.py:337
  42.5 4.1 %collective-permute-start.10 = (bf16[4,240,640]{2,1,0:T(8,128)(2,1)S(1)}, bf16[4,240,640]{2,1,0:T(8,128)(2,1)S(1)}, u32[]{:S(2)}, u32[]{:S(2)}) collective-permute-start(bf16[4,240,640]{2,1,0:T(8,128)(2,1)S(1)} %unpack.2.refs_1_.own_ref), channel_id=1, source_target_pairs={{0,1},{1,0},{2,3},{3,2},{4,5},{5,4},{6,7},{7,6},{8,9},{9,8},{10,11... | collective-permute-start | bytes 3686408 | tf_op jit(solution)/shard_map/ppermute | solution.py:337
  42.6 11.5 %collective-permute-start.14 = (bf16[2,4,192,128]{3,2,1,0:T(8,128)(2,1)S(1)}, bf16[2,4,192,128]{3,2,1,0:T(8,128)(2,1)S(1)}, u32[]{:S(2)}, u32[]{:S(2)}) collective-permute-start(bf16[2,4,192,128]{3,2,1,0:T(8,128)(2,1)S(1)} %pad_maximum_fusion.1.refs_4_), channel_id=1, source_target_pairs={{0,2},{1,3},{2,0},{3,1},{4,6},{5,7},{6,4},{7,5},{8,10},{9,11},{10,... | collective-permute-start | bytes 1179656 | tf_op jit(solution)/shard_map/ppermute | solution.py:337
  43.1 11.0 %collective-permute-start.11 = (bf16[4,112,128]{2,1,0:T(8,128)(2,1)S(1)}, bf16[4,112,128]{2,1,0:T(8,128)(2,1)S(1)}, u32[]{:S(2)}, u32[]{:S(2)}) collective-permute-start(bf16[4,112,128]{2,1,0:T(8,128)(2,1)S(1)} %copy-done.22), channel_id=1, source_target_pairs={{0,8},{8,0},{16,24},{24,16},{1,9},{9,1},{17,25},{25,17},{2,10},{10... | collective-permute-start | bytes 344072 | tf_op jit(solution)/shard_map/ppermute | solution.py:337
  44.0 10.1 %collective-permute-start.12 = (bf16[4,112,128]{2,1,0:T(8,128)(2,1)S(1)}, bf16[4,112,128]{2,1,0:T(8,128)(2,1)S(1)}, u32[]{:S(2)}, u32[]{:S(2)}) collective-permute-start(bf16[4,112,128]{2,1,0:T(8,128)(2,1)S(1)} %copy-done.22), channel_id=1, source_target_pairs={{0,16},{8,24},{16,0},{24,8},{1,17},{9,25},{17,1},{25,9},{2,18},{10... | collective-permute-start | bytes 344072 | tf_op jit(solution)/shard_map/ppermute | solution.py:337
  46.0 8.2 %collective-permute-start.13 = (bf16[4,112,128]{2,1,0:T(8,128)(2,1)S(1)}, bf16[4,112,128]{2,1,0:T(8,128)(2,1)S(1)}, u32[]{:S(2)}, u32[]{:S(2)}) collective-permute-start(bf16[4,112,128]{2,1,0:T(8,128)(2,1)S(1)} %copy-done.22), channel_id=1, source_target_pairs={{0,24},{8,16},{16,8},{24,0},{1,25},{9,17},{17,9},{25,1},{2,26},{10... | collective-permute-start | bytes 344072 | tf_op jit(solution)/shard_map/ppermute | solution.py:337
  55.7 3.0 %collective-permute-start.15 = (bf16[4,240,640]{2,1,0:T(8,128)(2,1)S(1)}, bf16[4,240,640]{2,1,0:T(8,128)(2,1)S(1)}, u32[]{:S(2)}, u32[]{:S(2)}) collective-permute-start(bf16[4,240,640]{2,1,0:T(8,128)(2,1)S(1)} %unpack.3.refs_1_.own_ref), channel_id=1, source_target_pairs={{0,1},{1,0},{2,3},{3,2},{4,5},{5,4},{6,7},{7,6},{8,9},{9,8},{10,11... | collective-permute-start | bytes 3686408 | tf_op jit(solution)/shard_map/ppermute | solution.py:337
  67.6 3.6 %collective-permute-start.16 = (bf16[976,640]{1,0:T(8,128)(2,1)S(1)}, bf16[976,640]{1,0:T(8,128)(2,1)S(1)}, u32[]{:S(2)}, u32[]{:S(2)}) collective-permute-start(bf16[976,640]{1,0:T(8,128)(2,1)S(1)} %get-tuple-element.89.own_ref), channel_id=1, source_target_pairs={{0,1},{1,0},{2,3},{3,2},{4,5},{5,4},{6,7},{7,6},{8,9},{9,8},{10,11... | collective-permute-start | bytes 3747848 | tf_op jit(solution)/shard_map/ppermute | solution.py:337
  72.2 10.4 %collective-permute-start.17 = (bf16[272,640]{1,0:T(8,128)(2,1)S(1)}, bf16[272,640]{1,0:T(8,128)(2,1)S(1)}, u32[]{:S(2)}, u32[]{:S(2)}) collective-permute-start(bf16[272,640]{1,0:T(8,128)(2,1)S(1)} %get-tuple-element.95.sent_ref), channel_id=1, source_target_pairs={{0,2},{1,3},{2,0},{3,1},{4,6},{5,7},{6,4},{7,5},{8,10},{9,11},{10,... | collective-permute-start | bytes 1044488 | tf_op jit(solution)/shard_map/ppermute | solution.py:337
  82.6 2.9 %collective-permute-start.18 = (bf16[960,640]{1,0:T(8,128)(2,1)S(1)}, bf16[960,640]{1,0:T(8,128)(2,1)S(1)}, u32[]{:S(2)}, u32[]{:S(2)}) collective-permute-start(bf16[960,640]{1,0:T(8,128)(2,1)S(1)} %get-tuple-element.100.own_ref), channel_id=1, source_target_pairs={{0,1},{1,0},{2,3},{3,2},{4,5},{5,4},{6,7},{7,6},{8,9},{9,8},{10,11... | collective-permute-start | bytes 3686408 | tf_op jit(solution)/shard_map/ppermute | solution.py:337
  86.5 8.6 %collective-permute-start.19 = (bf16[2,304,128]{2,1,0:T(8,128)(2,1)}, bf16[2,304,128]{2,1,0:T(8,128)(2,1)}, u32[]{:S(2)}, u32[]{:S(2)}) collective-permute-start(bf16[2,304,128]{2,1,0:T(8,128)(2,1)} %get-tuple-element.103), channel_id=1, source_target_pairs={{0,8},{8,0},{16,24},{24,16},{1,9},{9,1},{17,25},{25,17},{2,10},{10... | collective-permute-start | bytes 466952 | tf_op jit(solution)/shard_map/ppermute | solution.py:337
  88.6 29.9 %collective-permute-start.25 = (bf16[304,640]{1,0:T(8,128)(2,1)}, bf16[304,640]{1,0:T(8,128)(2,1)}, u32[]{:S(2)}, u32[]{:S(2)}) collective-permute-start(bf16[304,640]{1,0:T(8,128)(2,1)} %merge.3), channel_id=1, source_target_pairs={{0,4},{1,5},{2,6},{3,7},{4,0},{5,1},{6,2},{7,3},{8,12},{9,13},{10,... | collective-permute-start | bytes 1167368 | tf_op jit(solution)/shard_map/ppermute | solution.py:337
  91.1 16.4 %collective-permute-start.22 = (bf16[240,640]{1,0:T(8,128)(2,1)}, bf16[240,640]{1,0:T(8,128)(2,1)}, u32[]{:S(2)}, u32[]{:S(2)}) collective-permute-start(bf16[240,640]{1,0:T(8,128)(2,1)} %get-tuple-element.102.sent_ref), channel_id=1, source_target_pairs={{0,2},{1,3},{2,0},{3,1},{4,6},{5,7},{6,4},{7,5},{8,10},{9,11},{10,... | collective-permute-start | bytes 921608 | tf_op jit(solution)/shard_map/ppermute | solution.py:337
  92.8 25.7 %collective-permute-start.26 = (bf16[240,640]{1,0:T(8,128)(2,1)}, bf16[240,640]{1,0:T(8,128)(2,1)}, u32[]{:S(2)}, u32[]{:S(2)}) collective-permute-start(bf16[240,640]{1,0:T(8,128)(2,1)} %get-tuple-element.115), channel_id=1, source_target_pairs={{0,2},{1,3},{2,0},{3,1},{4,6},{5,7},{6,4},{7,5},{8,10},{9,11},{10,... | collective-permute-start | bytes 921608 | tf_op jit(solution)/shard_map/ppermute | solution.py:337
  93.1 8.9 %collective-permute-start.20 = (bf16[2,304,128]{2,1,0:T(8,128)(2,1)}, bf16[2,304,128]{2,1,0:T(8,128)(2,1)}, u32[]{:S(2)}, u32[]{:S(2)}) collective-permute-start(bf16[2,304,128]{2,1,0:T(8,128)(2,1)} %get-tuple-element.103), channel_id=1, source_target_pairs={{0,16},{8,24},{16,0},{24,8},{1,17},{9,25},{17,1},{25,9},{2,18},{10... | collective-permute-start | bytes 466952 | tf_op jit(solution)/shard_map/ppermute | solution.py:337
  95.0 6.9 %collective-permute-start.21 = (bf16[2,304,128]{2,1,0:T(8,128)(2,1)}, bf16[2,304,128]{2,1,0:T(8,128)(2,1)}, u32[]{:S(2)}, u32[]{:S(2)}) collective-permute-start(bf16[2,304,128]{2,1,0:T(8,128)(2,1)} %get-tuple-element.103), channel_id=1, source_target_pairs={{0,24},{8,16},{16,8},{24,0},{1,25},{9,17},{17,9},{25,1},{2,26},{10... | collective-permute-start | bytes 466952 | tf_op jit(solution)/shard_map/ppermute | solution.py:337
  95.5 11.9 %copy-start.16 = (f32[240,640]{1,0:T(8,128)S(1)}, f32[240,640]{1,0:T(8,128)}, u32[]{:S(2)}) copy-start(f32[240,640]{1,0:T(8,128)} %copy-done.15) | copy-start | bytes 1843204
  104.1 15.3 %copy-start.28 = (bf16[240,640]{1,0:T(8,128)(2,1)S(1)}, bf16[240,640]{1,0:T(8,128)(2,1)}, u32[]{:S(2)}) copy-start(bf16[240,640]{1,0:T(8,128)(2,1)} %copy-done.27) | copy-start | bytes 921604
  108.6 20.8 %collective-permute-start.23 = (bf16[240,640]{1,0:T(8,128)(2,1)S(1)}, bf16[240,640]{1,0:T(8,128)(2,1)S(1)}, u32[]{:S(2)}, u32[]{:S(2)}) collective-permute-start(bf16[240,640]{1,0:T(8,128)(2,1)S(1)} %merge.2), channel_id=1, source_target_pairs={{0,4},{1,5},{2,6},{3,7},{4,0},{5,1},{6,2},{7,3},{8,12},{9,13},{10,... | collective-permute-start | bytes 921608 | tf_op jit(solution)/shard_map/ppermute | solution.py:337
  119.5 9.9 %collective-permute-start.24 = (bf16[240,640]{1,0:T(8,128)(2,1)S(1)}, bf16[240,640]{1,0:T(8,128)(2,1)S(1)}, u32[]{:S(2)}, u32[]{:S(2)}) collective-permute-start(bf16[240,640]{1,0:T(8,128)(2,1)S(1)} %copy-done.28), channel_id=1, source_target_pairs={{0,2},{1,3},{2,0},{3,1},{4,6},{5,7},{6,4},{7,5},{8,10},{9,11},{10,... | collective-permute-start | bytes 921608 | tf_op jit(solution)/shard_map/ppermute | solution.py:337
  (24 other events, 82.8 us)

commit v5 on v4

--- a/solution.py
+++ b/solution.py
@@ -39,7 +39,7 @@
     return [pl.BlockSpec(memory_space=pltpu.SMEM)] * count
 
 
-def call(body, out_shape, scratch, name, in_specs):
+def call(body, out_shape, scratch, name, in_specs, limit=8):
     outs = len(out_shape)
     return pl.pallas_call(
         body,
@@ -47,7 +47,7 @@
         in_specs=in_specs,
         out_specs=tuple(vmem(outs)),
         scratch_shapes=scratch,
-        compiler_params=pltpu.CompilerParams(vmem_limit_bytes=24 * MEGA),
+        compiler_params=pltpu.CompilerParams(vmem_limit_bytes=limit * MEGA),
         cost_estimate=pl.CostEstimate(flops=0, bytes_accessed=1024, transcendentals=0),
         name=name,
     )
@@ -65,7 +65,7 @@
     return sums[0:1] + sums[16:17] + sums[32:33]
 
 
-def norm_stats(read, rows, channels, same_group):
+def norm_stats(read, rows, channels, same_ref, copy=None):
     counted = rows * (channels // GN_GROUPS)
     steps = rows // CHUNK
     total = lax.fori_loop(
@@ -74,6 +74,9 @@
         lambda i, acc: acc + read(i).reshape(CHUNK // 8, 8, channels).sum(axis=0),
         jnp.zeros((8, channels), F32),
     ).sum(axis=0, keepdims=True)
+    if copy is not None:
+        copy.wait()
+    same_group = same_ref[...]
     centre = spread(total, same_group) * (1.0 / counted)
 
     def squares(i, acc):
@@ -107,21 +110,19 @@
     return copies
 
 
-def enter_kernel(points, clip_hbm, same_hbm, padded_ref, turned_ref, same_ref, clip_ref, sems):
+def enter_kernel(points, clip_hbm, same_hbm, padded_ref, clip_ref, same_ref, sems):
     rows, channels = clip_ref.shape
     for copy in fetch((clip_hbm, same_hbm), (clip_ref, same_ref), sems):
         copy.wait()
     centre, inverse = norm_stats(
-        lambda i: clip_ref[at(i)].astype(F32), rows, channels, same_ref[...]
+        lambda i: clip_ref[at(i)].astype(F32), rows, channels, same_ref
     )
     clear_edges(padded_ref, points)
 
     @pl.loop(0, rows // CHUNK)
     def _(i):
         normal = (clip_ref[at(i)].astype(F32) - centre) * inverse
-        act = (normal / (1.0 + jnp.exp(-normal))).astype(BF16)
-        padded_ref[at(i, points)] = act
-        turned_ref[:, at(i)] = act.T
+        padded_ref[at(i, points)] = (normal / (1.0 + jnp.exp(-normal))).astype(BF16)
 
 
 def taps_of(padded_ref, start, size, points):
@@ -133,8 +134,8 @@
 def full_weight(weight_refs, full_ref):
     if len(weight_refs) == 1:
         return weight_refs[0]
-    place_ref, mine_ref, other_ref = weight_refs
-    member, rows = place_ref[1], mine_ref.shape[1]
+    member_ref, mine_ref, other_ref = weight_refs
+    member, rows = member_ref[0], mine_ref.shape[1]
 
     @pl.loop(0, mine_ref.shape[0])
     def _(k):
@@ -162,10 +163,11 @@
 
 
 def norm_kernel(
-    points, hidden_ref, same_ref, normal_ref, inverse_ref, padded_ref, turned_ref
+    points, hidden_ref, same_hbm, normal_ref, inverse_ref, padded_ref, turned_ref, same_ref, sems
 ):
     rows, channels = normal_ref.shape
-    centre, inverse = norm_stats(lambda i: hidden_ref[at(i)], rows, channels, same_ref[...])
+    (copy,) = fetch((same_hbm,), (same_ref,), sems)
+    centre, inverse = norm_stats(lambda i: hidden_ref[at(i)], rows, channels, same_ref, copy)
     inverse_ref[...] = inverse
     clear_edges(padded_ref, points)
 
@@ -225,8 +227,9 @@
 
 
 def norm_back_kernel(
-    points, act_grad_ref, normal_ref, inverse_ref, same_ref, out_ref, grad_ref
+    points, act_grad_ref, normal_ref, inverse_ref, same_hbm, out_ref, grad_ref, same_ref, sems
 ):
+    (copy,) = fetch((same_hbm,), (same_ref,), sems)
     rows, channels = normal_ref.shape
     counted = rows * (channels // GN_GROUPS)
 
@@ -243,6 +246,7 @@
 
     zero = jnp.zeros((8, channels), F32)
     plain, crossed = lax.fori_loop(0, rows // CHUNK, through, (zero, zero))
+    copy.wait()
     same_group = same_ref[...]
     mean = spread(plain.sum(axis=0, keepdims=True), same_group) * (1.0 / counted)
     slope = spread(crossed.sum(axis=0, keepdims=True), same_group) * (1.0 / counted)
@@ -264,10 +268,19 @@
     return [high, middle, row - high - middle]
 
 
-def grad_kernel(points, scale, block, centred, me_ref, turned_ref, cotangent_ref, *refs):
+def grad_kernel(points, scale, block, centred, me_ref, act_ref, cotangent_ref, *refs):
+    refs = list(refs)
+    turned_ref = refs.pop()
+    total_ref = refs.pop()
+    if act_ref.shape == turned_ref.shape:
+        turned_ref = act_ref
     channels, rows = turned_ref.shape
-    refs = list(refs)
-    total_ref = refs.pop()
+    if turned_ref is not act_ref:
+
+        @pl.loop(0, rows // CHUNK)
+        def _(i):
+            turned_ref[:, at(i)] = act_ref[at(i, points)].T
+
     if centred:
         ones = jnp.ones((rows, 128), BF16)
         mean = jnp.dot(turned_ref[...], ones, preferred_element_type=F32) * (1.0 / rows)
@@ -308,8 +321,9 @@
         refs[0][...] = factors
 
 
-def gradient(turned, cotangent, me, n_member, points, scale, centred):
-    channels, rows = turned.shape
+def gradient(act, cotangent, me, n_member, points, scale, centred):
+    channels, rows = cotangent.shape[1], cotangent.shape[0] - 2 * points
+    turned = pltpu.VMEM((channels, rows), BF16)
     block = 3 * channels // n_member
     specs = smem(1) + vmem(2)
     if block % 16 == 0:
@@ -318,17 +332,17 @@
         return call(
             functools.partial(grad_kernel, points, scale, block, centred),
             [((chips * block + extra, channels), BF16), ((chips, block, channels), F32)],
-            [pltpu.VMEM((3 * channels, channels), F32)],
-            "gradient", specs,
-        )(me[None], turned, cotangent)
+            [pltpu.VMEM((3 * channels, channels), F32), turned],
+            "gradient", specs, 24,
+        )(me, act, cotangent)
     factors = [((FACTOR_ROWS, channels), F32)] if centred else []
     found = call(
         functools.partial(grad_kernel, points, scale, None, centred),
         factors + [((3 * channels, channels), F32)],
-        [], "gradient", specs,
-    )(me[None], turned, cotangent)
+        [turned], "gradient", specs, 24,
+    )(me, act, cotangent)
     total = found[-1].reshape(n_member, block, channels)
-    order = [lax.dynamic_index_in_dim(total, me ^ j, 0, keepdims=False) for j in range(n_member)]
+    order = [lax.dynamic_index_in_dim(total, me[0] ^ j, 0, keepdims=False) for j in range(n_member)]
     away, home = jnp.stack(order[1::2]).astype(BF16), jnp.stack(order[0::2])
     return (away, home) + tuple(found[:-1])
 
@@ -341,11 +355,21 @@
     return lax.optimization_barrier((value, others))[0]
 
 
+def stack_kernel(*refs):
+    for k, source in enumerate(refs[:-1]):
+        refs[-1][k] = source[...]
+
+
+def stacked(*arrays):
+    shape = (len(arrays),) + arrays[0].shape
+    return call(stack_kernel, [(shape, BF16)], [], "stack", vmem(len(arrays)))(*arrays)[0]
+
+
 TAIL = 64
 
 
 def cut_of(rows):
-    return (rows + TAIL) * 3 // 128 * 16
+    return (rows + TAIL) // 32 * 16
 
 
 def pack_kernel(*refs):
@@ -390,10 +414,10 @@
         two_ref[k] = source[size:]
 
 
-def for_group(place_ref, n_group, half_ref, rows, block_of):
+def for_group(group_ref, n_group, half_ref, rows, block_of):
     for group in range(n_group):
 
-        @pl.when(place_ref[0] == group)
+        @pl.when(group_ref[0] == group)
         def _():
             block_of(
                 lambda k, pick: half_ref.__setitem__(
@@ -402,7 +426,7 @@
             )
 
 
-def two_step_kernel(rows, place_ref, *refs):
+def two_step_kernel(rows, group_ref, *refs):
     first, first_x, first_y, second, second_y, second_x, half_ref = refs
     half = half_ref.shape[0] // 2
 
@@ -414,10 +438,10 @@
             late = (second, second_x.at[0], second_y, second_x.at[1])
             store(half + k, lambda d: late[d][k])
 
-    for_group(place_ref, 4, half_ref, rows, fill)
-
-
-def direct_kernel(rows, n_group, place_ref, *refs):
+    for_group(group_ref, 4, half_ref, rows, fill)
+
+
+def direct_kernel(rows, n_group, group_ref, *refs):
     early_refs, late_refs, half_ref = refs[:n_group], refs[n_group:-1], refs[-1]
 
     def fill(store):
@@ -427,13 +451,17 @@
                 k = 2 * i + odd
                 store(k, lambda d: jnp.concatenate([early_refs[d][k], late_ref[i, d]], axis=0))
 
-    for_group(place_ref, n_group, half_ref, rows, fill)
-
-
-def rate_kernel(rows, n_group, place_ref, packed_ref, one_ref, two_ref):
-    group = place_ref[0]
-    for which, out in enumerate((one_ref, two_ref)):
-        out[...] = unpacked(lambda g: packed_ref[g ^ group, which], rows, n_group)
+    for_group(group_ref, n_group, half_ref, rows, fill)
+
+
+def rate_kernel(rows, n_group, group_ref, *refs):
+    packed_refs, outs = refs[:n_group], refs[n_group:]
+    for group in range(n_group):
+
+        @pl.when(group_ref[0] == group)
+        def _():
+            for which, out in enumerate(outs):
+                out[...] = unpacked(lambda g: packed_refs[g ^ group][which], rows, n_group)
 
 
 def along_z(value, n_member):
@@ -445,7 +473,7 @@
     return [value] + [swap(value, "group", n_group, k) for k in range(1, n_group)]
 
 
-def weights_and_rates(n_group, n_member, conv1, conv2, rate1, rate2, place, clip, enter, bias_row):
+def weights_and_rates(n_group, n_member, conv1, conv2, rate1, rate2, group, me, clip, enter, bias_row):
     rows, cols = conv1.shape
     width = n_group * cols
     if (cols, n_group, n_member, rows % 16) != (160, 4, 8, 0) or rows > 4 * TAIL:
@@ -468,7 +496,6 @@
         in_specs=hbm(4),
         out_specs=tuple(vmem(3)),
         scratch_shapes=[pltpu.VMEM((cols, rows), BF16)] * 4 + [pltpu.SemaphoreType.DMA((4,))],
-        compiler_params=pltpu.CompilerParams(vmem_limit_bytes=40 * MEGA),
         cost_estimate=pl.CostEstimate(flops=0, bytes_accessed=1024, transcendentals=0),
         name="pack",
     )(conv1.T, conv2.T, rate1.T, rate2.T)
@@ -476,13 +503,13 @@
     def unpack(kernel, *packed):
         (mine,) = call(
             kernel, [((chips, rows, width), BF16)], [], "unpack", smem(1) + vmem(len(packed))
-        )(place, *packed)
-        return place, mine, swap(mine, "member", n_member, 1)
+        )(group, *packed)
+        return me, mine, swap(mine, "member", n_member, 1)
 
     along = along_z(early_rows, n_member)
     late_x = swap(late, "group", n_group, 1)
     late_x, bias_row = order_after((late_x, bias_row), ())
-    late = jnp.stack([late, late_x])
+    late = stacked(late, late_x)
     late_y = swap(late, "group", n_group, 2)
     act = enter(order_after(clip, (late, bias_row)))
     along, late_y, act = order_after((along, late_y, act), ())
@@ -493,12 +520,13 @@
     )(*along)
     first_x = swap(first, "group", n_group, 1)
     second_y = swap(second, "group", n_group, 2)
-    late = order_after(jnp.concatenate([late, late_y]), first)
-    late = [late]
-    late_z = swap(late[0], "member", n_member, 2 * (chips // 2))
-    first_y = swap(jnp.stack([first, first_x]), "group", n_group, 2)
-    second_x = swap(jnp.stack([second, second_y]), "group", n_group, 1)
-    late = jnp.stack(late + [late_z])
+    late, late_y = order_after((late, late_y), first)
+    late = stacked(late, late_y).reshape(n_group, size - cut, 128)
+    late_z = swap(late, "member", n_member, 4)
+    first_x, second_y = order_after((first_x, second_y), late)
+    first_y = swap(stacked(first, first_x), "group", n_group, 2)
+    second_x = swap(stacked(second, second_y), "group", n_group, 1)
+    late = stacked(late, late_z)
     late_z = swap(late, "member", n_member, 2)
     halves_one = unpack(
         functools.partial(two_step_kernel, rows),
@@ -511,11 +539,11 @@
         return unpack(kernel, *along_two, *order_after((late, late_z), after))
 
     def rates(after):
-        blocks = jnp.stack(across_groups(order_after(both_rates, after), n_group))
+        blocks = across_groups(order_after(both_rates, after), n_group)
         return call(
             functools.partial(rate_kernel, rows, n_group),
-            [((rows, width), BF16)] * 2, [], "rates", smem(1) + vmem(1),
-        )(place, blocks)
+            [((rows, width), BF16)] * 2, [], "rates", smem(1) + vmem(n_group),
+        )(group, *blocks)
 
     return halves_one, halves_two, halves_one[1], rates, act, bias_row
 
@@ -544,15 +572,20 @@
         bit *= 2
 
 
-def pair_kernel(own_ref, home_ref, received_ref, far_ref, near_ref, middle_ref, kept_ref):
+def pair_kernel(own_ref, home_ref, received_ref, away_ref, middle_ref, kept_ref):
     rows = home_ref.shape[1]
-    for k, out in ((3, far_ref), (1, near_ref), (2, middle_ref), (0, kept_ref)):
-        total = home_ref[k] + received_ref[k * rows : (k + 1) * rows].astype(F32)
-        out[0:rows] = total.astype(out.dtype)
+
+    def total(k):
+        return home_ref[k] + received_ref[k * rows : (k + 1) * rows].astype(F32)
+
+    away_ref[0:rows] = total(3).astype(BF16)
+    away_ref[rows : 2 * rows] = total(1).astype(BF16)
+    middle_ref[...] = total(2)
+    kept_ref[...] = total(0)
     last = home_ref.shape[0] * rows
-    if far_ref.shape[0] > rows:
-        far_ref[rows : rows + FACTOR_ROWS] = own_ref[last:]
-        far_ref[rows + FACTOR_ROWS :] = received_ref[last:]
+    if away_ref.shape[0] > 2 * rows:
+        away_ref[2 * rows : 2 * rows + FACTOR_ROWS] = own_ref[last:]
+        away_ref[2 * rows + FACTOR_ROWS :] = received_ref[last:]
 
 
 def pair_sums(own, home, received):
@@ -561,23 +594,23 @@
     extra = 2 * (own.shape[0] - chips * rows)
     return call(
         pair_kernel,
-        [((rows + extra, channels), BF16), (shape, BF16), (shape, F32), (shape, F32)], [],
-        "pair", vmem(3),
+        [((2 * rows + extra, channels), BF16), (shape, F32), (shape, F32)], [],
+        "pair", vmem(3), 12,
     )(own, home, received)
 
 
 def merge_kernel(middle_ref, sent_ref, received_ref, out_ref):
     rows = middle_ref.shape[0]
-    known = sent_ref.shape[0] - rows
+    known = sent_ref.shape[0] - 2 * rows
     out_ref[0:rows] = (middle_ref[...] + received_ref[0:rows].astype(F32)).astype(BF16)
     if known:
-        out_ref[rows : rows + known] = sent_ref[rows:]
-        out_ref[rows + known :] = received_ref[rows:]
+        out_ref[rows : rows + known] = sent_ref[2 * rows :]
+        out_ref[rows + known :] = received_ref[2 * rows :]
 
 
 def merge(middle, sent, received):
     rows, channels = middle.shape
-    shape = (2 * sent.shape[0] - rows, channels)
+    shape = (rows + 2 * (sent.shape[0] - 2 * rows), channels)
     return call(merge_kernel, [(shape, BF16)], [], "merge", vmem(3))(middle, sent, received)[0]
 
 
@@ -585,8 +618,43 @@
     rows = rate_ref.shape[0]
     total = refs[0][...]
     for ref in refs[1:-1]:
-        total = total + ref[0:rows].astype(F32)
+        start = rows if ref.shape[0] == 2 * rows else 0
+        total = total + ref[start : start + rows].astype(F32)
     refs[-1][...] = own_ref[0].astype(F32) - rate_ref[...].astype(F32) * total
+
+
+def common_update_kernel(
+    me_ref, own_ref, rate_ref, kept_ref, half_ref, sent_ref, received_ref, out_ref
+):
+    rows, channels = rate_ref.shape
+    total = kept_ref[...] + half_ref[rows : 2 * rows].astype(F32)
+    total = total + received_ref[0:rows].astype(F32)
+    means, sums = [], []
+    for ref in (sent_ref, received_ref):
+        for start in range(rows, ref.shape[0], FACTOR_ROWS):
+            parts = ref[start : start + FACTOR_ROWS].astype(F32)
+            means.append(parts[0:1] + parts[1:2] + parts[2:3])
+            sums.append(parts[3:4] + parts[4:5] + parts[5:6])
+    means, sums = jnp.concatenate(means, axis=0), jnp.concatenate(sums, axis=0)
+    means = jnp.concatenate([means] * 3, axis=1)
+    for member in range(len(range(0, 3 * channels, rows))):
+
+        @pl.when(me_ref[0] == member)
+        def _():
+            common = lax.dot_general(
+                means[:, member * rows : (member + 1) * rows],
+                sums,
+                (((0,), (0,)), ((), ())),
+                precision=lax.Precision.HIGHEST,
+                preferred_element_type=F32,
+            )
+            out_ref[...] = own_ref[0].astype(F32) - rate_ref[...].astype(F32) * (total + common)
+
+
+def common_update(me, own, rate, *terms):
+    return call(
+        common_update_kernel, [(rate.shape, F32)], [], "update", smem(1) + vmem(6)
+    )(me, own, rate, *terms)[0]
 
 
 def update(own, rate, *terms):
@@ -601,7 +669,7 @@
     mean = every[:, 0] + every[:, 1] + every[:, 2]
     sums = every[:, 3] + every[:, 4] + every[:, 5]
     mean = jnp.concatenate([mean] * 3, axis=1)
-    mean = lax.dynamic_slice_in_dim(mean, me * own_rows, own_rows, 1)
+    mean = lax.dynamic_slice_in_dim(mean, me[0] * own_rows, own_rows, 1)
     return lax.dot_general(
         mean, sums, (((0,), (0,)), ((), ())), precision=lax.Precision.HIGHEST
     )
@@ -624,8 +692,8 @@
     frames, points, channels = (clips.shape[1], clips.shape[2], clips.shape[3])
     rows, padded = frames * points, (frames + 2) * points
     scale = 1.0 / math.sqrt(3 * channels)
-    group, me = lax.axis_index("group"), lax.axis_index("member")
-    place = jnp.stack([group, me]).astype(jnp.int32)
+    group = lax.axis_index("group").astype(jnp.int32)[None]
+    me = lax.axis_index("member").astype(jnp.int32)[None]
     own_rows = conv1_weight.shape[0]
     clip, target = clips.reshape(rows, channels), targets.reshape(rows, channels)
     blocks = np.arange(channels) // (channels // GN_GROUPS)
@@ -636,15 +704,18 @@
     def enter(clip):
         return call(
             functools.partial(enter_kernel, points),
-            [((padded, channels), BF16), ((channels, rows), BF16), (same_group.shape, BF16)],
-            [pltpu.VMEM((rows, channels), BF16), pltpu.SemaphoreType.DMA((2,))],
-            "enter", hbm(2),
-        )(clip, same_group)
-
-    weight_one, weight_two, own_one, rates, acts, bias_row = weights_and_rates(
-        n_group, n_member, conv1_weight, conv2_weight, rate1, rate2, place, clip, enter, bias_row
-    )
-    act_one, turned_one, same_group = acts
+            [((padded, channels), BF16)],
+            [
+                pltpu.VMEM((rows, channels), BF16),
+                pltpu.VMEM(same_group.shape, BF16),
+                pltpu.SemaphoreType.DMA((2,)),
+            ],
+            "enter", hbm(2), 12,
+        )(clip, same_group)[0]
+
+    weight_one, weight_two, own_one, rates, act_one, bias_row = weights_and_rates(
+        n_group, n_member, conv1_weight, conv2_weight, rate1, rate2, group, me, clip, enter, bias_row
+    )
 
     def weight_specs(weight):
         return vmem(1) if len(weight) == 1 else smem(1) + vmem(2)
@@ -653,7 +724,7 @@
         functools.partial(first_kernel, points, scale),
         [((rows, channels), F32)],
         [pltpu.VMEM((3 * channels, channels), BF16)],
-        "conv", vmem(2) + weight_specs(weight_one),
+        "conv", vmem(2) + weight_specs(weight_one), 20,
     )(act_one, bias_row, *weight_one)
     weight_two = weight_two(hidden)
     own_two = weight_two[1]
@@ -667,13 +738,14 @@
             ((padded, channels), BF16),
             ((channels, rows), BF16),
         ],
-        [], "norm", vmem(2),
+        [pltpu.VMEM(same_group.shape, BF16), pltpu.SemaphoreType.DMA((1,))],
+        "norm", vmem(1) + hbm(1), 20,
     )(order_after(hidden, weight_two[:2]), same_group)
     error, full_two = call(
         functools.partial(second_kernel, points, scale),
         [((padded, channels), BF16), ((3 * channels, channels), BF16)],
         [pltpu.VMEM((rows, channels), BF16)] * 2 + [pltpu.SemaphoreType.DMA((2,))],
-        "conv_error", vmem(1) + hbm(2) + weight_specs(weight_two),
+        "conv_error", vmem(1) + hbm(2) + weight_specs(weight_two), 24,
     )(act_two, clip, target, *weight_two)
     away_two, home_two, *factors = gradient(
         turned_two, error, me, n_member, points, scale, True
@@ -681,50 +753,51 @@
     received_two = swap(away_two, "member", n_member, 1)
     (grad_act,) = call(
         functools.partial(back_kernel, points, scale),
-        [((rows, channels), F32)], [], "back", vmem(2),
+        [((rows, channels), F32)], [], "back", vmem(2), 20,
     )(order_after(error, away_two), full_two)
     staged = n_member == 8 and not factors
     received_two, grad_act = lax.optimization_barrier((received_two, grad_act))
     if staged:
-        far_two, near_two, middle_two, kept_two = pair_sums(away_two, home_two, received_two)
-        from_two = swap(far_two, "member", n_member, 2)
-        grad_act = order_after(grad_act, far_two)
+        half_two, middle_two, kept_two = pair_sums(away_two, home_two, received_two)
+        from_two = swap(half_two, "member", n_member, 2)
+        grad_act = order_after(grad_act, half_two)
     (grad_hidden,) = call(
         functools.partial(norm_back_kernel, points),
         [((padded, channels), BF16)],
-        [pltpu.VMEM((rows, channels), F32)],
-        "norm_back", vmem(4),
+        [
+            pltpu.VMEM((rows, channels), F32),
+            pltpu.VMEM(same_group.shape, BF16),
+            pltpu.SemaphoreType.DMA((1,)),
+        ],
+        "norm_back", vmem(3) + hbm(1), 20,
     )(grad_act, normal, inverse, same_group)
     away_one, home_one = gradient(
-        turned_one, grad_hidden, me, n_member, points, scale, False
+        act_one, grad_hidden, me, n_member, points, scale, False
     )
     if staged:
-        away_one, from_two = order_after((away_one, from_two), ())
-        received_one = swap(away_one, "member", n_member, 1)
-        merged_two = merge(middle_two, far_two, from_two)
+        merged_two = merge(middle_two, half_two, order_after(from_two, away_one))
         across_two = swap(merged_two, "member", n_member, 4)
-        beside_two = swap(order_after(near_two, from_two), "member", n_member, 2)
-        far_one, near_one, middle_one, kept_one = pair_sums(away_one, home_one, received_one)
-        from_one = swap(far_one, "member", n_member, 2)
-        rate_one, rate_two = rates(far_one)
-        middle_one = order_after(middle_one, (rate_one, rate_two))
-        merged_one = merge(middle_one, far_one, from_one)
-        terms_one = [
-            kept_one,
-            swap(merged_one, "member", n_member, 4),
-            swap(order_after(near_one, from_one), "member", n_member, 2),
-        ]
-        across_two, beside_two = order_after((across_two, beside_two), merged_one)
-        terms_two = [kept_two, across_two, beside_two]
-        every = jnp.concatenate([merged_two[own_rows:], across_two[own_rows:]])
-        every = every.reshape(n_member, FACTOR_ROWS, channels)
+        received_one = swap(order_after(away_one, merged_two), "member", n_member, 1)
+        half_one, middle_one, kept_one = pair_sums(away_one, home_one, received_one)
+        from_one = swap(half_one, "member", n_member, 2)
+        rate_one, rate_two = rates(half_one)
+        from_one, across_two, rate_one, rate_two = order_after(
+            (from_one, across_two, rate_one, rate_two), ()
+        )
+        merged_one = merge(middle_one, half_one, from_one)
+        across_one = swap(merged_one, "member", n_member, 4)
+        adapted_two = common_update(
+            me, own_two, rate_two, kept_two, from_two, merged_two,
+            order_after(across_two, merged_one),
+        )
+        terms_one = [kept_one, from_one, across_one]
     else:
         received_one = swap(away_one, "member", n_member, 1)
         rate_one, rate_two = rates(away_one)
         every = lax.all_gather(factors[0], "member")
         terms_two = halve_to_owner(*add_received(home_two, received_two), None, n_member)
         terms_one = halve_to_owner(*add_received(home_one, received_one), None, n_member)
-    adapted_two = update(own_two, rate_two, *terms_two, common_term(every, me, own_rows))
+        adapted_two = update(own_two, rate_two, *terms_two, common_term(every, me, own_rows))
     adapted_one = update(own_one, rate_one, *terms_one)
     return (adapted_one[None], adapted_two[None])
 

time: 131 us -> 136 us (1.038)
  waiting for transfers between devices: 39.8 us -> 53.9 us
  local copies, waits for them, and re-layouts: 12 us -> 3.72 us
  Pallas kernels: 39.4 us -> 43.4 us
  other arithmetic: 3.3 us -> 0.07 us
    ppermute x27 -> x25, waiting for transfers between devices: 39.8 us -> 53.9 us  [swap(): return lax.ppermute(value, axis, [(i, i ^ offset) for i in range(size)])]
    unnamed x59 -> x34, local copies, waits for them, and re-layouts: 10.2 us -> 3.71 us
    another operation x6 -> x0, other arithmetic: 3.09 us -> none  [the longest x1 1.22 us: rates(): blocks = jnp.stack(across_groups(order_after(both_rates, after), n_group))]
    pallas_call x2 -> x8, Pallas kernels: 1.84 us -> 4.75 us  [the longest x5 2.47 us: stacked(): call(stack_kernel, [(shape, BF16)], [], 'stack', vmem(len(arrays)))(*arrays)]
    pallas_call x2, Pallas kernels: 2.76 us -> 4.99 us  [unpack(): call(kernel, [((chips, rows, width), BF16)], [], 'unpack', smem(1) + vmem...]
    pallas_call x2, Pallas kernels: 1.97 us -> 0.11 us  [merge(): call(merge_kernel, [(shape, BF16)], [], 'merge', vmem(3))]
    slice x2 -> x0, local copies, waits for them, and re-layouts: 1.85 us -> none  [shards(): every = jnp.concatenate([merged_two[own_rows:], across_two[own_rows:]])]
    pallas_call x2 -> x1, Pallas kernels: 3.15 us -> 2.31 us  [update(): call(update_kernel, [(shape, F32)], [], 'update', vmem(2 + len(terms)))]
  transfers between devices with their start and end apart: 27 -> 25, of which waited for: 12 -> 15; matrix products, arithmetic and copies ran while one was open for 6% -> 1% of each run, Pallas kernels for 18% -> 17%
where the time goes in v5:
time: 136 us
  waiting for transfers between devices  53.9 us (40%)
  Pallas kernels  43.4 us (32%)
  starting transfers between devices  30.9 us (23%)
  local copies, waits for them, and re-layouts  3.72 us (3%)
  between operations  2.24 us (2%)
  matrix products  1.53 us (1%)
    ppermute x25, waiting for transfers between devices, swap(): return lax.ppermute(value, axis, [(i, i ^ offset) for i in range(size)])  53.9 us
    ppermute x25, starting transfers between devices, swap(): return lax.ppermute(value, axis, [(i, i ^ offset) for i in range(size)])  30.9 us
    pallas_call x2, Pallas kernels, gradient(): call(functools.partial(grad_kernel, points, scale, block, centred), [((ch...  9.04 us
    pallas_call x1, Pallas kernels, shards(): call(functools.partial(first_kernel, points, scale), [((rows, channels),...  4.99 us
    pallas_call x2, Pallas kernels, unpack(): call(kernel, [((chips, rows, width), BF16)], [], 'unpack', smem(1) + vmem...  4.99 us
    pallas_call x1, Pallas kernels, shards(): call(functools.partial(second_kernel, points, scale), [((padded, channels...  3.86 us
    unnamed x34, local copies, waits for them, and re-layouts  3.71 us
    pallas_call x1, Pallas kernels, shards(): call(functools.partial(back_kernel, points, scale), [((rows, channels), F...  3.44 us
  transfers between devices with their start and end apart: 25, of which 15 were waited for; matrix products, arithmetic and copies ran while one was open for 1% of the time, Pallas kernels for 17%

profile of v5, /device:TPU:0, one launch (start us, length us, event | category | flops | bytes accessed | tf_op | source)
XLA Modules:
  0.0 135.8 jit_solution(10229252426595095656)
XLA Ops:
  0.6 2.3 %pack.1 = (bf16[448,128]{1,0:T(8,128)(2,1)}, bf16[160,128]{1,0:T(8,128)(2,1)}, bf16[2,304,128]{2,1,0:T(8,128)(2,1)}) custom-call(bf16[160,240]{1,0:T(8,128)(2,1)} %bitcast.27, bf16[160,240]{1,0:T(8,128)(2,1)} %bitcast.28, bf16[160,240]{1,0:T(8,128)(2,1)} %bitcast.29, bf16[160,240]{1,0:T(8,128)(2,1)} %bitcast.30), custom_call_target="tpu_custom_call" | custom-call | bytes 1024 | tf_op jit(solution)/shard_map/pack/pallas_call | solution.py:489
  3.0 5.1 %collective-permute-start.2 = (bf16[448,128]{1,0:T(8,128)(2,1)}, bf16[448,128]{1,0:T(8,128)(2,1)S(1)}, u32[]{:S(2)}, u32[]{:S(2)}) collective-permute-start(bf16[448,128]{1,0:T(8,128)(2,1)} %get-tuple-element.61.refs_0_), channel_id=1, source_target_pairs={{0,6},{1,7},{2,4},{3,5},{4,2},{5,3},{6,0},{7,1},{8,14},{9,15},{10,... | collective-permute-start | bytes 344072 | tf_op jit(solution)/shard_map/ppermute | solution.py:351
  8.8 1.6 %collective-permute-start.3 = (bf16[160,128]{1,0:T(8,128)(2,1)}, bf16[160,128]{1,0:T(8,128)(2,1)S(1)}, u32[]{:S(2)}, u32[]{:S(2)}) collective-permute-start(bf16[160,128]{1,0:T(8,128)(2,1)} %get-tuple-element.57.refs_0_), channel_id=1, source_target_pairs={{0,8},{8,0},{16,24},{24,16},{1,9},{9,1},{17,25},{25,17},{2,10},{10... | collective-permute-start | bytes 122888 | tf_op jit(solution)/shard_map/ppermute | solution.py:351
  13.4 1.6 %collective-permute-start.4 = (bf16[2,160,128]{2,1,0:T(8,128)(2,1)S(1)}, bf16[2,160,128]{2,1,0:T(8,128)(2,1)S(1)}, u32[]{:S(2)}, u32[]{:S(2)}) collective-permute-start(bf16[2,160,128]{2,1,0:T(8,128)(2,1)S(1)} %stack.5.refs_0_), channel_id=1, source_target_pairs={{0,16},{8,24},{16,0},{24,8},{1,17},{9,25},{17,1},{25,9},{2,18},{10... | collective-permute-start | bytes 245768 | tf_op jit(solution)/shard_map/ppermute | solution.py:351
  15.0 2.2 %enter.1.in_ref.act_ref = bf16[1024,640]{1,0:T(8,128)(2,1)S(1)} custom-call(bf16[896,640]{1,0:T(8,128)(2,1)S(1)} %bitcast.20, bf16[640,640]{1,0:T(8,128)(2,1)S(1)} %copy-done.1), custom_call_target="tpu_custom_call" | custom-call | bytes 1024 | tf_op jit(solution)/shard_map/enter/pallas_call | solution.py:705
  18.7 1.5 %collective-permute-start.7 = (bf16[2,304,128]{2,1,0:T(8,128)(2,1)S(1)}, bf16[2,304,128]{2,1,0:T(8,128)(2,1)S(1)}, u32[]{:S(2)}, u32[]{:S(2)}) collective-permute-start(bf16[2,304,128]{2,1,0:T(8,128)(2,1)S(1)} %get-tuple-element.70.refs_0_.refs_3_), channel_id=1, source_target_pairs={{0,16},{8,24},{16,0},{24,8},{1,17},{9,25},{17,1},{25,9},{2,18},{10... | collective-permute-start | bytes 466952 | tf_op jit(solution)/shard_map/ppermute | solution.py:351
  21.8 2.2 %collective-permute-done.7.refs_1_.refs_4_ = bf16[2,304,128]{2,1,0:T(8,128)(2,1)S(1)} collective-permute-done((bf16[2,304,128]{2,1,0:T(8,128)(2,1)S(1)}, bf16[2,304,128]{2,1,0:T(8,128)(2,1)S(1)}, u32[]{:S(2)}, u32[]{:S(2)}) %collective-permute-start.7) | collective-permute-done | bytes 155680 | tf_op jit(solution)/shard_map/ppermute | solution.py:351
  24.0 1.5 %collective-permute-done.6.refs_1_ = bf16[2,304,128]{2,1,0:T(8,128)(2,1)S(1)} collective-permute-done((bf16[2,304,128]{2,1,0:T(8,128)(2,1)S(1)}, bf16[2,304,128]{2,1,0:T(8,128)(2,1)S(1)}, u32[]{:S(2)}, u32[]{:S(2)}) %collective-permute-start.6) | collective-permute-done | bytes 155680 | tf_op jit(solution)/shard_map/ppermute | solution.py:351
  29.0 1.8 %collective-permute-start.5 = (bf16[4,160,128]{2,1,0:T(8,128)(2,1)S(1)}, bf16[4,160,128]{2,1,0:T(8,128)(2,1)}, u32[]{:S(2)}, u32[]{:S(2)}) collective-permute-start(bf16[4,160,128]{2,1,0:T(8,128)(2,1)S(1)} %bitcast.23), channel_id=1, source_target_pairs={{0,4},{1,5},{2,6},{3,7},{4,0},{5,1},{6,2},{7,3},{8,12},{9,13},{10,... | collective-permute-start | bytes 491528 | tf_op jit(solution)/shard_map/ppermute | solution.py:351
  30.8 6.3 %collective-permute-done.5.refs_1_ = bf16[4,160,128]{2,1,0:T(8,128)(2,1)} collective-permute-done((bf16[4,160,128]{2,1,0:T(8,128)(2,1)S(1)}, bf16[4,160,128]{2,1,0:T(8,128)(2,1)}, u32[]{:S(2)}, u32[]{:S(2)}) %collective-permute-start.5) | collective-permute-done | bytes 163872 | tf_op jit(solution)/shard_map/ppermute | solution.py:351
  41.7 2.9 %unpack.2.refs_1_.own_ref = bf16[4,240,640]{2,1,0:T(8,128)(2,1)} custom-call(s32[1]{0:T(128)} %bitcast.group_ref, bf16[2,304,128]{2,1,0:T(8,128)(2,1)S(1)} %copy-done.7, bf16[2,304,128]{2,1,0:T(8,128)(2,1)S(1)} %copy-done.13, bf16[2,2,304,128]{3,2,1,0:T(8,128)(2,1)} %collective-permute-done.8.refs_2_, bf16[2,304,128]{2,1,0:T(8,128)(2,1)S(1)} %copy-done.9, ...), custom_call_target="tpu_custom_call" | custom-call | bytes 1024 | tf_op jit(solution)/shard_map/unpack/pallas_call | solution.py:504
  48.1 5.0 %conv.1.hidden_ref = f32[896,640]{1,0:T(8,128)S(1)} custom-call(bf16[1024,640]{1,0:T(8,128)(2,1)S(1)} %enter.1.in_ref.act_ref, f32[1,640]{1,0:T(1,128)S(1)} %fusion.6.bias_ref, s32[1]{0:T(128)} %bitcast.10.refs_0_.me_ref, bf16[4,240,640]{2,1,0:T(8,128)(2,1)} %unpack.2.refs_1_.own_ref, bf16[4,240,640]{2,1,0:T(8,128)(2,1)} %collective-permute-done.10.refs_2_), custom_call_target="tpu_custom_call" | custom-call | bytes 1024 | tf_op jit(solution)/shard_map/conv/pallas_call | solution.py:723
  53.1 1.7 %collective-permute-done.14.refs_5_ = bf16[2,4,160,128]{3,2,1,0:T(8,128)(2,1)} collective-permute-done((bf16[2,4,160,128]{3,2,1,0:T(8,128)(2,1)S(1)}, bf16[2,4,160,128]{3,2,1,0:T(8,128)(2,1)}, u32[]{:S(2)}, u32[]{:S(2)}) %collective-permute-start.14) | collective-permute-done | bytes 327712 | tf_op jit(solution)/shard_map/ppermute | solution.py:351
  55.3 2.1 %unpack.3.refs_1_.own_ref = bf16[4,240,640]{2,1,0:T(8,128)(2,1)S(1)} custom-call(s32[1]{0:T(128)} %bitcast.group_ref, bf16[4,144,128]{2,1,0:T(8,128)(2,1)} %get-tuple-element.75.refs_0_, bf16[4,144,128]{2,1,0:T(8,128)(2,1)} %collective-permute-done.11.refs_1_, bf16[4,144,128]{2,1,0:T(8,128)(2,1)} %collective-permute-done.12.refs_2_, ...), custom_call_target="tpu_custom_call" | custom-call | bytes 1024 | tf_op jit(solution)/shard_map/unpack/pallas_call | solution.py:504
  57.5 2.3 %norm.1 = (f32[896,640]{1,0:T(8,128)S(1)}, f32[1,640]{1,0:T(1,128)S(1)}, bf16[1024,640]{1,0:T(8,128)(2,1)S(1)}, bf16[640,896]{1,0:T(8,128)(2,1)S(1)}) custom-call(f32[896,640]{1,0:T(8,128)S(1)} %conv.1.hidden_ref, bf16[640,640]{1,0:T(8,128)(2,1)S(1)} %copy-done.2), custom_call_target="tpu_custom_call" | custom-call | bytes 1024 | tf_op jit(solution)/shard_map/norm/pallas_call | solution.py:733
  60.4 3.9 %conv_error.1 = (bf16[1024,640]{1,0:T(8,128)(2,1)S(1)}, bf16[1920,640]{1,0:T(8,128)(2,1)S(1)}) custom-call(bf16[1024,640]{1,0:T(8,128)(2,1)S(1)} %get-tuple-element.80.in_ref, bf16[896,640]{1,0:T(8,128)(2,1)S(1)} %bitcast.21, bf16[896,640]{1,0:T(8,128)(2,1)S(1)} %bitcast.22, s32[1]{0:T(128)} %bitcast.10.refs_0_.me_ref, ...), custom_call_target="tpu_custom_call" | custom-call | bytes 1024 | tf_op jit(solution)/shard_map/conv_error/pallas_call | solution.py:744
  64.3 4.6 %gradient.2 = (bf16[976,640]{1,0:T(8,128)(2,1)S(1)}, f32[4,240,640]{2,1,0:T(8,128)S(1)}) custom-call(s32[1]{0:T(128)} %bitcast.10.refs_0_.me_ref, bf16[640,896]{1,0:T(8,128)(2,1)S(1)} %get-tuple-element.79.act_ref, bf16[1024,640]{1,0:T(8,128)(2,1)S(1)} %get-tuple-element.83.cotangent_ref.error_ref), custom_call_target="tpu_custom_call" | custom-call | bytes 1024 | tf_op jit(solution)/shard_map/gradient/pallas_call | solution.py:332
  69.1 3.4 %back.1.act_grad_ref = f32[896,640]{1,0:T(8,128)S(1)} custom-call(bf16[1024,640]{1,0:T(8,128)(2,1)S(1)} %get-tuple-element.83.cotangent_ref.error_ref, bf16[1920,640]{1,0:T(8,128)(2,1)S(1)} %get-tuple-element.84.weight_ref), custom_call_target="tpu_custom_call" | custom-call | bytes 1024 | tf_op jit(solution)/shard_map/back/pallas_call | solution.py:754
  72.8 1.8 %collective-permute-start.17 = (bf16[512,640]{1,0:T(8,128)(2,1)S(1)}, bf16[512,640]{1,0:T(8,128)(2,1)S(1)}, u32[]{:S(2)}, u32[]{:S(2)}) collective-permute-start(bf16[512,640]{1,0:T(8,128)(2,1)S(1)} %get-tuple-element.88.sent_ref), channel_id=1, source_target_pairs={{0,2},{1,3},{2,0},{3,1},{4,6},{5,7},{6,4},{7,5},{8,10},{9,11},{10,... | collective-permute-start | bytes 1966088 | tf_op jit(solution)/shard_map/ppermute | solution.py:351
  74.6 2.1 %norm_back.1.cotangent_ref = bf16[1024,640]{1,0:T(8,128)(2,1)S(1)} custom-call(f32[896,640]{1,0:T(8,128)S(1)} %back.1.act_grad_ref, f32[896,640]{1,0:T(8,128)S(1)} %get-tuple-element.90.normal_ref, f32[1,640]{1,0:T(1,128)S(1)} %get-tuple-element.91.inverse_ref, bf16[640,640]{1,0:T(8,128)(2,1)S(1)} %copy-done.2), custom_call_target="tpu_custom_call" | custom-call | bytes 1024 | tf_op jit(solution)/shard_map/norm_back/pallas_call | solution.py:764
  76.7 4.5 %gradient.3 = (bf16[960,640]{1,0:T(8,128)(2,1)S(1)}, f32[4,240,640]{2,1,0:T(8,128)S(1)}) custom-call(s32[1]{0:T(128)} %bitcast.10.refs_0_.me_ref, bf16[1024,640]{1,0:T(8,128)(2,1)S(1)} %enter.1.in_ref.act_ref, bf16[1024,640]{1,0:T(8,128)(2,1)S(1)} %norm_back.1.cotangent_ref), custom_call_target="tpu_custom_call" | custom-call | bytes 1024 | tf_op jit(solution)/shard_map/gradient/pallas_call | solution.py:332
  81.2 8.7 %collective-permute-done.17.received_ref.half_ref = bf16[512,640]{1,0:T(8,128)(2,1)S(1)} collective-permute-done((bf16[512,640]{1,0:T(8,128)(2,1)S(1)}, bf16[512,640]{1,0:T(8,128)(2,1)S(1)}, u32[]{:S(2)}, u32[]{:S(2)}) %collective-permute-start.17) | collective-permute-done | bytes 655392 | tf_op jit(solution)/shard_map/ppermute | solution.py:351
  90.0 2.9 %collective-permute-done.18.received_ref = bf16[960,640]{1,0:T(8,128)(2,1)S(1)} collective-permute-done((bf16[960,640]{1,0:T(8,128)(2,1)S(1)}, bf16[960,640]{1,0:T(8,128)(2,1)S(1)}, u32[]{:S(2)}, u32[]{:S(2)}) %collective-permute-start.18) | collective-permute-done | bytes 1228832 | tf_op jit(solution)/shard_map/ppermute | solution.py:351
  93.1 1.8 %collective-permute-start.19 = (bf16[480,640]{1,0:T(8,128)(2,1)S(1)}, bf16[480,640]{1,0:T(8,128)(2,1)S(1)}, u32[]{:S(2)}, u32[]{:S(2)}) collective-permute-start(bf16[480,640]{1,0:T(8,128)(2,1)S(1)} %get-tuple-element.97.sent_ref), channel_id=1, source_target_pairs={{0,2},{1,3},{2,0},{3,1},{4,6},{5,7},{6,4},{7,5},{8,10},{9,11},{10,... | collective-permute-start | bytes 1843208 | tf_op jit(solution)/shard_map/ppermute | solution.py:351
  96.4 1.6 %collective-permute-start.23 = (bf16[2,304,128]{2,1,0:T(8,128)(2,1)S(1)}, bf16[2,304,128]{2,1,0:T(8,128)(2,1)S(1)}, u32[]{:S(2)}, u32[]{:S(2)}) collective-permute-start(bf16[2,304,128]{2,1,0:T(8,128)(2,1)S(1)} %copy-done.14), channel_id=1, source_target_pairs={{0,24},{8,16},{16,8},{24,0},{1,25},{9,17},{17,9},{25,1},{2,26},{10... | collective-permute-start | bytes 466952 | tf_op jit(solution)/shard_map/ppermute | solution.py:351
  99.9 4.4 %collective-permute-done.23.refs_3_ = bf16[2,304,128]{2,1,0:T(8,128)(2,1)S(1)} collective-permute-done((bf16[2,304,128]{2,1,0:T(8,128)(2,1)S(1)}, bf16[2,304,128]{2,1,0:T(8,128)(2,1)S(1)}, u32[]{:S(2)}, u32[]{:S(2)}) %collective-permute-start.23) | collective-permute-done | bytes 155680 | tf_op jit(solution)/shard_map/ppermute | solution.py:351
  104.3 2.0 %collective-permute-done.22.refs_2_ = bf16[2,304,128]{2,1,0:T(8,128)(2,1)S(1)} collective-permute-done((bf16[2,304,128]{2,1,0:T(8,128)(2,1)S(1)}, bf16[2,304,128]{2,1,0:T(8,128)(2,1)S(1)}, u32[]{:S(2)}, u32[]{:S(2)}) %collective-permute-start.22) | collective-permute-done | bytes 155680 | tf_op jit(solution)/shard_map/ppermute | solution.py:351
  106.6 10.0 %collective-permute-done.20.received_ref = bf16[304,640]{1,0:T(8,128)(2,1)S(1)} collective-permute-done((bf16[304,640]{1,0:T(8,128)(2,1)S(1)}, bf16[304,640]{1,0:T(8,128)(2,1)S(1)}, u32[]{:S(2)}, u32[]{:S(2)}) %collective-permute-start.20) | collective-permute-done | bytes 389152 | tf_op jit(solution)/shard_map/ppermute | solution.py:351
  117.5 2.7 %collective-permute-start.24 = (bf16[240,640]{1,0:T(8,128)(2,1)S(1)}, bf16[240,640]{1,0:T(8,128)(2,1)S(1)}, u32[]{:S(2)}, u32[]{:S(2)}) collective-permute-start(bf16[240,640]{1,0:T(8,128)(2,1)S(1)} %merge.3), channel_id=1, source_target_pairs={{0,4},{1,5},{2,6},{3,7},{4,0},{5,1},{6,2},{7,3},{8,12},{9,13},{10,... | collective-permute-start | bytes 921608 | tf_op jit(solution)/shard_map/ppermute | solution.py:351
  120.2 1.8 %update.3 = f32[240,640]{1,0:T(8,128)} custom-call(s32[1]{0:T(128)} %bitcast.10.refs_0_.me_ref, bf16[4,240,640]{2,1,0:T(8,128)(2,1)S(1)} %unpack.3.refs_1_.own_ref, bf16[240,640]{1,0:T(8,128)(2,1)S(1)} %get-tuple-element.106.rate_ref, f32[240,640]{1,0:T(8,128)S(1)} %get-tuple-element.107.kept_ref, ...), custom_call_target="tpu_custom_call" | custom-call | bytes 1024 | tf_op jit(solution)/shard_map/update/pallas_call | solution.py:655
  122.0 11.5 %collective-permute-done.24.refs_2_ = bf16[240,640]{1,0:T(8,128)(2,1)S(1)} collective-permute-done((bf16[240,640]{1,0:T(8,128)(2,1)S(1)}, bf16[240,640]{1,0:T(8,128)(2,1)S(1)}, u32[]{:S(2)}, u32[]{:S(2)}) %collective-permute-start.24) | collective-permute-done | bytes 307232 | tf_op jit(solution)/shard_map/ppermute | solution.py:351
  133.5 2.3 %update.2 = f32[240,640]{1,0:T(8,128)} custom-call(bf16[4,240,640]{2,1,0:T(8,128)(2,1)} %unpack.2.refs_1_.own_ref, bf16[240,640]{1,0:T(8,128)(2,1)S(1)} %get-tuple-element.102.rate_ref, f32[240,640]{1,0:T(8,128)S(1)} %get-tuple-element.103.refs_0_, bf16[480,640]{1,0:T(8,128)(2,1)S(1)} %collective-permute-done.19.received_ref.refs_1_, ...), custom_call_target="tpu_custom_call" | custom-call | bytes 1024 | tf_op jit(solution)/shard_map/update/pallas_call | solution.py:662
  (81 shorter events, 23.5 us)
Async XLA Ops:
  0.6 12.4 %copy-start = (bf16[1280,640]{1,0:T(8,128)(2,1)S(1)}, bf16[1280,640]{1,0:T(8,128)(2,1)}, u32[]{:S(2)}) copy-start(bf16[1280,640]{1,0:T(8,128)(2,1)} %param.19) | copy-start | bytes 4915204
  3.0 10.4 %copy-start.16 = (bf16[160,128]{1,0:T(8,128)(2,1)S(1)}, bf16[160,128]{1,0:T(8,128)(2,1)}, u32[]{:S(2)}) copy-start(bf16[160,128]{1,0:T(8,128)(2,1)} %get-tuple-element.57.refs_0_) | copy-start | bytes 122884
  3.0 12.0 %copy-start.1 = (bf16[640,640]{1,0:T(8,128)(2,1)S(1)}, bf16[640,640]{1,0:T(8,128)(2,1)}, u32[]{:S(2)}) copy-start(bf16[640,640]{1,0:T(8,128)(2,1)} %constant.18.clone.same_hbm) | copy-start | bytes 2457604
  3.0 12.0 %copy-start.3 = (bf16[1,14,64,640]{3,2,1,0:T(8,128)(2,1)S(1)}, bf16[1,14,64,640]{3,2,1,0:T(8,128)(2,1)}, u32[]{:S(2)}) copy-start(bf16[1,14,64,640]{3,2,1,0:T(8,128)(2,1)} %param.11) | copy-start | bytes 3440644
  3.0 14.2 %collective-permute-start.2 = (bf16[448,128]{1,0:T(8,128)(2,1)}, bf16[448,128]{1,0:T(8,128)(2,1)S(1)}, u32[]{:S(2)}, u32[]{:S(2)}) collective-permute-start(bf16[448,128]{1,0:T(8,128)(2,1)} %get-tuple-element.61.refs_0_), channel_id=1, source_target_pairs={{0,6},{1,7},{2,4},{3,5},{4,2},{5,3},{6,0},{7,1},{8,14},{9,15},{10,... | collective-permute-start | bytes 344072 | tf_op jit(solution)/shard_map/ppermute | solution.py:351
  8.2 9.9 %collective-permute-start.1 = (bf16[448,128]{1,0:T(8,128)(2,1)}, bf16[448,128]{1,0:T(8,128)(2,1)S(1)}, u32[]{:S(2)}, u32[]{:S(2)}) collective-permute-start(bf16[448,128]{1,0:T(8,128)(2,1)} %get-tuple-element.61.refs_0_), channel_id=1, source_target_pairs={{0,4},{1,5},{2,6},{3,7},{4,0},{5,1},{6,2},{7,3},{8,12},{9,13},{10,... | collective-permute-start | bytes 344072 | tf_op jit(solution)/shard_map/ppermute | solution.py:351
  8.2 9.9 %collective-permute-start = (bf16[448,128]{1,0:T(8,128)(2,1)}, bf16[448,128]{1,0:T(8,128)(2,1)S(1)}, u32[]{:S(2)}, u32[]{:S(2)}) collective-permute-start(bf16[448,128]{1,0:T(8,128)(2,1)} %get-tuple-element.61.refs_0_), channel_id=1, source_target_pairs={{0,2},{1,3},{2,0},{3,1},{4,6},{5,7},{6,4},{7,5},{8,10},{9,11},{10,... | collective-permute-start | bytes 344072 | tf_op jit(solution)/shard_map/ppermute | solution.py:351
  8.8 4.6 %collective-permute-start.3 = (bf16[160,128]{1,0:T(8,128)(2,1)}, bf16[160,128]{1,0:T(8,128)(2,1)S(1)}, u32[]{:S(2)}, u32[]{:S(2)}) collective-permute-start(bf16[160,128]{1,0:T(8,128)(2,1)} %get-tuple-element.57.refs_0_), channel_id=1, source_target_pairs={{0,8},{8,0},{16,24},{24,16},{1,9},{9,1},{17,25},{25,17},{2,10},{10... | collective-permute-start | bytes 122888 | tf_op jit(solution)/shard_map/ppermute | solution.py:351
  13.4 4.6 %collective-permute-start.4 = (bf16[2,160,128]{2,1,0:T(8,128)(2,1)S(1)}, bf16[2,160,128]{2,1,0:T(8,128)(2,1)S(1)}, u32[]{:S(2)}, u32[]{:S(2)}) collective-permute-start(bf16[2,160,128]{2,1,0:T(8,128)(2,1)S(1)} %stack.5.refs_0_), channel_id=1, source_target_pairs={{0,16},{8,24},{16,0},{24,8},{1,17},{9,25},{17,1},{25,9},{2,18},{10... | collective-permute-start | bytes 245768 | tf_op jit(solution)/shard_map/ppermute | solution.py:351
  18.7 12.0 %copy-start.6 = (bf16[2,304,128]{2,1,0:T(8,128)(2,1)}, bf16[2,304,128]{2,1,0:T(8,128)(2,1)S(1)}, u32[]{:S(2)}) copy-start(bf16[2,304,128]{2,1,0:T(8,128)(2,1)S(1)} %get-tuple-element.69.refs_0_) | copy-start | bytes 466948
  18.7 12.0 %copy-start.8 = (bf16[2,304,128]{2,1,0:T(8,128)(2,1)}, bf16[2,304,128]{2,1,0:T(8,128)(2,1)S(1)}, u32[]{:S(2)}) copy-start(bf16[2,304,128]{2,1,0:T(8,128)(2,1)S(1)} %get-tuple-element.70.refs_0_.refs_3_) | copy-start | bytes 466948
  18.7 5.2 %collective-permute-start.7 = (bf16[2,304,128]{2,1,0:T(8,128)(2,1)S(1)}, bf16[2,304,128]{2,1,0:T(8,128)(2,1)S(1)}, u32[]{:S(2)}, u32[]{:S(2)}) collective-permute-start(bf16[2,304,128]{2,1,0:T(8,128)(2,1)S(1)} %get-tuple-element.70.refs_0_.refs_3_), channel_id=1, source_target_pairs={{0,16},{8,24},{16,0},{24,8},{1,17},{9,25},{17,1},{25,9},{2,18},{10... | collective-permute-start | bytes 466952 | tf_op jit(solution)/shard_map/ppermute | solution.py:351
  20.3 5.2 %collective-permute-start.6 = (bf16[2,304,128]{2,1,0:T(8,128)(2,1)S(1)}, bf16[2,304,128]{2,1,0:T(8,128)(2,1)S(1)}, u32[]{:S(2)}, u32[]{:S(2)}) collective-permute-start(bf16[2,304,128]{2,1,0:T(8,128)(2,1)S(1)} %get-tuple-element.69.refs_0_), channel_id=1, source_target_pairs={{0,8},{8,0},{16,24},{24,16},{1,9},{9,1},{17,25},{25,17},{2,10},{10... | collective-permute-start | bytes 466952 | tf_op jit(solution)/shard_map/ppermute | solution.py:351
  24.0 4.5 %copy-start.10 = (bf16[2,304,128]{2,1,0:T(8,128)(2,1)}, bf16[2,304,128]{2,1,0:T(8,128)(2,1)S(1)}, u32[]{:S(2)}) copy-start(bf16[2,304,128]{2,1,0:T(8,128)(2,1)S(1)} %collective-permute-done.7.refs_1_.refs_4_) | copy-start | bytes 466948
  27.0 11.0 %collective-permute-start.9 = (bf16[2,2,304,128]{3,2,1,0:T(8,128)(2,1)}, bf16[2,2,304,128]{3,2,1,0:T(8,128)(2,1)}, u32[]{:S(2)}, u32[]{:S(2)}) collective-permute-start(bf16[2,2,304,128]{3,2,1,0:T(8,128)(2,1)} %stack.9), channel_id=1, source_target_pairs={{0,8},{8,0},{16,24},{24,16},{1,9},{9,1},{17,25},{25,17},{2,10},{10... | collective-permute-start | bytes 933896 | tf_op jit(solution)/shard_map/ppermute | solution.py:351
  28.5 9.5 %collective-permute-start.8 = (bf16[2,2,304,128]{3,2,1,0:T(8,128)(2,1)}, bf16[2,2,304,128]{3,2,1,0:T(8,128)(2,1)}, u32[]{:S(2)}, u32[]{:S(2)}) collective-permute-start(bf16[2,2,304,128]{3,2,1,0:T(8,128)(2,1)} %stack.8), channel_id=1, source_target_pairs={{0,16},{8,24},{16,0},{24,8},{1,17},{9,25},{17,1},{25,9},{2,18},{10... | collective-permute-start | bytes 933896 | tf_op jit(solution)/shard_map/ppermute | solution.py:351
  29.0 8.1 %collective-permute-start.5 = (bf16[4,160,128]{2,1,0:T(8,128)(2,1)S(1)}, bf16[4,160,128]{2,1,0:T(8,128)(2,1)}, u32[]{:S(2)}, u32[]{:S(2)}) collective-permute-start(bf16[4,160,128]{2,1,0:T(8,128)(2,1)S(1)} %bitcast.23), channel_id=1, source_target_pairs={{0,4},{1,5},{2,6},{3,7},{4,0},{5,1},{6,2},{7,3},{8,12},{9,13},{10,... | collective-permute-start | bytes 491528 | tf_op jit(solution)/shard_map/ppermute | solution.py:351
  44.6 3.5 %collective-permute-start.10 = (bf16[4,240,640]{2,1,0:T(8,128)(2,1)}, bf16[4,240,640]{2,1,0:T(8,128)(2,1)}, u32[]{:S(2)}, u32[]{:S(2)}) collective-permute-start(bf16[4,240,640]{2,1,0:T(8,128)(2,1)} %unpack.2.refs_1_.own_ref), channel_id=1, source_target_pairs={{0,1},{1,0},{2,3},{3,2},{4,5},{5,4},{6,7},{7,6},{8,9},{9,8},{10,11... | collective-permute-start | bytes 3686408 | tf_op jit(solution)/shard_map/ppermute | solution.py:351
  44.6 10.2 %collective-permute-start.14 = (bf16[2,4,160,128]{3,2,1,0:T(8,128)(2,1)S(1)}, bf16[2,4,160,128]{3,2,1,0:T(8,128)(2,1)}, u32[]{:S(2)}, u32[]{:S(2)}) collective-permute-start(bf16[2,4,160,128]{3,2,1,0:T(8,128)(2,1)S(1)} %stack.7.refs_4_), channel_id=1, source_target_pairs={{0,2},{1,3},{2,0},{3,1},{4,6},{5,7},{6,4},{7,5},{8,10},{9,11},{10,... | collective-permute-start | bytes 983048 | tf_op jit(solution)/shard_map/ppermute | solution.py:351
  44.6 10.2 %collective-permute-start.13 = (bf16[4,144,128]{2,1,0:T(8,128)(2,1)}, bf16[4,144,128]{2,1,0:T(8,128)(2,1)S(1)}, u32[]{:S(2)}, u32[]{:S(2)}) collective-permute-start(bf16[4,144,128]{2,1,0:T(8,128)(2,1)} %get-tuple-element.75.refs_0_), channel_id=1, source_target_pairs={{0,24},{8,16},{16,8},{24,0},{1,25},{9,17},{17,9},{25,1},{2,26},{10... | collective-permute-start | bytes 442376 | tf_op jit(solution)/shard_map/ppermute | solution.py:351
  46.0 9.2 %collective-permute-start.12 = (bf16[4,144,128]{2,1,0:T(8,128)(2,1)}, bf16[4,144,128]{2,1,0:T(8,128)(2,1)}, u32[]{:S(2)}, u32[]{:S(2)}) collective-permute-start(bf16[4,144,128]{2,1,0:T(8,128)(2,1)} %get-tuple-element.75.refs_0_), channel_id=1, source_target_pairs={{0,16},{8,24},{16,0},{24,8},{1,17},{9,25},{17,1},{25,9},{2,18},{10... | collective-permute-start | bytes 442376 | tf_op jit(solution)/shard_map/ppermute | solution.py:351
  46.6 8.7 %collective-permute-start.11 = (bf16[4,144,128]{2,1,0:T(8,128)(2,1)}, bf16[4,144,128]{2,1,0:T(8,128)(2,1)}, u32[]{:S(2)}, u32[]{:S(2)}) collective-permute-start(bf16[4,144,128]{2,1,0:T(8,128)(2,1)} %get-tuple-element.75.refs_0_), channel_id=1, source_target_pairs={{0,8},{8,0},{16,24},{24,16},{1,9},{9,1},{17,25},{25,17},{2,10},{10... | collective-permute-start | bytes 442376 | tf_op jit(solution)/shard_map/ppermute | solution.py:351
  57.4 3.0 %collective-permute-start.15 = (bf16[4,240,640]{2,1,0:T(8,128)(2,1)S(1)}, bf16[4,240,640]{2,1,0:T(8,128)(2,1)S(1)}, u32[]{:S(2)}, u32[]{:S(2)}) collective-permute-start(bf16[4,240,640]{2,1,0:T(8,128)(2,1)S(1)} %unpack.3.refs_1_.own_ref), channel_id=1, source_target_pairs={{0,1},{1,0},{2,3},{3,2},{4,5},{5,4},{6,7},{7,6},{8,9},{9,8},{10,11... | collective-permute-start | bytes 3686408 | tf_op jit(solution)/shard_map/ppermute | solution.py:351
  68.9 3.6 %collective-permute-start.16 = (bf16[976,640]{1,0:T(8,128)(2,1)S(1)}, bf16[976,640]{1,0:T(8,128)(2,1)S(1)}, u32[]{:S(2)}, u32[]{:S(2)}) collective-permute-start(bf16[976,640]{1,0:T(8,128)(2,1)S(1)} %get-tuple-element.82.own_ref), channel_id=1, source_target_pairs={{0,1},{1,0},{2,3},{3,2},{4,5},{5,4},{6,7},{7,6},{8,9},{9,8},{10,11... | collective-permute-start | bytes 3747848 | tf_op jit(solution)/shard_map/ppermute | solution.py:351
  72.8 17.1 %collective-permute-start.17 = (bf16[512,640]{1,0:T(8,128)(2,1)S(1)}, bf16[512,640]{1,0:T(8,128)(2,1)S(1)}, u32[]{:S(2)}, u32[]{:S(2)}) collective-permute-start(bf16[512,640]{1,0:T(8,128)(2,1)S(1)} %get-tuple-element.88.sent_ref), channel_id=1, source_target_pairs={{0,2},{1,3},{2,0},{3,1},{4,6},{5,7},{6,4},{7,5},{8,10},{9,11},{10,... | collective-permute-start | bytes 1966088 | tf_op jit(solution)/shard_map/ppermute | solution.py:351
  89.9 3.0 %collective-permute-start.18 = (bf16[960,640]{1,0:T(8,128)(2,1)S(1)}, bf16[960,640]{1,0:T(8,128)(2,1)S(1)}, u32[]{:S(2)}, u32[]{:S(2)}) collective-permute-start(bf16[960,640]{1,0:T(8,128)(2,1)S(1)} %get-tuple-element.96.own_ref), channel_id=1, source_target_pairs={{0,1},{1,0},{2,3},{3,2},{4,5},{5,4},{6,7},{7,6},{8,9},{9,8},{10,11... | collective-permute-start | bytes 3686408 | tf_op jit(solution)/shard_map/ppermute | solution.py:351
  93.1 24.3 %collective-permute-start.19 = (bf16[480,640]{1,0:T(8,128)(2,1)S(1)}, bf16[480,640]{1,0:T(8,128)(2,1)S(1)}, u32[]{:S(2)}, u32[]{:S(2)}) collective-permute-start(bf16[480,640]{1,0:T(8,128)(2,1)S(1)} %get-tuple-element.97.sent_ref), channel_id=1, source_target_pairs={{0,2},{1,3},{2,0},{3,1},{4,6},{5,7},{6,4},{7,5},{8,10},{9,11},{10,... | collective-permute-start | bytes 1843208 | tf_op jit(solution)/shard_map/ppermute | solution.py:351
  94.9 21.8 %collective-permute-start.20 = (bf16[304,640]{1,0:T(8,128)(2,1)S(1)}, bf16[304,640]{1,0:T(8,128)(2,1)S(1)}, u32[]{:S(2)}, u32[]{:S(2)}) collective-permute-start(bf16[304,640]{1,0:T(8,128)(2,1)S(1)} %merge.2.sent_ref), channel_id=1, source_target_pairs={{0,4},{1,5},{2,6},{3,7},{4,0},{5,1},{6,2},{7,3},{8,12},{9,13},{10,... | collective-permute-start | bytes 1167368 | tf_op jit(solution)/shard_map/ppermute | solution.py:351
  96.4 7.8 %collective-permute-start.23 = (bf16[2,304,128]{2,1,0:T(8,128)(2,1)S(1)}, bf16[2,304,128]{2,1,0:T(8,128)(2,1)S(1)}, u32[]{:S(2)}, u32[]{:S(2)}) collective-permute-start(bf16[2,304,128]{2,1,0:T(8,128)(2,1)S(1)} %copy-done.14), channel_id=1, source_target_pairs={{0,24},{8,16},{16,8},{24,0},{1,25},{9,17},{17,9},{25,1},{2,26},{10... | collective-permute-start | bytes 466952 | tf_op jit(solution)/shard_map/ppermute | solution.py:351
  98.0 8.2 %collective-permute-start.22 = (bf16[2,304,128]{2,1,0:T(8,128)(2,1)S(1)}, bf16[2,304,128]{2,1,0:T(8,128)(2,1)S(1)}, u32[]{:S(2)}, u32[]{:S(2)}) collective-permute-start(bf16[2,304,128]{2,1,0:T(8,128)(2,1)S(1)} %copy-done.14), channel_id=1, source_target_pairs={{0,16},{8,24},{16,0},{24,8},{1,17},{9,25},{17,1},{25,9},{2,18},{10... | collective-permute-start | bytes 466952 | tf_op jit(solution)/shard_map/ppermute | solution.py:351
  98.6 7.6 %collective-permute-start.21 = (bf16[2,304,128]{2,1,0:T(8,128)(2,1)S(1)}, bf16[2,304,128]{2,1,0:T(8,128)(2,1)S(1)}, u32[]{:S(2)}, u32[]{:S(2)}) collective-permute-start(bf16[2,304,128]{2,1,0:T(8,128)(2,1)S(1)} %copy-done.14), channel_id=1, source_target_pairs={{0,8},{8,0},{16,24},{24,16},{1,9},{9,1},{17,25},{25,17},{2,10},{10... | collective-permute-start | bytes 466952 | tf_op jit(solution)/shard_map/ppermute | solution.py:351
  117.5 16.0 %collective-permute-start.24 = (bf16[240,640]{1,0:T(8,128)(2,1)S(1)}, bf16[240,640]{1,0:T(8,128)(2,1)S(1)}, u32[]{:S(2)}, u32[]{:S(2)}) collective-permute-start(bf16[240,640]{1,0:T(8,128)(2,1)S(1)} %merge.3), channel_id=1, source_target_pairs={{0,4},{1,5},{2,6},{3,7},{4,0},{5,1},{6,2},{7,3},{8,12},{9,13},{10,... | collective-permute-start | bytes 921608 | tf_op jit(solution)/shard_map/ppermute | solution.py:351
  (10 other events, 24.2 us)

commit v6 on v5

--- a/solution.py
+++ b/solution.py
@@ -303,20 +303,22 @@
         total_ref[pl.ds(pl.multiple_of(t * channels, 128), channels)] = product
 
     if block is not None:
-        away_ref, home_ref = refs[:2]
+        home_ref, away_refs = refs[0], refs[1:]
         me = me_ref[0]
         count = home_ref.shape[0]
 
-        @pl.loop(0, count)
-        def _(j):
+        for j in range(count):
             away = pl.multiple_of((me ^ (2 * j + 1)) * block, 16)
             home = pl.multiple_of((me ^ (2 * j)) * block, 16)
-            place = pl.ds(pl.multiple_of(j * block, 16), block)
-            away_ref[place] = total_ref[pl.ds(away, block)].astype(BF16)
+            part = total_ref[pl.ds(away, block)].astype(BF16)
+            if centred:
+                away_refs[0][j * block : (j + 1) * block] = part
+            else:
+                away_refs[j][...] = part
             home_ref[j] = total_ref[pl.ds(home, block)]
 
         if centred:
-            away_ref[count * block :] = factors.astype(BF16)
+            away_refs[0][count * block :] = factors.astype(BF16)
     elif centred:
         refs[0][...] = factors
 
@@ -328,13 +330,16 @@
     specs = smem(1) + vmem(2)
     if block % 16 == 0:
         chips = n_member // 2
-        extra = FACTOR_ROWS if centred else 0
-        return call(
+        away = [((block, channels), BF16)] * chips
+        if centred:
+            away = [((chips * block + FACTOR_ROWS, channels), BF16)]
+        home, *away = call(
             functools.partial(grad_kernel, points, scale, block, centred),
-            [((chips * block + extra, channels), BF16), ((chips, block, channels), F32)],
+            [((chips, block, channels), F32)] + away,
             [pltpu.VMEM((3 * channels, channels), F32), turned],
             "gradient", specs, 24,
         )(me, act, cotangent)
+        return away, home, None
     factors = [((FACTOR_ROWS, channels), F32)] if centred else []
     found = call(
         functools.partial(grad_kernel, points, scale, None, centred),
@@ -344,7 +349,7 @@
     total = found[-1].reshape(n_member, block, channels)
     order = [lax.dynamic_index_in_dim(total, me[0] ^ j, 0, keepdims=False) for j in range(n_member)]
     away, home = jnp.stack(order[1::2]).astype(BF16), jnp.stack(order[0::2])
-    return (away, home) + tuple(found[:-1])
+    return [away], home, found[0] if centred else None
 
 
 def swap(value, axis, size, offset):
@@ -373,6 +378,7 @@
 
 
 def pack_kernel(*refs):
+    refs = refs[:4] + refs[6:]
     sources, (early_ref, late_ref, rates_ref) = refs[:4], refs[4:7]
     held, sems = refs[7:11], refs[11]
     copies = fetch(sources, held, sems)
@@ -493,12 +499,12 @@
             jax.ShapeDtypeStruct((size - cut, 128), BF16),
             jax.ShapeDtypeStruct((2, size, 128), BF16),
         ),
-        in_specs=hbm(4),
+        in_specs=hbm(4) + smem(2),
         out_specs=tuple(vmem(3)),
         scratch_shapes=[pltpu.VMEM((cols, rows), BF16)] * 4 + [pltpu.SemaphoreType.DMA((4,))],
         cost_estimate=pl.CostEstimate(flops=0, bytes_accessed=1024, transcendentals=0),
         name="pack",
-    )(conv1.T, conv2.T, rate1.T, rate2.T)
+    )(conv1.T, conv2.T, rate1.T, rate2.T, group, me)
 
     def unpack(kernel, *packed):
         (mine,) = call(
@@ -523,7 +529,6 @@
     late, late_y = order_after((late, late_y), first)
     late = stacked(late, late_y).reshape(n_group, size - cut, 128)
     late_z = swap(late, "member", n_member, 4)
-    first_x, second_y = order_after((first_x, second_y), late)
     first_y = swap(stacked(first, first_x), "group", n_group, 2)
     second_x = swap(stacked(second, second_y), "group", n_group, 1)
     late = stacked(late, late_z)
@@ -599,33 +604,50 @@
     )(own, home, received)
 
 
-def merge_kernel(middle_ref, sent_ref, received_ref, out_ref):
+def parts_kernel(home_ref, *refs):
+    received_refs, outs = refs[:4], refs[4:]
+    for k, out in zip((3, 1, 2, 0), outs):
+        out[...] = (home_ref[k] + received_refs[k][...].astype(F32)).astype(out.dtype)
+
+
+def pair_parts(home, received):
+    shape = home.shape[1:]
+    return call(
+        parts_kernel, [(shape, BF16), (shape, BF16), (shape, F32), (shape, F32)], [],
+        "pair", vmem(5), 12,
+    )(home, *received)
+
+
+def merge_kernel(middle_ref, *refs):
+    *sent_refs, received_ref, out_ref = refs
     rows = middle_ref.shape[0]
-    known = sent_ref.shape[0] - 2 * rows
     out_ref[0:rows] = (middle_ref[...] + received_ref[0:rows].astype(F32)).astype(BF16)
-    if known:
+    for sent_ref in sent_refs:
+        known = sent_ref.shape[0] - 2 * rows
         out_ref[rows : rows + known] = sent_ref[2 * rows :]
         out_ref[rows + known :] = received_ref[2 * rows :]
 
 
-def merge(middle, sent, received):
+def merge(middle, received, *sent):
     rows, channels = middle.shape
-    shape = (rows + 2 * (sent.shape[0] - 2 * rows), channels)
-    return call(merge_kernel, [(shape, BF16)], [], "merge", vmem(3))(middle, sent, received)[0]
+    known = [part.shape[0] - 2 * rows for part in sent]
+    shape = (rows + 2 * sum(known), channels)
+    operands = (middle,) + sent + (received,)
+    return call(merge_kernel, [(shape, BF16)], [], "merge", vmem(len(operands)))(*operands)[0]
 
 
 def update_kernel(own_ref, rate_ref, *refs):
-    rows = rate_ref.shape[0]
     total = refs[0][...]
     for ref in refs[1:-1]:
-        start = rows if ref.shape[0] == 2 * rows else 0
-        total = total + ref[start : start + rows].astype(F32)
+        total = total + ref[...].astype(F32)
     refs[-1][...] = own_ref[0].astype(F32) - rate_ref[...].astype(F32) * total
 
 
-def common_update_kernel(
-    me_ref, own_ref, rate_ref, kept_ref, half_ref, sent_ref, received_ref, out_ref
+def both_kernel(
+    me_ref, own_ref, rate_ref, kept_ref, half_ref, sent_ref, received_ref, *refs
 ):
+    *first_refs, first_out, out_ref = refs
+    update_kernel(*first_refs, first_out)
     rows, channels = rate_ref.shape
     total = kept_ref[...] + half_ref[rows : 2 * rows].astype(F32)
     total = total + received_ref[0:rows].astype(F32)
@@ -637,7 +659,7 @@
             sums.append(parts[3:4] + parts[4:5] + parts[5:6])
     means, sums = jnp.concatenate(means, axis=0), jnp.concatenate(sums, axis=0)
     means = jnp.concatenate([means] * 3, axis=1)
-    for member in range(len(range(0, 3 * channels, rows))):
+    for member in range(3 * channels // rows):
 
         @pl.when(me_ref[0] == member)
         def _():
@@ -651,10 +673,12 @@
             out_ref[...] = own_ref[0].astype(F32) - rate_ref[...].astype(F32) * (total + common)
 
 
-def common_update(me, own, rate, *terms):
+def update_both(me, second_terms, first_terms):
+    terms = second_terms + first_terms
+    shape = (second_terms[1].shape, F32)
     return call(
-        common_update_kernel, [(rate.shape, F32)], [], "update", smem(1) + vmem(6)
-    )(me, own, rate, *terms)[0]
+        both_kernel, [shape, shape], [], "update", smem(1) + vmem(len(terms)), 16
+    )(me, *terms)
 
 
 def update(own, rate, *terms):
@@ -747,7 +771,7 @@
         [pltpu.VMEM((rows, channels), BF16)] * 2 + [pltpu.SemaphoreType.DMA((2,))],
         "conv_error", vmem(1) + hbm(2) + weight_specs(weight_two), 24,
     )(act_two, clip, target, *weight_two)
-    away_two, home_two, *factors = gradient(
+    (away_two,), home_two, factors = gradient(
         turned_two, error, me, n_member, points, scale, True
     )
     received_two = swap(away_two, "member", n_member, 1)
@@ -755,7 +779,7 @@
         functools.partial(back_kernel, points, scale),
         [((rows, channels), F32)], [], "back", vmem(2), 20,
     )(order_after(error, away_two), full_two)
-    staged = n_member == 8 and not factors
+    staged = n_member == 8 and factors is None
     received_two, grad_act = lax.optimization_barrier((received_two, grad_act))
     if staged:
         half_two, middle_two, kept_two = pair_sums(away_two, home_two, received_two)
@@ -771,34 +795,31 @@
         ],
         "norm_back", vmem(3) + hbm(1), 20,
     )(grad_act, normal, inverse, same_group)
-    away_one, home_one = gradient(
+    away_one, home_one, _ = gradient(
         act_one, grad_hidden, me, n_member, points, scale, False
     )
+    received_one = [swap(part, "member", n_member, 1) for part in away_one]
     if staged:
-        merged_two = merge(middle_two, half_two, order_after(from_two, away_one))
+        far_one, near_one, middle_one, kept_one = pair_parts(home_one, received_one)
+        from_one = swap(far_one, "member", n_member, 2)
+        beside_one = swap(near_one, "member", n_member, 2)
+        merged_two = merge(middle_two, from_two, half_two)
         across_two = swap(merged_two, "member", n_member, 4)
-        received_one = swap(order_after(away_one, merged_two), "member", n_member, 1)
-        half_one, middle_one, kept_one = pair_sums(away_one, home_one, received_one)
-        from_one = swap(half_one, "member", n_member, 2)
-        rate_one, rate_two = rates(half_one)
-        from_one, across_two, rate_one, rate_two = order_after(
-            (from_one, across_two, rate_one, rate_two), ()
+        rate_one, rate_two = rates(far_one)
+        middle_one = order_after(middle_one, (rate_one, rate_two))
+        across_one = swap(merge(middle_one, from_one), "member", n_member, 4)
+        adapted_one, adapted_two = update_both(
+            me,
+            (own_two, rate_two, kept_two, from_two, merged_two, across_two),
+            (own_one, rate_one, kept_one, beside_one, across_one),
         )
-        merged_one = merge(middle_one, half_one, from_one)
-        across_one = swap(merged_one, "member", n_member, 4)
-        adapted_two = common_update(
-            me, own_two, rate_two, kept_two, from_two, merged_two,
-            order_after(across_two, merged_one),
-        )
-        terms_one = [kept_one, from_one, across_one]
     else:
-        received_one = swap(away_one, "member", n_member, 1)
         rate_one, rate_two = rates(away_one)
-        every = lax.all_gather(factors[0], "member")
+        every = lax.all_gather(factors, "member")
         terms_two = halve_to_owner(*add_received(home_two, received_two), None, n_member)
-        terms_one = halve_to_owner(*add_received(home_one, received_one), None, n_member)
+        terms_one = halve_to_owner(*add_received(home_one, received_one[0]), None, n_member)
         adapted_two = update(own_two, rate_two, *terms_two, common_term(every, me, own_rows))
-    adapted_one = update(own_one, rate_one, *terms_one)
+        adapted_one = update(own_one, rate_one, *terms_one)
     return (adapted_one[None], adapted_two[None])
 
 

time: 136 us -> 116 us (0.85)
  Pallas kernels: 43.4 us -> 33.6 us
  waiting for transfers between devices: 53.9 us -> 47.1 us
  local copies, waits for them, and re-layouts: 3.72 us -> 0.05 us
    ppermute x25 -> x29, waiting for transfers between devices: 53.9 us -> 47.1 us  [swap(): return lax.ppermute(value, axis, [(i, i ^ offset) for i in range(size)])]
    unnamed x34 -> x14, local copies, waits for them, and re-layouts: 3.71 us -> 0.04 us
    pallas_call x2, Pallas kernels: 4.99 us -> 1.67 us  [unpack(): call(kernel, [((chips, rows, width), BF16)], [], 'unpack', smem(1) + vmem...]
    pallas_call x5, Pallas kernels: 2.47 us -> 0.09 us  [stacked(): call(stack_kernel, [(shape, BF16)], [], 'stack', vmem(len(arrays)))(*arrays)]
    pallas_call x4, Pallas kernels: 4.22 us -> 2.57 us  [the longest x1 2.19 us: update_both(): call(both_kernel, [shape, shape], [], 'update', smem(1) + vmem(len(terms)...]
    pallas_call x1, Pallas kernels: 4.99 us -> 3.37 us  [shards(): call(functools.partial(first_kernel, points, scale), [((rows, channels),...]
    ppermute x25 -> x29, starting transfers between devices: 30.9 us -> 31.2 us  [swap(): return lax.ppermute(value, axis, [(i, i ^ offset) for i in range(size)])]
  transfers between devices with their start and end apart: 25 -> 29, of which waited for: 15 -> 17; matrix products, arithmetic and copies ran while one was open for 1% -> 1% of each run, Pallas kernels for 17% -> 16%
where the time goes in v6:
time: 116 us
  waiting for transfers between devices  47.1 us (41%)
  Pallas kernels  33.6 us (29%)
  starting transfers between devices  31.2 us (27%)
  between operations  2.24 us (2%)
  matrix products  1.53 us (1%)
    ppermute x29, waiting for transfers between devices, swap(): return lax.ppermute(value, axis, [(i, i ^ offset) for i in range(size)])  47.1 us
    ppermute x29, starting transfers between devices, swap(): return lax.ppermute(value, axis, [(i, i ^ offset) for i in range(size)])  31.2 us
    pallas_call x2, Pallas kernels, gradient(): call(functools.partial(grad_kernel, points, scale, block, centred), [((ch...  9.02 us
    pallas_call x1, Pallas kernels, shards(): call(functools.partial(second_kernel, points, scale), [((padded, channels...  3.86 us
    pallas_call x1, Pallas kernels, shards(): call(functools.partial(back_kernel, points, scale), [((rows, channels), F...  3.43 us
    pallas_call x1, Pallas kernels, shards(): call(functools.partial(first_kernel, points, scale), [((rows, channels),...  3.37 us
    pallas_call x1, Pallas kernels, weights_and_rates(): pl.pallas_call(pack_kernel, out_shape=(jax.ShapeDtypeStruct((size + cut,...  2.39 us
  transfers between devices with their start and end apart: 29, of which 17 were waited for; matrix products, arithmetic and copies ran while one was open for 1% of the time, Pallas kernels for 16%

profile of v6, /device:TPU:0, one launch (start us, length us, event | category | flops | bytes accessed | tf_op | source)
XLA Modules:
  0.0 115.8 jit_solution(14872914063731484755)
XLA Ops:
  0.7 2.4 %pack.1 = (bf16[448,128]{1,0:T(8,128)(2,1)}, bf16[160,128]{1,0:T(8,128)(2,1)}, bf16[2,304,128]{2,1,0:T(8,128)(2,1)}) custom-call(bf16[160,240]{1,0:T(8,128)(2,1)} %bitcast.25, bf16[160,240]{1,0:T(8,128)(2,1)} %bitcast.26, bf16[160,240]{1,0:T(8,128)(2,1)} %bitcast.27, bf16[160,240]{1,0:T(8,128)(2,1)} %bitcast.28, s32[1]{0:T(128)} %bitcast.1.refs_4_.group_ref, ...), custom_call_target="tpu_custom_call" | custom-call | bytes 1024 | tf_op jit(solution)/shard_map/pack/pallas_call | solution.py:495
  3.1 5.1 %collective-permute-start.2 = (bf16[448,128]{1,0:T(8,128)(2,1)}, bf16[448,128]{1,0:T(8,128)(2,1)S(1)}, u32[]{:S(2)}, u32[]{:S(2)}) collective-permute-start(bf16[448,128]{1,0:T(8,128)(2,1)} %get-tuple-element.59.refs_0_), channel_id=1, source_target_pairs={{0,6},{1,7},{2,4},{3,5},{4,2},{5,3},{6,0},{7,1},{8,14},{9,15},{10,... | collective-permute-start | bytes 344072 | tf_op jit(solution)/shard_map/ppermute | solution.py:356
  8.8 1.6 %collective-permute-start.3 = (bf16[160,128]{1,0:T(8,128)(2,1)}, bf16[160,128]{1,0:T(8,128)(2,1)S(1)}, u32[]{:S(2)}, u32[]{:S(2)}) collective-permute-start(bf16[160,128]{1,0:T(8,128)(2,1)} %get-tuple-element.55.refs_0_), channel_id=1, source_target_pairs={{0,8},{8,0},{16,24},{24,16},{1,9},{9,1},{17,25},{25,17},{2,10},{10... | collective-permute-start | bytes 122888 | tf_op jit(solution)/shard_map/ppermute | solution.py:356
  11.8 1.2 %convolution_reduce_fusion = f32[1280]{0:T(1024)S(1)} fusion(f32[64,1280]{1,0:T(8,128)} %param.20, s32[]{:T(128)} %bitcast.19), kind=kOutput, calls=%fused_computation | convolution fusion | flops 983104 | bytes 332804 | tf_op jit(solution)/shard_map/dot_general | solution.py:25
  13.5 1.6 %collective-permute-start.4 = (bf16[2,160,128]{2,1,0:T(8,128)(2,1)S(1)}, bf16[2,160,128]{2,1,0:T(8,128)(2,1)S(1)}, u32[]{:S(2)}, u32[]{:S(2)}) collective-permute-start(bf16[2,160,128]{2,1,0:T(8,128)(2,1)S(1)} %stack.5.refs_0_), channel_id=1, source_target_pairs={{0,16},{8,24},{16,0},{24,8},{1,17},{9,25},{17,1},{25,9},{2,18},{10... | collective-permute-start | bytes 245768 | tf_op jit(solution)/shard_map/ppermute | solution.py:356
  15.0 2.2 %enter.1.in_ref.act_ref = bf16[1024,640]{1,0:T(8,128)(2,1)S(1)} custom-call(bf16[896,640]{1,0:T(8,128)(2,1)S(1)} %bitcast.20, bf16[640,640]{1,0:T(8,128)(2,1)S(1)} %copy-done.1), custom_call_target="tpu_custom_call" | custom-call | bytes 1024 | tf_op jit(solution)/shard_map/enter/pallas_call | solution.py:729
  18.1 1.6 %collective-permute-start.8 = (bf16[2,304,128]{2,1,0:T(8,128)(2,1)S(1)}, bf16[2,304,128]{2,1,0:T(8,128)(2,1)S(1)}, u32[]{:S(2)}, u32[]{:S(2)}) collective-permute-start(bf16[2,304,128]{2,1,0:T(8,128)(2,1)S(1)} %get-tuple-element.69.refs_0_.refs_3_), channel_id=1, source_target_pairs={{0,16},{8,24},{16,0},{24,8},{1,17},{9,25},{17,1},{25,9},{2,18},{10... | collective-permute-start | bytes 466952 | tf_op jit(solution)/shard_map/ppermute | solution.py:356
  19.7 1.5 %collective-permute-start.6 = (bf16[2,304,128]{2,1,0:T(8,128)(2,1)S(1)}, bf16[2,304,128]{2,1,0:T(8,128)(2,1)S(1)}, u32[]{:S(2)}, u32[]{:S(2)}) collective-permute-start(bf16[2,304,128]{2,1,0:T(8,128)(2,1)S(1)} %get-tuple-element.68.refs_0_), channel_id=1, source_target_pairs={{0,8},{8,0},{16,24},{24,16},{1,9},{9,1},{17,25},{25,17},{2,10},{10... | collective-permute-start | bytes 466952 | tf_op jit(solution)/shard_map/ppermute | solution.py:356
  21.2 2.2 %collective-permute-done.8.refs_1_.refs_4_ = bf16[2,304,128]{2,1,0:T(8,128)(2,1)S(1)} collective-permute-done((bf16[2,304,128]{2,1,0:T(8,128)(2,1)S(1)}, bf16[2,304,128]{2,1,0:T(8,128)(2,1)S(1)}, u32[]{:S(2)}, u32[]{:S(2)}) %collective-permute-start.8) | collective-permute-done | bytes 155680 | tf_op jit(solution)/shard_map/ppermute | solution.py:356
  23.5 1.6 %collective-permute-start.9 = (bf16[2,2,304,128]{3,2,1,0:T(8,128)(2,1)S(1)}, bf16[2,2,304,128]{3,2,1,0:T(8,128)(2,1)S(1)}, u32[]{:S(2)}, u32[]{:S(2)}) collective-permute-start(bf16[2,2,304,128]{3,2,1,0:T(8,128)(2,1)S(1)} %stack.9), channel_id=1, source_target_pairs={{0,8},{8,0},{16,24},{24,16},{1,9},{9,1},{17,25},{25,17},{2,10},{10... | collective-permute-start | bytes 933896 | tf_op jit(solution)/shard_map/ppermute | solution.py:356
  26.6 2.2 %collective-permute-start.5 = (bf16[4,160,128]{2,1,0:T(8,128)(2,1)S(1)}, bf16[4,160,128]{2,1,0:T(8,128)(2,1)S(1)}, u32[]{:S(2)}, u32[]{:S(2)}) collective-permute-start(bf16[4,160,128]{2,1,0:T(8,128)(2,1)S(1)} %bitcast.23), channel_id=1, source_target_pairs={{0,4},{1,5},{2,6},{3,7},{4,0},{5,1},{6,2},{7,3},{8,12},{9,13},{10,... | collective-permute-start | bytes 491528 | tf_op jit(solution)/shard_map/ppermute | solution.py:356
  28.8 5.9 %collective-permute-done.5.refs_1_ = bf16[4,160,128]{2,1,0:T(8,128)(2,1)S(1)} collective-permute-done((bf16[4,160,128]{2,1,0:T(8,128)(2,1)S(1)}, bf16[4,160,128]{2,1,0:T(8,128)(2,1)S(1)}, u32[]{:S(2)}, u32[]{:S(2)}) %collective-permute-start.5) | collective-permute-done | bytes 163872 | tf_op jit(solution)/shard_map/ppermute | solution.py:356
  35.8 2.7 %collective-permute-start.12 = (bf16[4,144,128]{2,1,0:T(8,128)(2,1)S(1)}, bf16[4,144,128]{2,1,0:T(8,128)(2,1)S(1)}, u32[]{:S(2)}, u32[]{:S(2)}) collective-permute-start(bf16[4,144,128]{2,1,0:T(8,128)(2,1)S(1)} %get-tuple-element.70.refs_0_), channel_id=1, source_target_pairs={{0,24},{8,16},{16,8},{24,0},{1,25},{9,17},{17,9},{25,1},{2,26},{10... | collective-permute-start | bytes 442376 | tf_op jit(solution)/shard_map/ppermute | solution.py:356
  39.3 3.4 %conv.1.hidden_ref = f32[896,640]{1,0:T(8,128)S(1)} custom-call(bf16[1024,640]{1,0:T(8,128)(2,1)S(1)} %enter.1.in_ref.act_ref, f32[1,640]{1,0:T(1,128)S(1)} %fusion.6.bias_ref, s32[1]{0:T(128)} %bitcast.refs_5_.refs_0_.me_ref, bf16[4,240,640]{2,1,0:T(8,128)(2,1)S(1)} %unpack.2.refs_1_.refs_0_, bf16[4,240,640]{2,1,0:T(8,128)(2,1)S(1)} %collective-permute-done.14.refs_2_), custom_call_target="tpu_custom_call" | custom-call | bytes 1024 | tf_op jit(solution)/shard_map/conv/pallas_call | solution.py:747
  42.7 3.0 %collective-permute-done.13.refs_5_ = bf16[2,4,160,128]{3,2,1,0:T(8,128)(2,1)S(1)} collective-permute-done((bf16[2,4,160,128]{3,2,1,0:T(8,128)(2,1)S(1)}, bf16[2,4,160,128]{3,2,1,0:T(8,128)(2,1)S(1)}, u32[]{:S(2)}, u32[]{:S(2)}) %collective-permute-start.13) | collective-permute-done | bytes 327712 | tf_op jit(solution)/shard_map/ppermute | solution.py:356
  46.4 0.9 unpack.3.refs_1_.own_ref
  47.4 2.3 %norm.1 = (f32[896,640]{1,0:T(8,128)S(1)}, f32[1,640]{1,0:T(1,128)S(1)}, bf16[1024,640]{1,0:T(8,128)(2,1)S(1)}, bf16[640,896]{1,0:T(8,128)(2,1)S(1)}) custom-call(f32[896,640]{1,0:T(8,128)S(1)} %conv.1.hidden_ref, bf16[640,640]{1,0:T(8,128)(2,1)S(1)} %copy-done.1), custom_call_target="tpu_custom_call" | custom-call | bytes 1024 | tf_op jit(solution)/shard_map/norm/pallas_call | solution.py:757
  50.3 3.9 %conv_error.1 = (bf16[1024,640]{1,0:T(8,128)(2,1)S(1)}, bf16[1920,640]{1,0:T(8,128)(2,1)S(1)}) custom-call(bf16[1024,640]{1,0:T(8,128)(2,1)S(1)} %get-tuple-element.77.in_ref, bf16[896,640]{1,0:T(8,128)(2,1)S(1)} %bitcast.21, bf16[896,640]{1,0:T(8,128)(2,1)S(1)} %bitcast.22, s32[1]{0:T(128)} %bitcast.refs_5_.refs_0_.me_ref, ...), custom_call_target="tpu_custom_call" | custom-call | bytes 1024 | tf_op jit(solution)/shard_map/conv_error/pallas_call | solution.py:768
  54.2 4.5 %gradient.2 = (f32[4,240,640]{2,1,0:T(8,128)S(1)}, bf16[976,640]{1,0:T(8,128)(2,1)S(1)}) custom-call(s32[1]{0:T(128)} %bitcast.refs_5_.refs_0_.me_ref, bf16[640,896]{1,0:T(8,128)(2,1)S(1)} %get-tuple-element.76.act_ref, bf16[1024,640]{1,0:T(8,128)(2,1)S(1)} %get-tuple-element.80.cotangent_ref.error_ref), custom_call_target="tpu_custom_call" | custom-call | bytes 1024 | tf_op jit(solution)/shard_map/gradient/pallas_call | solution.py:336
  58.9 3.4 %back.1.act_grad_ref = f32[896,640]{1,0:T(8,128)S(1)} custom-call(bf16[1024,640]{1,0:T(8,128)(2,1)S(1)} %get-tuple-element.80.cotangent_ref.error_ref, bf16[1920,640]{1,0:T(8,128)(2,1)S(1)} %get-tuple-element.81.weight_ref), custom_call_target="tpu_custom_call" | custom-call | bytes 1024 | tf_op jit(solution)/shard_map/back/pallas_call | solution.py:778
  62.7 1.3 %collective-permute-start.24 = (bf16[512,640]{1,0:T(8,128)(2,1)S(1)}, bf16[512,640]{1,0:T(8,128)(2,1)S(1)}, u32[]{:S(2)}, u32[]{:S(2)}) collective-permute-start(bf16[512,640]{1,0:T(8,128)(2,1)S(1)} %get-tuple-element.85.refs_0_), channel_id=1, source_target_pairs={{0,2},{1,3},{2,0},{3,1},{4,6},{5,7},{6,4},{7,5},{8,10},{9,11},{10,... | collective-permute-start | bytes 1966088 | tf_op jit(solution)/shard_map/ppermute | solution.py:356
  64.0 2.0 %norm_back.1.cotangent_ref = bf16[1024,640]{1,0:T(8,128)(2,1)S(1)} custom-call(f32[896,640]{1,0:T(8,128)S(1)} %back.1.act_grad_ref, f32[896,640]{1,0:T(8,128)S(1)} %get-tuple-element.87.normal_ref, f32[1,640]{1,0:T(1,128)S(1)} %get-tuple-element.88.inverse_ref, bf16[640,640]{1,0:T(8,128)(2,1)S(1)} %copy-done.1), custom_call_target="tpu_custom_call" | custom-call | bytes 1024 | tf_op jit(solution)/shard_map/norm_back/pallas_call | solution.py:788
  66.0 4.5 %gradient.3 = (f32[4,240,640]{2,1,0:T(8,128)S(1)}, bf16[240,640]{1,0:T(8,128)(2,1)S(1)}, bf16[240,640]{1,0:T(8,128)(2,1)S(1)}, bf16[240,640]{1,0:T(8,128)(2,1)S(1)}, bf16[240,640]{1,0:T(8,128)(2,1)S(1)}) custom-call(s32[1]{0:T(128)} %bitcast.refs_5_.refs_0_.me_ref, bf16[1024,640]{1,0:T(8,128)(2,1)S(1)} %enter.1.in_ref.act_ref, ...), custom_call_target="tpu_custom_call" | custom-call | bytes 1024 | tf_op jit(solution)/shard_map/gradient/pallas_call | solution.py:336
  73.8 0.8 collective-permute-start.27
  74.6 1.6 %collective-permute-start.23 = (bf16[2,304,128]{2,1,0:T(8,128)(2,1)S(1)}, bf16[2,304,128]{2,1,0:T(8,128)(2,1)S(1)}, u32[]{:S(2)}, u32[]{:S(2)}) collective-permute-start(bf16[2,304,128]{2,1,0:T(8,128)(2,1)S(1)} %copy-done.4), channel_id=1, source_target_pairs={{0,24},{8,16},{16,8},{24,0},{1,25},{9,17},{17,9},{25,1},{2,26},{10... | collective-permute-start | bytes 466952 | tf_op jit(solution)/shard_map/ppermute | solution.py:356
  76.2 1.1 collective-permute-start.22
  78.1 2.2 %collective-permute-done.24.refs_1_.half_ref = bf16[512,640]{1,0:T(8,128)(2,1)S(1)} collective-permute-done((bf16[512,640]{1,0:T(8,128)(2,1)S(1)}, bf16[512,640]{1,0:T(8,128)(2,1)S(1)}, u32[]{:S(2)}, u32[]{:S(2)}) %collective-permute-start.24) | collective-permute-done | bytes 655392 | tf_op jit(solution)/shard_map/ppermute | solution.py:356
  80.4 3.4 %collective-permute-start.25 = (bf16[304,640]{1,0:T(8,128)(2,1)S(1)}, bf16[304,640]{1,0:T(8,128)(2,1)S(1)}, u32[]{:S(2)}, u32[]{:S(2)}) collective-permute-start(bf16[304,640]{1,0:T(8,128)(2,1)S(1)} %merge.2.sent_ref), channel_id=1, source_target_pairs={{0,4},{1,5},{2,6},{3,7},{4,0},{5,1},{6,2},{7,3},{8,12},{9,13},{10,... | collective-permute-start | bytes 1167368 | tf_op jit(solution)/shard_map/ppermute | solution.py:356
  85.1 7.3 %collective-permute-done.27.refs_0_ = bf16[240,640]{1,0:T(8,128)(2,1)S(1)} collective-permute-done((bf16[240,640]{1,0:T(8,128)(2,1)S(1)}, bf16[240,640]{1,0:T(8,128)(2,1)S(1)}, u32[]{:S(2)}, u32[]{:S(2)}) %collective-permute-start.27) | collective-permute-done | bytes 307232 | tf_op jit(solution)/shard_map/ppermute | solution.py:356
  92.5 12.5 %collective-permute-done.26.refs_3_ = bf16[240,640]{1,0:T(8,128)(2,1)S(1)} collective-permute-done((bf16[240,640]{1,0:T(8,128)(2,1)S(1)}, bf16[240,640]{1,0:T(8,128)(2,1)S(1)}, u32[]{:S(2)}, u32[]{:S(2)}) %collective-permute-start.26) | collective-permute-done | bytes 307232 | tf_op jit(solution)/shard_map/ppermute | solution.py:356
  105.0 8.6 %collective-permute-done.28.refs_4_ = bf16[240,640]{1,0:T(8,128)(2,1)S(1)} collective-permute-done((bf16[240,640]{1,0:T(8,128)(2,1)S(1)}, bf16[240,640]{1,0:T(8,128)(2,1)S(1)}, u32[]{:S(2)}, u32[]{:S(2)}) %collective-permute-start.28) | collective-permute-done | bytes 307232 | tf_op jit(solution)/shard_map/ppermute | solution.py:356
  113.6 2.2 %update.1 = (f32[240,640]{1,0:T(8,128)}, f32[240,640]{1,0:T(8,128)}) custom-call(s32[1]{0:T(128)} %bitcast.refs_5_.refs_0_.me_ref, bf16[4,240,640]{2,1,0:T(8,128)(2,1)S(1)} %unpack.3.refs_1_.own_ref, bf16[240,640]{1,0:T(8,128)(2,1)S(1)} %get-tuple-element.96.rate_ref, f32[240,640]{1,0:T(8,128)S(1)} %get-tuple-element.97.kept_ref, ...), custom_call_target="tpu_custom_call" | custom-call | bytes 1024 | tf_op jit(solution)/shard_map/update/pallas_call | solution.py:679
  (68 shorter events, 12.9 us)
Async XLA Ops:
  0.6 12.5 %copy-start = (bf16[1280,640]{1,0:T(8,128)(2,1)S(1)}, bf16[1280,640]{1,0:T(8,128)(2,1)}, u32[]{:S(2)}) copy-start(bf16[1280,640]{1,0:T(8,128)(2,1)} %param.19) | copy-start | bytes 4915204
  0.6 14.4 %copy-start.1 = (bf16[640,640]{1,0:T(8,128)(2,1)S(1)}, bf16[640,640]{1,0:T(8,128)(2,1)}, u32[]{:S(2)}) copy-start(bf16[640,640]{1,0:T(8,128)(2,1)} %constant.18.clone.same_hbm) | copy-start | bytes 2457604
  3.1 12.0 %copy-start.2 = (bf16[1,14,64,640]{3,2,1,0:T(8,128)(2,1)S(1)}, bf16[1,14,64,640]{3,2,1,0:T(8,128)(2,1)}, u32[]{:S(2)}) copy-start(bf16[1,14,64,640]{3,2,1,0:T(8,128)(2,1)} %param.11) | copy-start | bytes 3440644
  3.1 14.2 %collective-permute-start.2 = (bf16[448,128]{1,0:T(8,128)(2,1)}, bf16[448,128]{1,0:T(8,128)(2,1)S(1)}, u32[]{:S(2)}, u32[]{:S(2)}) collective-permute-start(bf16[448,128]{1,0:T(8,128)(2,1)} %get-tuple-element.59.refs_0_), channel_id=1, source_target_pairs={{0,6},{1,7},{2,4},{3,5},{4,2},{5,3},{6,0},{7,1},{8,14},{9,15},{10,... | collective-permute-start | bytes 344072 | tf_op jit(solution)/shard_map/ppermute | solution.py:356
  8.2 9.9 %collective-permute-start.1 = (bf16[448,128]{1,0:T(8,128)(2,1)}, bf16[448,128]{1,0:T(8,128)(2,1)S(1)}, u32[]{:S(2)}, u32[]{:S(2)}) collective-permute-start(bf16[448,128]{1,0:T(8,128)(2,1)} %get-tuple-element.59.refs_0_), channel_id=1, source_target_pairs={{0,4},{1,5},{2,6},{3,7},{4,0},{5,1},{6,2},{7,3},{8,12},{9,13},{10,... | collective-permute-start | bytes 344072 | tf_op jit(solution)/shard_map/ppermute | solution.py:356
  8.2 9.9 %collective-permute-start = (bf16[448,128]{1,0:T(8,128)(2,1)}, bf16[448,128]{1,0:T(8,128)(2,1)S(1)}, u32[]{:S(2)}, u32[]{:S(2)}) collective-permute-start(bf16[448,128]{1,0:T(8,128)(2,1)} %get-tuple-element.59.refs_0_), channel_id=1, source_target_pairs={{0,2},{1,3},{2,0},{3,1},{4,6},{5,7},{6,4},{7,5},{8,10},{9,11},{10,... | collective-permute-start | bytes 344072 | tf_op jit(solution)/shard_map/ppermute | solution.py:356
  8.8 4.6 %collective-permute-start.3 = (bf16[160,128]{1,0:T(8,128)(2,1)}, bf16[160,128]{1,0:T(8,128)(2,1)S(1)}, u32[]{:S(2)}, u32[]{:S(2)}) collective-permute-start(bf16[160,128]{1,0:T(8,128)(2,1)} %get-tuple-element.55.refs_0_), channel_id=1, source_target_pairs={{0,8},{8,0},{16,24},{24,16},{1,9},{9,1},{17,25},{25,17},{2,10},{10... | collective-permute-start | bytes 122888 | tf_op jit(solution)/shard_map/ppermute | solution.py:356
  13.5 4.6 %collective-permute-start.4 = (bf16[2,160,128]{2,1,0:T(8,128)(2,1)S(1)}, bf16[2,160,128]{2,1,0:T(8,128)(2,1)S(1)}, u32[]{:S(2)}, u32[]{:S(2)}) collective-permute-start(bf16[2,160,128]{2,1,0:T(8,128)(2,1)S(1)} %stack.5.refs_0_), channel_id=1, source_target_pairs={{0,16},{8,24},{16,0},{24,8},{1,17},{9,25},{17,1},{25,9},{2,18},{10... | collective-permute-start | bytes 245768 | tf_op jit(solution)/shard_map/ppermute | solution.py:356
  18.1 5.3 %collective-permute-start.8 = (bf16[2,304,128]{2,1,0:T(8,128)(2,1)S(1)}, bf16[2,304,128]{2,1,0:T(8,128)(2,1)S(1)}, u32[]{:S(2)}, u32[]{:S(2)}) collective-permute-start(bf16[2,304,128]{2,1,0:T(8,128)(2,1)S(1)} %get-tuple-element.69.refs_0_.refs_3_), channel_id=1, source_target_pairs={{0,16},{8,24},{16,0},{24,8},{1,17},{9,25},{17,1},{25,9},{2,18},{10... | collective-permute-start | bytes 466952 | tf_op jit(solution)/shard_map/ppermute | solution.py:356
  19.7 6.1 %collective-permute-start.6 = (bf16[2,304,128]{2,1,0:T(8,128)(2,1)S(1)}, bf16[2,304,128]{2,1,0:T(8,128)(2,1)S(1)}, u32[]{:S(2)}, u32[]{:S(2)}) collective-permute-start(bf16[2,304,128]{2,1,0:T(8,128)(2,1)S(1)} %get-tuple-element.68.refs_0_), channel_id=1, source_target_pairs={{0,8},{8,0},{16,24},{24,16},{1,9},{9,1},{17,25},{25,17},{2,10},{10... | collective-permute-start | bytes 466952 | tf_op jit(solution)/shard_map/ppermute | solution.py:356
  23.5 11.3 %collective-permute-start.9 = (bf16[2,2,304,128]{3,2,1,0:T(8,128)(2,1)S(1)}, bf16[2,2,304,128]{3,2,1,0:T(8,128)(2,1)S(1)}, u32[]{:S(2)}, u32[]{:S(2)}) collective-permute-start(bf16[2,2,304,128]{3,2,1,0:T(8,128)(2,1)S(1)} %stack.9), channel_id=1, source_target_pairs={{0,8},{8,0},{16,24},{24,16},{1,9},{9,1},{17,25},{25,17},{2,10},{10... | collective-permute-start | bytes 933896 | tf_op jit(solution)/shard_map/ppermute | solution.py:356
  25.8 8.9 %collective-permute-start.7 = (bf16[2,2,304,128]{3,2,1,0:T(8,128)(2,1)S(1)}, bf16[2,2,304,128]{3,2,1,0:T(8,128)(2,1)S(1)}, u32[]{:S(2)}, u32[]{:S(2)}) collective-permute-start(bf16[2,2,304,128]{3,2,1,0:T(8,128)(2,1)S(1)} %stack.8), channel_id=1, source_target_pairs={{0,16},{8,24},{16,0},{24,8},{1,17},{9,25},{17,1},{25,9},{2,18},{10... | collective-permute-start | bytes 933896 | tf_op jit(solution)/shard_map/ppermute | solution.py:356
  26.6 8.0 %collective-permute-start.5 = (bf16[4,160,128]{2,1,0:T(8,128)(2,1)S(1)}, bf16[4,160,128]{2,1,0:T(8,128)(2,1)S(1)}, u32[]{:S(2)}, u32[]{:S(2)}) collective-permute-start(bf16[4,160,128]{2,1,0:T(8,128)(2,1)S(1)} %bitcast.23), channel_id=1, source_target_pairs={{0,4},{1,5},{2,6},{3,7},{4,0},{5,1},{6,2},{7,3},{8,12},{9,13},{10,... | collective-permute-start | bytes 491528 | tf_op jit(solution)/shard_map/ppermute | solution.py:356
  35.5 3.8 %collective-permute-start.14 = (bf16[4,240,640]{2,1,0:T(8,128)(2,1)S(1)}, bf16[4,240,640]{2,1,0:T(8,128)(2,1)S(1)}, u32[]{:S(2)}, u32[]{:S(2)}) collective-permute-start(bf16[4,240,640]{2,1,0:T(8,128)(2,1)S(1)} %unpack.2.refs_1_.refs_0_), channel_id=1, source_target_pairs={{0,1},{1,0},{2,3},{3,2},{4,5},{5,4},{6,7},{7,6},{8,9},{9,8},{10,11... | collective-permute-start | bytes 3686408 | tf_op jit(solution)/shard_map/ppermute | solution.py:356
  35.6 10.1 %collective-permute-start.13 = (bf16[2,4,160,128]{3,2,1,0:T(8,128)(2,1)S(1)}, bf16[2,4,160,128]{3,2,1,0:T(8,128)(2,1)S(1)}, u32[]{:S(2)}, u32[]{:S(2)}) collective-permute-start(bf16[2,4,160,128]{3,2,1,0:T(8,128)(2,1)S(1)} %stack.7.refs_4_), channel_id=1, source_target_pairs={{0,2},{1,3},{2,0},{3,1},{4,6},{5,7},{6,4},{7,5},{8,10},{9,11},{10,... | collective-permute-start | bytes 983048 | tf_op jit(solution)/shard_map/ppermute | solution.py:356
  35.8 9.9 %collective-permute-start.12 = (bf16[4,144,128]{2,1,0:T(8,128)(2,1)S(1)}, bf16[4,144,128]{2,1,0:T(8,128)(2,1)S(1)}, u32[]{:S(2)}, u32[]{:S(2)}) collective-permute-start(bf16[4,144,128]{2,1,0:T(8,128)(2,1)S(1)} %get-tuple-element.70.refs_0_), channel_id=1, source_target_pairs={{0,24},{8,16},{16,8},{24,0},{1,25},{9,17},{17,9},{25,1},{2,26},{10... | collective-permute-start | bytes 442376 | tf_op jit(solution)/shard_map/ppermute | solution.py:356
  38.5 7.4 %collective-permute-start.11 = (bf16[4,144,128]{2,1,0:T(8,128)(2,1)S(1)}, bf16[4,144,128]{2,1,0:T(8,128)(2,1)S(1)}, u32[]{:S(2)}, u32[]{:S(2)}) collective-permute-start(bf16[4,144,128]{2,1,0:T(8,128)(2,1)S(1)} %get-tuple-element.70.refs_0_), channel_id=1, source_target_pairs={{0,16},{8,24},{16,0},{24,8},{1,17},{9,25},{17,1},{25,9},{2,18},{10... | collective-permute-start | bytes 442376 | tf_op jit(solution)/shard_map/ppermute | solution.py:356
  38.8 7.6 %collective-permute-start.10 = (bf16[4,144,128]{2,1,0:T(8,128)(2,1)S(1)}, bf16[4,144,128]{2,1,0:T(8,128)(2,1)S(1)}, u32[]{:S(2)}, u32[]{:S(2)}) collective-permute-start(bf16[4,144,128]{2,1,0:T(8,128)(2,1)S(1)} %get-tuple-element.70.refs_0_), channel_id=1, source_target_pairs={{0,8},{8,0},{16,24},{24,16},{1,9},{9,1},{17,25},{25,17},{2,10},{10... | collective-permute-start | bytes 442376 | tf_op jit(solution)/shard_map/ppermute | solution.py:356
  47.3 3.0 %collective-permute-start.15 = (bf16[4,240,640]{2,1,0:T(8,128)(2,1)S(1)}, bf16[4,240,640]{2,1,0:T(8,128)(2,1)S(1)}, u32[]{:S(2)}, u32[]{:S(2)}) collective-permute-start(bf16[4,240,640]{2,1,0:T(8,128)(2,1)S(1)} %unpack.3.refs_1_.own_ref), channel_id=1, source_target_pairs={{0,1},{1,0},{2,3},{3,2},{4,5},{5,4},{6,7},{7,6},{8,9},{9,8},{10,11... | collective-permute-start | bytes 3686408 | tf_op jit(solution)/shard_map/ppermute | solution.py:356
  58.7 3.6 %collective-permute-start.16 = (bf16[976,640]{1,0:T(8,128)(2,1)S(1)}, bf16[976,640]{1,0:T(8,128)(2,1)S(1)}, u32[]{:S(2)}, u32[]{:S(2)}) collective-permute-start(bf16[976,640]{1,0:T(8,128)(2,1)S(1)} %get-tuple-element.79.own_ref), channel_id=1, source_target_pairs={{0,1},{1,0},{2,3},{3,2},{4,5},{5,4},{6,7},{7,6},{8,9},{9,8},{10,11... | collective-permute-start | bytes 3747848 | tf_op jit(solution)/shard_map/ppermute | solution.py:356
  62.7 17.6 %collective-permute-start.24 = (bf16[512,640]{1,0:T(8,128)(2,1)S(1)}, bf16[512,640]{1,0:T(8,128)(2,1)S(1)}, u32[]{:S(2)}, u32[]{:S(2)}) collective-permute-start(bf16[512,640]{1,0:T(8,128)(2,1)S(1)} %get-tuple-element.85.refs_0_), channel_id=1, source_target_pairs={{0,2},{1,3},{2,0},{3,1},{4,6},{5,7},{6,4},{7,5},{8,10},{9,11},{10,... | collective-permute-start | bytes 1966088 | tf_op jit(solution)/shard_map/ppermute | solution.py:356
  70.5 1.7 %collective-permute-start.17 = (bf16[240,640]{1,0:T(8,128)(2,1)S(1)}, bf16[240,640]{1,0:T(8,128)(2,1)S(1)}, u32[]{:S(2)}, u32[]{:S(2)}) collective-permute-start(bf16[240,640]{1,0:T(8,128)(2,1)S(1)} %get-tuple-element.90), channel_id=1, source_target_pairs={{0,1},{1,0},{2,3},{3,2},{4,5},{5,4},{6,7},{7,6},{8,9},{9,8},{10,11... | collective-permute-start | bytes 921608 | tf_op jit(solution)/shard_map/ppermute | solution.py:356
  70.7 1.9 %collective-permute-start.18 = (bf16[240,640]{1,0:T(8,128)(2,1)S(1)}, bf16[240,640]{1,0:T(8,128)(2,1)S(1)}, u32[]{:S(2)}, u32[]{:S(2)}) collective-permute-start(bf16[240,640]{1,0:T(8,128)(2,1)S(1)} %get-tuple-element.91), channel_id=1, source_target_pairs={{0,1},{1,0},{2,3},{3,2},{4,5},{5,4},{6,7},{7,6},{8,9},{9,8},{10,11... | collective-permute-start | bytes 921608 | tf_op jit(solution)/shard_map/ppermute | solution.py:356
  71.1 2.0 %collective-permute-start.19 = (bf16[240,640]{1,0:T(8,128)(2,1)S(1)}, bf16[240,640]{1,0:T(8,128)(2,1)S(1)}, u32[]{:S(2)}, u32[]{:S(2)}) collective-permute-start(bf16[240,640]{1,0:T(8,128)(2,1)S(1)} %get-tuple-element.92), channel_id=1, source_target_pairs={{0,1},{1,0},{2,3},{3,2},{4,5},{5,4},{6,7},{7,6},{8,9},{9,8},{10,11... | collective-permute-start | bytes 921608 | tf_op jit(solution)/shard_map/ppermute | solution.py:356
  71.2 2.3 %collective-permute-start.20 = (bf16[240,640]{1,0:T(8,128)(2,1)S(1)}, bf16[240,640]{1,0:T(8,128)(2,1)S(1)}, u32[]{:S(2)}, u32[]{:S(2)}) collective-permute-start(bf16[240,640]{1,0:T(8,128)(2,1)S(1)} %get-tuple-element.93), channel_id=1, source_target_pairs={{0,1},{1,0},{2,3},{3,2},{4,5},{5,4},{6,7},{7,6},{8,9},{9,8},{10,11... | collective-permute-start | bytes 921608 | tf_op jit(solution)/shard_map/ppermute | solution.py:356
  73.8 18.6 %collective-permute-start.27 = (bf16[240,640]{1,0:T(8,128)(2,1)S(1)}, bf16[240,640]{1,0:T(8,128)(2,1)S(1)}, u32[]{:S(2)}, u32[]{:S(2)}) collective-permute-start(bf16[240,640]{1,0:T(8,128)(2,1)S(1)} %get-tuple-element.94), channel_id=1, source_target_pairs={{0,2},{1,3},{2,0},{3,1},{4,6},{5,7},{6,4},{7,5},{8,10},{9,11},{10,... | collective-permute-start | bytes 921608 | tf_op jit(solution)/shard_map/ppermute | solution.py:356
  74.6 9.2 %collective-permute-start.23 = (bf16[2,304,128]{2,1,0:T(8,128)(2,1)S(1)}, bf16[2,304,128]{2,1,0:T(8,128)(2,1)S(1)}, u32[]{:S(2)}, u32[]{:S(2)}) collective-permute-start(bf16[2,304,128]{2,1,0:T(8,128)(2,1)S(1)} %copy-done.4), channel_id=1, source_target_pairs={{0,24},{8,16},{16,8},{24,0},{1,25},{9,17},{17,9},{25,1},{2,26},{10... | collective-permute-start | bytes 466952 | tf_op jit(solution)/shard_map/ppermute | solution.py:356
  76.2 8.6 %collective-permute-start.22 = (bf16[2,304,128]{2,1,0:T(8,128)(2,1)S(1)}, bf16[2,304,128]{2,1,0:T(8,128)(2,1)S(1)}, u32[]{:S(2)}, u32[]{:S(2)}) collective-permute-start(bf16[2,304,128]{2,1,0:T(8,128)(2,1)S(1)} %copy-done.4), channel_id=1, source_target_pairs={{0,16},{8,24},{16,0},{24,8},{1,17},{9,25},{17,1},{25,9},{2,18},{10... | collective-permute-start | bytes 466952 | tf_op jit(solution)/shard_map/ppermute | solution.py:356
  77.3 7.5 %collective-permute-start.21 = (bf16[2,304,128]{2,1,0:T(8,128)(2,1)S(1)}, bf16[2,304,128]{2,1,0:T(8,128)(2,1)S(1)}, u32[]{:S(2)}, u32[]{:S(2)}) collective-permute-start(bf16[2,304,128]{2,1,0:T(8,128)(2,1)S(1)} %copy-done.4), channel_id=1, source_target_pairs={{0,8},{8,0},{16,24},{24,16},{1,9},{9,1},{17,25},{25,17},{2,10},{10... | collective-permute-start | bytes 466952 | tf_op jit(solution)/shard_map/ppermute | solution.py:356
  80.4 33.2 %collective-permute-start.25 = (bf16[304,640]{1,0:T(8,128)(2,1)S(1)}, bf16[304,640]{1,0:T(8,128)(2,1)S(1)}, u32[]{:S(2)}, u32[]{:S(2)}) collective-permute-start(bf16[304,640]{1,0:T(8,128)(2,1)S(1)} %merge.2.sent_ref), channel_id=1, source_target_pairs={{0,4},{1,5},{2,6},{3,7},{4,0},{5,1},{6,2},{7,3},{8,12},{9,13},{10,... | collective-permute-start | bytes 1167368 | tf_op jit(solution)/shard_map/ppermute | solution.py:356
  83.8 21.2 %collective-permute-start.26 = (bf16[240,640]{1,0:T(8,128)(2,1)S(1)}, bf16[240,640]{1,0:T(8,128)(2,1)S(1)}, u32[]{:S(2)}, u32[]{:S(2)}) collective-permute-start(bf16[240,640]{1,0:T(8,128)(2,1)S(1)} %get-tuple-element.101), channel_id=1, source_target_pairs={{0,2},{1,3},{2,0},{3,1},{4,6},{5,7},{6,4},{7,5},{8,10},{9,11},{10,... | collective-permute-start | bytes 921608 | tf_op jit(solution)/shard_map/ppermute | solution.py:356
  92.5 21.1 %collective-permute-start.28 = (bf16[240,640]{1,0:T(8,128)(2,1)S(1)}, bf16[240,640]{1,0:T(8,128)(2,1)S(1)}, u32[]{:S(2)}, u32[]{:S(2)}) collective-permute-start(bf16[240,640]{1,0:T(8,128)(2,1)S(1)} %merge.3), channel_id=1, source_target_pairs={{0,4},{1,5},{2,6},{3,7},{4,0},{5,1},{6,2},{7,3},{8,12},{9,13},{10,... | collective-permute-start | bytes 921608 | tf_op jit(solution)/shard_map/ppermute | solution.py:356
  (4 other events, 17.5 us)

commit v7 on v6

--- a/solution.py
+++ b/solution.py
@@ -260,12 +260,19 @@
 
 
 FACTOR_ROWS = 16
+MEMBER_ROWS = 4
 
 
 def split_rows(row):
     high = row.astype(BF16).astype(F32)
-    middle = (row - high).astype(BF16).astype(F32)
-    return [high, middle, row - high - middle]
+    return [high, row - high]
+
+
+def join_factors(first, second, count):
+    rest = jnp.zeros((FACTOR_ROWS - 2 * count, first.shape[1]), F32)
+    rows = [first.astype(F32)[0:count], second.astype(F32)[0:count]]
+    rows += [rest] if rest.shape[0] else []
+    return jnp.concatenate(rows, axis=0).astype(BF16)
 
 
 def grad_kernel(points, scale, block, centred, me_ref, act_ref, cotangent_ref, *refs):
@@ -289,8 +296,7 @@
             cotangent_ref[pl.ds(points, rows)],
             preferred_element_type=F32,
         )
-        factors = split_rows(mean.T[0:1]) + split_rows(sums[0:1])
-        factors += [jnp.zeros((FACTOR_ROWS - len(factors), channels), F32)]
+        factors = [mean.T[0:1], sums[0:1], jnp.zeros((FACTOR_ROWS - 2, channels), F32)]
         factors = jnp.concatenate(factors, axis=0)
         common = jnp.concatenate([mean] * (channels // 128), axis=1) * sums[0:1]
 
@@ -310,17 +316,89 @@
         for j in range(count):
             away = pl.multiple_of((me ^ (2 * j + 1)) * block, 16)
             home = pl.multiple_of((me ^ (2 * j)) * block, 16)
-            part = total_ref[pl.ds(away, block)].astype(BF16)
-            if centred:
-                away_refs[0][j * block : (j + 1) * block] = part
-            else:
-                away_refs[j][...] = part
+            away_refs[j][...] = total_ref[pl.ds(away, block)].astype(BF16)
             home_ref[j] = total_ref[pl.ds(home, block)]
 
-        if centred:
-            away_refs[0][count * block :] = factors.astype(BF16)
     elif centred:
         refs[0][...] = factors
+
+
+def mean_and_sums(scale, turned, cotangent):
+    rows = turned.shape[1]
+    mean = jnp.dot(turned, jnp.ones((rows, 128), BF16), preferred_element_type=F32) * (1.0 / rows)
+    sums = jnp.dot(jnp.ones((16, rows), BF16), cotangent, preferred_element_type=F32)
+    return mean, scale * sums[0:8]
+
+
+def half_kernel(points, scale, odd, me_ref, turned_ref, cotangent_ref, *refs):
+    refs, total_ref = refs[:-1], refs[-1]
+    channels, rows = turned_ref.shape
+    if odd:
+        away_ref, home_ref, mean_ref, sums_ref = refs
+        mean, sums = mean_and_sums(scale, turned_ref[...], cotangent_ref[pl.ds(points, rows)])
+        mean_ref[...] = mean
+        sums_ref[...] = sums
+        factors = split_rows(mean.T[0:1]) + split_rows(sums[0:1])
+        factors += [jnp.zeros((FACTOR_ROWS - MEMBER_ROWS, channels), F32)]
+    else:
+        mean_ref, sums_ref, away_ref, home_ref = refs
+    size, block = total_ref.shape[0] // 2, home_ref.shape[1]
+    chip = lax.shift_right_logical(me_ref[0], 1)
+    for first in range(2):
+
+        @pl.when(((chip & 1) ^ odd) == first)
+        def _():
+            for i, start in enumerate((first * size, (first + 2) * size)):
+                row = start
+                while row < start + size:
+                    t, low = divmod(row, channels)
+                    high = min(channels, low + start + size - row)
+                    shift = (2 - t) * points
+                    product = scale * jnp.dot(
+                        turned_ref[low:high],
+                        cotangent_ref[shift : shift + rows],
+                        preferred_element_type=F32,
+                    )
+                    common = jnp.concatenate([mean_ref[low:high]] * (channels // 128), axis=1)
+                    place = i * size + row - start
+                    total_ref[place : place + high - low] = product - common * sums_ref[0:1]
+                    row += high - low
+
+    for k, top in enumerate((1, 0)):
+        start = (lax.shift_right_logical(chip, 1) ^ top) * size
+        for ref, core in ((away_ref, 1 - (me_ref[0] & 1)), (home_ref, me_ref[0] & 1)):
+            part = total_ref[pl.ds(pl.multiple_of(start + core * block, 16), block)]
+            if ref is home_ref:
+                home_ref[k] = part
+            else:
+                away_ref[k * block : (k + 1) * block] = part.astype(BF16)
+    if odd:
+        away_ref[2 * block :] = jnp.concatenate(factors, axis=0).astype(BF16)
+
+
+def odd_half(turned, cotangent, me, block, points, scale):
+    channels = turned.shape[0]
+    return call(
+        functools.partial(half_kernel, points, scale, 1),
+        [
+            ((2 * block + FACTOR_ROWS, channels), BF16),
+            ((2, block, channels), F32),
+            ((channels, 128), F32),
+            ((8, channels), F32),
+        ],
+        [pltpu.VMEM((4 * block, channels), F32)],
+        "gradient_odd", smem(1) + vmem(2), 20,
+    )(me, turned, cotangent)
+
+
+def even_half(turned, cotangent, me, block, points, scale, mean, sums):
+    channels = turned.shape[0]
+    return call(
+        functools.partial(half_kernel, points, scale, 0),
+        [((2 * block, channels), BF16), ((2, block, channels), F32)],
+        [pltpu.VMEM((4 * block, channels), F32)],
+        "gradient_even", smem(1) + vmem(4), 20,
+    )(me, turned, cotangent, mean, sums)
 
 
 def gradient(act, cotangent, me, n_member, points, scale, centred):
@@ -328,11 +406,9 @@
     turned = pltpu.VMEM((channels, rows), BF16)
     block = 3 * channels // n_member
     specs = smem(1) + vmem(2)
-    if block % 16 == 0:
+    if block % 16 == 0 and not centred:
         chips = n_member // 2
         away = [((block, channels), BF16)] * chips
-        if centred:
-            away = [((chips * block + FACTOR_ROWS, channels), BF16)]
         home, *away = call(
             functools.partial(grad_kernel, points, scale, block, centred),
             [((chips, block, channels), F32)] + away,
@@ -577,31 +653,18 @@
         bit *= 2
 
 
-def pair_kernel(own_ref, home_ref, received_ref, away_ref, middle_ref, kept_ref):
+def pair_kernel(own_ref, home_ref, received_ref, away_ref):
     rows = home_ref.shape[1]
-
-    def total(k):
-        return home_ref[k] + received_ref[k * rows : (k + 1) * rows].astype(F32)
-
-    away_ref[0:rows] = total(3).astype(BF16)
-    away_ref[rows : 2 * rows] = total(1).astype(BF16)
-    middle_ref[...] = total(2)
-    kept_ref[...] = total(0)
-    last = home_ref.shape[0] * rows
-    if away_ref.shape[0] > 2 * rows:
-        away_ref[2 * rows : 2 * rows + FACTOR_ROWS] = own_ref[last:]
-        away_ref[2 * rows + FACTOR_ROWS :] = received_ref[last:]
+    for k in range(2):
+        here = slice(k * rows, (k + 1) * rows)
+        away_ref[here] = (home_ref[k] + received_ref[here].astype(F32)).astype(BF16)
+    away_ref[2 * rows :] = join_factors(
+        own_ref[2 * rows :], received_ref[2 * rows :], MEMBER_ROWS
+    )
 
 
 def pair_sums(own, home, received):
-    chips, rows, channels = home.shape
-    shape = (rows, channels)
-    extra = 2 * (own.shape[0] - chips * rows)
-    return call(
-        pair_kernel,
-        [((2 * rows + extra, channels), BF16), (shape, F32), (shape, F32)], [],
-        "pair", vmem(3), 12,
-    )(own, home, received)
+    return call(pair_kernel, [(own.shape, BF16)], [], "pair", vmem(3), 12)(own, home, received)[0]
 
 
 def parts_kernel(home_ref, *refs):
@@ -618,22 +681,28 @@
     )(home, *received)
 
 
-def merge_kernel(middle_ref, *refs):
-    *sent_refs, received_ref, out_ref = refs
-    rows = middle_ref.shape[0]
-    out_ref[0:rows] = (middle_ref[...] + received_ref[0:rows].astype(F32)).astype(BF16)
-    for sent_ref in sent_refs:
-        known = sent_ref.shape[0] - 2 * rows
-        out_ref[rows : rows + known] = sent_ref[2 * rows :]
-        out_ref[rows + known :] = received_ref[2 * rows :]
-
-
-def merge(middle, received, *sent):
-    rows, channels = middle.shape
-    known = [part.shape[0] - 2 * rows for part in sent]
-    shape = (rows + 2 * sum(known), channels)
-    operands = (middle,) + sent + (received,)
-    return call(merge_kernel, [(shape, BF16)], [], "merge", vmem(len(operands)))(*operands)[0]
+def merge_kernel(middle_ref, received_ref, out_ref):
+    out_ref[...] = (middle_ref[...] + received_ref[...].astype(F32)).astype(BF16)
+
+
+def merge(middle, received):
+    return call(merge_kernel, [(middle.shape, BF16)], [], "merge", vmem(2))(middle, received)[0]
+
+
+def merge_factors_kernel(home_ref, pair_ref, sent_ref, received_ref, out_ref):
+    rows = home_ref.shape[1]
+    total = home_ref[0] + pair_ref[0:rows].astype(F32) + received_ref[0:rows].astype(F32)
+    out_ref[0:rows] = total.astype(BF16)
+    out_ref[rows:] = join_factors(
+        sent_ref[2 * rows :], received_ref[2 * rows :], 2 * MEMBER_ROWS
+    )
+
+
+def merge_factors(home, pair, sent, received):
+    shape = (home.shape[1] + FACTOR_ROWS, home.shape[2])
+    return call(merge_factors_kernel, [(shape, BF16)], [], "merge", vmem(4))(
+        home, pair, sent, received
+    )[0]
 
 
 def update_kernel(own_ref, rate_ref, *refs):
@@ -643,20 +712,18 @@
     refs[-1][...] = own_ref[0].astype(F32) - rate_ref[...].astype(F32) * total
 
 
-def both_kernel(
-    me_ref, own_ref, rate_ref, kept_ref, half_ref, sent_ref, received_ref, *refs
+def common_update_kernel(
+    me_ref, own_ref, rate_ref, home_ref, pair_ref, half_ref, sent_ref, received_ref, out_ref
 ):
-    *first_refs, first_out, out_ref = refs
-    update_kernel(*first_refs, first_out)
     rows, channels = rate_ref.shape
-    total = kept_ref[...] + half_ref[rows : 2 * rows].astype(F32)
-    total = total + received_ref[0:rows].astype(F32)
+    total = home_ref[1] + pair_ref[rows : 2 * rows].astype(F32)
+    total = total + half_ref[rows : 2 * rows].astype(F32) + received_ref[0:rows].astype(F32)
     means, sums = [], []
     for ref in (sent_ref, received_ref):
-        for start in range(rows, ref.shape[0], FACTOR_ROWS):
-            parts = ref[start : start + FACTOR_ROWS].astype(F32)
-            means.append(parts[0:1] + parts[1:2] + parts[2:3])
-            sums.append(parts[3:4] + parts[4:5] + parts[5:6])
+        parts = ref[rows:].astype(F32)
+        for start in range(0, FACTOR_ROWS, MEMBER_ROWS):
+            means.append(parts[start : start + 1] + parts[start + 1 : start + 2])
+            sums.append(parts[start + 2 : start + 3] + parts[start + 3 : start + 4])
     means, sums = jnp.concatenate(means, axis=0), jnp.concatenate(sums, axis=0)
     means = jnp.concatenate([means] * 3, axis=1)
     for member in range(3 * channels // rows):
@@ -673,12 +740,10 @@
             out_ref[...] = own_ref[0].astype(F32) - rate_ref[...].astype(F32) * (total + common)
 
 
-def update_both(me, second_terms, first_terms):
-    terms = second_terms + first_terms
-    shape = (second_terms[1].shape, F32)
+def common_update(me, own, rate, *terms):
     return call(
-        both_kernel, [shape, shape], [], "update", smem(1) + vmem(len(terms)), 16
-    )(me, *terms)
+        common_update_kernel, [(rate.shape, F32)], [], "update", smem(1) + vmem(7), 12
+    )(me, own, rate, *terms)[0]
 
 
 def update(own, rate, *terms):
@@ -689,10 +754,8 @@
 
 
 def common_term(every, me, own_rows):
-    every = every.astype(F32)
-    mean = every[:, 0] + every[:, 1] + every[:, 2]
-    sums = every[:, 3] + every[:, 4] + every[:, 5]
-    mean = jnp.concatenate([mean] * 3, axis=1)
+    sums = every[:, 1]
+    mean = jnp.concatenate([every[:, 0]] * 3, axis=1)
     mean = lax.dynamic_slice_in_dim(mean, me[0] * own_rows, own_rows, 1)
     return lax.dot_general(
         mean, sums, (((0,), (0,)), ((), ())), precision=lax.Precision.HIGHEST
@@ -771,20 +834,26 @@
         [pltpu.VMEM((rows, channels), BF16)] * 2 + [pltpu.SemaphoreType.DMA((2,))],
         "conv_error", vmem(1) + hbm(2) + weight_specs(weight_two), 24,
     )(act_two, clip, target, *weight_two)
-    (away_two,), home_two, factors = gradient(
-        turned_two, error, me, n_member, points, scale, True
-    )
-    received_two = swap(away_two, "member", n_member, 1)
+    staged = n_member == 8 and own_rows % 16 == 0
+    if staged:
+        away_two, home_two, *means = odd_half(turned_two, error, me, own_rows, points, scale)
+        received_two = swap(away_two, "member", n_member, 1)
+        away_even, home_even = even_half(
+            turned_two, error, me, own_rows, points, scale, *means
+        )
+        received_even = swap(away_even, "member", n_member, 1)
+        half_two = pair_sums(away_two, home_two, order_after(received_two, away_even))
+        from_two = swap(half_two, "member", n_member, 2)
+        error = order_after(error, half_two)
+    else:
+        (away_two,), home_two, factors = gradient(
+            turned_two, error, me, n_member, points, scale, True
+        )
+        received_two = swap(away_two, "member", n_member, 1)
     (grad_act,) = call(
         functools.partial(back_kernel, points, scale),
         [((rows, channels), F32)], [], "back", vmem(2), 20,
-    )(order_after(error, away_two), full_two)
-    staged = n_member == 8 and factors is None
-    received_two, grad_act = lax.optimization_barrier((received_two, grad_act))
-    if staged:
-        half_two, middle_two, kept_two = pair_sums(away_two, home_two, received_two)
-        from_two = swap(half_two, "member", n_member, 2)
-        grad_act = order_after(grad_act, half_two)
+    )(error, full_two)
     (grad_hidden,) = call(
         functools.partial(norm_back_kernel, points),
         [((padded, channels), BF16)],
@@ -800,19 +869,22 @@
     )
     received_one = [swap(part, "member", n_member, 1) for part in away_one]
     if staged:
+        received_one, from_two = order_after((received_one, from_two), ())
         far_one, near_one, middle_one, kept_one = pair_parts(home_one, received_one)
         from_one = swap(far_one, "member", n_member, 2)
         beside_one = swap(near_one, "member", n_member, 2)
-        merged_two = merge(middle_two, from_two, half_two)
+        merged_two = merge_factors(home_even, received_even, half_two, from_two)
         across_two = swap(merged_two, "member", n_member, 4)
         rate_one, rate_two = rates(far_one)
         middle_one = order_after(middle_one, (rate_one, rate_two))
-        across_one = swap(merge(middle_one, from_one), "member", n_member, 4)
-        adapted_one, adapted_two = update_both(
-            me,
-            (own_two, rate_two, kept_two, from_two, merged_two, across_two),
-            (own_one, rate_one, kept_one, beside_one, across_one),
+        merged_one = merge(middle_one, from_one)
+        across_one = swap(merged_one, "member", n_member, 4)
+        adapted_two = common_update(
+            me, own_two, rate_two, home_even, received_even, from_two, merged_two,
+            order_after(across_two, merged_one),
         )
+        kept_one, adapted_two = order_after((kept_one, adapted_two), ())
+        adapted_one = update(own_one, rate_one, kept_one, beside_one, across_one)
     else:
         rate_one, rate_two = rates(away_one)
         every = lax.all_gather(factors, "member")

time: 116 us -> 112 us (0.966)
  waiting for transfers between devices: 47.1 us -> 41.3 us
  starting transfers between devices: 31.2 us -> 32.6 us
    ppermute x29 -> x30, waiting for transfers between devices: 47.1 us -> 41.3 us  [swap(): return lax.ppermute(value, axis, [(i, i ^ offset) for i in range(size)])]
    pallas_call x4 -> x7, Pallas kernels: 2.6 us -> 7.67 us  [the longest x1 2.49 us: odd_half(): call(functools.partial(half_kernel, points, scale, 1), [((2 * block + FAC...]
    pallas_call x2 -> x1, Pallas kernels: 9.02 us -> 4.49 us  [gradient(): call(functools.partial(grad_kernel, points, scale, block, centred), [((ch...]
    ppermute x29 -> x30, starting transfers between devices: 31.2 us -> 32.6 us  [swap(): return lax.ppermute(value, axis, [(i, i ^ offset) for i in range(size)])]
  transfers between devices with their start and end apart: 29 -> 30, of which waited for: 17 -> 17; matrix products, arithmetic and copies ran while one was open for 1% -> 1% of each run, Pallas kernels for 16% -> 20%
where the time goes in v7:
time: 112 us
  waiting for transfers between devices  41.3 us (37%)
  Pallas kernels  34 us (30%)
  starting transfers between devices  32.6 us (29%)
  between operations  2.26 us (2%)
  matrix products  1.53 us (1%)
    ppermute x30, waiting for transfers between devices, swap(): return lax.ppermute(value, axis, [(i, i ^ offset) for i in range(size)])  41.3 us
    ppermute x30, starting transfers between devices, swap(): return lax.ppermute(value, axis, [(i, i ^ offset) for i in range(size)])  32.6 us
    pallas_call x1, Pallas kernels, gradient(): call(functools.partial(grad_kernel, points, scale, block, centred), [((ch...  4.49 us
    pallas_call x1, Pallas kernels, shards(): call(functools.partial(second_kernel, points, scale), [((padded, channels...  3.86 us
    pallas_call x1, Pallas kernels, shards(): call(functools.partial(back_kernel, points, scale), [((rows, channels), F...  3.43 us
    pallas_call x1, Pallas kernels, shards(): call(functools.partial(first_kernel, points, scale), [((rows, channels),...  3.37 us
    pallas_call x1, Pallas kernels, odd_half(): call(functools.partial(half_kernel, points, scale, 1), [((2 * block + FAC...  2.49 us
    pallas_call x1, Pallas kernels, weights_and_rates(): pl.pallas_call(pack_kernel, out_shape=(jax.ShapeDtypeStruct((size + cut,...  2.39 us
  transfers between devices with their start and end apart: 30, of which 17 were waited for; matrix products, arithmetic and copies ran while one was open for 1% of the time, Pallas kernels for 20%

profile of v7, /device:TPU:0, one launch (start us, length us, event | category | flops | bytes accessed | tf_op | source)
XLA Modules:
  0.0 111.8 jit_solution(822075884559681621)
XLA Ops:
  0.7 2.4 %pack.1 = (bf16[448,128]{1,0:T(8,128)(2,1)}, bf16[160,128]{1,0:T(8,128)(2,1)}, bf16[2,304,128]{2,1,0:T(8,128)(2,1)}) custom-call(bf16[160,240]{1,0:T(8,128)(2,1)} %bitcast.27, bf16[160,240]{1,0:T(8,128)(2,1)} %bitcast.28, bf16[160,240]{1,0:T(8,128)(2,1)} %bitcast.29, bf16[160,240]{1,0:T(8,128)(2,1)} %bitcast.30, s32[1]{0:T(128)} %bitcast.refs_4_.group_ref, ...), custom_call_target="tpu_custom_call" | custom-call | bytes 1024 | tf_op jit(solution)/shard_map/pack/pallas_call | solution.py:571
  3.1 3.1 %collective-permute-start = (bf16[448,128]{1,0:T(8,128)(2,1)}, bf16[448,128]{1,0:T(8,128)(2,1)S(1)}, u32[]{:S(2)}, u32[]{:S(2)}) collective-permute-start(bf16[448,128]{1,0:T(8,128)(2,1)} %get-tuple-element.64.refs_0_), channel_id=1, source_target_pairs={{0,2},{1,3},{2,0},{3,1},{4,6},{5,7},{6,4},{7,5},{8,10},{9,11},{10,... | collective-permute-start | bytes 344072 | tf_op jit(solution)/shard_map/ppermute | solution.py:432
  6.2 2.6 %collective-permute-start.1 = (bf16[448,128]{1,0:T(8,128)(2,1)}, bf16[448,128]{1,0:T(8,128)(2,1)S(1)}, u32[]{:S(2)}, u32[]{:S(2)}) collective-permute-start(bf16[448,128]{1,0:T(8,128)(2,1)} %get-tuple-element.64.refs_0_), channel_id=1, source_target_pairs={{0,4},{1,5},{2,6},{3,7},{4,0},{5,1},{6,2},{7,3},{8,12},{9,13},{10,... | collective-permute-start | bytes 344072 | tf_op jit(solution)/shard_map/ppermute | solution.py:432
  8.8 1.7 %collective-permute-start.3 = (bf16[160,128]{1,0:T(8,128)(2,1)}, bf16[160,128]{1,0:T(8,128)(2,1)S(1)}, u32[]{:S(2)}, u32[]{:S(2)}) collective-permute-start(bf16[160,128]{1,0:T(8,128)(2,1)} %get-tuple-element.60.refs_0_), channel_id=1, source_target_pairs={{0,8},{8,0},{16,24},{24,16},{1,9},{9,1},{17,25},{25,17},{2,10},{10... | collective-permute-start | bytes 122888 | tf_op jit(solution)/shard_map/ppermute | solution.py:432
  13.5 1.6 %collective-permute-start.4 = (bf16[2,160,128]{2,1,0:T(8,128)(2,1)S(1)}, bf16[2,160,128]{2,1,0:T(8,128)(2,1)S(1)}, u32[]{:S(2)}, u32[]{:S(2)}) collective-permute-start(bf16[2,160,128]{2,1,0:T(8,128)(2,1)S(1)} %stack.5.refs_0_), channel_id=1, source_target_pairs={{0,16},{8,24},{16,0},{24,8},{1,17},{9,25},{17,1},{25,9},{2,18},{10... | collective-permute-start | bytes 245768 | tf_op jit(solution)/shard_map/ppermute | solution.py:432
  15.0 2.2 %enter.1.in_ref.act_ref = bf16[1024,640]{1,0:T(8,128)(2,1)S(1)} custom-call(bf16[896,640]{1,0:T(8,128)(2,1)S(1)} %bitcast.20, bf16[640,640]{1,0:T(8,128)(2,1)S(1)} %copy-done.1), custom_call_target="tpu_custom_call" | custom-call | bytes 1024 | tf_op jit(solution)/shard_map/enter/pallas_call | solution.py:792
  18.1 1.6 %collective-permute-start.8 = (bf16[2,304,128]{2,1,0:T(8,128)(2,1)S(1)}, bf16[2,304,128]{2,1,0:T(8,128)(2,1)S(1)}, u32[]{:S(2)}, u32[]{:S(2)}) collective-permute-start(bf16[2,304,128]{2,1,0:T(8,128)(2,1)S(1)} %get-tuple-element.73.refs_0_.refs_3_), channel_id=1, source_target_pairs={{0,16},{8,24},{16,0},{24,8},{1,17},{9,25},{17,1},{25,9},{2,18},{10... | collective-permute-start | bytes 466952 | tf_op jit(solution)/shard_map/ppermute | solution.py:432
  19.7 1.5 %collective-permute-start.6 = (bf16[2,304,128]{2,1,0:T(8,128)(2,1)S(1)}, bf16[2,304,128]{2,1,0:T(8,128)(2,1)S(1)}, u32[]{:S(2)}, u32[]{:S(2)}) collective-permute-start(bf16[2,304,128]{2,1,0:T(8,128)(2,1)S(1)} %get-tuple-element.72.refs_0_), channel_id=1, source_target_pairs={{0,8},{8,0},{16,24},{24,16},{1,9},{9,1},{17,25},{25,17},{2,10},{10... | collective-permute-start | bytes 466952 | tf_op jit(solution)/shard_map/ppermute | solution.py:432
  21.2 2.2 %collective-permute-done.8.refs_1_.refs_4_ = bf16[2,304,128]{2,1,0:T(8,128)(2,1)S(1)} collective-permute-done((bf16[2,304,128]{2,1,0:T(8,128)(2,1)S(1)}, bf16[2,304,128]{2,1,0:T(8,128)(2,1)S(1)}, u32[]{:S(2)}, u32[]{:S(2)}) %collective-permute-start.8) | collective-permute-done | bytes 155680 | tf_op jit(solution)/shard_map/ppermute | solution.py:432
  23.5 1.6 %collective-permute-start.9 = (bf16[2,2,304,128]{3,2,1,0:T(8,128)(2,1)S(1)}, bf16[2,2,304,128]{3,2,1,0:T(8,128)(2,1)S(1)}, u32[]{:S(2)}, u32[]{:S(2)}) collective-permute-start(bf16[2,2,304,128]{3,2,1,0:T(8,128)(2,1)S(1)} %stack.9), channel_id=1, source_target_pairs={{0,8},{8,0},{16,24},{24,16},{1,9},{9,1},{17,25},{25,17},{2,10},{10... | collective-permute-start | bytes 933896 | tf_op jit(solution)/shard_map/ppermute | solution.py:432
  25.0 1.5 %collective-permute-done.6.refs_1_ = bf16[2,304,128]{2,1,0:T(8,128)(2,1)S(1)} collective-permute-done((bf16[2,304,128]{2,1,0:T(8,128)(2,1)S(1)}, bf16[2,304,128]{2,1,0:T(8,128)(2,1)S(1)}, u32[]{:S(2)}, u32[]{:S(2)}) %collective-permute-start.6) | collective-permute-done | bytes 155680 | tf_op jit(solution)/shard_map/ppermute | solution.py:432
  27.0 2.5 %collective-permute-start.5 = (bf16[4,160,128]{2,1,0:T(8,128)(2,1)S(1)}, bf16[4,160,128]{2,1,0:T(8,128)(2,1)S(1)}, u32[]{:S(2)}, u32[]{:S(2)}) collective-permute-start(bf16[4,160,128]{2,1,0:T(8,128)(2,1)S(1)} %bitcast.23), channel_id=1, source_target_pairs={{0,4},{1,5},{2,6},{3,7},{4,0},{5,1},{6,2},{7,3},{8,12},{9,13},{10,... | collective-permute-start | bytes 491528 | tf_op jit(solution)/shard_map/ppermute | solution.py:432
  29.5 5.5 %collective-permute-done.5.refs_1_ = bf16[4,160,128]{2,1,0:T(8,128)(2,1)S(1)} collective-permute-done((bf16[4,160,128]{2,1,0:T(8,128)(2,1)S(1)}, bf16[4,160,128]{2,1,0:T(8,128)(2,1)S(1)}, u32[]{:S(2)}, u32[]{:S(2)}) %collective-permute-start.5) | collective-permute-done | bytes 163872 | tf_op jit(solution)/shard_map/ppermute | solution.py:432
  37.8 2.0 %collective-permute-start.12 = (bf16[4,144,128]{2,1,0:T(8,128)(2,1)S(1)}, bf16[4,144,128]{2,1,0:T(8,128)(2,1)S(1)}, u32[]{:S(2)}, u32[]{:S(2)}) collective-permute-start(bf16[4,144,128]{2,1,0:T(8,128)(2,1)S(1)} %get-tuple-element.77.refs_0_), channel_id=1, source_target_pairs={{0,16},{8,24},{16,0},{24,8},{1,17},{9,25},{17,1},{25,9},{2,18},{10... | collective-permute-start | bytes 442376 | tf_op jit(solution)/shard_map/ppermute | solution.py:432
  39.9 3.4 %conv.1.hidden_ref = f32[896,640]{1,0:T(8,128)S(1)} custom-call(bf16[1024,640]{1,0:T(8,128)(2,1)S(1)} %enter.1.in_ref.act_ref, f32[1,640]{1,0:T(1,128)S(1)} %fusion.6.bias_ref, s32[1]{0:T(128)} %bitcast.5.refs_5_.refs_0_.me_ref, bf16[4,240,640]{2,1,0:T(8,128)(2,1)S(1)} %unpack.2.refs_1_.own_ref, bf16[4,240,640]{2,1,0:T(8,128)(2,1)S(1)} %collective-permute-done.10.refs_2_), custom_call_target="tpu_custom_call" | custom-call | bytes 1024 | tf_op jit(solution)/shard_map/conv/pallas_call | solution.py:810
  43.3 2.8 %collective-permute-done.14.refs_5_ = bf16[2,4,160,128]{3,2,1,0:T(8,128)(2,1)S(1)} collective-permute-done((bf16[2,4,160,128]{3,2,1,0:T(8,128)(2,1)S(1)}, bf16[2,4,160,128]{3,2,1,0:T(8,128)(2,1)S(1)}, u32[]{:S(2)}, u32[]{:S(2)}) %collective-permute-start.14) | collective-permute-done | bytes 327712 | tf_op jit(solution)/shard_map/ppermute | solution.py:432
  47.7 2.3 %norm.1 = (f32[896,640]{1,0:T(8,128)S(1)}, f32[1,640]{1,0:T(1,128)S(1)}, bf16[1024,640]{1,0:T(8,128)(2,1)S(1)}, bf16[640,896]{1,0:T(8,128)(2,1)S(1)}) custom-call(f32[896,640]{1,0:T(8,128)S(1)} %conv.1.hidden_ref, bf16[640,640]{1,0:T(8,128)(2,1)S(1)} %copy-done.1), custom_call_target="tpu_custom_call" | custom-call | bytes 1024 | tf_op jit(solution)/shard_map/norm/pallas_call | solution.py:820
  50.6 3.9 %conv_error.1 = (bf16[1024,640]{1,0:T(8,128)(2,1)S(1)}, bf16[1920,640]{1,0:T(8,128)(2,1)S(1)}) custom-call(bf16[1024,640]{1,0:T(8,128)(2,1)S(1)} %get-tuple-element.81.in_ref, bf16[896,640]{1,0:T(8,128)(2,1)S(1)} %bitcast.21, bf16[896,640]{1,0:T(8,128)(2,1)S(1)} %bitcast.22, s32[1]{0:T(128)} %bitcast.5.refs_5_.refs_0_.me_ref, ...), custom_call_target="tpu_custom_call" | custom-call | bytes 1024 | tf_op jit(solution)/shard_map/conv_error/pallas_call | solution.py:831
  54.5 2.5 %gradient_odd.1 = (bf16[496,640]{1,0:T(8,128)(2,1)S(1)}, f32[2,240,640]{2,1,0:T(8,128)S(1)}, f32[640,128]{1,0:T(8,128)S(1)}, f32[8,640]{1,0:T(8,128)S(1)}) custom-call(s32[1]{0:T(128)} %bitcast.5.refs_5_.refs_0_.me_ref, bf16[640,896]{1,0:T(8,128)(2,1)S(1)} %get-tuple-element.83.turned_ref, bf16[1024,640]{1,0:T(8,128)(2,1)S(1)} %get-tuple-element.90.cotangent_ref.error_ref), custom_call_target="tpu_custom_call" | custom-call | bytes 1024 | tf_op jit(solution)/shard_map/gradient_odd/pallas_call | solution.py:381
  57.1 2.0 %gradient_even.1 = (bf16[480,640]{1,0:T(8,128)(2,1)S(1)}, f32[2,240,640]{2,1,0:T(8,128)S(1)}) custom-call(s32[1]{0:T(128)} %bitcast.5.refs_5_.refs_0_.me_ref, bf16[640,896]{1,0:T(8,128)(2,1)S(1)} %get-tuple-element.83.turned_ref, bf16[1024,640]{1,0:T(8,128)(2,1)S(1)} %get-tuple-element.90.cotangent_ref.error_ref, f32[640,128]{1,0:T(8,128)S(1)} %get-tuple-element.86.refs_0_, ...), custom_call_target="tpu_custom_call" | custom-call | bytes 1024 | tf_op jit(solution)/shard_map/gradient_even/pallas_call | solution.py:396
  59.3 1.4 %collective-permute-start.21 = (bf16[496,640]{1,0:T(8,128)(2,1)S(1)}, bf16[496,640]{1,0:T(8,128)(2,1)S(1)}, u32[]{:S(2)}, u32[]{:S(2)}) collective-permute-start(bf16[496,640]{1,0:T(8,128)(2,1)S(1)} %pair.2.sent_ref), channel_id=1, source_target_pairs={{0,2},{1,3},{2,0},{3,1},{4,6},{5,7},{6,4},{7,5},{8,10},{9,11},{10,... | collective-permute-start | bytes 1904648 | tf_op jit(solution)/shard_map/ppermute | solution.py:432
  60.7 3.4 %back.1.act_grad_ref = f32[896,640]{1,0:T(8,128)S(1)} custom-call(bf16[1024,640]{1,0:T(8,128)(2,1)S(1)} %get-tuple-element.90.cotangent_ref.error_ref, bf16[1920,640]{1,0:T(8,128)(2,1)S(1)} %get-tuple-element.91.weight_ref), custom_call_target="tpu_custom_call" | custom-call | bytes 1024 | tf_op jit(solution)/shard_map/back/pallas_call | solution.py:853
  64.2 2.1 %norm_back.1.cotangent_ref = bf16[1024,640]{1,0:T(8,128)(2,1)S(1)} custom-call(f32[896,640]{1,0:T(8,128)S(1)} %back.1.act_grad_ref, f32[896,640]{1,0:T(8,128)S(1)} %get-tuple-element.92.normal_ref, f32[1,640]{1,0:T(1,128)S(1)} %get-tuple-element.93.inverse_ref, bf16[640,640]{1,0:T(8,128)(2,1)S(1)} %copy-done.1), custom_call_target="tpu_custom_call" | custom-call | bytes 1024 | tf_op jit(solution)/shard_map/norm_back/pallas_call | solution.py:857
  66.2 4.5 %gradient.1 = (f32[4,240,640]{2,1,0:T(8,128)S(1)}, bf16[240,640]{1,0:T(8,128)(2,1)S(1)}, bf16[240,640]{1,0:T(8,128)(2,1)S(1)}, bf16[240,640]{1,0:T(8,128)(2,1)S(1)}, bf16[240,640]{1,0:T(8,128)(2,1)S(1)}) custom-call(s32[1]{0:T(128)} %bitcast.5.refs_5_.refs_0_.me_ref, bf16[1024,640]{1,0:T(8,128)(2,1)S(1)} %enter.1.in_ref.act_ref, ...), custom_call_target="tpu_custom_call" | custom-call | bytes 1024 | tf_op jit(solution)/shard_map/gradient/pallas_call | solution.py:412
  77.6 1.4 %collective-permute-start.22 = (bf16[2,304,128]{2,1,0:T(8,128)(2,1)S(1)}, bf16[2,304,128]{2,1,0:T(8,128)(2,1)S(1)}, u32[]{:S(2)}, u32[]{:S(2)}) collective-permute-start(bf16[2,304,128]{2,1,0:T(8,128)(2,1)S(1)} %copy-done.4), channel_id=1, source_target_pairs={{0,8},{8,0},{16,24},{24,16},{1,9},{9,1},{17,25},{25,17},{2,10},{10... | collective-permute-start | bytes 466952 | tf_op jit(solution)/shard_map/ppermute | solution.py:432
  81.2 2.7 %collective-permute-start.26 = (bf16[256,640]{1,0:T(8,128)(2,1)S(1)}, bf16[256,640]{1,0:T(8,128)(2,1)S(1)}, u32[]{:S(2)}, u32[]{:S(2)}) collective-permute-start(bf16[256,640]{1,0:T(8,128)(2,1)S(1)} %merge.2.sent_ref), channel_id=1, source_target_pairs={{0,4},{1,5},{2,6},{3,7},{4,0},{5,1},{6,2},{7,3},{8,12},{9,13},{10,... | collective-permute-start | bytes 983048 | tf_op jit(solution)/shard_map/ppermute | solution.py:432
  83.9 1.4 %collective-permute-start.28 = (bf16[240,640]{1,0:T(8,128)(2,1)S(1)}, bf16[240,640]{1,0:T(8,128)(2,1)S(1)}, u32[]{:S(2)}, u32[]{:S(2)}) collective-permute-start(bf16[240,640]{1,0:T(8,128)(2,1)S(1)} %get-tuple-element.114), channel_id=1, source_target_pairs={{0,2},{1,3},{2,0},{3,1},{4,6},{5,7},{6,4},{7,5},{8,10},{9,11},{10,... | collective-permute-start | bytes 921608 | tf_op jit(solution)/shard_map/ppermute | solution.py:432
  85.4 1.9 %collective-permute-done.23.refs_2_ = bf16[2,304,128]{2,1,0:T(8,128)(2,1)S(1)} collective-permute-done((bf16[2,304,128]{2,1,0:T(8,128)(2,1)S(1)}, bf16[2,304,128]{2,1,0:T(8,128)(2,1)S(1)}, u32[]{:S(2)}, u32[]{:S(2)}) %collective-permute-start.23) | collective-permute-done | bytes 155680 | tf_op jit(solution)/shard_map/ppermute | solution.py:432
  87.7 3.1 %collective-permute-done.27.received_ref = bf16[240,640]{1,0:T(8,128)(2,1)S(1)} collective-permute-done((bf16[240,640]{1,0:T(8,128)(2,1)S(1)}, bf16[240,640]{1,0:T(8,128)(2,1)S(1)}, u32[]{:S(2)}, u32[]{:S(2)}) %collective-permute-start.27) | collective-permute-done | bytes 307232 | tf_op jit(solution)/shard_map/ppermute | solution.py:432
  90.9 9.0 %collective-permute-done.26.received_ref = bf16[256,640]{1,0:T(8,128)(2,1)S(1)} collective-permute-done((bf16[256,640]{1,0:T(8,128)(2,1)S(1)}, bf16[256,640]{1,0:T(8,128)(2,1)S(1)}, u32[]{:S(2)}, u32[]{:S(2)}) %collective-permute-start.26) | collective-permute-done | bytes 327712 | tf_op jit(solution)/shard_map/ppermute | solution.py:432
  99.9 1.9 %update.2 = f32[240,640]{1,0:T(8,128)} custom-call(s32[1]{0:T(128)} %bitcast.5.refs_5_.refs_0_.me_ref, bf16[4,240,640]{2,1,0:T(8,128)(2,1)S(1)} %unpack.3.refs_1_.own_ref, bf16[240,640]{1,0:T(8,128)(2,1)S(1)} %get-tuple-element.107.rate_ref, f32[2,240,640]{2,1,0:T(8,128)S(1)} %get-tuple-element.108.home_ref, ...), custom_call_target="tpu_custom_call" | custom-call | bytes 1024 | tf_op jit(solution)/shard_map/update/pallas_call | solution.py:744
  102.0 8.8 %collective-permute-done.29.refs_2_ = bf16[240,640]{1,0:T(8,128)(2,1)S(1)} collective-permute-done((bf16[240,640]{1,0:T(8,128)(2,1)S(1)}, bf16[240,640]{1,0:T(8,128)(2,1)S(1)}, u32[]{:S(2)}, u32[]{:S(2)}) %collective-permute-start.29) | collective-permute-done | bytes 307232 | tf_op jit(solution)/shard_map/ppermute | solution.py:432
  (72 shorter events, 19.1 us)
Async XLA Ops:
  0.6 12.5 %copy-start = (bf16[1280,640]{1,0:T(8,128)(2,1)S(1)}, bf16[1280,640]{1,0:T(8,128)(2,1)}, u32[]{:S(2)}) copy-start(bf16[1280,640]{1,0:T(8,128)(2,1)} %param.19) | copy-start | bytes 4915204
  0.6 14.4 %copy-start.1 = (bf16[640,640]{1,0:T(8,128)(2,1)S(1)}, bf16[640,640]{1,0:T(8,128)(2,1)}, u32[]{:S(2)}) copy-start(bf16[640,640]{1,0:T(8,128)(2,1)} %constant.18.clone.same_hbm) | copy-start | bytes 2457604
  3.1 14.2 %collective-permute-start = (bf16[448,128]{1,0:T(8,128)(2,1)}, bf16[448,128]{1,0:T(8,128)(2,1)S(1)}, u32[]{:S(2)}, u32[]{:S(2)}) collective-permute-start(bf16[448,128]{1,0:T(8,128)(2,1)} %get-tuple-element.64.refs_0_), channel_id=1, source_target_pairs={{0,2},{1,3},{2,0},{3,1},{4,6},{5,7},{6,4},{7,5},{8,10},{9,11},{10,... | collective-permute-start | bytes 344072 | tf_op jit(solution)/shard_map/ppermute | solution.py:432
  6.2 11.9 %collective-permute-start.1 = (bf16[448,128]{1,0:T(8,128)(2,1)}, bf16[448,128]{1,0:T(8,128)(2,1)S(1)}, u32[]{:S(2)}, u32[]{:S(2)}) collective-permute-start(bf16[448,128]{1,0:T(8,128)(2,1)} %get-tuple-element.64.refs_0_), channel_id=1, source_target_pairs={{0,4},{1,5},{2,6},{3,7},{4,0},{5,1},{6,2},{7,3},{8,12},{9,13},{10,... | collective-permute-start | bytes 344072 | tf_op jit(solution)/shard_map/ppermute | solution.py:432
  8.8 9.3 %collective-permute-start.2 = (bf16[448,128]{1,0:T(8,128)(2,1)}, bf16[448,128]{1,0:T(8,128)(2,1)S(1)}, u32[]{:S(2)}, u32[]{:S(2)}) collective-permute-start(bf16[448,128]{1,0:T(8,128)(2,1)} %get-tuple-element.64.refs_0_), channel_id=1, source_target_pairs={{0,6},{1,7},{2,4},{3,5},{4,2},{5,3},{6,0},{7,1},{8,14},{9,15},{10,... | collective-permute-start | bytes 344072 | tf_op jit(solution)/shard_map/ppermute | solution.py:432
  8.8 4.7 %collective-permute-start.3 = (bf16[160,128]{1,0:T(8,128)(2,1)}, bf16[160,128]{1,0:T(8,128)(2,1)S(1)}, u32[]{:S(2)}, u32[]{:S(2)}) collective-permute-start(bf16[160,128]{1,0:T(8,128)(2,1)} %get-tuple-element.60.refs_0_), channel_id=1, source_target_pairs={{0,8},{8,0},{16,24},{24,16},{1,9},{9,1},{17,25},{25,17},{2,10},{10... | collective-permute-start | bytes 122888 | tf_op jit(solution)/shard_map/ppermute | solution.py:432
  13.5 4.6 %collective-permute-start.4 = (bf16[2,160,128]{2,1,0:T(8,128)(2,1)S(1)}, bf16[2,160,128]{2,1,0:T(8,128)(2,1)S(1)}, u32[]{:S(2)}, u32[]{:S(2)}) collective-permute-start(bf16[2,160,128]{2,1,0:T(8,128)(2,1)S(1)} %stack.5.refs_0_), channel_id=1, source_target_pairs={{0,16},{8,24},{16,0},{24,8},{1,17},{9,25},{17,1},{25,9},{2,18},{10... | collective-permute-start | bytes 245768 | tf_op jit(solution)/shard_map/ppermute | solution.py:432
  18.1 5.3 %collective-permute-start.8 = (bf16[2,304,128]{2,1,0:T(8,128)(2,1)S(1)}, bf16[2,304,128]{2,1,0:T(8,128)(2,1)S(1)}, u32[]{:S(2)}, u32[]{:S(2)}) collective-permute-start(bf16[2,304,128]{2,1,0:T(8,128)(2,1)S(1)} %get-tuple-element.73.refs_0_.refs_3_), channel_id=1, source_target_pairs={{0,16},{8,24},{16,0},{24,8},{1,17},{9,25},{17,1},{25,9},{2,18},{10... | collective-permute-start | bytes 466952 | tf_op jit(solution)/shard_map/ppermute | solution.py:432
  19.7 6.8 %collective-permute-start.6 = (bf16[2,304,128]{2,1,0:T(8,128)(2,1)S(1)}, bf16[2,304,128]{2,1,0:T(8,128)(2,1)S(1)}, u32[]{:S(2)}, u32[]{:S(2)}) collective-permute-start(bf16[2,304,128]{2,1,0:T(8,128)(2,1)S(1)} %get-tuple-element.72.refs_0_), channel_id=1, source_target_pairs={{0,8},{8,0},{16,24},{24,16},{1,9},{9,1},{17,25},{25,17},{2,10},{10... | collective-permute-start | bytes 466952 | tf_op jit(solution)/shard_map/ppermute | solution.py:432
  23.5 11.6 %collective-permute-start.9 = (bf16[2,2,304,128]{3,2,1,0:T(8,128)(2,1)S(1)}, bf16[2,2,304,128]{3,2,1,0:T(8,128)(2,1)S(1)}, u32[]{:S(2)}, u32[]{:S(2)}) collective-permute-start(bf16[2,2,304,128]{3,2,1,0:T(8,128)(2,1)S(1)} %stack.9), channel_id=1, source_target_pairs={{0,8},{8,0},{16,24},{24,16},{1,9},{9,1},{17,25},{25,17},{2,10},{10... | collective-permute-start | bytes 933896 | tf_op jit(solution)/shard_map/ppermute | solution.py:432
  26.6 8.4 %collective-permute-start.7 = (bf16[2,2,304,128]{3,2,1,0:T(8,128)(2,1)S(1)}, bf16[2,2,304,128]{3,2,1,0:T(8,128)(2,1)S(1)}, u32[]{:S(2)}, u32[]{:S(2)}) collective-permute-start(bf16[2,2,304,128]{3,2,1,0:T(8,128)(2,1)S(1)} %stack.8), channel_id=1, source_target_pairs={{0,16},{8,24},{16,0},{24,8},{1,17},{9,25},{17,1},{25,9},{2,18},{10... | collective-permute-start | bytes 933896 | tf_op jit(solution)/shard_map/ppermute | solution.py:432
  27.0 8.0 %collective-permute-start.5 = (bf16[4,160,128]{2,1,0:T(8,128)(2,1)S(1)}, bf16[4,160,128]{2,1,0:T(8,128)(2,1)S(1)}, u32[]{:S(2)}, u32[]{:S(2)}) collective-permute-start(bf16[4,160,128]{2,1,0:T(8,128)(2,1)S(1)} %bitcast.23), channel_id=1, source_target_pairs={{0,4},{1,5},{2,6},{3,7},{4,0},{5,1},{6,2},{7,3},{8,12},{9,13},{10,... | collective-permute-start | bytes 491528 | tf_op jit(solution)/shard_map/ppermute | solution.py:432
  35.8 4.1 %collective-permute-start.10 = (bf16[4,240,640]{2,1,0:T(8,128)(2,1)S(1)}, bf16[4,240,640]{2,1,0:T(8,128)(2,1)S(1)}, u32[]{:S(2)}, u32[]{:S(2)}) collective-permute-start(bf16[4,240,640]{2,1,0:T(8,128)(2,1)S(1)} %unpack.2.refs_1_.own_ref), channel_id=1, source_target_pairs={{0,1},{1,0},{2,3},{3,2},{4,5},{5,4},{6,7},{7,6},{8,9},{9,8},{10,11... | collective-permute-start | bytes 3686408 | tf_op jit(solution)/shard_map/ppermute | solution.py:432
  35.9 10.1 %collective-permute-start.14 = (bf16[2,4,160,128]{3,2,1,0:T(8,128)(2,1)S(1)}, bf16[2,4,160,128]{3,2,1,0:T(8,128)(2,1)S(1)}, u32[]{:S(2)}, u32[]{:S(2)}) collective-permute-start(bf16[2,4,160,128]{3,2,1,0:T(8,128)(2,1)S(1)} %stack.7.refs_4_), channel_id=1, source_target_pairs={{0,2},{1,3},{2,0},{3,1},{4,6},{5,7},{6,4},{7,5},{8,10},{9,11},{10,... | collective-permute-start | bytes 983048 | tf_op jit(solution)/shard_map/ppermute | solution.py:432
  36.4 9.6 %collective-permute-start.11 = (bf16[4,144,128]{2,1,0:T(8,128)(2,1)S(1)}, bf16[4,144,128]{2,1,0:T(8,128)(2,1)S(1)}, u32[]{:S(2)}, u32[]{:S(2)}) collective-permute-start(bf16[4,144,128]{2,1,0:T(8,128)(2,1)S(1)} %get-tuple-element.77.refs_0_), channel_id=1, source_target_pairs={{0,8},{8,0},{16,24},{24,16},{1,9},{9,1},{17,25},{25,17},{2,10},{10... | collective-permute-start | bytes 442376 | tf_op jit(solution)/shard_map/ppermute | solution.py:432
  37.8 9.1 %collective-permute-start.12 = (bf16[4,144,128]{2,1,0:T(8,128)(2,1)S(1)}, bf16[4,144,128]{2,1,0:T(8,128)(2,1)S(1)}, u32[]{:S(2)}, u32[]{:S(2)}) collective-permute-start(bf16[4,144,128]{2,1,0:T(8,128)(2,1)S(1)} %get-tuple-element.77.refs_0_), channel_id=1, source_target_pairs={{0,16},{8,24},{16,0},{24,8},{1,17},{9,25},{17,1},{25,9},{2,18},{10... | collective-permute-start | bytes 442376 | tf_op jit(solution)/shard_map/ppermute | solution.py:432
  39.8 7.1 %collective-permute-start.13 = (bf16[4,144,128]{2,1,0:T(8,128)(2,1)S(1)}, bf16[4,144,128]{2,1,0:T(8,128)(2,1)S(1)}, u32[]{:S(2)}, u32[]{:S(2)}) collective-permute-start(bf16[4,144,128]{2,1,0:T(8,128)(2,1)S(1)} %get-tuple-element.77.refs_0_), channel_id=1, source_target_pairs={{0,24},{8,16},{16,8},{24,0},{1,25},{9,17},{17,9},{25,1},{2,26},{10... | collective-permute-start | bytes 442376 | tf_op jit(solution)/shard_map/ppermute | solution.py:432
  47.6 3.0 %collective-permute-start.15 = (bf16[4,240,640]{2,1,0:T(8,128)(2,1)S(1)}, bf16[4,240,640]{2,1,0:T(8,128)(2,1)S(1)}, u32[]{:S(2)}, u32[]{:S(2)}) collective-permute-start(bf16[4,240,640]{2,1,0:T(8,128)(2,1)S(1)} %unpack.3.refs_1_.own_ref), channel_id=1, source_target_pairs={{0,1},{1,0},{2,3},{3,2},{4,5},{5,4},{6,7},{7,6},{8,9},{9,8},{10,11... | collective-permute-start | bytes 3686408 | tf_op jit(solution)/shard_map/ppermute | solution.py:432
  57.0 2.2 %collective-permute-start.16 = (bf16[496,640]{1,0:T(8,128)(2,1)S(1)}, bf16[496,640]{1,0:T(8,128)(2,1)S(1)}, u32[]{:S(2)}, u32[]{:S(2)}) collective-permute-start(bf16[496,640]{1,0:T(8,128)(2,1)S(1)} %get-tuple-element.84.own_ref), channel_id=1, source_target_pairs={{0,1},{1,0},{2,3},{3,2},{4,5},{5,4},{6,7},{7,6},{8,9},{9,8},{10,11... | collective-permute-start | bytes 1904648 | tf_op jit(solution)/shard_map/ppermute | solution.py:432
  59.3 16.6 %collective-permute-start.21 = (bf16[496,640]{1,0:T(8,128)(2,1)S(1)}, bf16[496,640]{1,0:T(8,128)(2,1)S(1)}, u32[]{:S(2)}, u32[]{:S(2)}) collective-permute-start(bf16[496,640]{1,0:T(8,128)(2,1)S(1)} %pair.2.sent_ref), channel_id=1, source_target_pairs={{0,2},{1,3},{2,0},{3,1},{4,6},{5,7},{6,4},{7,5},{8,10},{9,11},{10,... | collective-permute-start | bytes 1904648 | tf_op jit(solution)/shard_map/ppermute | solution.py:432
  70.7 1.7 %collective-permute-start.17 = (bf16[240,640]{1,0:T(8,128)(2,1)S(1)}, bf16[240,640]{1,0:T(8,128)(2,1)S(1)}, u32[]{:S(2)}, u32[]{:S(2)}) collective-permute-start(bf16[240,640]{1,0:T(8,128)(2,1)S(1)} %get-tuple-element.95), channel_id=1, source_target_pairs={{0,1},{1,0},{2,3},{3,2},{4,5},{5,4},{6,7},{7,6},{8,9},{9,8},{10,11... | collective-permute-start | bytes 921608 | tf_op jit(solution)/shard_map/ppermute | solution.py:432
  70.8 10.2 %collective-permute-start.25 = (bf16[480,640]{1,0:T(8,128)(2,1)S(1)}, bf16[480,640]{1,0:T(8,128)(2,1)S(1)}, u32[]{:S(2)}, u32[]{:S(2)}) collective-permute-start(bf16[480,640]{1,0:T(8,128)(2,1)S(1)} %get-tuple-element.88), channel_id=1, source_target_pairs={{0,1},{1,0},{2,3},{3,2},{4,5},{5,4},{6,7},{7,6},{8,9},{9,8},{10,11... | collective-permute-start | bytes 1843208 | tf_op jit(solution)/shard_map/ppermute | solution.py:432
  71.3 2.4 %collective-permute-start.18 = (bf16[240,640]{1,0:T(8,128)(2,1)S(1)}, bf16[240,640]{1,0:T(8,128)(2,1)S(1)}, u32[]{:S(2)}, u32[]{:S(2)}) collective-permute-start(bf16[240,640]{1,0:T(8,128)(2,1)S(1)} %get-tuple-element.96), channel_id=1, source_target_pairs={{0,1},{1,0},{2,3},{3,2},{4,5},{5,4},{6,7},{7,6},{8,9},{9,8},{10,11... | collective-permute-start | bytes 921608 | tf_op jit(solution)/shard_map/ppermute | solution.py:432
  71.4 2.8 %collective-permute-start.19 = (bf16[240,640]{1,0:T(8,128)(2,1)S(1)}, bf16[240,640]{1,0:T(8,128)(2,1)S(1)}, u32[]{:S(2)}, u32[]{:S(2)}) collective-permute-start(bf16[240,640]{1,0:T(8,128)(2,1)S(1)} %get-tuple-element.97), channel_id=1, source_target_pairs={{0,1},{1,0},{2,3},{3,2},{4,5},{5,4},{6,7},{7,6},{8,9},{9,8},{10,11... | collective-permute-start | bytes 921608 | tf_op jit(solution)/shard_map/ppermute | solution.py:432
  72.4 2.2 %collective-permute-start.20 = (bf16[240,640]{1,0:T(8,128)(2,1)S(1)}, bf16[240,640]{1,0:T(8,128)(2,1)S(1)}, u32[]{:S(2)}, u32[]{:S(2)}) collective-permute-start(bf16[240,640]{1,0:T(8,128)(2,1)S(1)} %get-tuple-element.98), channel_id=1, source_target_pairs={{0,1},{1,0},{2,3},{3,2},{4,5},{5,4},{6,7},{7,6},{8,9},{9,8},{10,11... | collective-permute-start | bytes 921608 | tf_op jit(solution)/shard_map/ppermute | solution.py:432
  76.2 14.5 %collective-permute-start.27 = (bf16[240,640]{1,0:T(8,128)(2,1)S(1)}, bf16[240,640]{1,0:T(8,128)(2,1)S(1)}, u32[]{:S(2)}, u32[]{:S(2)}) collective-permute-start(bf16[240,640]{1,0:T(8,128)(2,1)S(1)} %get-tuple-element.103), channel_id=1, source_target_pairs={{0,2},{1,3},{2,0},{3,1},{4,6},{5,7},{6,4},{7,5},{8,10},{9,11},{10,... | collective-permute-start | bytes 921608 | tf_op jit(solution)/shard_map/ppermute | solution.py:432
  77.6 6.4 %collective-permute-start.22 = (bf16[2,304,128]{2,1,0:T(8,128)(2,1)S(1)}, bf16[2,304,128]{2,1,0:T(8,128)(2,1)S(1)}, u32[]{:S(2)}, u32[]{:S(2)}) collective-permute-start(bf16[2,304,128]{2,1,0:T(8,128)(2,1)S(1)} %copy-done.4), channel_id=1, source_target_pairs={{0,8},{8,0},{16,24},{24,16},{1,9},{9,1},{17,25},{25,17},{2,10},{10... | collective-permute-start | bytes 466952 | tf_op jit(solution)/shard_map/ppermute | solution.py:432
  79.0 8.3 %collective-permute-start.23 = (bf16[2,304,128]{2,1,0:T(8,128)(2,1)S(1)}, bf16[2,304,128]{2,1,0:T(8,128)(2,1)S(1)}, u32[]{:S(2)}, u32[]{:S(2)}) collective-permute-start(bf16[2,304,128]{2,1,0:T(8,128)(2,1)S(1)} %copy-done.4), channel_id=1, source_target_pairs={{0,16},{8,24},{16,0},{24,8},{1,17},{9,25},{17,1},{25,9},{2,18},{10... | collective-permute-start | bytes 466952 | tf_op jit(solution)/shard_map/ppermute | solution.py:432
  79.8 7.5 %collective-permute-start.24 = (bf16[2,304,128]{2,1,0:T(8,128)(2,1)S(1)}, bf16[2,304,128]{2,1,0:T(8,128)(2,1)S(1)}, u32[]{:S(2)}, u32[]{:S(2)}) collective-permute-start(bf16[2,304,128]{2,1,0:T(8,128)(2,1)S(1)} %copy-done.4), channel_id=1, source_target_pairs={{0,24},{8,16},{16,8},{24,0},{1,25},{9,17},{17,9},{25,1},{2,26},{10... | collective-permute-start | bytes 466952 | tf_op jit(solution)/shard_map/ppermute | solution.py:432
  81.2 18.7 %collective-permute-start.26 = (bf16[256,640]{1,0:T(8,128)(2,1)S(1)}, bf16[256,640]{1,0:T(8,128)(2,1)S(1)}, u32[]{:S(2)}, u32[]{:S(2)}) collective-permute-start(bf16[256,640]{1,0:T(8,128)(2,1)S(1)} %merge.2.sent_ref), channel_id=1, source_target_pairs={{0,4},{1,5},{2,6},{3,7},{4,0},{5,1},{6,2},{7,3},{8,12},{9,13},{10,... | collective-permute-start | bytes 983048 | tf_op jit(solution)/shard_map/ppermute | solution.py:432
  83.9 18.0 %collective-permute-start.28 = (bf16[240,640]{1,0:T(8,128)(2,1)S(1)}, bf16[240,640]{1,0:T(8,128)(2,1)S(1)}, u32[]{:S(2)}, u32[]{:S(2)}) collective-permute-start(bf16[240,640]{1,0:T(8,128)(2,1)S(1)} %get-tuple-element.114), channel_id=1, source_target_pairs={{0,2},{1,3},{2,0},{3,1},{4,6},{5,7},{6,4},{7,5},{8,10},{9,11},{10,... | collective-permute-start | bytes 921608 | tf_op jit(solution)/shard_map/ppermute | solution.py:432
  90.8 20.0 %collective-permute-start.29 = (bf16[240,640]{1,0:T(8,128)(2,1)S(1)}, bf16[240,640]{1,0:T(8,128)(2,1)S(1)}, u32[]{:S(2)}, u32[]{:S(2)}) collective-permute-start(bf16[240,640]{1,0:T(8,128)(2,1)S(1)} %merge.3), channel_id=1, source_target_pairs={{0,4},{1,5},{2,6},{3,7},{4,0},{5,1},{6,2},{7,3},{8,12},{9,13},{10,... | collective-permute-start | bytes 921608 | tf_op jit(solution)/shard_map/ppermute | solution.py:432
  (5 other events, 30.0 us)

commit v8 on v7

--- a/solution.py
+++ b/solution.py
@@ -453,29 +453,31 @@
     return (rows + TAIL) // 32 * 16
 
 
+def packed_block(whole):
+    rows, cols = whole.shape
+    rest = jnp.concatenate(
+        [whole[:, 128:cols], jnp.zeros((4 * TAIL - rows, cols - 128), BF16)], axis=0
+    )
+    rest = [rest[q * TAIL : (q + 1) * TAIL] for q in range(4)]
+    return jnp.concatenate([whole[:, 0:128], jnp.concatenate(rest, axis=1)], axis=0)
+
+
 def pack_kernel(*refs):
-    refs = refs[:4] + refs[6:]
-    sources, (early_ref, late_ref, rates_ref) = refs[:4], refs[4:7]
-    held, sems = refs[7:11], refs[11]
+    sources, (early_ref, late_ref), held, sems = refs[:2], refs[4:6], refs[6:8], refs[8]
     copies = fetch(sources, held, sems)
     cols, rows = held[0].shape
     size, cut = rows + TAIL, cut_of(rows)
-
-    def packed(i):
-        copies[i].wait()
-        whole = held[i][...].T
-        rest = jnp.concatenate(
-            [whole[:, 128:cols], jnp.zeros((4 * TAIL - rows, cols - 128), BF16)], axis=0
-        )
-        rest = [rest[q * TAIL : (q + 1) * TAIL] for q in range(4)]
-        return jnp.concatenate([whole[:, 0:128], jnp.concatenate(rest, axis=1)], axis=0)
-
-    early_ref[0:size] = packed(0)
-    second = packed(1)
+    copies[0].wait()
+    early_ref[0:size] = packed_block(held[0][...].T)
+    copies[1].wait()
+    second = packed_block(held[1][...].T)
     early_ref[size:] = second[0:cut]
     late_ref[...] = second[cut:]
-    rates_ref[0] = packed(2)
-    rates_ref[1] = packed(3)
+
+
+def pack_rates_kernel(one_ref, two_ref, out_ref):
+    out_ref[0] = packed_block(one_ref[...].T)
+    out_ref[1] = packed_block(two_ref[...].T)
 
 
 def unpacked(block_of, rows, n_group):
@@ -568,19 +570,18 @@
         second = lambda after: (full[1], own[1][None])
         return (full[0],), second, own[0][None], rates, enter(clip), bias_row
     size, cut, chips = rows + TAIL, cut_of(rows), n_member // 2
-    early_rows, late, both_rates = pl.pallas_call(
+    early_rows, late = pl.pallas_call(
         pack_kernel,
         out_shape=(
             jax.ShapeDtypeStruct((size + cut, 128), BF16),
             jax.ShapeDtypeStruct((size - cut, 128), BF16),
-            jax.ShapeDtypeStruct((2, size, 128), BF16),
         ),
-        in_specs=hbm(4) + smem(2),
-        out_specs=tuple(vmem(3)),
-        scratch_shapes=[pltpu.VMEM((cols, rows), BF16)] * 4 + [pltpu.SemaphoreType.DMA((4,))],
+        in_specs=hbm(2) + smem(2),
+        out_specs=tuple(vmem(2)),
+        scratch_shapes=[pltpu.VMEM((cols, rows), BF16)] * 2 + [pltpu.SemaphoreType.DMA((2,))],
         cost_estimate=pl.CostEstimate(flops=0, bytes_accessed=1024, transcendentals=0),
         name="pack",
-    )(conv1.T, conv2.T, rate1.T, rate2.T, group, me)
+    )(conv1.T, conv2.T, group, me)
 
     def unpack(kernel, *packed):
         (mine,) = call(
@@ -620,7 +621,10 @@
         return unpack(kernel, *along_two, *order_after((late, late_z), after))
 
     def rates(after):
-        blocks = across_groups(order_after(both_rates, after), n_group)
+        (both,) = call(pack_rates_kernel, [((2, size, 128), BF16)], [], "pack_rates", vmem(2))(
+            rate1.T, rate2.T
+        )
+        blocks = across_groups(order_after(both, after), n_group)
         return call(
             functools.partial(rate_kernel, rows, n_group),
             [((rows, width), BF16)] * 2, [], "rates", smem(1) + vmem(n_group),
@@ -872,11 +876,10 @@
         received_one, from_two = order_after((received_one, from_two), ())
         far_one, near_one, middle_one, kept_one = pair_parts(home_one, received_one)
         from_one = swap(far_one, "member", n_member, 2)
-        beside_one = swap(near_one, "member", n_member, 2)
+        beside_one = swap(order_after(near_one, from_one), "member", n_member, 2)
         merged_two = merge_factors(home_even, received_even, half_two, from_two)
         across_two = swap(merged_two, "member", n_member, 4)
-        rate_one, rate_two = rates(far_one)
-        middle_one = order_after(middle_one, (rate_one, rate_two))
+        rate_one, rate_two = rates(from_one)
         merged_one = merge(middle_one, from_one)
         across_one = swap(merged_one, "member", n_member, 4)
         adapted_two = common_update(

time: 112 us -> 109 us (0.973)
  waiting for transfers between devices: 41.3 us -> 39.6 us
    ppermute x30, waiting for transfers between devices: 41.3 us -> 39.6 us  [swap(): return lax.ppermute(value, axis, [(i, i ^ offset) for i in range(size)])]
  transfers between devices with their start and end apart: 30 -> 30, of which waited for: 17 -> 17; matrix products, arithmetic and copies ran while one was open for 1% -> 1% of each run, Pallas kernels for 20% -> 21%
where the time goes in v8:
time: 109 us
  waiting for transfers between devices  39.6 us (36%)
  Pallas kernels  33.9 us (31%)
  starting transfers between devices  31.8 us (29%)
  between operations  2.26 us (2%)
  matrix products  1.53 us (1%)
    ppermute x30, waiting for transfers between devices, swap(): return lax.ppermute(value, axis, [(i, i ^ offset) for i in range(size)])  39.6 us
    ppermute x30, starting transfers between devices, swap(): return lax.ppermute(value, axis, [(i, i ^ offset) for i in range(size)])  31.8 us
    pallas_call x1, Pallas kernels, gradient(): call(functools.partial(grad_kernel, points, scale, block, centred), [((ch...  4.49 us
    pallas_call x1, Pallas kernels, shards(): call(functools.partial(second_kernel, points, scale), [((padded, channels...  3.86 us
    pallas_call x1, Pallas kernels, shards(): call(functools.partial(back_kernel, points, scale), [((rows, channels), F...  3.43 us
    pallas_call x1, Pallas kernels, shards(): call(functools.partial(first_kernel, points, scale), [((rows, channels),...  3.37 us
    pallas_call x1, Pallas kernels, odd_half(): call(functools.partial(half_kernel, points, scale, 1), [((2 * block + FAC...  2.49 us
    pallas_call x1, Pallas kernels, shards(): call(functools.partial(norm_kernel, points), [((rows, channels), F32), ((...  2.25 us
  transfers between devices with their start and end apart: 30, of which 17 were waited for; matrix products, arithmetic and copies ran while one was open for 1% of the time, Pallas kernels for 21%

profile of v8, /device:TPU:0, one launch (start us, length us, event | category | flops | bytes accessed | tf_op | source)
XLA Modules:
  0.0 109.2 jit_solution(1936259221806613669)
XLA Ops:
  0.7 2.0 %pack.1 = (bf16[448,128]{1,0:T(8,128)(2,1)}, bf16[160,128]{1,0:T(8,128)(2,1)}) custom-call(bf16[160,240]{1,0:T(8,128)(2,1)} %bitcast.29, bf16[160,240]{1,0:T(8,128)(2,1)} %bitcast.30, s32[1]{0:T(128)} %bitcast.refs_2_.group_ref, s32[1]{0:T(128)} %bitcast.3.refs_3_.refs_0_.me_ref), custom_call_target="tpu_custom_call" | custom-call | bytes 1024 | tf_op jit(solution)/shard_map/pack/pallas_call | solution.py:573
  2.7 3.1 %collective-permute-start = (bf16[448,128]{1,0:T(8,128)(2,1)}, bf16[448,128]{1,0:T(8,128)(2,1)S(1)}, u32[]{:S(2)}, u32[]{:S(2)}) collective-permute-start(bf16[448,128]{1,0:T(8,128)(2,1)} %get-tuple-element.63.refs_0_), channel_id=1, source_target_pairs={{0,2},{1,3},{2,0},{3,1},{4,6},{5,7},{6,4},{7,5},{8,10},{9,11},{10,... | collective-permute-start | bytes 344072 | tf_op jit(solution)/shard_map/ppermute | solution.py:432
  5.8 2.6 %collective-permute-start.1 = (bf16[448,128]{1,0:T(8,128)(2,1)}, bf16[448,128]{1,0:T(8,128)(2,1)S(1)}, u32[]{:S(2)}, u32[]{:S(2)}) collective-permute-start(bf16[448,128]{1,0:T(8,128)(2,1)} %get-tuple-element.63.refs_0_), channel_id=1, source_target_pairs={{0,4},{1,5},{2,6},{3,7},{4,0},{5,1},{6,2},{7,3},{8,12},{9,13},{10,... | collective-permute-start | bytes 344072 | tf_op jit(solution)/shard_map/ppermute | solution.py:432
  8.4 1.7 %collective-permute-start.3 = (bf16[160,128]{1,0:T(8,128)(2,1)}, bf16[160,128]{1,0:T(8,128)(2,1)S(1)}, u32[]{:S(2)}, u32[]{:S(2)}) collective-permute-start(bf16[160,128]{1,0:T(8,128)(2,1)} %get-tuple-element.59.refs_0_), channel_id=1, source_target_pairs={{0,8},{8,0},{16,24},{24,16},{1,9},{9,1},{17,25},{25,17},{2,10},{10... | collective-permute-start | bytes 122888 | tf_op jit(solution)/shard_map/ppermute | solution.py:432
  13.1 1.6 %collective-permute-start.4 = (bf16[2,160,128]{2,1,0:T(8,128)(2,1)S(1)}, bf16[2,160,128]{2,1,0:T(8,128)(2,1)S(1)}, u32[]{:S(2)}, u32[]{:S(2)}) collective-permute-start(bf16[2,160,128]{2,1,0:T(8,128)(2,1)S(1)} %stack.5.refs_0_), channel_id=1, source_target_pairs={{0,16},{8,24},{16,0},{24,8},{1,17},{9,25},{17,1},{25,9},{2,18},{10... | collective-permute-start | bytes 245768 | tf_op jit(solution)/shard_map/ppermute | solution.py:432
  14.7 2.2 %enter.1.in_ref.act_ref = bf16[1024,640]{1,0:T(8,128)(2,1)S(1)} custom-call(bf16[896,640]{1,0:T(8,128)(2,1)S(1)} %bitcast.20, bf16[640,640]{1,0:T(8,128)(2,1)S(1)} %copy-done.1), custom_call_target="tpu_custom_call" | custom-call | bytes 1024 | tf_op jit(solution)/shard_map/enter/pallas_call | solution.py:796
  17.8 1.6 %collective-permute-start.8 = (bf16[2,304,128]{2,1,0:T(8,128)(2,1)S(1)}, bf16[2,304,128]{2,1,0:T(8,128)(2,1)S(1)}, u32[]{:S(2)}, u32[]{:S(2)}) collective-permute-start(bf16[2,304,128]{2,1,0:T(8,128)(2,1)S(1)} %get-tuple-element.72.refs_0_.refs_3_), channel_id=1, source_target_pairs={{0,16},{8,24},{16,0},{24,8},{1,17},{9,25},{17,1},{25,9},{2,18},{10... | collective-permute-start | bytes 466952 | tf_op jit(solution)/shard_map/ppermute | solution.py:432
  19.4 1.5 %collective-permute-start.6 = (bf16[2,304,128]{2,1,0:T(8,128)(2,1)S(1)}, bf16[2,304,128]{2,1,0:T(8,128)(2,1)S(1)}, u32[]{:S(2)}, u32[]{:S(2)}) collective-permute-start(bf16[2,304,128]{2,1,0:T(8,128)(2,1)S(1)} %get-tuple-element.71.refs_0_), channel_id=1, source_target_pairs={{0,8},{8,0},{16,24},{24,16},{1,9},{9,1},{17,25},{25,17},{2,10},{10... | collective-permute-start | bytes 466952 | tf_op jit(solution)/shard_map/ppermute | solution.py:432
  20.9 2.2 %collective-permute-done.8.refs_1_.refs_4_ = bf16[2,304,128]{2,1,0:T(8,128)(2,1)S(1)} collective-permute-done((bf16[2,304,128]{2,1,0:T(8,128)(2,1)S(1)}, bf16[2,304,128]{2,1,0:T(8,128)(2,1)S(1)}, u32[]{:S(2)}, u32[]{:S(2)}) %collective-permute-start.8) | collective-permute-done | bytes 155680 | tf_op jit(solution)/shard_map/ppermute | solution.py:432
  23.1 1.6 %collective-permute-start.9 = (bf16[2,2,304,128]{3,2,1,0:T(8,128)(2,1)S(1)}, bf16[2,2,304,128]{3,2,1,0:T(8,128)(2,1)S(1)}, u32[]{:S(2)}, u32[]{:S(2)}) collective-permute-start(bf16[2,2,304,128]{3,2,1,0:T(8,128)(2,1)S(1)} %stack.9), channel_id=1, source_target_pairs={{0,8},{8,0},{16,24},{24,16},{1,9},{9,1},{17,25},{25,17},{2,10},{10... | collective-permute-start | bytes 933896 | tf_op jit(solution)/shard_map/ppermute | solution.py:432
  24.7 1.5 %collective-permute-done.6.refs_1_ = bf16[2,304,128]{2,1,0:T(8,128)(2,1)S(1)} collective-permute-done((bf16[2,304,128]{2,1,0:T(8,128)(2,1)S(1)}, bf16[2,304,128]{2,1,0:T(8,128)(2,1)S(1)}, u32[]{:S(2)}, u32[]{:S(2)}) %collective-permute-start.6) | collective-permute-done | bytes 155680 | tf_op jit(solution)/shard_map/ppermute | solution.py:432
  26.6 2.5 %collective-permute-start.5 = (bf16[4,160,128]{2,1,0:T(8,128)(2,1)S(1)}, bf16[4,160,128]{2,1,0:T(8,128)(2,1)S(1)}, u32[]{:S(2)}, u32[]{:S(2)}) collective-permute-start(bf16[4,160,128]{2,1,0:T(8,128)(2,1)S(1)} %bitcast.23), channel_id=1, source_target_pairs={{0,4},{1,5},{2,6},{3,7},{4,0},{5,1},{6,2},{7,3},{8,12},{9,13},{10,... | collective-permute-start | bytes 491528 | tf_op jit(solution)/shard_map/ppermute | solution.py:432
  29.1 5.5 %collective-permute-done.5.refs_1_ = bf16[4,160,128]{2,1,0:T(8,128)(2,1)S(1)} collective-permute-done((bf16[4,160,128]{2,1,0:T(8,128)(2,1)S(1)}, bf16[4,160,128]{2,1,0:T(8,128)(2,1)S(1)}, u32[]{:S(2)}, u32[]{:S(2)}) %collective-permute-start.5) | collective-permute-done | bytes 163872 | tf_op jit(solution)/shard_map/ppermute | solution.py:432
  37.4 2.0 %collective-permute-start.12 = (bf16[4,144,128]{2,1,0:T(8,128)(2,1)S(1)}, bf16[4,144,128]{2,1,0:T(8,128)(2,1)S(1)}, u32[]{:S(2)}, u32[]{:S(2)}) collective-permute-start(bf16[4,144,128]{2,1,0:T(8,128)(2,1)S(1)} %get-tuple-element.75.refs_0_), channel_id=1, source_target_pairs={{0,16},{8,24},{16,0},{24,8},{1,17},{9,25},{17,1},{25,9},{2,18},{10... | collective-permute-start | bytes 442376 | tf_op jit(solution)/shard_map/ppermute | solution.py:432
  39.5 3.4 %conv.1.hidden_ref = f32[896,640]{1,0:T(8,128)S(1)} custom-call(bf16[1024,640]{1,0:T(8,128)(2,1)S(1)} %enter.1.in_ref.act_ref, f32[1,640]{1,0:T(1,128)S(1)} %fusion.6.bias_ref, s32[1]{0:T(128)} %bitcast.3.refs_3_.refs_0_.me_ref, bf16[4,240,640]{2,1,0:T(8,128)(2,1)S(1)} %unpack.2.refs_1_.own_ref, bf16[4,240,640]{2,1,0:T(8,128)(2,1)S(1)} %collective-permute-done.10.refs_2_), custom_call_target="tpu_custom_call" | custom-call | bytes 1024 | tf_op jit(solution)/shard_map/conv/pallas_call | solution.py:814
  42.9 2.8 %collective-permute-done.14.refs_5_ = bf16[2,4,160,128]{3,2,1,0:T(8,128)(2,1)S(1)} collective-permute-done((bf16[2,4,160,128]{3,2,1,0:T(8,128)(2,1)S(1)}, bf16[2,4,160,128]{3,2,1,0:T(8,128)(2,1)S(1)}, u32[]{:S(2)}, u32[]{:S(2)}) %collective-permute-start.14) | collective-permute-done | bytes 327712 | tf_op jit(solution)/shard_map/ppermute | solution.py:432
  47.3 2.3 %norm.1 = (f32[896,640]{1,0:T(8,128)S(1)}, f32[1,640]{1,0:T(1,128)S(1)}, bf16[1024,640]{1,0:T(8,128)(2,1)S(1)}, bf16[640,896]{1,0:T(8,128)(2,1)S(1)}) custom-call(f32[896,640]{1,0:T(8,128)S(1)} %conv.1.hidden_ref, bf16[640,640]{1,0:T(8,128)(2,1)S(1)} %copy-done.1), custom_call_target="tpu_custom_call" | custom-call | bytes 1024 | tf_op jit(solution)/shard_map/norm/pallas_call | solution.py:824
  50.2 3.9 %conv_error.1 = (bf16[1024,640]{1,0:T(8,128)(2,1)S(1)}, bf16[1920,640]{1,0:T(8,128)(2,1)S(1)}) custom-call(bf16[1024,640]{1,0:T(8,128)(2,1)S(1)} %get-tuple-element.79.in_ref, bf16[896,640]{1,0:T(8,128)(2,1)S(1)} %bitcast.21, bf16[896,640]{1,0:T(8,128)(2,1)S(1)} %bitcast.22, s32[1]{0:T(128)} %bitcast.3.refs_3_.refs_0_.me_ref, ...), custom_call_target="tpu_custom_call" | custom-call | bytes 1024 | tf_op jit(solution)/shard_map/conv_error/pallas_call | solution.py:835
  54.1 2.5 %gradient_odd.1 = (bf16[496,640]{1,0:T(8,128)(2,1)S(1)}, f32[2,240,640]{2,1,0:T(8,128)S(1)}, f32[640,128]{1,0:T(8,128)S(1)}, f32[8,640]{1,0:T(8,128)S(1)}) custom-call(s32[1]{0:T(128)} %bitcast.3.refs_3_.refs_0_.me_ref, bf16[640,896]{1,0:T(8,128)(2,1)S(1)} %get-tuple-element.81.turned_ref, bf16[1024,640]{1,0:T(8,128)(2,1)S(1)} %get-tuple-element.88.cotangent_ref.error_ref), custom_call_target="tpu_custom_call" | custom-call | bytes 1024 | tf_op jit(solution)/shard_map/gradient_odd/pallas_call | solution.py:381
  56.8 2.0 %gradient_even.1 = (bf16[480,640]{1,0:T(8,128)(2,1)S(1)}, f32[2,240,640]{2,1,0:T(8,128)S(1)}) custom-call(s32[1]{0:T(128)} %bitcast.3.refs_3_.refs_0_.me_ref, bf16[640,896]{1,0:T(8,128)(2,1)S(1)} %get-tuple-element.81.turned_ref, bf16[1024,640]{1,0:T(8,128)(2,1)S(1)} %get-tuple-element.88.cotangent_ref.error_ref, f32[640,128]{1,0:T(8,128)S(1)} %get-tuple-element.84.refs_0_, ...), custom_call_target="tpu_custom_call" | custom-call | bytes 1024 | tf_op jit(solution)/shard_map/gradient_even/pallas_call | solution.py:396
  58.9 1.4 %collective-permute-start.21 = (bf16[496,640]{1,0:T(8,128)(2,1)S(1)}, bf16[496,640]{1,0:T(8,128)(2,1)S(1)}, u32[]{:S(2)}, u32[]{:S(2)}) collective-permute-start(bf16[496,640]{1,0:T(8,128)(2,1)S(1)} %pair.2.sent_ref), channel_id=1, source_target_pairs={{0,2},{1,3},{2,0},{3,1},{4,6},{5,7},{6,4},{7,5},{8,10},{9,11},{10,... | collective-permute-start | bytes 1904648 | tf_op jit(solution)/shard_map/ppermute | solution.py:432
  60.4 3.4 %back.1.act_grad_ref = f32[896,640]{1,0:T(8,128)S(1)} custom-call(bf16[1024,640]{1,0:T(8,128)(2,1)S(1)} %get-tuple-element.88.cotangent_ref.error_ref, bf16[1920,640]{1,0:T(8,128)(2,1)S(1)} %get-tuple-element.89.weight_ref), custom_call_target="tpu_custom_call" | custom-call | bytes 1024 | tf_op jit(solution)/shard_map/back/pallas_call | solution.py:857
  63.8 2.1 %norm_back.1.cotangent_ref = bf16[1024,640]{1,0:T(8,128)(2,1)S(1)} custom-call(f32[896,640]{1,0:T(8,128)S(1)} %back.1.act_grad_ref, f32[896,640]{1,0:T(8,128)S(1)} %get-tuple-element.90.normal_ref, f32[1,640]{1,0:T(1,128)S(1)} %get-tuple-element.91.inverse_ref, bf16[640,640]{1,0:T(8,128)(2,1)S(1)} %copy-done.1), custom_call_target="tpu_custom_call" | custom-call | bytes 1024 | tf_op jit(solution)/shard_map/norm_back/pallas_call | solution.py:861
  65.9 4.5 %gradient.1 = (f32[4,240,640]{2,1,0:T(8,128)S(1)}, bf16[240,640]{1,0:T(8,128)(2,1)S(1)}, bf16[240,640]{1,0:T(8,128)(2,1)S(1)}, bf16[240,640]{1,0:T(8,128)(2,1)S(1)}, bf16[240,640]{1,0:T(8,128)(2,1)S(1)}) custom-call(s32[1]{0:T(128)} %bitcast.3.refs_3_.refs_0_.me_ref, bf16[1024,640]{1,0:T(8,128)(2,1)S(1)} %enter.1.in_ref.act_ref, ...), custom_call_target="tpu_custom_call" | custom-call | bytes 1024 | tf_op jit(solution)/shard_map/gradient/pallas_call | solution.py:412
  77.3 2.4 %collective-permute-start.27 = (bf16[256,640]{1,0:T(8,128)(2,1)S(1)}, bf16[256,640]{1,0:T(8,128)(2,1)S(1)}, u32[]{:S(2)}, u32[]{:S(2)}) collective-permute-start(bf16[256,640]{1,0:T(8,128)(2,1)S(1)} %merge.2.sent_ref), channel_id=1, source_target_pairs={{0,4},{1,5},{2,6},{3,7},{4,0},{5,1},{6,2},{7,3},{8,12},{9,13},{10,... | collective-permute-start | bytes 983048 | tf_op jit(solution)/shard_map/ppermute | solution.py:432
  79.8 11.9 %collective-permute-done.22.received_ref = bf16[240,640]{1,0:T(8,128)(2,1)S(1)} collective-permute-done((bf16[240,640]{1,0:T(8,128)(2,1)S(1)}, bf16[240,640]{1,0:T(8,128)(2,1)S(1)}, u32[]{:S(2)}, u32[]{:S(2)}) %collective-permute-start.22) | collective-permute-done | bytes 307232 | tf_op jit(solution)/shard_map/ppermute | solution.py:432
  92.8 1.5 %collective-permute-start.23 = (bf16[2,304,128]{2,1,0:T(8,128)(2,1)S(1)}, bf16[2,304,128]{2,1,0:T(8,128)(2,1)S(1)}, u32[]{:S(2)}, u32[]{:S(2)}) collective-permute-start(bf16[2,304,128]{2,1,0:T(8,128)(2,1)S(1)} %pack_rates.1.refs_0_), channel_id=1, source_target_pairs={{0,8},{8,0},{16,24},{24,16},{1,9},{9,1},{17,25},{25,17},{2,10},{10... | collective-permute-start | bytes 466952 | tf_op jit(solution)/shard_map/ppermute | solution.py:432
  96.4 3.0 %collective-permute-done.23.refs_1_ = bf16[2,304,128]{2,1,0:T(8,128)(2,1)S(1)} collective-permute-done((bf16[2,304,128]{2,1,0:T(8,128)(2,1)S(1)}, bf16[2,304,128]{2,1,0:T(8,128)(2,1)S(1)}, u32[]{:S(2)}, u32[]{:S(2)}) %collective-permute-start.23) | collective-permute-done | bytes 155680 | tf_op jit(solution)/shard_map/ppermute | solution.py:432
  99.4 2.2 %collective-permute-done.24.refs_2_ = bf16[2,304,128]{2,1,0:T(8,128)(2,1)S(1)} collective-permute-done((bf16[2,304,128]{2,1,0:T(8,128)(2,1)S(1)}, bf16[2,304,128]{2,1,0:T(8,128)(2,1)S(1)}, u32[]{:S(2)}, u32[]{:S(2)}) %collective-permute-start.24) | collective-permute-done | bytes 155680 | tf_op jit(solution)/shard_map/ppermute | solution.py:432
  102.1 1.9 %update.2 = f32[240,640]{1,0:T(8,128)} custom-call(s32[1]{0:T(128)} %bitcast.3.refs_3_.refs_0_.me_ref, bf16[4,240,640]{2,1,0:T(8,128)(2,1)S(1)} %unpack.3.refs_1_.own_ref, bf16[240,640]{1,0:T(8,128)(2,1)S(1)} %get-tuple-element.105.rate_ref, f32[2,240,640]{2,1,0:T(8,128)S(1)} %get-tuple-element.106.home_ref, ...), custom_call_target="tpu_custom_call" | custom-call | bytes 1024 | tf_op jit(solution)/shard_map/update/pallas_call | solution.py:748
  103.9 1.7 %collective-permute-done.28.refs_1_ = bf16[240,640]{1,0:T(8,128)(2,1)S(1)} collective-permute-done((bf16[240,640]{1,0:T(8,128)(2,1)S(1)}, bf16[240,640]{1,0:T(8,128)(2,1)S(1)}, u32[]{:S(2)}, u32[]{:S(2)}) %collective-permute-start.28) | collective-permute-done | bytes 307232 | tf_op jit(solution)/shard_map/ppermute | solution.py:432
  105.7 2.5 %collective-permute-done.29.refs_2_ = bf16[240,640]{1,0:T(8,128)(2,1)S(1)} collective-permute-done((bf16[240,640]{1,0:T(8,128)(2,1)S(1)}, bf16[240,640]{1,0:T(8,128)(2,1)S(1)}, u32[]{:S(2)}, u32[]{:S(2)}) %collective-permute-start.29) | collective-permute-done | bytes 307232 | tf_op jit(solution)/shard_map/ppermute | solution.py:432
  (75 shorter events, 19.9 us)
Async XLA Ops:
  2.7 14.2 %collective-permute-start = (bf16[448,128]{1,0:T(8,128)(2,1)}, bf16[448,128]{1,0:T(8,128)(2,1)S(1)}, u32[]{:S(2)}, u32[]{:S(2)}) collective-permute-start(bf16[448,128]{1,0:T(8,128)(2,1)} %get-tuple-element.63.refs_0_), channel_id=1, source_target_pairs={{0,2},{1,3},{2,0},{3,1},{4,6},{5,7},{6,4},{7,5},{8,10},{9,11},{10,... | collective-permute-start | bytes 344072 | tf_op jit(solution)/shard_map/ppermute | solution.py:432
  5.8 11.9 %collective-permute-start.1 = (bf16[448,128]{1,0:T(8,128)(2,1)}, bf16[448,128]{1,0:T(8,128)(2,1)S(1)}, u32[]{:S(2)}, u32[]{:S(2)}) collective-permute-start(bf16[448,128]{1,0:T(8,128)(2,1)} %get-tuple-element.63.refs_0_), channel_id=1, source_target_pairs={{0,4},{1,5},{2,6},{3,7},{4,0},{5,1},{6,2},{7,3},{8,12},{9,13},{10,... | collective-permute-start | bytes 344072 | tf_op jit(solution)/shard_map/ppermute | solution.py:432
  8.4 9.3 %collective-permute-start.2 = (bf16[448,128]{1,0:T(8,128)(2,1)}, bf16[448,128]{1,0:T(8,128)(2,1)S(1)}, u32[]{:S(2)}, u32[]{:S(2)}) collective-permute-start(bf16[448,128]{1,0:T(8,128)(2,1)} %get-tuple-element.63.refs_0_), channel_id=1, source_target_pairs={{0,6},{1,7},{2,4},{3,5},{4,2},{5,3},{6,0},{7,1},{8,14},{9,15},{10,... | collective-permute-start | bytes 344072 | tf_op jit(solution)/shard_map/ppermute | solution.py:432
  8.4 4.7 %collective-permute-start.3 = (bf16[160,128]{1,0:T(8,128)(2,1)}, bf16[160,128]{1,0:T(8,128)(2,1)S(1)}, u32[]{:S(2)}, u32[]{:S(2)}) collective-permute-start(bf16[160,128]{1,0:T(8,128)(2,1)} %get-tuple-element.59.refs_0_), channel_id=1, source_target_pairs={{0,8},{8,0},{16,24},{24,16},{1,9},{9,1},{17,25},{25,17},{2,10},{10... | collective-permute-start | bytes 122888 | tf_op jit(solution)/shard_map/ppermute | solution.py:432
  13.1 4.6 %collective-permute-start.4 = (bf16[2,160,128]{2,1,0:T(8,128)(2,1)S(1)}, bf16[2,160,128]{2,1,0:T(8,128)(2,1)S(1)}, u32[]{:S(2)}, u32[]{:S(2)}) collective-permute-start(bf16[2,160,128]{2,1,0:T(8,128)(2,1)S(1)} %stack.5.refs_0_), channel_id=1, source_target_pairs={{0,16},{8,24},{16,0},{24,8},{1,17},{9,25},{17,1},{25,9},{2,18},{10... | collective-permute-start | bytes 245768 | tf_op jit(solution)/shard_map/ppermute | solution.py:432
  17.8 5.3 %collective-permute-start.8 = (bf16[2,304,128]{2,1,0:T(8,128)(2,1)S(1)}, bf16[2,304,128]{2,1,0:T(8,128)(2,1)S(1)}, u32[]{:S(2)}, u32[]{:S(2)}) collective-permute-start(bf16[2,304,128]{2,1,0:T(8,128)(2,1)S(1)} %get-tuple-element.72.refs_0_.refs_3_), channel_id=1, source_target_pairs={{0,16},{8,24},{16,0},{24,8},{1,17},{9,25},{17,1},{25,9},{2,18},{10... | collective-permute-start | bytes 466952 | tf_op jit(solution)/shard_map/ppermute | solution.py:432
  19.4 6.8 %collective-permute-start.6 = (bf16[2,304,128]{2,1,0:T(8,128)(2,1)S(1)}, bf16[2,304,128]{2,1,0:T(8,128)(2,1)S(1)}, u32[]{:S(2)}, u32[]{:S(2)}) collective-permute-start(bf16[2,304,128]{2,1,0:T(8,128)(2,1)S(1)} %get-tuple-element.71.refs_0_), channel_id=1, source_target_pairs={{0,8},{8,0},{16,24},{24,16},{1,9},{9,1},{17,25},{25,17},{2,10},{10... | collective-permute-start | bytes 466952 | tf_op jit(solution)/shard_map/ppermute | solution.py:432
  23.1 11.6 %collective-permute-start.9 = (bf16[2,2,304,128]{3,2,1,0:T(8,128)(2,1)S(1)}, bf16[2,2,304,128]{3,2,1,0:T(8,128)(2,1)S(1)}, u32[]{:S(2)}, u32[]{:S(2)}) collective-permute-start(bf16[2,2,304,128]{3,2,1,0:T(8,128)(2,1)S(1)} %stack.9), channel_id=1, source_target_pairs={{0,8},{8,0},{16,24},{24,16},{1,9},{9,1},{17,25},{25,17},{2,10},{10... | collective-permute-start | bytes 933896 | tf_op jit(solution)/shard_map/ppermute | solution.py:432
  26.2 8.4 %collective-permute-start.7 = (bf16[2,2,304,128]{3,2,1,0:T(8,128)(2,1)S(1)}, bf16[2,2,304,128]{3,2,1,0:T(8,128)(2,1)S(1)}, u32[]{:S(2)}, u32[]{:S(2)}) collective-permute-start(bf16[2,2,304,128]{3,2,1,0:T(8,128)(2,1)S(1)} %stack.8), channel_id=1, source_target_pairs={{0,16},{8,24},{16,0},{24,8},{1,17},{9,25},{17,1},{25,9},{2,18},{10... | collective-permute-start | bytes 933896 | tf_op jit(solution)/shard_map/ppermute | solution.py:432
  26.6 8.0 %collective-permute-start.5 = (bf16[4,160,128]{2,1,0:T(8,128)(2,1)S(1)}, bf16[4,160,128]{2,1,0:T(8,128)(2,1)S(1)}, u32[]{:S(2)}, u32[]{:S(2)}) collective-permute-start(bf16[4,160,128]{2,1,0:T(8,128)(2,1)S(1)} %bitcast.23), channel_id=1, source_target_pairs={{0,4},{1,5},{2,6},{3,7},{4,0},{5,1},{6,2},{7,3},{8,12},{9,13},{10,... | collective-permute-start | bytes 491528 | tf_op jit(solution)/shard_map/ppermute | solution.py:432
  35.4 4.1 %collective-permute-start.10 = (bf16[4,240,640]{2,1,0:T(8,128)(2,1)S(1)}, bf16[4,240,640]{2,1,0:T(8,128)(2,1)S(1)}, u32[]{:S(2)}, u32[]{:S(2)}) collective-permute-start(bf16[4,240,640]{2,1,0:T(8,128)(2,1)S(1)} %unpack.2.refs_1_.own_ref), channel_id=1, source_target_pairs={{0,1},{1,0},{2,3},{3,2},{4,5},{5,4},{6,7},{7,6},{8,9},{9,8},{10,11... | collective-permute-start | bytes 3686408 | tf_op jit(solution)/shard_map/ppermute | solution.py:432
  35.5 10.1 %collective-permute-start.14 = (bf16[2,4,160,128]{3,2,1,0:T(8,128)(2,1)S(1)}, bf16[2,4,160,128]{3,2,1,0:T(8,128)(2,1)S(1)}, u32[]{:S(2)}, u32[]{:S(2)}) collective-permute-start(bf16[2,4,160,128]{3,2,1,0:T(8,128)(2,1)S(1)} %stack.7.refs_4_), channel_id=1, source_target_pairs={{0,2},{1,3},{2,0},{3,1},{4,6},{5,7},{6,4},{7,5},{8,10},{9,11},{10,... | collective-permute-start | bytes 983048 | tf_op jit(solution)/shard_map/ppermute | solution.py:432
  36.0 9.6 %collective-permute-start.11 = (bf16[4,144,128]{2,1,0:T(8,128)(2,1)S(1)}, bf16[4,144,128]{2,1,0:T(8,128)(2,1)S(1)}, u32[]{:S(2)}, u32[]{:S(2)}) collective-permute-start(bf16[4,144,128]{2,1,0:T(8,128)(2,1)S(1)} %get-tuple-element.75.refs_0_), channel_id=1, source_target_pairs={{0,8},{8,0},{16,24},{24,16},{1,9},{9,1},{17,25},{25,17},{2,10},{10... | collective-permute-start | bytes 442376 | tf_op jit(solution)/shard_map/ppermute | solution.py:432
  37.4 9.1 %collective-permute-start.12 = (bf16[4,144,128]{2,1,0:T(8,128)(2,1)S(1)}, bf16[4,144,128]{2,1,0:T(8,128)(2,1)S(1)}, u32[]{:S(2)}, u32[]{:S(2)}) collective-permute-start(bf16[4,144,128]{2,1,0:T(8,128)(2,1)S(1)} %get-tuple-element.75.refs_0_), channel_id=1, source_target_pairs={{0,16},{8,24},{16,0},{24,8},{1,17},{9,25},{17,1},{25,9},{2,18},{10... | collective-permute-start | bytes 442376 | tf_op jit(solution)/shard_map/ppermute | solution.py:432
  39.4 7.1 %collective-permute-start.13 = (bf16[4,144,128]{2,1,0:T(8,128)(2,1)S(1)}, bf16[4,144,128]{2,1,0:T(8,128)(2,1)S(1)}, u32[]{:S(2)}, u32[]{:S(2)}) collective-permute-start(bf16[4,144,128]{2,1,0:T(8,128)(2,1)S(1)} %get-tuple-element.75.refs_0_), channel_id=1, source_target_pairs={{0,24},{8,16},{16,8},{24,0},{1,25},{9,17},{17,9},{25,1},{2,26},{10... | collective-permute-start | bytes 442376 | tf_op jit(solution)/shard_map/ppermute | solution.py:432
  47.3 3.0 %collective-permute-start.15 = (bf16[4,240,640]{2,1,0:T(8,128)(2,1)S(1)}, bf16[4,240,640]{2,1,0:T(8,128)(2,1)S(1)}, u32[]{:S(2)}, u32[]{:S(2)}) collective-permute-start(bf16[4,240,640]{2,1,0:T(8,128)(2,1)S(1)} %unpack.3.refs_1_.own_ref), channel_id=1, source_target_pairs={{0,1},{1,0},{2,3},{3,2},{4,5},{5,4},{6,7},{7,6},{8,9},{9,8},{10,11... | collective-permute-start | bytes 3686408 | tf_op jit(solution)/shard_map/ppermute | solution.py:432
  56.6 2.2 %collective-permute-start.16 = (bf16[496,640]{1,0:T(8,128)(2,1)S(1)}, bf16[496,640]{1,0:T(8,128)(2,1)S(1)}, u32[]{:S(2)}, u32[]{:S(2)}) collective-permute-start(bf16[496,640]{1,0:T(8,128)(2,1)S(1)} %get-tuple-element.82.own_ref), channel_id=1, source_target_pairs={{0,1},{1,0},{2,3},{3,2},{4,5},{5,4},{6,7},{7,6},{8,9},{9,8},{10,11... | collective-permute-start | bytes 1904648 | tf_op jit(solution)/shard_map/ppermute | solution.py:432
  58.9 16.6 %collective-permute-start.21 = (bf16[496,640]{1,0:T(8,128)(2,1)S(1)}, bf16[496,640]{1,0:T(8,128)(2,1)S(1)}, u32[]{:S(2)}, u32[]{:S(2)}) collective-permute-start(bf16[496,640]{1,0:T(8,128)(2,1)S(1)} %pair.2.sent_ref), channel_id=1, source_target_pairs={{0,2},{1,3},{2,0},{3,1},{4,6},{5,7},{6,4},{7,5},{8,10},{9,11},{10,... | collective-permute-start | bytes 1904648 | tf_op jit(solution)/shard_map/ppermute | solution.py:432
  70.4 1.7 %collective-permute-start.17 = (bf16[240,640]{1,0:T(8,128)(2,1)S(1)}, bf16[240,640]{1,0:T(8,128)(2,1)S(1)}, u32[]{:S(2)}, u32[]{:S(2)}) collective-permute-start(bf16[240,640]{1,0:T(8,128)(2,1)S(1)} %get-tuple-element.93), channel_id=1, source_target_pairs={{0,1},{1,0},{2,3},{3,2},{4,5},{5,4},{6,7},{7,6},{8,9},{9,8},{10,11... | collective-permute-start | bytes 921608 | tf_op jit(solution)/shard_map/ppermute | solution.py:432
  70.5 6.7 %collective-permute-start.26 = (bf16[480,640]{1,0:T(8,128)(2,1)S(1)}, bf16[480,640]{1,0:T(8,128)(2,1)S(1)}, u32[]{:S(2)}, u32[]{:S(2)}) collective-permute-start(bf16[480,640]{1,0:T(8,128)(2,1)S(1)} %get-tuple-element.86), channel_id=1, source_target_pairs={{0,1},{1,0},{2,3},{3,2},{4,5},{5,4},{6,7},{7,6},{8,9},{9,8},{10,11... | collective-permute-start | bytes 1843208 | tf_op jit(solution)/shard_map/ppermute | solution.py:432
  71.0 2.4 %collective-permute-start.18 = (bf16[240,640]{1,0:T(8,128)(2,1)S(1)}, bf16[240,640]{1,0:T(8,128)(2,1)S(1)}, u32[]{:S(2)}, u32[]{:S(2)}) collective-permute-start(bf16[240,640]{1,0:T(8,128)(2,1)S(1)} %get-tuple-element.94), channel_id=1, source_target_pairs={{0,1},{1,0},{2,3},{3,2},{4,5},{5,4},{6,7},{7,6},{8,9},{9,8},{10,11... | collective-permute-start | bytes 921608 | tf_op jit(solution)/shard_map/ppermute | solution.py:432
  71.0 2.8 %collective-permute-start.19 = (bf16[240,640]{1,0:T(8,128)(2,1)S(1)}, bf16[240,640]{1,0:T(8,128)(2,1)S(1)}, u32[]{:S(2)}, u32[]{:S(2)}) collective-permute-start(bf16[240,640]{1,0:T(8,128)(2,1)S(1)} %get-tuple-element.95), channel_id=1, source_target_pairs={{0,1},{1,0},{2,3},{3,2},{4,5},{5,4},{6,7},{7,6},{8,9},{9,8},{10,11... | collective-permute-start | bytes 921608 | tf_op jit(solution)/shard_map/ppermute | solution.py:432
  72.1 2.2 %collective-permute-start.20 = (bf16[240,640]{1,0:T(8,128)(2,1)S(1)}, bf16[240,640]{1,0:T(8,128)(2,1)S(1)}, u32[]{:S(2)}, u32[]{:S(2)}) collective-permute-start(bf16[240,640]{1,0:T(8,128)(2,1)S(1)} %get-tuple-element.96), channel_id=1, source_target_pairs={{0,1},{1,0},{2,3},{3,2},{4,5},{5,4},{6,7},{7,6},{8,9},{9,8},{10,11... | collective-permute-start | bytes 921608 | tf_op jit(solution)/shard_map/ppermute | solution.py:432
  75.8 15.8 %collective-permute-start.22 = (bf16[240,640]{1,0:T(8,128)(2,1)S(1)}, bf16[240,640]{1,0:T(8,128)(2,1)S(1)}, u32[]{:S(2)}, u32[]{:S(2)}) collective-permute-start(bf16[240,640]{1,0:T(8,128)(2,1)S(1)} %get-tuple-element.101), channel_id=1, source_target_pairs={{0,2},{1,3},{2,0},{3,1},{4,6},{5,7},{6,4},{7,5},{8,10},{9,11},{10,... | collective-permute-start | bytes 921608 | tf_op jit(solution)/shard_map/ppermute | solution.py:432
  77.2 15.4 %copy-start.5 = (bf16[240,160]{0,1:T(8,128)(2,1)S(1)}, bf16[240,160]{0,1:T(8,128)(2,1)}, u32[]{:S(2)}) copy-start(bf16[240,160]{0,1:T(8,128)(2,1)} %param.17) | copy-start | bytes 230404
  77.2 15.4 %copy-start.6 = (bf16[240,160]{0,1:T(8,128)(2,1)S(1)}, bf16[240,160]{0,1:T(8,128)(2,1)}, u32[]{:S(2)}) copy-start(bf16[240,160]{0,1:T(8,128)(2,1)} %param.18) | copy-start | bytes 230404
  77.3 18.0 %collective-permute-start.27 = (bf16[256,640]{1,0:T(8,128)(2,1)S(1)}, bf16[256,640]{1,0:T(8,128)(2,1)S(1)}, u32[]{:S(2)}, u32[]{:S(2)}) collective-permute-start(bf16[256,640]{1,0:T(8,128)(2,1)S(1)} %merge.2.sent_ref), channel_id=1, source_target_pairs={{0,4},{1,5},{2,6},{3,7},{4,0},{5,1},{6,2},{7,3},{8,12},{9,13},{10,... | collective-permute-start | bytes 983048 | tf_op jit(solution)/shard_map/ppermute | solution.py:432
  91.7 14.0 %collective-permute-start.28 = (bf16[240,640]{1,0:T(8,128)(2,1)S(1)}, bf16[240,640]{1,0:T(8,128)(2,1)S(1)}, u32[]{:S(2)}, u32[]{:S(2)}) collective-permute-start(bf16[240,640]{1,0:T(8,128)(2,1)S(1)} %get-tuple-element.112), channel_id=1, source_target_pairs={{0,2},{1,3},{2,0},{3,1},{4,6},{5,7},{6,4},{7,5},{8,10},{9,11},{10,... | collective-permute-start | bytes 921608 | tf_op jit(solution)/shard_map/ppermute | solution.py:432
  91.7 16.4 %collective-permute-start.29 = (bf16[240,640]{1,0:T(8,128)(2,1)S(1)}, bf16[240,640]{1,0:T(8,128)(2,1)S(1)}, u32[]{:S(2)}, u32[]{:S(2)}) collective-permute-start(bf16[240,640]{1,0:T(8,128)(2,1)S(1)} %merge.3), channel_id=1, source_target_pairs={{0,4},{1,5},{2,6},{3,7},{4,0},{5,1},{6,2},{7,3},{8,12},{9,13},{10,... | collective-permute-start | bytes 921608 | tf_op jit(solution)/shard_map/ppermute | solution.py:432
  92.8 6.6 %collective-permute-start.23 = (bf16[2,304,128]{2,1,0:T(8,128)(2,1)S(1)}, bf16[2,304,128]{2,1,0:T(8,128)(2,1)S(1)}, u32[]{:S(2)}, u32[]{:S(2)}) collective-permute-start(bf16[2,304,128]{2,1,0:T(8,128)(2,1)S(1)} %pack_rates.1.refs_0_), channel_id=1, source_target_pairs={{0,8},{8,0},{16,24},{24,16},{1,9},{9,1},{17,25},{25,17},{2,10},{10... | collective-permute-start | bytes 466952 | tf_op jit(solution)/shard_map/ppermute | solution.py:432
  94.3 7.3 %collective-permute-start.24 = (bf16[2,304,128]{2,1,0:T(8,128)(2,1)S(1)}, bf16[2,304,128]{2,1,0:T(8,128)(2,1)S(1)}, u32[]{:S(2)}, u32[]{:S(2)}) collective-permute-start(bf16[2,304,128]{2,1,0:T(8,128)(2,1)S(1)} %pack_rates.1.refs_0_), channel_id=1, source_target_pairs={{0,16},{8,24},{16,0},{24,8},{1,17},{9,25},{17,1},{25,9},{2,18},{10... | collective-permute-start | bytes 466952 | tf_op jit(solution)/shard_map/ppermute | solution.py:432
  95.3 6.4 %collective-permute-start.25 = (bf16[2,304,128]{2,1,0:T(8,128)(2,1)S(1)}, bf16[2,304,128]{2,1,0:T(8,128)(2,1)S(1)}, u32[]{:S(2)}, u32[]{:S(2)}) collective-permute-start(bf16[2,304,128]{2,1,0:T(8,128)(2,1)S(1)} %pack_rates.1.refs_0_), channel_id=1, source_target_pairs={{0,24},{8,16},{16,8},{24,0},{1,25},{9,17},{17,9},{25,1},{2,26},{10... | collective-permute-start | bytes 466952 | tf_op jit(solution)/shard_map/ppermute | solution.py:432
  (6 other events, 54.5 us)

commit v9 on v8

--- a/solution.py
+++ b/solution.py
@@ -65,17 +65,17 @@
     return sums[0:1] + sums[16:17] + sums[32:33]
 
 
-def norm_stats(read, rows, channels, same_ref, copy=None):
+def norm_stats(read, rows, channels, same_ref, total=None):
     counted = rows * (channels // GN_GROUPS)
     steps = rows // CHUNK
-    total = lax.fori_loop(
-        0,
-        steps,
-        lambda i, acc: acc + read(i).reshape(CHUNK // 8, 8, channels).sum(axis=0),
-        jnp.zeros((8, channels), F32),
-    ).sum(axis=0, keepdims=True)
-    if copy is not None:
-        copy.wait()
+    if total is None:
+        total = lax.fori_loop(
+            0,
+            steps,
+            lambda i, acc: acc + read(i).reshape(CHUNK // 8, 8, channels).sum(axis=0),
+            jnp.zeros((8, channels), F32),
+        )
+    total = total.sum(axis=0, keepdims=True)
     same_group = same_ref[...]
     centre = spread(total, same_group) * (1.0 / counted)
 
@@ -110,7 +110,9 @@
     return copies
 
 
-def enter_kernel(points, clip_hbm, same_hbm, padded_ref, clip_ref, same_ref, sems):
+def enter_kernel(
+    points, clip_hbm, same_hbm, padded_ref, turned_ref, clip_ref, same_ref, sems
+):
     rows, channels = clip_ref.shape
     for copy in fetch((clip_hbm, same_hbm), (clip_ref, same_ref), sems):
         copy.wait()
@@ -122,7 +124,9 @@
     @pl.loop(0, rows // CHUNK)
     def _(i):
         normal = (clip_ref[at(i)].astype(F32) - centre) * inverse
-        padded_ref[at(i, points)] = (normal / (1.0 + jnp.exp(-normal))).astype(BF16)
+        act = (normal / (1.0 + jnp.exp(-normal))).astype(BF16)
+        padded_ref[at(i, points)] = act
+        turned_ref[:, at(i)] = act.T
 
 
 def taps_of(padded_ref, start, size, points):
@@ -147,27 +151,26 @@
 
 
 def first_kernel(points, scale, in_ref, bias_ref, *refs):
-    weight_refs = refs[:-2]
-    hidden_ref, full_ref = refs[-2:]
-    half = hidden_ref.shape[0] // 2
-    bias = bias_ref[...]
+    weight_refs = refs[:-3]
+    hidden_ref, sums_ref, full_ref = refs[-3:]
+    rows, channels = hidden_ref.shape
     weight_ref = full_weight(weight_refs, full_ref)
-
-    @pl.loop(0, 2)
-    def _(i):
-        start = pl.multiple_of(i * half, 64)
-        mixed = jnp.dot(
-            taps_of(in_ref, start, half, points), weight_ref[...], preferred_element_type=F32
-        )
-        hidden_ref[pl.ds(start, half)] = scale * mixed + bias
+    mixed = jnp.dot(
+        taps_of(in_ref, 0, rows, points), weight_ref[...], preferred_element_type=F32
+    )
+    hidden = scale * mixed + bias_ref[...]
+    hidden_ref[...] = hidden
+    sums_ref[...] = hidden.reshape(rows // 8, 8, channels).sum(axis=0)
 
 
 def norm_kernel(
-    points, hidden_ref, same_hbm, normal_ref, inverse_ref, padded_ref, turned_ref, same_ref, sems
+    points, hidden_ref, sums_ref, same_ref,
+    normal_ref, inverse_ref, padded_ref, turned_ref, mean_ref,
 ):
     rows, channels = normal_ref.shape
-    (copy,) = fetch((same_hbm,), (same_ref,), sems)
-    centre, inverse = norm_stats(lambda i: hidden_ref[at(i)], rows, channels, same_ref, copy)
+    centre, inverse = norm_stats(
+        lambda i: hidden_ref[at(i)], rows, channels, same_ref, sums_ref[...]
+    )
     inverse_ref[...] = inverse
     clear_edges(padded_ref, points)
 
@@ -179,31 +182,23 @@
         padded_ref[at(i, points)] = act
         turned_ref[:, at(i)] = act.T
 
-
-def second_kernel(points, scale, in_ref, clip_hbm, target_hbm, *refs):
-    weight_refs = refs[:-5]
-    error_ref, full_ref, clip_ref, target_ref, sems = refs[-5:]
-    copies = fetch((clip_hbm, target_hbm), (clip_ref, target_ref), sems)
+    ones = jnp.ones((rows, 128), BF16)
+    mean_ref[...] = jnp.dot(turned_ref[...], ones, preferred_element_type=F32) * (1.0 / rows)
+
+
+def second_kernel(points, scale, in_ref, clip_ref, target_ref, *refs):
+    weight_refs = refs[:-2]
+    error_ref, full_ref = refs[-2:]
     rows = clip_ref.shape[0]
-    half = rows // 2
     clear_edges(error_ref, points)
     weight_ref = full_weight(weight_refs, full_ref)
     if len(weight_refs) == 1:
         full_ref[...] = weight_ref[...]
-    for copy in copies:
-        copy.wait()
-
-    @pl.loop(0, 2)
-    def _(i):
-        start = pl.multiple_of(i * half, 64)
-        mixed = jnp.dot(
-            taps_of(in_ref, start, half, points), weight_ref[...], preferred_element_type=F32
-        )
-        here = pl.ds(start, half)
-        output = clip_ref[here].astype(F32) + scale * mixed
-        error_ref[pl.ds(pl.multiple_of(start + points, 64), half)] = (
-            output - target_ref[here].astype(F32)
-        ).astype(BF16)
+    mixed = jnp.dot(
+        taps_of(in_ref, 0, rows, points), weight_ref[...], preferred_element_type=F32
+    )
+    output = clip_ref[...].astype(F32) + scale * mixed
+    error_ref[points : points + rows] = (output - target_ref[...].astype(F32)).astype(BF16)
 
 
 def back_kernel(points, scale, error_ref, weight_ref, grad_ref):
@@ -323,25 +318,22 @@
         refs[0][...] = factors
 
 
-def mean_and_sums(scale, turned, cotangent):
-    rows = turned.shape[1]
-    mean = jnp.dot(turned, jnp.ones((rows, 128), BF16), preferred_element_type=F32) * (1.0 / rows)
-    sums = jnp.dot(jnp.ones((16, rows), BF16), cotangent, preferred_element_type=F32)
-    return mean, scale * sums[0:8]
-
-
-def half_kernel(points, scale, odd, me_ref, turned_ref, cotangent_ref, *refs):
+def half_kernel(points, scale, odd, me_ref, turned_ref, cotangent_ref, mean_ref, *refs):
     refs, total_ref = refs[:-1], refs[-1]
     channels, rows = turned_ref.shape
     if odd:
-        away_ref, home_ref, mean_ref, sums_ref = refs
-        mean, sums = mean_and_sums(scale, turned_ref[...], cotangent_ref[pl.ds(points, rows)])
-        mean_ref[...] = mean
+        away_ref, home_ref, sums_ref = refs
+        sums = jnp.dot(
+            jnp.ones((16, rows), BF16),
+            cotangent_ref[pl.ds(points, rows)],
+            preferred_element_type=F32,
+        )
+        sums = scale * sums[0:8]
         sums_ref[...] = sums
-        factors = split_rows(mean.T[0:1]) + split_rows(sums[0:1])
+        factors = split_rows(mean_ref[...].T[0:1]) + split_rows(sums[0:1])
         factors += [jnp.zeros((FACTOR_ROWS - MEMBER_ROWS, channels), F32)]
     else:
-        mean_ref, sums_ref, away_ref, home_ref = refs
+        sums_ref, away_ref, home_ref = refs
     size, block = total_ref.shape[0] // 2, home_ref.shape[1]
     chip = lax.shift_right_logical(me_ref[0], 1)
     for first in range(2):
@@ -376,19 +368,18 @@
         away_ref[2 * block :] = jnp.concatenate(factors, axis=0).astype(BF16)
 
 
-def odd_half(turned, cotangent, me, block, points, scale):
+def odd_half(turned, cotangent, me, block, points, scale, mean):
     channels = turned.shape[0]
     return call(
         functools.partial(half_kernel, points, scale, 1),
         [
             ((2 * block + FACTOR_ROWS, channels), BF16),
             ((2, block, channels), F32),
-            ((channels, 128), F32),
             ((8, channels), F32),
         ],
         [pltpu.VMEM((4 * block, channels), F32)],
-        "gradient_odd", smem(1) + vmem(2), 20,
-    )(me, turned, cotangent)
+        "gradient_odd", smem(1) + vmem(3), 20,
+    )(me, turned, cotangent, mean)
 
 
 def even_half(turned, cotangent, me, block, points, scale, mean, sums):
@@ -795,25 +786,27 @@
     def enter(clip):
         return call(
             functools.partial(enter_kernel, points),
-            [((padded, channels), BF16)],
+            [((padded, channels), BF16), ((channels, rows), BF16)],
             [
                 pltpu.VMEM((rows, channels), BF16),
                 pltpu.VMEM(same_group.shape, BF16),
                 pltpu.SemaphoreType.DMA((2,)),
             ],
             "enter", hbm(2), 12,
-        )(clip, same_group)[0]
-
-    weight_one, weight_two, own_one, rates, act_one, bias_row = weights_and_rates(
+        )(clip, same_group)
+
+    weight_one, weight_two, own_one, rates, acts, bias_row = weights_and_rates(
         n_group, n_member, conv1_weight, conv2_weight, rate1, rate2, group, me, clip, enter, bias_row
     )
+
+    act_one, turned_one = acts
 
     def weight_specs(weight):
         return vmem(1) if len(weight) == 1 else smem(1) + vmem(2)
 
-    (hidden,) = call(
+    hidden, sums = call(
         functools.partial(first_kernel, points, scale),
-        [((rows, channels), F32)],
+        [((rows, channels), F32), ((8, channels), F32)],
         [pltpu.VMEM((3 * channels, channels), BF16)],
         "conv", vmem(2) + weight_specs(weight_one), 20,
     )(act_one, bias_row, *weight_one)
@@ -821,29 +814,30 @@
     own_two = weight_two[1]
     if len(weight_two) == 2:
         weight_two = weight_two[:1]
-    normal, inverse, act_two, turned_two = call(
+    normal, inverse, act_two, turned_two, mean_two = call(
         functools.partial(norm_kernel, points),
         [
             ((rows, channels), F32),
             ((1, channels), F32),
             ((padded, channels), BF16),
             ((channels, rows), BF16),
+            ((channels, 128), F32),
         ],
-        [pltpu.VMEM(same_group.shape, BF16), pltpu.SemaphoreType.DMA((1,))],
-        "norm", vmem(1) + hbm(1), 20,
-    )(order_after(hidden, weight_two[:2]), same_group)
+        [], "norm", vmem(3), 20,
+    )(order_after(hidden, weight_two[:2]), sums, same_group)
     error, full_two = call(
         functools.partial(second_kernel, points, scale),
         [((padded, channels), BF16), ((3 * channels, channels), BF16)],
-        [pltpu.VMEM((rows, channels), BF16)] * 2 + [pltpu.SemaphoreType.DMA((2,))],
-        "conv_error", vmem(1) + hbm(2) + weight_specs(weight_two), 24,
+        [], "conv_error", vmem(3) + weight_specs(weight_two), 24,
     )(act_two, clip, target, *weight_two)
     staged = n_member == 8 and own_rows % 16 == 0
     if staged:
-        away_two, home_two, *means = odd_half(turned_two, error, me, own_rows, points, scale)
+        away_two, home_two, sums_two = odd_half(
+            turned_two, error, me, own_rows, points, scale, mean_two
+        )
         received_two = swap(away_two, "member", n_member, 1)
         away_even, home_even = even_half(
-            turned_two, error, me, own_rows, points, scale, *means
+            turned_two, error, me, own_rows, points, scale, mean_two, sums_two
         )
         received_even = swap(away_even, "member", n_member, 1)
         half_two = pair_sums(away_two, home_two, order_after(received_two, away_even))
@@ -869,7 +863,7 @@
         "norm_back", vmem(3) + hbm(1), 20,
     )(grad_act, normal, inverse, same_group)
     away_one, home_one, _ = gradient(
-        act_one, grad_hidden, me, n_member, points, scale, False
+        turned_one, grad_hidden, me, n_member, points, scale, False
     )
     received_one = [swap(part, "member", n_member, 1) for part in away_one]
     if staged:

time: 109 us -> 108 us (level)
  Pallas kernels: 33.9 us -> 32.5 us
  transfers between devices with their start and end apart: 30 -> 30, of which waited for: 17 -> 19; matrix products, arithmetic and copies ran while one was open for 1% -> 1% of each run, Pallas kernels for 21% -> 21%
where the time goes in v9:
time: 108 us
  waiting for transfers between devices  39.6 us (37%)
  Pallas kernels  32.5 us (30%)
  starting transfers between devices  32 us (30%)
  between operations  2.26 us (2%)
  matrix products  1.53 us (1%)
    ppermute x30, waiting for transfers between devices, swap(): return lax.ppermute(value, axis, [(i, i ^ offset) for i in range(size)])  39.6 us
    ppermute x30, starting transfers between devices, swap(): return lax.ppermute(value, axis, [(i, i ^ offset) for i in range(size)])  32 us
    pallas_call x1, Pallas kernels, gradient(): call(functools.partial(grad_kernel, points, scale, block, centred), [((ch...  3.76 us
    pallas_call x1, Pallas kernels, shards(): call(functools.partial(back_kernel, points, scale), [((rows, channels), F...  3.47 us
    pallas_call x1, Pallas kernels, shards(): call(functools.partial(second_kernel, points, scale), [((padded, channels...  3.26 us
    pallas_call x1, Pallas kernels, shards(): call(functools.partial(first_kernel, points, scale), [((rows, channels),...  3.17 us
    pallas_call x1, Pallas kernels, enter(): call(functools.partial(enter_kernel, points), [((padded, channels), BF16)...  2.68 us
    pallas_call x1, Pallas kernels, shards(): call(functools.partial(norm_kernel, points), [((rows, channels), F32), ((...  2.43 us
  transfers between devices with their start and end apart: 30, of which 19 were waited for; matrix products, arithmetic and copies ran while one was open for 1% of the time, Pallas kernels for 21%

profile of v9, /device:TPU:0, one launch (start us, length us, event | category | flops | bytes accessed | tf_op | source)
XLA Modules:
  0.0 108.0 jit_solution(1622912331880571412)
XLA Ops:
  0.7 2.0 %pack.1 = (bf16[448,128]{1,0:T(8,128)(2,1)}, bf16[160,128]{1,0:T(8,128)(2,1)}) custom-call(bf16[160,240]{1,0:T(8,128)(2,1)} %bitcast.29, bf16[160,240]{1,0:T(8,128)(2,1)} %bitcast.30, s32[1]{0:T(128)} %bitcast.refs_2_.group_ref, s32[1]{0:T(128)} %bitcast.3.refs_3_.refs_0_.me_ref), custom_call_target="tpu_custom_call" | custom-call | bytes 1024 | tf_op jit(solution)/shard_map/pack/pallas_call | solution.py:564
  2.7 3.1 %collective-permute-start = (bf16[448,128]{1,0:T(8,128)(2,1)}, bf16[448,128]{1,0:T(8,128)(2,1)S(1)}, u32[]{:S(2)}, u32[]{:S(2)}) collective-permute-start(bf16[448,128]{1,0:T(8,128)(2,1)} %get-tuple-element.70.refs_0_), channel_id=1, source_target_pairs={{0,2},{1,3},{2,0},{3,1},{4,6},{5,7},{6,4},{7,5},{8,10},{9,11},{10,... | collective-permute-start | bytes 344072 | tf_op jit(solution)/shard_map/ppermute | solution.py:423
  5.8 2.6 %collective-permute-start.1 = (bf16[448,128]{1,0:T(8,128)(2,1)}, bf16[448,128]{1,0:T(8,128)(2,1)S(1)}, u32[]{:S(2)}, u32[]{:S(2)}) collective-permute-start(bf16[448,128]{1,0:T(8,128)(2,1)} %get-tuple-element.70.refs_0_), channel_id=1, source_target_pairs={{0,4},{1,5},{2,6},{3,7},{4,0},{5,1},{6,2},{7,3},{8,12},{9,13},{10,... | collective-permute-start | bytes 344072 | tf_op jit(solution)/shard_map/ppermute | solution.py:423
  8.4 1.7 %collective-permute-start.3 = (bf16[160,128]{1,0:T(8,128)(2,1)}, bf16[160,128]{1,0:T(8,128)(2,1)S(1)}, u32[]{:S(2)}, u32[]{:S(2)}) collective-permute-start(bf16[160,128]{1,0:T(8,128)(2,1)} %get-tuple-element.64.refs_0_), channel_id=1, source_target_pairs={{0,8},{8,0},{16,24},{24,16},{1,9},{9,1},{17,25},{25,17},{2,10},{10... | collective-permute-start | bytes 122888 | tf_op jit(solution)/shard_map/ppermute | solution.py:423
  13.1 1.6 %collective-permute-start.4 = (bf16[2,160,128]{2,1,0:T(8,128)(2,1)S(1)}, bf16[2,160,128]{2,1,0:T(8,128)(2,1)S(1)}, u32[]{:S(2)}, u32[]{:S(2)}) collective-permute-start(bf16[2,160,128]{2,1,0:T(8,128)(2,1)S(1)} %stack.5.refs_0_), channel_id=1, source_target_pairs={{0,16},{8,24},{16,0},{24,8},{1,17},{9,25},{17,1},{25,9},{2,18},{10... | collective-permute-start | bytes 245768 | tf_op jit(solution)/shard_map/ppermute | solution.py:423
  14.7 2.7 %enter.1 = (bf16[1024,640]{1,0:T(8,128)(2,1)S(1)}, bf16[640,896]{1,0:T(8,128)(2,1)S(1)}) custom-call(bf16[896,640]{1,0:T(8,128)(2,1)S(1)} %bitcast.20, bf16[640,640]{1,0:T(8,128)(2,1)S(1)} %copy-done.1), custom_call_target="tpu_custom_call" | custom-call | bytes 1024 | tf_op jit(solution)/shard_map/enter/pallas_call | solution.py:787
  17.8 1.6 %collective-permute-start.8 = (bf16[2,304,128]{2,1,0:T(8,128)(2,1)S(1)}, bf16[2,304,128]{2,1,0:T(8,128)(2,1)S(1)}, u32[]{:S(2)}, u32[]{:S(2)}) collective-permute-start(bf16[2,304,128]{2,1,0:T(8,128)(2,1)S(1)} %get-tuple-element.79.refs_0_.refs_3_), channel_id=1, source_target_pairs={{0,16},{8,24},{16,0},{24,8},{1,17},{9,25},{17,1},{25,9},{2,18},{10... | collective-permute-start | bytes 466952 | tf_op jit(solution)/shard_map/ppermute | solution.py:423
  19.4 1.5 %collective-permute-start.6 = (bf16[2,304,128]{2,1,0:T(8,128)(2,1)S(1)}, bf16[2,304,128]{2,1,0:T(8,128)(2,1)S(1)}, u32[]{:S(2)}, u32[]{:S(2)}) collective-permute-start(bf16[2,304,128]{2,1,0:T(8,128)(2,1)S(1)} %get-tuple-element.78.refs_0_), channel_id=1, source_target_pairs={{0,8},{8,0},{16,24},{24,16},{1,9},{9,1},{17,25},{25,17},{2,10},{10... | collective-permute-start | bytes 466952 | tf_op jit(solution)/shard_map/ppermute | solution.py:423
  20.9 2.2 %collective-permute-done.8.refs_1_.refs_4_ = bf16[2,304,128]{2,1,0:T(8,128)(2,1)S(1)} collective-permute-done((bf16[2,304,128]{2,1,0:T(8,128)(2,1)S(1)}, bf16[2,304,128]{2,1,0:T(8,128)(2,1)S(1)}, u32[]{:S(2)}, u32[]{:S(2)}) %collective-permute-start.8) | collective-permute-done | bytes 155680 | tf_op jit(solution)/shard_map/ppermute | solution.py:423
  23.1 1.6 %collective-permute-start.9 = (bf16[2,2,304,128]{3,2,1,0:T(8,128)(2,1)S(1)}, bf16[2,2,304,128]{3,2,1,0:T(8,128)(2,1)S(1)}, u32[]{:S(2)}, u32[]{:S(2)}) collective-permute-start(bf16[2,2,304,128]{3,2,1,0:T(8,128)(2,1)S(1)} %stack.9), channel_id=1, source_target_pairs={{0,8},{8,0},{16,24},{24,16},{1,9},{9,1},{17,25},{25,17},{2,10},{10... | collective-permute-start | bytes 933896 | tf_op jit(solution)/shard_map/ppermute | solution.py:423
  24.7 1.6 %collective-permute-done.6.refs_1_ = bf16[2,304,128]{2,1,0:T(8,128)(2,1)S(1)} collective-permute-done((bf16[2,304,128]{2,1,0:T(8,128)(2,1)S(1)}, bf16[2,304,128]{2,1,0:T(8,128)(2,1)S(1)}, u32[]{:S(2)}, u32[]{:S(2)}) %collective-permute-start.6) | collective-permute-done | bytes 155680 | tf_op jit(solution)/shard_map/ppermute | solution.py:423
  26.6 2.5 %collective-permute-start.5 = (bf16[4,160,128]{2,1,0:T(8,128)(2,1)S(1)}, bf16[4,160,128]{2,1,0:T(8,128)(2,1)S(1)}, u32[]{:S(2)}, u32[]{:S(2)}) collective-permute-start(bf16[4,160,128]{2,1,0:T(8,128)(2,1)S(1)} %bitcast.23), channel_id=1, source_target_pairs={{0,4},{1,5},{2,6},{3,7},{4,0},{5,1},{6,2},{7,3},{8,12},{9,13},{10,... | collective-permute-start | bytes 491528 | tf_op jit(solution)/shard_map/ppermute | solution.py:423
  29.1 5.5 %collective-permute-done.5.refs_1_ = bf16[4,160,128]{2,1,0:T(8,128)(2,1)S(1)} collective-permute-done((bf16[4,160,128]{2,1,0:T(8,128)(2,1)S(1)}, bf16[4,160,128]{2,1,0:T(8,128)(2,1)S(1)}, u32[]{:S(2)}, u32[]{:S(2)}) %collective-permute-start.5) | collective-permute-done | bytes 163872 | tf_op jit(solution)/shard_map/ppermute | solution.py:423
  37.4 2.0 %collective-permute-start.12 = (bf16[4,144,128]{2,1,0:T(8,128)(2,1)S(1)}, bf16[4,144,128]{2,1,0:T(8,128)(2,1)S(1)}, u32[]{:S(2)}, u32[]{:S(2)}) collective-permute-start(bf16[4,144,128]{2,1,0:T(8,128)(2,1)S(1)} %get-tuple-element.84.refs_0_), channel_id=1, source_target_pairs={{0,16},{8,24},{16,0},{24,8},{1,17},{9,25},{17,1},{25,9},{2,18},{10... | collective-permute-start | bytes 442376 | tf_op jit(solution)/shard_map/ppermute | solution.py:423
  39.5 3.2 %conv.1 = (f32[896,640]{1,0:T(8,128)S(1)}, f32[8,640]{1,0:T(8,128)S(1)}) custom-call(bf16[1024,640]{1,0:T(8,128)(2,1)S(1)} %get-tuple-element.81.in_ref, f32[1,640]{1,0:T(1,128)S(1)} %fusion.6.bias_ref, s32[1]{0:T(128)} %bitcast.3.refs_3_.refs_0_.me_ref, bf16[4,240,640]{2,1,0:T(8,128)(2,1)S(1)} %unpack.2.refs_1_.own_ref, ...), custom_call_target="tpu_custom_call" | custom-call | bytes 1024 | tf_op jit(solution)/shard_map/conv/pallas_call | solution.py:807
  42.7 2.9 %collective-permute-done.14.refs_5_ = bf16[2,4,160,128]{3,2,1,0:T(8,128)(2,1)S(1)} collective-permute-done((bf16[2,4,160,128]{3,2,1,0:T(8,128)(2,1)S(1)}, bf16[2,4,160,128]{3,2,1,0:T(8,128)(2,1)S(1)}, u32[]{:S(2)}, u32[]{:S(2)}) %collective-permute-start.14) | collective-permute-done | bytes 327712 | tf_op jit(solution)/shard_map/ppermute | solution.py:423
  47.3 2.4 %norm.1 = (f32[896,640]{1,0:T(8,128)S(1)}, f32[1,640]{1,0:T(1,128)S(1)}, bf16[1024,640]{1,0:T(8,128)(2,1)S(1)}, bf16[640,896]{1,0:T(8,128)(2,1)S(1)}, f32[640,128]{1,0:T(8,128)S(1)}) custom-call(f32[896,640]{1,0:T(8,128)S(1)} %get-tuple-element.87.hidden_ref, f32[8,640]{1,0:T(8,128)S(1)} %get-tuple-element.88.sums_ref, bf16[640,640]{1,0:T(8,128)(2,1)S(1)} %copy-done.1), custom_call_target="tpu_custom_call" | custom-call | bytes 1024 | tf_op jit(solution)/shard_map/norm/pallas_call | solution.py:817
  50.2 3.3 %conv_error.1 = (bf16[1024,640]{1,0:T(8,128)(2,1)S(1)}, bf16[1920,640]{1,0:T(8,128)(2,1)S(1)}) custom-call(bf16[1024,640]{1,0:T(8,128)(2,1)S(1)} %get-tuple-element.89.in_ref, bf16[896,640]{1,0:T(8,128)(2,1)S(1)} %bitcast.21, bf16[896,640]{1,0:T(8,128)(2,1)S(1)} %bitcast.22, s32[1]{0:T(128)} %bitcast.3.refs_3_.refs_0_.me_ref, ...), custom_call_target="tpu_custom_call" | custom-call | bytes 1024 | tf_op jit(solution)/shard_map/conv_error/pallas_call | solution.py:828
  53.5 2.3 %gradient_odd.1 = (bf16[496,640]{1,0:T(8,128)(2,1)S(1)}, f32[2,240,640]{2,1,0:T(8,128)S(1)}, f32[8,640]{1,0:T(8,128)S(1)}) custom-call(s32[1]{0:T(128)} %bitcast.3.refs_3_.refs_0_.me_ref, bf16[640,896]{1,0:T(8,128)(2,1)S(1)} %get-tuple-element.91.turned_ref, bf16[1024,640]{1,0:T(8,128)(2,1)S(1)} %get-tuple-element.98.cotangent_ref.error_ref, ...), custom_call_target="tpu_custom_call" | custom-call | bytes 1024 | tf_op jit(solution)/shard_map/gradient_odd/pallas_call | solution.py:373
  56.0 1.8 %gradient_even.1 = (bf16[480,640]{1,0:T(8,128)(2,1)S(1)}, f32[2,240,640]{2,1,0:T(8,128)S(1)}) custom-call(s32[1]{0:T(128)} %bitcast.3.refs_3_.refs_0_.me_ref, bf16[640,896]{1,0:T(8,128)(2,1)S(1)} %get-tuple-element.91.turned_ref, bf16[1024,640]{1,0:T(8,128)(2,1)S(1)} %get-tuple-element.98.cotangent_ref.error_ref, f32[640,128]{1,0:T(8,128)S(1)} %get-tuple-element.92.mean_ref, ...), custom_call_target="tpu_custom_call" | custom-call | bytes 1024 | tf_op jit(solution)/shard_map/gradient_even/pallas_call | solution.py:387
  58.0 1.5 %collective-permute-start.21 = (bf16[496,640]{1,0:T(8,128)(2,1)S(1)}, bf16[496,640]{1,0:T(8,128)(2,1)S(1)}, u32[]{:S(2)}, u32[]{:S(2)}) collective-permute-start(bf16[496,640]{1,0:T(8,128)(2,1)S(1)} %pair.2.sent_ref), channel_id=1, source_target_pairs={{0,2},{1,3},{2,0},{3,1},{4,6},{5,7},{6,4},{7,5},{8,10},{9,11},{10,... | collective-permute-start | bytes 1904648 | tf_op jit(solution)/shard_map/ppermute | solution.py:423
  59.5 3.5 %back.1.act_grad_ref = f32[896,640]{1,0:T(8,128)S(1)} custom-call(bf16[1024,640]{1,0:T(8,128)(2,1)S(1)} %get-tuple-element.98.cotangent_ref.error_ref, bf16[1920,640]{1,0:T(8,128)(2,1)S(1)} %get-tuple-element.99.weight_ref), custom_call_target="tpu_custom_call" | custom-call | bytes 1024 | tf_op jit(solution)/shard_map/back/pallas_call | solution.py:851
  63.0 2.0 %norm_back.1.cotangent_ref = bf16[1024,640]{1,0:T(8,128)(2,1)S(1)} custom-call(f32[896,640]{1,0:T(8,128)S(1)} %back.1.act_grad_ref, f32[896,640]{1,0:T(8,128)S(1)} %get-tuple-element.100.normal_ref, f32[1,640]{1,0:T(1,128)S(1)} %get-tuple-element.101.inverse_ref, bf16[640,640]{1,0:T(8,128)(2,1)S(1)} %copy-done.1), custom_call_target="tpu_custom_call" | custom-call | bytes 1024 | tf_op jit(solution)/shard_map/norm_back/pallas_call | solution.py:855
  65.0 3.8 %gradient.1 = (f32[4,240,640]{2,1,0:T(8,128)S(1)}, bf16[240,640]{1,0:T(8,128)(2,1)S(1)}, bf16[240,640]{1,0:T(8,128)(2,1)S(1)}, bf16[240,640]{1,0:T(8,128)(2,1)S(1)}, bf16[240,640]{1,0:T(8,128)(2,1)S(1)}) custom-call(s32[1]{0:T(128)} %bitcast.3.refs_3_.refs_0_.me_ref, bf16[640,896]{1,0:T(8,128)(2,1)S(1)} %get-tuple-element.80.act_ref, ...), custom_call_target="tpu_custom_call" | custom-call | bytes 1024 | tf_op jit(solution)/shard_map/gradient/pallas_call | solution.py:403
  72.7 1.9 %collective-permute-done.21.received_ref.half_ref = bf16[496,640]{1,0:T(8,128)(2,1)S(1)} collective-permute-done((bf16[496,640]{1,0:T(8,128)(2,1)S(1)}, bf16[496,640]{1,0:T(8,128)(2,1)S(1)}, u32[]{:S(2)}, u32[]{:S(2)}) %collective-permute-start.21) | collective-permute-done | bytes 634912 | tf_op jit(solution)/shard_map/ppermute | solution.py:423
  74.8 1.5 %collective-permute-start.22 = (bf16[240,640]{1,0:T(8,128)(2,1)S(1)}, bf16[240,640]{1,0:T(8,128)(2,1)S(1)}, u32[]{:S(2)}, u32[]{:S(2)}) collective-permute-start(bf16[240,640]{1,0:T(8,128)(2,1)S(1)} %get-tuple-element.111), channel_id=1, source_target_pairs={{0,2},{1,3},{2,0},{3,1},{4,6},{5,7},{6,4},{7,5},{8,10},{9,11},{10,... | collective-permute-start | bytes 921608 | tf_op jit(solution)/shard_map/ppermute | solution.py:423
  76.5 2.3 %collective-permute-start.27 = (bf16[256,640]{1,0:T(8,128)(2,1)S(1)}, bf16[256,640]{1,0:T(8,128)(2,1)S(1)}, u32[]{:S(2)}, u32[]{:S(2)}) collective-permute-start(bf16[256,640]{1,0:T(8,128)(2,1)S(1)} %merge.2.sent_ref), channel_id=1, source_target_pairs={{0,4},{1,5},{2,6},{3,7},{4,0},{5,1},{6,2},{7,3},{8,12},{9,13},{10,... | collective-permute-start | bytes 983048 | tf_op jit(solution)/shard_map/ppermute | solution.py:423
  78.7 11.8 %collective-permute-done.22.received_ref = bf16[240,640]{1,0:T(8,128)(2,1)S(1)} collective-permute-done((bf16[240,640]{1,0:T(8,128)(2,1)S(1)}, bf16[240,640]{1,0:T(8,128)(2,1)S(1)}, u32[]{:S(2)}, u32[]{:S(2)}) %collective-permute-start.22) | collective-permute-done | bytes 307232 | tf_op jit(solution)/shard_map/ppermute | solution.py:423
  91.8 1.5 %collective-permute-start.23 = (bf16[2,304,128]{2,1,0:T(8,128)(2,1)S(1)}, bf16[2,304,128]{2,1,0:T(8,128)(2,1)S(1)}, u32[]{:S(2)}, u32[]{:S(2)}) collective-permute-start(bf16[2,304,128]{2,1,0:T(8,128)(2,1)S(1)} %pack_rates.1.refs_0_), channel_id=1, source_target_pairs={{0,8},{8,0},{16,24},{24,16},{1,9},{9,1},{17,25},{25,17},{2,10},{10... | collective-permute-start | bytes 466952 | tf_op jit(solution)/shard_map/ppermute | solution.py:423
  95.4 2.8 %collective-permute-done.23.refs_1_ = bf16[2,304,128]{2,1,0:T(8,128)(2,1)S(1)} collective-permute-done((bf16[2,304,128]{2,1,0:T(8,128)(2,1)S(1)}, bf16[2,304,128]{2,1,0:T(8,128)(2,1)S(1)}, u32[]{:S(2)}, u32[]{:S(2)}) %collective-permute-start.23) | collective-permute-done | bytes 155680 | tf_op jit(solution)/shard_map/ppermute | solution.py:423
  101.3 1.9 %update.2 = f32[240,640]{1,0:T(8,128)} custom-call(s32[1]{0:T(128)} %bitcast.3.refs_3_.refs_0_.me_ref, bf16[4,240,640]{2,1,0:T(8,128)(2,1)S(1)} %unpack.3.refs_1_.own_ref, bf16[240,640]{1,0:T(8,128)(2,1)S(1)} %get-tuple-element.115.rate_ref, f32[2,240,640]{2,1,0:T(8,128)S(1)} %get-tuple-element.116.home_ref, ...), custom_call_target="tpu_custom_call" | custom-call | bytes 1024 | tf_op jit(solution)/shard_map/update/pallas_call | solution.py:739
  104.4 2.6 %collective-permute-done.29.refs_2_ = bf16[240,640]{1,0:T(8,128)(2,1)S(1)} collective-permute-done((bf16[240,640]{1,0:T(8,128)(2,1)S(1)}, bf16[240,640]{1,0:T(8,128)(2,1)S(1)}, u32[]{:S(2)}, u32[]{:S(2)}) %collective-permute-start.29) | collective-permute-done | bytes 307232 | tf_op jit(solution)/shard_map/ppermute | solution.py:423
  (75 shorter events, 20.7 us)
Async XLA Ops:
  2.7 14.7 %collective-permute-start = (bf16[448,128]{1,0:T(8,128)(2,1)}, bf16[448,128]{1,0:T(8,128)(2,1)S(1)}, u32[]{:S(2)}, u32[]{:S(2)}) collective-permute-start(bf16[448,128]{1,0:T(8,128)(2,1)} %get-tuple-element.70.refs_0_), channel_id=1, source_target_pairs={{0,2},{1,3},{2,0},{3,1},{4,6},{5,7},{6,4},{7,5},{8,10},{9,11},{10,... | collective-permute-start | bytes 344072 | tf_op jit(solution)/shard_map/ppermute | solution.py:423
  5.8 11.9 %collective-permute-start.1 = (bf16[448,128]{1,0:T(8,128)(2,1)}, bf16[448,128]{1,0:T(8,128)(2,1)S(1)}, u32[]{:S(2)}, u32[]{:S(2)}) collective-permute-start(bf16[448,128]{1,0:T(8,128)(2,1)} %get-tuple-element.70.refs_0_), channel_id=1, source_target_pairs={{0,4},{1,5},{2,6},{3,7},{4,0},{5,1},{6,2},{7,3},{8,12},{9,13},{10,... | collective-permute-start | bytes 344072 | tf_op jit(solution)/shard_map/ppermute | solution.py:423
  8.4 9.3 %collective-permute-start.2 = (bf16[448,128]{1,0:T(8,128)(2,1)}, bf16[448,128]{1,0:T(8,128)(2,1)S(1)}, u32[]{:S(2)}, u32[]{:S(2)}) collective-permute-start(bf16[448,128]{1,0:T(8,128)(2,1)} %get-tuple-element.70.refs_0_), channel_id=1, source_target_pairs={{0,6},{1,7},{2,4},{3,5},{4,2},{5,3},{6,0},{7,1},{8,14},{9,15},{10,... | collective-permute-start | bytes 344072 | tf_op jit(solution)/shard_map/ppermute | solution.py:423
  8.4 4.7 %collective-permute-start.3 = (bf16[160,128]{1,0:T(8,128)(2,1)}, bf16[160,128]{1,0:T(8,128)(2,1)S(1)}, u32[]{:S(2)}, u32[]{:S(2)}) collective-permute-start(bf16[160,128]{1,0:T(8,128)(2,1)} %get-tuple-element.64.refs_0_), channel_id=1, source_target_pairs={{0,8},{8,0},{16,24},{24,16},{1,9},{9,1},{17,25},{25,17},{2,10},{10... | collective-permute-start | bytes 122888 | tf_op jit(solution)/shard_map/ppermute | solution.py:423
  13.1 4.6 %collective-permute-start.4 = (bf16[2,160,128]{2,1,0:T(8,128)(2,1)S(1)}, bf16[2,160,128]{2,1,0:T(8,128)(2,1)S(1)}, u32[]{:S(2)}, u32[]{:S(2)}) collective-permute-start(bf16[2,160,128]{2,1,0:T(8,128)(2,1)S(1)} %stack.5.refs_0_), channel_id=1, source_target_pairs={{0,16},{8,24},{16,0},{24,8},{1,17},{9,25},{17,1},{25,9},{2,18},{10... | collective-permute-start | bytes 245768 | tf_op jit(solution)/shard_map/ppermute | solution.py:423
  17.8 5.3 %collective-permute-start.8 = (bf16[2,304,128]{2,1,0:T(8,128)(2,1)S(1)}, bf16[2,304,128]{2,1,0:T(8,128)(2,1)S(1)}, u32[]{:S(2)}, u32[]{:S(2)}) collective-permute-start(bf16[2,304,128]{2,1,0:T(8,128)(2,1)S(1)} %get-tuple-element.79.refs_0_.refs_3_), channel_id=1, source_target_pairs={{0,16},{8,24},{16,0},{24,8},{1,17},{9,25},{17,1},{25,9},{2,18},{10... | collective-permute-start | bytes 466952 | tf_op jit(solution)/shard_map/ppermute | solution.py:423
  19.4 6.9 %collective-permute-start.6 = (bf16[2,304,128]{2,1,0:T(8,128)(2,1)S(1)}, bf16[2,304,128]{2,1,0:T(8,128)(2,1)S(1)}, u32[]{:S(2)}, u32[]{:S(2)}) collective-permute-start(bf16[2,304,128]{2,1,0:T(8,128)(2,1)S(1)} %get-tuple-element.78.refs_0_), channel_id=1, source_target_pairs={{0,8},{8,0},{16,24},{24,16},{1,9},{9,1},{17,25},{25,17},{2,10},{10... | collective-permute-start | bytes 466952 | tf_op jit(solution)/shard_map/ppermute | solution.py:423
  23.1 11.6 %collective-permute-start.9 = (bf16[2,2,304,128]{3,2,1,0:T(8,128)(2,1)S(1)}, bf16[2,2,304,128]{3,2,1,0:T(8,128)(2,1)S(1)}, u32[]{:S(2)}, u32[]{:S(2)}) collective-permute-start(bf16[2,2,304,128]{3,2,1,0:T(8,128)(2,1)S(1)} %stack.9), channel_id=1, source_target_pairs={{0,8},{8,0},{16,24},{24,16},{1,9},{9,1},{17,25},{25,17},{2,10},{10... | collective-permute-start | bytes 933896 | tf_op jit(solution)/shard_map/ppermute | solution.py:423
  26.3 8.4 %collective-permute-start.7 = (bf16[2,2,304,128]{3,2,1,0:T(8,128)(2,1)S(1)}, bf16[2,2,304,128]{3,2,1,0:T(8,128)(2,1)S(1)}, u32[]{:S(2)}, u32[]{:S(2)}) collective-permute-start(bf16[2,2,304,128]{3,2,1,0:T(8,128)(2,1)S(1)} %stack.8), channel_id=1, source_target_pairs={{0,16},{8,24},{16,0},{24,8},{1,17},{9,25},{17,1},{25,9},{2,18},{10... | collective-permute-start | bytes 933896 | tf_op jit(solution)/shard_map/ppermute | solution.py:423
  26.6 8.0 %collective-permute-start.5 = (bf16[4,160,128]{2,1,0:T(8,128)(2,1)S(1)}, bf16[4,160,128]{2,1,0:T(8,128)(2,1)S(1)}, u32[]{:S(2)}, u32[]{:S(2)}) collective-permute-start(bf16[4,160,128]{2,1,0:T(8,128)(2,1)S(1)} %bitcast.23), channel_id=1, source_target_pairs={{0,4},{1,5},{2,6},{3,7},{4,0},{5,1},{6,2},{7,3},{8,12},{9,13},{10,... | collective-permute-start | bytes 491528 | tf_op jit(solution)/shard_map/ppermute | solution.py:423
  35.4 4.1 %collective-permute-start.10 = (bf16[4,240,640]{2,1,0:T(8,128)(2,1)S(1)}, bf16[4,240,640]{2,1,0:T(8,128)(2,1)S(1)}, u32[]{:S(2)}, u32[]{:S(2)}) collective-permute-start(bf16[4,240,640]{2,1,0:T(8,128)(2,1)S(1)} %unpack.2.refs_1_.own_ref), channel_id=1, source_target_pairs={{0,1},{1,0},{2,3},{3,2},{4,5},{5,4},{6,7},{7,6},{8,9},{9,8},{10,11... | collective-permute-start | bytes 3686408 | tf_op jit(solution)/shard_map/ppermute | solution.py:423
  35.5 10.1 %collective-permute-start.14 = (bf16[2,4,160,128]{3,2,1,0:T(8,128)(2,1)S(1)}, bf16[2,4,160,128]{3,2,1,0:T(8,128)(2,1)S(1)}, u32[]{:S(2)}, u32[]{:S(2)}) collective-permute-start(bf16[2,4,160,128]{3,2,1,0:T(8,128)(2,1)S(1)} %stack.7.refs_4_), channel_id=1, source_target_pairs={{0,2},{1,3},{2,0},{3,1},{4,6},{5,7},{6,4},{7,5},{8,10},{9,11},{10,... | collective-permute-start | bytes 983048 | tf_op jit(solution)/shard_map/ppermute | solution.py:423
  36.0 9.6 %collective-permute-start.11 = (bf16[4,144,128]{2,1,0:T(8,128)(2,1)S(1)}, bf16[4,144,128]{2,1,0:T(8,128)(2,1)S(1)}, u32[]{:S(2)}, u32[]{:S(2)}) collective-permute-start(bf16[4,144,128]{2,1,0:T(8,128)(2,1)S(1)} %get-tuple-element.84.refs_0_), channel_id=1, source_target_pairs={{0,8},{8,0},{16,24},{24,16},{1,9},{9,1},{17,25},{25,17},{2,10},{10... | collective-permute-start | bytes 442376 | tf_op jit(solution)/shard_map/ppermute | solution.py:423
  37.4 9.1 %collective-permute-start.12 = (bf16[4,144,128]{2,1,0:T(8,128)(2,1)S(1)}, bf16[4,144,128]{2,1,0:T(8,128)(2,1)S(1)}, u32[]{:S(2)}, u32[]{:S(2)}) collective-permute-start(bf16[4,144,128]{2,1,0:T(8,128)(2,1)S(1)} %get-tuple-element.84.refs_0_), channel_id=1, source_target_pairs={{0,16},{8,24},{16,0},{24,8},{1,17},{9,25},{17,1},{25,9},{2,18},{10... | collective-permute-start | bytes 442376 | tf_op jit(solution)/shard_map/ppermute | solution.py:423
  39.4 7.1 %collective-permute-start.13 = (bf16[4,144,128]{2,1,0:T(8,128)(2,1)S(1)}, bf16[4,144,128]{2,1,0:T(8,128)(2,1)S(1)}, u32[]{:S(2)}, u32[]{:S(2)}) collective-permute-start(bf16[4,144,128]{2,1,0:T(8,128)(2,1)S(1)} %get-tuple-element.84.refs_0_), channel_id=1, source_target_pairs={{0,24},{8,16},{16,8},{24,0},{1,25},{9,17},{17,9},{25,1},{2,26},{10... | collective-permute-start | bytes 442376 | tf_op jit(solution)/shard_map/ppermute | solution.py:423
  47.2 3.0 %collective-permute-start.15 = (bf16[4,240,640]{2,1,0:T(8,128)(2,1)S(1)}, bf16[4,240,640]{2,1,0:T(8,128)(2,1)S(1)}, u32[]{:S(2)}, u32[]{:S(2)}) collective-permute-start(bf16[4,240,640]{2,1,0:T(8,128)(2,1)S(1)} %unpack.3.refs_1_.own_ref), channel_id=1, source_target_pairs={{0,1},{1,0},{2,3},{3,2},{4,5},{5,4},{6,7},{7,6},{8,9},{9,8},{10,11... | collective-permute-start | bytes 3686408 | tf_op jit(solution)/shard_map/ppermute | solution.py:423
  55.8 2.1 %collective-permute-start.16 = (bf16[496,640]{1,0:T(8,128)(2,1)S(1)}, bf16[496,640]{1,0:T(8,128)(2,1)S(1)}, u32[]{:S(2)}, u32[]{:S(2)}) collective-permute-start(bf16[496,640]{1,0:T(8,128)(2,1)S(1)} %get-tuple-element.93.own_ref), channel_id=1, source_target_pairs={{0,1},{1,0},{2,3},{3,2},{4,5},{5,4},{6,7},{7,6},{8,9},{9,8},{10,11... | collective-permute-start | bytes 1904648 | tf_op jit(solution)/shard_map/ppermute | solution.py:423
  58.0 16.5 %collective-permute-start.21 = (bf16[496,640]{1,0:T(8,128)(2,1)S(1)}, bf16[496,640]{1,0:T(8,128)(2,1)S(1)}, u32[]{:S(2)}, u32[]{:S(2)}) collective-permute-start(bf16[496,640]{1,0:T(8,128)(2,1)S(1)} %pair.2.sent_ref), channel_id=1, source_target_pairs={{0,2},{1,3},{2,0},{3,1},{4,6},{5,7},{6,4},{7,5},{8,10},{9,11},{10,... | collective-permute-start | bytes 1904648 | tf_op jit(solution)/shard_map/ppermute | solution.py:423
  68.8 1.7 %collective-permute-start.17 = (bf16[240,640]{1,0:T(8,128)(2,1)S(1)}, bf16[240,640]{1,0:T(8,128)(2,1)S(1)}, u32[]{:S(2)}, u32[]{:S(2)}) collective-permute-start(bf16[240,640]{1,0:T(8,128)(2,1)S(1)} %get-tuple-element.103), channel_id=1, source_target_pairs={{0,1},{1,0},{2,3},{3,2},{4,5},{5,4},{6,7},{7,6},{8,9},{9,8},{10,11... | collective-permute-start | bytes 921608 | tf_op jit(solution)/shard_map/ppermute | solution.py:423
  68.9 7.5 %collective-permute-start.26 = (bf16[480,640]{1,0:T(8,128)(2,1)S(1)}, bf16[480,640]{1,0:T(8,128)(2,1)S(1)}, u32[]{:S(2)}, u32[]{:S(2)}) collective-permute-start(bf16[480,640]{1,0:T(8,128)(2,1)S(1)} %get-tuple-element.96), channel_id=1, source_target_pairs={{0,1},{1,0},{2,3},{3,2},{4,5},{5,4},{6,7},{7,6},{8,9},{9,8},{10,11... | collective-permute-start | bytes 1843208 | tf_op jit(solution)/shard_map/ppermute | solution.py:423
  69.4 2.4 %collective-permute-start.18 = (bf16[240,640]{1,0:T(8,128)(2,1)S(1)}, bf16[240,640]{1,0:T(8,128)(2,1)S(1)}, u32[]{:S(2)}, u32[]{:S(2)}) collective-permute-start(bf16[240,640]{1,0:T(8,128)(2,1)S(1)} %get-tuple-element.104), channel_id=1, source_target_pairs={{0,1},{1,0},{2,3},{3,2},{4,5},{5,4},{6,7},{7,6},{8,9},{9,8},{10,11... | collective-permute-start | bytes 921608 | tf_op jit(solution)/shard_map/ppermute | solution.py:423
  69.5 2.8 %collective-permute-start.19 = (bf16[240,640]{1,0:T(8,128)(2,1)S(1)}, bf16[240,640]{1,0:T(8,128)(2,1)S(1)}, u32[]{:S(2)}, u32[]{:S(2)}) collective-permute-start(bf16[240,640]{1,0:T(8,128)(2,1)S(1)} %get-tuple-element.105), channel_id=1, source_target_pairs={{0,1},{1,0},{2,3},{3,2},{4,5},{5,4},{6,7},{7,6},{8,9},{9,8},{10,11... | collective-permute-start | bytes 921608 | tf_op jit(solution)/shard_map/ppermute | solution.py:423
  70.5 2.2 %collective-permute-start.20 = (bf16[240,640]{1,0:T(8,128)(2,1)S(1)}, bf16[240,640]{1,0:T(8,128)(2,1)S(1)}, u32[]{:S(2)}, u32[]{:S(2)}) collective-permute-start(bf16[240,640]{1,0:T(8,128)(2,1)S(1)} %get-tuple-element.106), channel_id=1, source_target_pairs={{0,1},{1,0},{2,3},{3,2},{4,5},{5,4},{6,7},{7,6},{8,9},{9,8},{10,11... | collective-permute-start | bytes 921608 | tf_op jit(solution)/shard_map/ppermute | solution.py:423
  74.8 15.7 %collective-permute-start.22 = (bf16[240,640]{1,0:T(8,128)(2,1)S(1)}, bf16[240,640]{1,0:T(8,128)(2,1)S(1)}, u32[]{:S(2)}, u32[]{:S(2)}) collective-permute-start(bf16[240,640]{1,0:T(8,128)(2,1)S(1)} %get-tuple-element.111), channel_id=1, source_target_pairs={{0,2},{1,3},{2,0},{3,1},{4,6},{5,7},{6,4},{7,5},{8,10},{9,11},{10,... | collective-permute-start | bytes 921608 | tf_op jit(solution)/shard_map/ppermute | solution.py:423
  76.4 15.3 %copy-start.5 = (bf16[240,160]{0,1:T(8,128)(2,1)S(1)}, bf16[240,160]{0,1:T(8,128)(2,1)}, u32[]{:S(2)}) copy-start(bf16[240,160]{0,1:T(8,128)(2,1)} %param.17) | copy-start | bytes 230404
  76.4 15.3 %copy-start.6 = (bf16[240,160]{0,1:T(8,128)(2,1)S(1)}, bf16[240,160]{0,1:T(8,128)(2,1)}, u32[]{:S(2)}) copy-start(bf16[240,160]{0,1:T(8,128)(2,1)} %param.18) | copy-start | bytes 230404
  76.5 18.3 %collective-permute-start.27 = (bf16[256,640]{1,0:T(8,128)(2,1)S(1)}, bf16[256,640]{1,0:T(8,128)(2,1)S(1)}, u32[]{:S(2)}, u32[]{:S(2)}) collective-permute-start(bf16[256,640]{1,0:T(8,128)(2,1)S(1)} %merge.2.sent_ref), channel_id=1, source_target_pairs={{0,4},{1,5},{2,6},{3,7},{4,0},{5,1},{6,2},{7,3},{8,12},{9,13},{10,... | collective-permute-start | bytes 983048 | tf_op jit(solution)/shard_map/ppermute | solution.py:423
  90.5 13.9 %collective-permute-start.28 = (bf16[240,640]{1,0:T(8,128)(2,1)S(1)}, bf16[240,640]{1,0:T(8,128)(2,1)S(1)}, u32[]{:S(2)}, u32[]{:S(2)}) collective-permute-start(bf16[240,640]{1,0:T(8,128)(2,1)S(1)} %get-tuple-element.122), channel_id=1, source_target_pairs={{0,2},{1,3},{2,0},{3,1},{4,6},{5,7},{6,4},{7,5},{8,10},{9,11},{10,... | collective-permute-start | bytes 921608 | tf_op jit(solution)/shard_map/ppermute | solution.py:423
  90.6 16.4 %collective-permute-start.29 = (bf16[240,640]{1,0:T(8,128)(2,1)S(1)}, bf16[240,640]{1,0:T(8,128)(2,1)S(1)}, u32[]{:S(2)}, u32[]{:S(2)}) collective-permute-start(bf16[240,640]{1,0:T(8,128)(2,1)S(1)} %merge.3), channel_id=1, source_target_pairs={{0,4},{1,5},{2,6},{3,7},{4,0},{5,1},{6,2},{7,3},{8,12},{9,13},{10,... | collective-permute-start | bytes 921608 | tf_op jit(solution)/shard_map/ppermute | solution.py:423
  91.8 6.3 %collective-permute-start.23 = (bf16[2,304,128]{2,1,0:T(8,128)(2,1)S(1)}, bf16[2,304,128]{2,1,0:T(8,128)(2,1)S(1)}, u32[]{:S(2)}, u32[]{:S(2)}) collective-permute-start(bf16[2,304,128]{2,1,0:T(8,128)(2,1)S(1)} %pack_rates.1.refs_0_), channel_id=1, source_target_pairs={{0,8},{8,0},{16,24},{24,16},{1,9},{9,1},{17,25},{25,17},{2,10},{10... | collective-permute-start | bytes 466952 | tf_op jit(solution)/shard_map/ppermute | solution.py:423
  93.3 6.3 %collective-permute-start.24 = (bf16[2,304,128]{2,1,0:T(8,128)(2,1)S(1)}, bf16[2,304,128]{2,1,0:T(8,128)(2,1)S(1)}, u32[]{:S(2)}, u32[]{:S(2)}) collective-permute-start(bf16[2,304,128]{2,1,0:T(8,128)(2,1)S(1)} %pack_rates.1.refs_0_), channel_id=1, source_target_pairs={{0,16},{8,24},{16,0},{24,8},{1,17},{9,25},{17,1},{25,9},{2,18},{10... | collective-permute-start | bytes 466952 | tf_op jit(solution)/shard_map/ppermute | solution.py:423
  94.8 6.1 %collective-permute-start.25 = (bf16[2,304,128]{2,1,0:T(8,128)(2,1)S(1)}, bf16[2,304,128]{2,1,0:T(8,128)(2,1)S(1)}, u32[]{:S(2)}, u32[]{:S(2)}) collective-permute-start(bf16[2,304,128]{2,1,0:T(8,128)(2,1)S(1)} %pack_rates.1.refs_0_), channel_id=1, source_target_pairs={{0,24},{8,16},{16,8},{24,0},{1,25},{9,17},{17,9},{25,1},{2,26},{10... | collective-permute-start | bytes 466952 | tf_op jit(solution)/shard_map/ppermute | solution.py:423
  (6 other events, 56.1 us)
